TPU v7x, 32 devices: a whole 2x2x4 slice. The times are simulated.
32 devices in a mesh: grp: 2 (over core), ep: 16 (over z, y, x).
Axes of the slice: x: 2, y: 2, z: 4, core: 2. Of those that a mesh axis runs over, the one named last changes fastest.
Arguments:
- layer_input: bfloat16 [4096, 2048], P(('grp', 'ep')), may hold values from -6 to 6
- attention_gain: bfloat16 [2048], P('ep'), may hold values from 0.099609375 to 1.8984375
- query_weight: bfloat16 [2048, 3072], P('ep'), may hold values from -0.125 to 0.125
- latent_weight: bfloat16 [2048, 576], P('ep'), may hold values from -0.125 to 0.125
- latent_gain: bfloat16 [512], P('ep'), may hold values from 0.099609375 to 1.8984375
- expand_weight: bfloat16 [512, 4096], P('ep'), may hold values from -0.25 to 0.25
- output_weight: bfloat16 [2048, 2048], P('ep'), may hold values from -4 to 4
- feedforward_gain: bfloat16 [2048], P('ep'), may hold values from 0.099609375 to 1.8984375
- router_weight: bfloat16 [2048, 16], P('ep'), may hold values from -0.0625 to 0.0625
- shared_gate: bfloat16 [2048, 2816], P('ep'), may hold values from -0.125 to 0.125
- shared_up: bfloat16 [2048, 2816], P('ep'), may hold values from -0.125 to 0.125
- shared_down: bfloat16 [2816, 2048], P('ep'), may hold values from -0.109375 to 0.109375
- expert_gate: bfloat16 [16, 2048, 1408], P('ep'), may hold values from -0.125 to 0.125
- expert_up: bfloat16 [16, 2048, 1408], P('ep'), may hold values from -0.125 to 0.125
- expert_down: bfloat16 [16, 1408, 2048], P('ep'), may hold values from -0.625 to 0.625
- expert_routes: int32 [4096, 6], P(('grp', 'ep')), may hold values from 0 to 15, all different within a row
- prefix_length: int32 [2], P('grp'), may hold values from 128 to 1024
- output_grad: bfloat16 [4096, 2048], P(('grp', 'ep')), may hold values from -6 to 6
Outputs:
- layer_output: bfloat16 [4096, 2048], P(('grp', 'ep'))
- input_grad: bfloat16 [4096, 2048], P(('grp', 'ep'))
- attention_gain_grad: float32 [2048], P(('grp', 'ep'))
- query_weight_grad: float32 [2048, 3072], P(('grp', 'ep'))
- latent_weight_grad: float32 [2048, 576], P(('grp', 'ep'))
- latent_gain_grad: float32 [512], P(('grp', 'ep'))
- expand_weight_grad: float32 [512, 4096], P(('grp', 'ep'))
- output_weight_grad: float32 [2048, 2048], P(('grp', 'ep'))
- feedforward_gain_grad: float32 [2048], P(('grp', 'ep'))
- router_weight_grad: float32 [2048, 16], P(('grp', 'ep'))
- shared_gate_grad: float32 [2048, 2816], P(('grp', 'ep'))
- shared_up_grad: float32 [2048, 2816], P(('grp', 'ep'))
- shared_down_grad: float32 [2816, 2048], P(('grp', 'ep'))
- expert_gate_grad: float32 [16, 2048, 1408], P('ep', 'grp')
- expert_up_grad: float32 [16, 2048, 1408], P('ep', 'grp')
- expert_down_grad: float32 [16, 1408, 2048], P('ep', 'grp')
Inputs may be any that keep to these rules, and one draw needn't show every extreme that they name: `expert_routes`: each row names 6 different experts.
All inputs are finite; a program needn't handle non-finite values.
Results may differ from a plain program's by a relative error of at most 0.02.
Values may be sent and summed in bfloat16 or wider, within the bound.
A program may use at most 384 MiB of HBM per device.

v0:
```python
import math

import jax
import jax.numpy as jnp
from jax import lax
from jax.sharding import PartitionSpec as P

D = 2048
HEADS = 16
NOPE = 128
ROPE = 64
VH = 128
LATENT = 512
TOPK = 6


EPSILON = 1e-06
MASKED = -1e30
HIGHEST = lax.Precision.HIGHEST


def product(form, left, right):
    return jnp.einsum(form, left, right, preferred_element_type=jnp.float32)


def exact_product(form, left, right):
    return jnp.einsum(form, left, right, precision=HIGHEST)


def rms_scale(values):
    return lax.rsqrt(jnp.mean(values * values, axis=-1, keepdims=True) + EPSILON)


def rotary_tables(positions):
    halfway = ROPE // 2
    inverse = 10000.0 ** (-(jnp.arange(halfway, dtype=jnp.float32) * 2.0 / ROPE))
    angles = positions[:, None] * inverse[None, :]
    return (jnp.cos(angles), jnp.sin(angles))


def rotate(values, cos_table, sin_table):
    halfway = values.shape[-1] // 2
    first = values[..., :halfway]
    second = values[..., halfway:]
    return jnp.concatenate(
        [first * cos_table - second * sin_table, second * cos_table + first * sin_table], axis=-1
    )


def unrotate(grads, cos_table, sin_table):
    halfway = grads.shape[-1] // 2
    first = grads[..., :halfway]
    second = grads[..., halfway:]
    return jnp.concatenate(
        [first * cos_table + second * sin_table, second * cos_table - first * sin_table], axis=-1
    )


def norm_back(grad_unit, unit_values, scale_values):
    return scale_values * (
        grad_unit - unit_values * jnp.mean(grad_unit * unit_values, axis=-1, keepdims=True)
    )


def silu_back(grad_hidden, gate_value, up_value):
    sigmoid = jax.nn.sigmoid(gate_value)
    grad_gate = grad_hidden * up_value * sigmoid * (1.0 + gate_value * (1.0 - sigmoid))
    grad_up = grad_hidden * gate_value * sigmoid
    return (grad_gate.astype(jnp.bfloat16), grad_up.astype(jnp.bfloat16))


def attention_scores(query_b, key_nope, key_rope, visible):
    scale = 1.0 / math.sqrt(NOPE + ROPE)
    scores = product("qhd,khd->hqk", query_b[..., :NOPE], key_nope)
    scores = scores + product("qhd,kd->hqk", query_b[..., NOPE:], key_rope)
    return jnp.where(visible[None], scores * scale, MASKED)


def per_device(
    layer_input,
    attention_gain,
    query_weight,
    latent_weight,
    latent_gain,
    expand_weight,
    output_weight,
    feedforward_gain,
    router_weight,
    shared_gate,
    shared_up,
    shared_down,
    expert_gate,
    expert_up,
    expert_down,
    expert_routes,
    prefix_length,
    output_grad,
):
    group_size = lax.axis_size("ep")
    position = lax.axis_index("ep")
    tokens = layer_input.shape[0]
    length = tokens * group_size
    capacity = tokens * TOPK * 4 // (3 * group_size)
    scale = 1.0 / math.sqrt(NOPE + ROPE)
    attention_gain, query_weight, latent_weight, latent_gain, expand_weight, output_weight = (
        lax.all_gather(attention_gain, "ep", axis=0, tiled=True),
        lax.all_gather(query_weight, "ep", axis=0, tiled=True),
        lax.all_gather(latent_weight, "ep", axis=0, tiled=True),
        lax.all_gather(latent_gain, "ep", axis=0, tiled=True),
        lax.all_gather(expand_weight, "ep", axis=0, tiled=True),
        lax.all_gather(output_weight, "ep", axis=0, tiled=True),
    )
    residual_in = layer_input.astype(jnp.float32)
    input_scale = rms_scale(residual_in)
    input_unit = residual_in * input_scale
    attn_gain_values = attention_gain.astype(jnp.float32)
    normed = (input_unit * attn_gain_values).astype(jnp.bfloat16)
    query_rows = position * tokens + jnp.arange(tokens, dtype=jnp.int32)
    cos_table, sin_table = rotary_tables(query_rows.astype(jnp.float32))
    query_raw = product("td,dc->tc", normed, query_weight).reshape(tokens, HEADS, NOPE + ROPE)
    query_b = jnp.concatenate(
        [
            query_raw[..., :NOPE],
            rotate(query_raw[..., NOPE:], cos_table[:, None], sin_table[:, None]),
        ],
        axis=-1,
    ).astype(jnp.bfloat16)
    compressed = product("td,dc->tc", normed, latent_weight)
    latent_raw = compressed[:, :LATENT]
    latent_scale = rms_scale(latent_raw)
    latent_unit = latent_raw * latent_scale
    latent_gain_values = latent_gain.astype(jnp.float32)
    latent_b = (latent_unit * latent_gain_values).astype(jnp.bfloat16)
    key_rope_b = rotate(compressed[:, LATENT:], cos_table, sin_table).astype(jnp.bfloat16)
    all_latent, all_rope = (
        lax.all_gather(latent_b, "ep", axis=0, tiled=True),
        lax.all_gather(key_rope_b, "ep", axis=0, tiled=True),
    )
    expanded = product("tl,lc->tc", all_latent, expand_weight).astype(jnp.bfloat16)
    expanded = expanded.reshape(length, HEADS, NOPE + VH)
    key_nope = expanded[..., :NOPE]
    values = expanded[..., NOPE:]
    key_places = jnp.arange(length, dtype=jnp.int32)
    visible = (key_places[None, :] <= query_rows[:, None]) | (
        key_places[None, :] < prefix_length[0]
    )
    scores = attention_scores(query_b, key_nope, all_rope, visible)
    row_max = jnp.max(scores, axis=-1, keepdims=True)
    log_total = row_max + jnp.log(jnp.sum(jnp.exp(scores - row_max), axis=-1, keepdims=True))
    weights_b = jnp.exp(scores - log_total).astype(jnp.bfloat16)
    attended_b = (
        product("hqk,khd->qhd", weights_b, values).astype(jnp.bfloat16).reshape(tokens, HEADS * VH)
    )
    residual_mid = residual_in + product("ta,ad->td", attended_b, output_weight)
    feedforward_gain, router_weight, shared_gate, shared_up, shared_down = (
        lax.all_gather(feedforward_gain, "ep", axis=0, tiled=True),
        lax.all_gather(router_weight, "ep", axis=0, tiled=True),
        lax.all_gather(shared_gate, "ep", axis=0, tiled=True),
        lax.all_gather(shared_up, "ep", axis=0, tiled=True),
        lax.all_gather(shared_down, "ep", axis=0, tiled=True),
    )
    mid_scale = rms_scale(residual_mid)
    mid_unit = residual_mid * mid_scale
    ffn_gain_values = feedforward_gain.astype(jnp.float32)
    ffn_in = (mid_unit * ffn_gain_values).astype(jnp.bfloat16)
    logits = product("td,de->te", ffn_in, router_weight)
    router_probs = jax.nn.softmax(logits, axis=-1)
    expert_ids = jnp.arange(group_size, dtype=jnp.int32)
    route_hot = (expert_routes[:, :, None] == expert_ids).astype(jnp.float32)
    gate_values = jnp.sum(route_hot * router_probs[:, None, :], axis=-1)
    shared_g = product("td,df->tf", ffn_in, shared_gate)
    shared_u = product("td,df->tf", ffn_in, shared_up)
    shared_hidden = (jax.nn.silu(shared_g) * shared_u).astype(jnp.bfloat16)
    shared_out = product("tf,fd->td", shared_hidden, shared_down)
    flat_routes = expert_routes.reshape(tokens * TOPK)
    expert_hot = (flat_routes[:, None] == expert_ids).astype(jnp.int32)
    place = jnp.sum((jnp.cumsum(expert_hot, axis=0) - 1) * expert_hot, axis=1)
    kept_mask = place < capacity
    kept_values = kept_mask.reshape(tokens, TOPK).astype(jnp.float32)
    slot_index = flat_routes * capacity + place
    slot_match = (
        (slot_index[:, None] == jnp.arange(group_size * capacity, dtype=jnp.int32))
        & kept_mask[:, None]
    ).astype(jnp.float32)
    dispatch = jnp.sum(slot_match.reshape(tokens, TOPK, group_size * capacity), axis=1).astype(
        jnp.bfloat16
    )
    outgoing = (
        product("ts,td->sd", dispatch, ffn_in).astype(jnp.bfloat16).reshape(group_size, capacity, D)
    )
    incoming = lax.all_to_all(outgoing, "ep", split_axis=0, concat_axis=0, tiled=True).reshape(
        group_size * capacity, D
    )
    gate_matrix = expert_gate[0]
    up_matrix = expert_up[0]
    down_matrix = expert_down[0]
    expert_g = product("rd,df->rf", incoming, gate_matrix)
    expert_u = product("rd,df->rf", incoming, up_matrix)
    expert_hidden = (jax.nn.silu(expert_g) * expert_u).astype(jnp.bfloat16)
    expert_out = (
        product("rf,fd->rd", expert_hidden, down_matrix)
        .astype(jnp.bfloat16)
        .reshape(group_size, capacity, D)
    )
    returned = lax.all_to_all(expert_out, "ep", split_axis=0, concat_axis=0, tiled=True).reshape(
        group_size * capacity, D
    )
    safe_slot = jnp.where(kept_mask, slot_index, 0)
    picked = jnp.take(returned, safe_slot, axis=0).astype(jnp.float32).reshape(tokens, TOPK, D)
    kept_gate = gate_values * kept_values
    mixture = jnp.sum(picked * kept_gate[:, :, None], axis=1)
    layer_output = (residual_mid + shared_out + mixture).astype(jnp.bfloat16)
    grad_out = output_grad.astype(jnp.float32)
    grad_shared_down = product("tf,td->fd", shared_hidden, output_grad)
    grad_shared_hidden = product("td,fd->tf", output_grad, shared_down)
    grad_shared_g, grad_shared_u = silu_back(grad_shared_hidden, shared_g, shared_u)
    grad_shared_gate = product("td,tf->df", ffn_in, grad_shared_g)
    grad_shared_up = product("td,tf->df", ffn_in, grad_shared_u)
    grad_ffn_in = product("tf,df->td", grad_shared_g, shared_gate) + product(
        "tf,df->td", grad_shared_u, shared_up
    )
    grad_gates = jnp.sum(picked * grad_out[:, None, :], axis=-1) * kept_values
    grad_probs = jnp.sum(grad_gates[:, :, None] * route_hot, axis=1)
    grad_logits = (
        router_probs * (grad_probs - jnp.sum(router_probs * grad_probs, axis=-1, keepdims=True))
    ).astype(jnp.bfloat16)
    grad_router = product("td,te->de", ffn_in, grad_logits)
    grad_ffn_in = grad_ffn_in + product("te,de->td", grad_logits, router_weight)
    slot_gate = jnp.sum(slot_match * kept_gate.reshape(tokens * TOPK)[:, None], axis=0)
    grad_slots = (
        (product("ts,td->sd", dispatch, output_grad) * slot_gate[:, None])
        .astype(jnp.bfloat16)
        .reshape(group_size, capacity, D)
    )
    grad_incoming = lax.all_to_all(
        grad_slots, "ep", split_axis=0, concat_axis=0, tiled=True
    ).reshape(group_size * capacity, D)
    grad_down_matrix = product("rf,rd->fd", expert_hidden, grad_incoming)
    grad_expert_hidden = product("rd,fd->rf", grad_incoming, down_matrix)
    grad_expert_g, grad_expert_u = silu_back(grad_expert_hidden, expert_g, expert_u)
    grad_gate_matrix = product("rd,rf->df", incoming, grad_expert_g)
    grad_up_matrix = product("rd,rf->df", incoming, grad_expert_u)
    grad_rows = (
        (
            product("rf,df->rd", grad_expert_g, gate_matrix)
            + product("rf,df->rd", grad_expert_u, up_matrix)
        )
        .astype(jnp.bfloat16)
        .reshape(group_size, capacity, D)
    )
    grad_returned = lax.all_to_all(
        grad_rows, "ep", split_axis=0, concat_axis=0, tiled=True
    ).reshape(group_size * capacity, D)
    grad_ffn_in = grad_ffn_in + product("ts,sd->td", dispatch, grad_returned)
    expert_gate_grad, expert_up_grad, expert_down_grad = (
        lax.psum_scatter(
            grad_gate_matrix[None].astype(jnp.bfloat16), "grp", scatter_dimension=1, tiled=True
        ).astype(jnp.float32),
        lax.psum_scatter(
            grad_up_matrix[None].astype(jnp.bfloat16), "grp", scatter_dimension=1, tiled=True
        ).astype(jnp.float32),
        lax.psum_scatter(
            grad_down_matrix[None].astype(jnp.bfloat16), "grp", scatter_dimension=1, tiled=True
        ).astype(jnp.float32),
    )
    grad_ffn_gain = jnp.sum(grad_ffn_in * mid_unit, axis=0)
    grad_mid = grad_out + norm_back(grad_ffn_in * ffn_gain_values, mid_unit, mid_scale)
    (
        feedforward_gain_grad,
        router_weight_grad,
        shared_gate_grad,
        shared_up_grad,
        shared_down_grad,
    ) = (
        lax.psum_scatter(grad_ffn_gain, ("grp", "ep"), scatter_dimension=0, tiled=True),
        lax.psum_scatter(grad_router, ("grp", "ep"), scatter_dimension=0, tiled=True),
        lax.psum_scatter(grad_shared_gate, ("grp", "ep"), scatter_dimension=0, tiled=True),
        lax.psum_scatter(grad_shared_up, ("grp", "ep"), scatter_dimension=0, tiled=True),
        lax.psum_scatter(grad_shared_down, ("grp", "ep"), scatter_dimension=0, tiled=True),
    )
    attn_grad_b = grad_mid.astype(jnp.bfloat16)
    grad_output_matrix = product("ta,td->ad", attended_b, attn_grad_b)
    grad_attended = (
        product("td,ad->ta", attn_grad_b, output_weight)
        .astype(jnp.bfloat16)
        .reshape(tokens, HEADS, VH)
    )
    scores = attention_scores(query_b, key_nope, all_rope, visible)
    probs = jnp.exp(scores - log_total)
    grad_weights = product("qhd,khd->hqk", grad_attended, values)
    delta = jnp.sum(probs * grad_weights, axis=-1, keepdims=True)
    grad_scores = (probs * (grad_weights - delta)).astype(jnp.bfloat16)
    grad_query_nope = product("hqk,khd->qhd", grad_scores, key_nope) * scale
    grad_query_rope = product("hqk,kd->qhd", grad_scores, all_rope) * scale
    grad_key_nope = product("hqk,qhd->khd", grad_scores, query_b[..., :NOPE]) * scale
    grad_key_rope = product("hqk,qhd->kd", grad_scores, query_b[..., NOPE:]) * scale
    grad_values = product("hqk,qhd->khd", weights_b, grad_attended)
    grad_expanded = jnp.concatenate([grad_key_nope, grad_values], axis=-1).reshape(
        length, HEADS * (NOPE + VH)
    )
    expand_values = expand_weight.astype(jnp.float32)
    partial_latent = exact_product("tc,lc->tl", grad_expanded, expand_values)
    grad_expand_matrix = exact_product("tl,tc->lc", all_latent.astype(jnp.float32), grad_expanded)
    grad_latent, own_grad_rope = (
        lax.psum_scatter(
            partial_latent.astype(jnp.bfloat16), "ep", scatter_dimension=0, tiled=True
        ).astype(jnp.float32),
        lax.psum_scatter(
            grad_key_rope.astype(jnp.bfloat16), "ep", scatter_dimension=0, tiled=True
        ).astype(jnp.float32),
    )
    grad_latent_gain = jnp.sum(grad_latent * latent_unit, axis=0)
    grad_latent_raw = norm_back(grad_latent * latent_gain_values, latent_unit, latent_scale)
    grad_compressed = jnp.concatenate(
        [grad_latent_raw, unrotate(own_grad_rope, cos_table, sin_table)], axis=-1
    ).astype(jnp.bfloat16)
    grad_query = jnp.concatenate(
        [grad_query_nope, unrotate(grad_query_rope, cos_table[:, None], sin_table[:, None])],
        axis=-1,
    )
    grad_query = grad_query.astype(jnp.bfloat16).reshape(tokens, HEADS * (NOPE + ROPE))
    grad_query_matrix = product("td,tc->dc", normed, grad_query)
    grad_latent_matrix = product("td,tc->dc", normed, grad_compressed)
    grad_normed = product("tc,dc->td", grad_query, query_weight) + product(
        "tc,dc->td", grad_compressed, latent_weight
    )
    grad_attn_gain = jnp.sum(grad_normed * input_unit, axis=0)
    input_grad = (
        grad_mid + norm_back(grad_normed * attn_gain_values, input_unit, input_scale)
    ).astype(jnp.bfloat16)
    (
        attention_gain_grad,
        query_weight_grad,
        latent_weight_grad,
        latent_gain_grad,
        expand_weight_grad,
        output_weight_grad,
    ) = (
        lax.psum_scatter(grad_attn_gain, ("grp", "ep"), scatter_dimension=0, tiled=True),
        lax.psum_scatter(grad_query_matrix, ("grp", "ep"), scatter_dimension=0, tiled=True),
        lax.psum_scatter(grad_latent_matrix, ("grp", "ep"), scatter_dimension=0, tiled=True),
        lax.psum_scatter(grad_latent_gain, ("grp", "ep"), scatter_dimension=0, tiled=True),
        lax.psum_scatter(grad_expand_matrix, ("grp", "ep"), scatter_dimension=0, tiled=True),
        lax.psum_scatter(grad_output_matrix, ("grp", "ep"), scatter_dimension=0, tiled=True),
    )
    return (
        layer_output,
        input_grad,
        attention_gain_grad,
        query_weight_grad,
        latent_weight_grad,
        latent_gain_grad,
        expand_weight_grad,
        output_weight_grad,
        feedforward_gain_grad,
        router_weight_grad,
        shared_gate_grad,
        shared_up_grad,
        shared_down_grad,
        expert_gate_grad,
        expert_up_grad,
        expert_down_grad,
    )


def solution(mesh):
    return jax.shard_map(
        per_device,
        mesh=mesh,
        in_specs=(
            P(("grp", "ep"), None),
            P("ep"),
            P("ep", None),
            P("ep", None),
            P("ep"),
            P("ep", None),
            P("ep", None),
            P("ep"),
            P("ep", None),
            P("ep", None),
            P("ep", None),
            P("ep", None),
            P("ep", None, None),
            P("ep", None, None),
            P("ep", None, None),
            P(("grp", "ep"), None),
            P("grp"),
            P(("grp", "ep"), None),
        ),
        out_specs=(
            P(("grp", "ep"), None),
            P(("grp", "ep"), None),
            P(("grp", "ep")),
            P(("grp", "ep"), None),
            P(("grp", "ep"), None),
            P(("grp", "ep")),
            P(("grp", "ep"), None),
            P(("grp", "ep"), None),
            P(("grp", "ep")),
            P(("grp", "ep"), None),
            P(("grp", "ep"), None),
            P(("grp", "ep"), None),
            P(("grp", "ep"), None),
            P("ep", "grp", None),
            P("ep", "grp", None),
            P("ep", "grp", None),
        ),
        check_vma=False,
    )
```

profile of v0, /device:TPU:0, one launch (start us, length us, event | category | flops | bytes accessed | tf_op | source)
XLA Modules:
  0.0 4073.1 jit_solution(3315430470992910162)
XLA Ops:
  11.5 43.8 %all-reduce = bf16[512]{0:T(512)(128)(2,1)S(1)} all-reduce(bf16[512]{0:T(512)(128)(2,1)S(1)} %dynamic-update-slice), channel_id=1, replica_groups=mesh['grp'=2,'ep'=16] {'ep'}, use_global_device_ids=true, to_apply=%add | all-reduce | flops 512 | bytes 2048
  55.3 35.6 all-gather
  99.4 37.5 all-gather.1
  140.4 38.0 all_gather.45
  178.4 47.0 %all-gather.13.cloned.1.call-done = bf16[2048,512]{0,1:T(8,128)(2,1)} async-done(((bf16[128,512]{0,1:T(8,128)(2,1)}), bf16[2048,512]{0,1:T(8,128)(2,1)}) %all-gather.13.cloned.1.call-update) | async-done | bytes 2097168 | tf_op jit(solution)/shard_map/all_gather | solution.py:136
  225.4 14.9 convolution_convert_fusion
  257.5 12.6 copy.141
  270.0 108.2 %all-gather.17.cloned.1.call-done = bf16[2048,3072]{1,0:T(8,128)(2,1)} async-done(((bf16[128,3072]{1,0:T(8,128)(2,1)}), bf16[2048,3072]{1,0:T(8,128)(2,1)}) %all-gather.17.cloned.1.call-update) | async-done | bytes 12582928 | tf_op jit(solution)/shard_map/all_gather | solution.py:107
  398.1 11.8 fusion.114
  429.0 62.9 %all-gather.19.cloned.1.call-done = bf16[2048,2048]{1,0:T(8,128)(2,1)} async-done(((bf16[128,2048]{1,0:T(8,128)(2,1)}), bf16[2048,2048]{1,0:T(8,128)(2,1)}) %all-gather.19.cloned.1.call-update) | async-done | bytes 8388624 | tf_op jit(solution)/shard_map/all_gather | solution.py:111
  498.3 171.0 %all_to_all.20 = bf16[16,64,2048]{2,1,0:T(8,128)(2,1)S(1)} all-to-all(bf16[16,64,2048]{2,1,0:T(8,128)(2,1)S(1)} %bitcast.171), channel_id=1, replica_groups=mesh['grp'=2,'ep'=16] {'ep'}, dimensions={0} | all-to-all | bytes 8388608 | tf_op jit(solution)/shard_map/all_to_all | solution.py:191
  716.1 124.9 %all_gather.51 = bf16[2048,16]{0,1:T(8,128)(2,1)S(1)} all-gather(bf16[128,16]{0,1:T(8,128)(2,1)S(1)} %copy-done.57), channel_id=1, replica_groups=mesh['grp'=2,'ep'=16] {'ep'}, dimensions={0}, use_global_device_ids=true | all-gather | bytes 69632 | tf_op jit(solution)/shard_map/all_gather | solution.py:157
  859.0 186.3 %all_to_all.21 = bf16[16,64,2048]{2,1,0:T(8,128)(2,1)S(1)} all-to-all(bf16[16,64,2048]{2,1,0:T(8,128)(2,1)S(1)} %bitcast.170), channel_id=1, replica_groups=mesh['grp'=2,'ep'=16] {'ep'}, dimensions={0} | all-to-all | bytes 8388608 | tf_op jit(solution)/shard_map/all_to_all | solution.py:235
  1045.3 14.0 multiply_convert_fusion.3
  1100.9 79.6 %all-gather.25.cloned.1.call-done = bf16[2816,2048]{1,0:T(8,128)(2,1)} async-done(((bf16[176,2048]{1,0:T(8,128)(2,1)}), bf16[2816,2048]{1,0:T(8,128)(2,1)}) %all-gather.25.cloned.1.call-update) | async-done | bytes 11534352 | tf_op jit(solution)/shard_map/all_gather | solution.py:160
  1216.3 15.0 multiply_reduce_fusion
  1231.3 14.0 convolution_bitcast_fusion
  1245.3 11.9 multiply_convert_fusion
  1269.7 23.7 pad_maximum_fusion
  1293.4 58.1 %convolution_convert_fusion.5 = bf16[2048,512]{1,0:T(8,128)(2,1)} fusion(f32[2048,4096]{0,1:T(8,128)} %bitcast.168, bf16[512,4096]{1,0:T(8,128)(2,1)S(1)} %copy-done.63), kind=kOutput, calls=%fused_computation.51 | convolution fusion | flops 51540656128 | bytes 39845888 | tf_op jit(solution)/shard_map/tc,lc->tl/dot_general | solution.py:27
  1387.0 48.7 %reduce-scatter.40.cloned.1.call-done = bf16[128,512]{1,0:T(8,128)(2,1)} async-done(((bf16[2048,512]{1,0:T(8,128)(2,1)}), bf16[128,512]{1,0:T(8,128)(2,1)}) %reduce-scatter.40.cloned.1.call-update) | async-done | bytes 131088
  1473.4 31.9 fusion.120
  1592.4 12.9 reduce-scatter.36.cloned.1.call-done
  1610.1 13.1 reduce-scatter.34.cloned.1.call-done
  1629.8 45.0 %all-reduce.4 = (f32[2048]{0:T(1024)S(1)}, f32[512]{0:T(512)S(1)}, f32[2048]{0:T(1024)S(1)}) all-reduce(f32[2048]{0:T(1024)S(1)} %get-tuple-element.18, f32[512]{0:T(512)S(1)} %copy-done.54, f32[2048]{0:T(1024)S(1)} %copy-done.51), channel_id=4, replica_groups=mesh['grp'=2,'ep'=16] {'grp','ep'}, use_global_device_ids=true, to_apply=%region_24.25.clone | all-reduce | flops 4608 | bytes 36864
  1678.9 96.2 %reduce-scatter.22.cloned.1.call-done = f32[64,576]{1,0:T(8,128)} async-done(((f32[2048,576]{1,0:T(8,128)}), f32[64,576]{1,0:T(8,128)}) %reduce-scatter.22.cloned.1.call-update) | async-done | bytes 147472 | tf_op jit(solution)/shard_map/reduce_scatter | solution.py:341
  1775.0 490.9 %reduce-scatter.32.cloned.1.call-done = f32[88,2048]{1,0:T(8,128)} async-done(((f32[2816,2048]{1,0:T(8,128)}), f32[88,2048]{1,0:T(8,128)}) %reduce-scatter.32.cloned.1.call-update) | async-done | bytes 720912 | tf_op jit(solution)/shard_map/reduce_scatter | solution.py:279
  2265.9 495.6 %reduce-scatter.30.cloned.1.call-done = f32[64,2816]{1,0:T(8,128)} async-done(((f32[2048,2816]{1,0:T(8,128)}), f32[64,2816]{1,0:T(8,128)}) %reduce-scatter.30.cloned.1.call-update) | async-done | bytes 720912 | tf_op jit(solution)/shard_map/reduce_scatter | solution.py:278
  2761.5 495.6 %reduce-scatter.28.cloned.1.call-done = f32[64,2816]{1,0:T(8,128)} async-done(((f32[2048,2816]{1,0:T(8,128)}), f32[64,2816]{1,0:T(8,128)}) %reduce-scatter.28.cloned.1.call-update) | async-done | bytes 720912 | tf_op jit(solution)/shard_map/reduce_scatter | solution.py:277
  3257.1 191.6 %reduce-scatter.24.cloned.1.call-done = f32[16,4096]{1,0:T(8,128)} async-done(((f32[512,4096]{1,0:T(8,128)}), f32[16,4096]{1,0:T(8,128)}) %reduce-scatter.24.cloned.1.call-update) | async-done | bytes 262160 | tf_op jit(solution)/shard_map/reduce_scatter | solution.py:343
  3448.7 360.9 %reduce-scatter.26.cloned.1.call-done = f32[64,2048]{1,0:T(8,128)} async-done(((f32[2048,2048]{1,0:T(8,128)}), f32[64,2048]{1,0:T(8,128)}) %reduce-scatter.26.cloned.1.call-update) | async-done | bytes 524304 | tf_op jit(solution)/shard_map/reduce_scatter | solution.py:344
  3809.6 256.3 %reduce-scatter.20.cloned.1.call-done = f32[64,3072]{1,0:T(8,128)} async-done(((f32[2048,3072]{1,0:T(8,128)}), f32[64,3072]{1,0:T(8,128)}) %reduce-scatter.20.cloned.1.call-update) | async-done | bytes 786448 | tf_op jit(solution)/shard_map/reduce_scatter | solution.py:340
  (341 shorter events, 406.3 us)
Async XLA Ops:
  7.2 85.0 %all-gather.11.cloned.1.call-start = ((), (), s32[]{:S(2)}) async-start(), calls=%async_computation.17 | async-start | bytes 2506752 | tf_op jit(solution)/shard_map/all_gather | solution.py:108
  7.9 170.5 %all-gather.15.cloned.1.call-start = ((), (), s32[]{:S(2)}) async-start(), calls=%async_computation.19 | async-start | bytes 4456448 | tf_op jit(solution)/shard_map/all_gather | solution.py:110
  8.7 216.7 %all-gather.13.cloned.1.call-start = ((), (), s32[]{:S(2)}) async-start(), calls=%async_computation.18 | async-start | bytes 2228224 | tf_op jit(solution)/shard_map/all_gather | solution.py:136
  90.9 287.4 %copy-start.32 = (f32[16,1,128]{2,1,0:T(1,128)}, f32[16,1,128]{2,1,0:T(1,128)S(1)}, u32[]{:S(2)}) copy-start(f32[16,1,128]{2,1,0:T(1,128)S(1)} %convert_element_type.211) | copy-start | bytes 24580
  92.1 286.1 %copy-start.49 = (f32[128]{0:T(128)}, f32[128]{0:T(128)S(1)}, u32[]{:S(2)}) copy-start(f32[128]{0:T(128)S(1)} %add_rsqrt_fusion.2) | copy-start | bytes 1540
  95.8 282.4 %all-gather.17.cloned.1.call-start = ((), (), s32[]{:S(2)}) async-start(), calls=%async_computation.20 | async-start | bytes 13369344 | tf_op jit(solution)/shard_map/all_gather | solution.py:107
  96.4 395.5 %all-gather.19.cloned.1.call-start = ((), (), s32[]{:S(2)}) async-start(), calls=%async_computation.21 | async-start | bytes 8912896 | tf_op jit(solution)/shard_map/all_gather | solution.py:111
  97.0 989.8 %all-gather.23.cloned.1.call-start = ((), (), s32[]{:S(2)}) async-start(), calls=%async_computation.23 | async-start | bytes 12255232 | tf_op jit(solution)/shard_map/all_gather | solution.py:159
  97.5 996.3 %all-gather.21.cloned.1.call-start = ((), (), s32[]{:S(2)}) async-start(), calls=%async_computation.22 | async-start | bytes 12255232 | tf_op jit(solution)/shard_map/all_gather | solution.py:158
  139.3 717.1 %copy-start.52 = (pred[128,6]{0,1:T(8,128)(4,1)}, pred[128,6]{0,1:T(8,128)(4,1)S(1)}, u32[]{:S(2)}) copy-start(pred[128,6]{0,1:T(8,128)(4,1)S(1)} %get-tuple-element.31) | copy-start | bytes 2308
  140.4 257.5 %copy-start.38 = (f32[128,32]{0,1:T(8,128)}, f32[128,32]{0,1:T(8,128)S(1)}, u32[]{:S(2)}) copy-start(f32[128,32]{0,1:T(8,128)S(1)} %get-tuple-element.47) | copy-start | bytes 49156
  140.4 257.5 %copy-start.40 = (f32[128,32]{0,1:T(8,128)}, f32[128,32]{0,1:T(8,128)S(1)}, u32[]{:S(2)}) copy-start(f32[128,32]{0,1:T(8,128)S(1)} %get-tuple-element.48) | copy-start | bytes 49156
  178.4 219.6 %copy-start.24 = (bf16[2048,64]{0,1:T(8,128)(2,1)}, bf16[2048,64]{0,1:T(8,128)(2,1)S(1)}, u32[]{:S(2)}) copy-start(bf16[2048,64]{0,1:T(8,128)(2,1)S(1)} %all_gather.45) | copy-start | bytes 786436
  496.8 711.4 %copy-start.4 = (f32[128,2048]{1,0:T(8,128)}, f32[128,2048]{1,0:T(8,128)S(1)}, u32[]{:S(2)}) copy-start(f32[128,2048]{1,0:T(8,128)S(1)} %get-tuple-element.54) | copy-start | bytes 3145732
  693.0 148.4 %all-to-all-start.1 = ((bf16[16,64,2048]{2,1,0:T(8,128)(2,1)}), bf16[16,64,2048]{2,1,0:T(8,128)(2,1)}, u32[]{:S(2)}, u32[]{:S(2)}) async-start(bf16[16,64,2048]{2,1,0:T(8,128)(2,1)} %bitcast.189), calls=%async_computation.1 | async-start | bytes 8388608 | tf_op jit(solution)/shard_map/all_to_all | solution.py:205
  702.1 478.4 %all-gather.25.cloned.1.call-start = ((), (), s32[]{:S(2)}) async-start(), calls=%async_computation.24 | async-start | bytes 12255232 | tf_op jit(solution)/shard_map/all_gather | solution.py:160
  856.4 188.8 %copy-start.45 = (f32[128,6]{0,1:T(8,128)}, f32[128,6]{0,1:T(8,128)S(1)}, u32[]{:S(2)}) copy-start(f32[128,6]{0,1:T(8,128)S(1)} %get-tuple-element.23) | copy-start | bytes 9220
  1080.1 123.9 %all-to-all-start.3 = ((bf16[16,64,2048]{2,1,0:T(8,128)(2,1)}), bf16[16,64,2048]{2,1,0:T(8,128)(2,1)}, u32[]{:S(2)}, u32[]{:S(2)}) async-start(bf16[16,64,2048]{2,1,0:T(8,128)(2,1)} %bitcast.188), calls=%async_computation.3 | async-start | bytes 8388608 | tf_op jit(solution)/shard_map/all_to_all | solution.py:251
  1086.3 299.5 %reduce-scatter.42.cloned.1.call-start = ((), (), s32[]{:S(2)}) async-start(), calls=%async_computation.36 | async-start | bytes 557056
  1190.0 251.2 %copy-start.17 = (bf16[128,2816]{1,0:T(8,128)(2,1)}, bf16[128,2816]{1,0:T(8,128)(2,1)S(1)}, u32[]{:S(2)}) copy-start(bf16[128,2816]{1,0:T(8,128)(2,1)S(1)} %get-tuple-element.38) | copy-start | bytes 2162692
  1269.6 166.1 %reduce-scatter.40.cloned.1.call-start = ((), (), s32[]{:S(2)}) async-start(), calls=%async_computation.35 | async-start | bytes 2228224
  1351.6 222.2 %reduce-scatter.44.cloned.1.call-start = ((), (), s32[]{:S(2)}) async-start(), calls=%async_computation.37 | async-start | bytes 1081344
  1353.0 234.3 %reduce-scatter.38.cloned.1.call-start = ((), (), s32[]{:S(2)}) async-start(), calls=%async_computation.34 | async-start | bytes 8650752 | tf_op jit(solution)/shard_map/reduce_scatter | solution.py:262
  1363.5 241.8 %reduce-scatter.36.cloned.1.call-start = ((), (), s32[]{:S(2)}) async-start(), calls=%async_computation.33 | async-start | bytes 8650752 | tf_op jit(solution)/shard_map/reduce_scatter | solution.py:259
  1374.6 248.6 %reduce-scatter.34.cloned.1.call-start = ((), (), s32[]{:S(2)}) async-start(), calls=%async_computation.32 | async-start | bytes 8650752 | tf_op jit(solution)/shard_map/reduce_scatter | solution.py:256
  1385.7 389.3 %reduce-scatter.22.cloned.1.call-start = ((), (), s32[]{:S(2)}) async-start(), calls=%async_computation.26 | async-start | bytes 5406720 | tf_op jit(solution)/shard_map/reduce_scatter | solution.py:341
  1441.1 824.8 %reduce-scatter.32.cloned.1.call-start = ((), (), s32[]{:S(2)}) async-start(), calls=%async_computation.31 | async-start | bytes 23789568 | tf_op jit(solution)/shard_map/reduce_scatter | solution.py:279
  1450.8 1310.7 %reduce-scatter.30.cloned.1.call-start = ((), (), s32[]{:S(2)}) async-start(), calls=%async_computation.30 | async-start | bytes 23789568 | tf_op jit(solution)/shard_map/reduce_scatter | solution.py:278
  1461.2 1795.8 %reduce-scatter.28.cloned.1.call-start = ((), (), s32[]{:S(2)}) async-start(), calls=%async_computation.29 | async-start | bytes 23789568 | tf_op jit(solution)/shard_map/reduce_scatter | solution.py:277
  1471.8 1976.9 %reduce-scatter.24.cloned.1.call-start = ((), (), s32[]{:S(2)}) async-start(), calls=%async_computation.27 | async-start | bytes 8650752 | tf_op jit(solution)/shard_map/reduce_scatter | solution.py:343
  1505.3 2304.2 %reduce-scatter.26.cloned.1.call-start = ((), (), s32[]{:S(2)}) async-start(), calls=%async_computation.28 | async-start | bytes 17301504 | tf_op jit(solution)/shard_map/reduce_scatter | solution.py:344
  1514.9 2551.0 %reduce-scatter.20.cloned.1.call-start = ((), (), s32[]{:S(2)}) async-start(), calls=%async_computation.25 | async-start | bytes 25952256 | tf_op jit(solution)/shard_map/reduce_scatter | solution.py:340
  (70 other events, 2626.2 us)
Sparse Core Ops, SparseCore 0:
  10.7 69.7 all-gather.10
  83.3 76.6 all-gather.14
  163.3 62.0 all-gather.12
  228.0 150.1 all-gather.16
  380.9 111.0 all-gather.18
  494.5 210.1 all-gather.22
  707.5 242.2 all-gather.20
  952.5 228.0 all-gather.24
  1269.8 79.9 reduce-scatter.41
  1352.0 83.6 reduce-scatter.39
  1438.0 135.6 reduce-scatter.43
  1576.5 10.7 reduce-scatter.37
  1590.3 15.0 reduce-scatter.35
  1608.1 15.0 reduce-scatter.33
  1626.0 149.0 reduce-scatter.21
  1777.9 487.9 reduce-scatter.31
  2268.7 492.7 reduce-scatter.29
  2764.3 492.7 reduce-scatter.27
  3260.1 188.5 reduce-scatter.23
  3451.5 358.0 reduce-scatter.25
  3817.7 248.1 reduce-scatter.19
where the time goes:
time: 4080 us; the launch traced here: 4070 us
  waiting for transfers between devices  2780 us (68%)
  blocking collectives  682 us (17%)
  matrix products  423 us (10%)
  other arithmetic  79.5 us (2%)
  local copies, waits for them, and re-layouts  77.8 us (2%)
    reduce_scatter x1, waiting for transfers between devices, per_device(): lax.psum_scatter(grad_shared_gate, ('grp', 'ep'), scatter_dimension=0, ti...  496 us
    reduce_scatter x1, waiting for transfers between devices, per_device(): lax.psum_scatter(grad_shared_up, ('grp', 'ep'), scatter_dimension=0, tile...  496 us
    reduce_scatter x1, waiting for transfers between devices, per_device(): lax.psum_scatter(grad_shared_down, ('grp', 'ep'), scatter_dimension=0, ti...  491 us
    reduce_scatter x1, waiting for transfers between devices, per_device(): lax.psum_scatter(grad_output_matrix, ('grp', 'ep'), scatter_dimension=0,...  361 us
    dot_general x42, matrix products, product(): return jnp.einsum(form, left, right, preferred_element_type=jnp.float32)  332 us
    reduce_scatter x1, waiting for transfers between devices, per_device(): lax.psum_scatter(grad_query_matrix, ('grp', 'ep'), scatter_dimension=0, t...  256 us
    reduce_scatter x1, waiting for transfers between devices, per_device(): lax.psum_scatter(grad_expand_matrix, ('grp', 'ep'), scatter_dimension=0,...  192 us
    all_to_all x1, blocking collectives, per_device(): lax.all_to_all(grad_slots, 'ep', split_axis=0, concat_axis=0, tiled=True)  186 us
  transfers between devices with their start and end apart: 23, of which 16 were waited for; matrix products, arithmetic and copies ran while one was open for 13% of the time, Pallas kernels for 0%

commit v1 on v0

v1 whole, which is shorter than its diff:
```python
import functools
import math

import jax
import jax.numpy as jnp
from jax import lax
from jax.experimental import pallas as pl
from jax.experimental.pallas import tpu as pltpu
from jax.sharding import PartitionSpec as P

D = 2048
HEADS = 16
NOPE = 128
ROPE = 64
VH = 128
LATENT = 512
TOPK = 6

EPSILON = 1e-06
MASKED = -1e30

MESH = pl.DeviceIdType.MESH
ANY = pl.BlockSpec(memory_space=pl.ANY)
DMA = pltpu.SemaphoreType.DMA
F32 = jnp.float32
BF16 = jnp.bfloat16


def remote(src, dst, send, recv, peer):
    return pltpu.make_async_remote_copy(
        src_ref=src,
        dst_ref=dst,
        send_sem=send,
        recv_sem=recv,
        device_id={"ep": peer},
        device_id_type=MESH,
    )


def greet(peers):
    barrier = pltpu.get_barrier_semaphore()
    for peer in peers:
        pl.semaphore_signal(barrier, inc=1, device_id={"ep": peer}, device_id_type=MESH)
    pl.semaphore_wait(barrier, len(peers))


def around(n):
    me = lax.axis_index("ep")
    x, y = me % 2, (me // 2) % 2
    return me, me // 4, y, x, me + 1 - 2 * x, me + 2 - 4 * y


def gather_kernel(n, x_ref, o_ref, own, zs, zr, xs, xr, ys, yr):
    me, z, y, x, px, py = around(n)
    nz = n // 4
    low = me % 4
    half = x_ref.shape[0] // 2
    top, bottom = pl.ds(0, half), pl.ds(half, half)
    at = [((z + k) % nz) * 4 + low for k in range(nz)]
    back = [((z + nz - k) % nz) * 4 + low for k in range(nz)]
    greet([px, py] + at[1:])
    local = pltpu.make_async_copy(x_ref, o_ref.at[me], own)
    local.start()
    sends = []

    def send(copy):
        copy.start()
        sends.append(copy)

    def over_x(src, b, part, i):
        return remote(src.at[part], o_ref.at[b, part], xs.at[i], xr.at[i], px)

    def over_y(src, b, part, i):
        return remote(src.at[part], o_ref.at[b, part], ys.at[i], yr.at[i], py)

    for k in range(1, nz):
        send(remote(x_ref, o_ref.at[me], zs.at[k], zr.at[k], at[k]))
    for k in range(nz):
        b = back[k]
        if k:
            remote(x_ref, o_ref.at[b], zs.at[k], zr.at[k], at[k]).wait_recv()
        src = o_ref.at[b] if k else x_ref
        send(over_x(src, b, top, k))
        send(over_y(src, b, bottom, k))
        send(over_y(src, b, top, nz + k))
        send(over_x(src, b, bottom, nz + k))
    for k in range(nz):
        bx = back[k] + px - me
        by = back[k] + py - me
        over_x(o_ref.at[bx], bx, top, k).wait_recv()
        send(over_y(o_ref.at[bx], bx, top, 2 * nz + k))
        over_y(o_ref.at[by], by, bottom, k).wait_recv()
        send(over_x(o_ref.at[by], by, bottom, 2 * nz + k))
    for k in range(nz):
        bx = back[k] + px - me
        by = back[k] + py - me
        bxy = bx + py - me
        over_y(o_ref.at[by], by, top, nz + k).wait_recv()
        over_x(o_ref.at[bx], bx, bottom, nz + k).wait_recv()
        over_y(o_ref.at[bxy], bxy, top, 2 * nz + k).wait_recv()
        over_x(o_ref.at[bxy], bxy, bottom, 2 * nz + k).wait_recv()
    for copy in sends:
        copy.wait_send()
    local.wait()


def gather(x, cid):
    n = lax.axis_size("ep")
    nz = n // 4
    return pl.pallas_call(
        functools.partial(gather_kernel, n),
        out_shape=jax.ShapeDtypeStruct((n,) + x.shape, x.dtype),
        in_specs=[ANY],
        out_specs=ANY,
        scratch_shapes=[DMA, DMA((nz,)), DMA((nz,))] + [DMA((3 * nz,))] * 4,
        compiler_params=pltpu.CompilerParams(collective_id=cid, has_side_effects=True),
        name="gather",
    )(x)


def add_rows(dst, left, right, rows):
    step = 16

    def body(i, carry):
        r = pl.ds(pl.multiple_of(i * step, step), step)
        dst[r] = (left[r].astype(F32) + right[r].astype(F32)).astype(dst.dtype)
        return carry

    lax.fori_loop(0, rows // step, body, 0)


def scatter_kernel(
    n, p_ref, o_ref, la, lb, a1, b1, a2, b2, zb, lsa, lsb, xs, xr, ys, yr, zs, zr
):
    me, z, y, x, px, py = around(n)
    nz = n // 4
    low = me % 4
    half = p_ref.shape[3] // 2
    top, bottom = pl.ds(0, half), pl.ds(half, half)
    to = [(z + k) % nz for k in range(nz)]
    at = [t * 4 + low for t in to]
    greet([px, py] + at[1:])
    order = list(range(1, nz)) + [0]
    first, second, third = {}, {}, {}
    sends = []
    for k in order:
        t = to[k]
        c = remote(p_ref.at[t, 1 - y, :, top], a1.at[k], ys.at[k], yr.at[k], py)
        d = remote(p_ref.at[t, :, 1 - x, bottom], b1.at[k], xs.at[k], xr.at[k], px)
        c.start()
        d.start()
        e = pltpu.make_async_copy(p_ref.at[t, y, :, top], la.at[k], lsa.at[k])
        f = pltpu.make_async_copy(p_ref.at[t, :, x, bottom], lb.at[k], lsb.at[k])
        e.start()
        f.start()
        first[k] = (c, d, e, f)
        sends += [c, d]
    for k in order:
        c, d, e, f = first[k]
        e.wait()
        c.wait_recv()
        for i in range(2):
            add_rows(la.at[k, i], la.at[k, i], a1.at[k, i], half)
        g = remote(la.at[k, 1 - x], a2.at[k], xs.at[nz + k], xr.at[nz + k], px)
        g.start()
        f.wait()
        d.wait_recv()
        for i in range(2):
            add_rows(lb.at[k, i], lb.at[k, i], b1.at[k, i], half)
        h = remote(lb.at[k, 1 - y], b2.at[k], ys.at[nz + k], yr.at[nz + k], py)
        h.start()
        second[k] = (g, h)
        sends += [g, h]
    for k in order:
        g, h = second[k]
        g.wait_recv()
        add_rows(a2.at[k], la.at[k, x], a2.at[k], half)
        if k:
            c = remote(a2.at[k], zb.at[k, top], zs.at[k], zr.at[k], at[k])
            c.start()
        h.wait_recv()
        add_rows(b2.at[k], lb.at[k, y], b2.at[k], half)
        if k:
            d = remote(b2.at[k], zb.at[k, bottom], zs.at[nz + k], zr.at[nz + k], at[k])
            d.start()
            third[k] = (c, d)
            sends += [c, d]
    for k in range(1, nz):
        c, d = third[k]
        c.wait_recv()
        d.wait_recv()
    for part, offset in ((a2, 0), (b2, half)):

        def body(i, carry, part=part, offset=offset):
            r = pl.ds(pl.multiple_of(i * 16, 16), 16)
            q = pl.ds(pl.multiple_of(i * 16 + offset, 16), 16)
            total = part[0, r].astype(F32)
            for k in range(1, nz):
                total = total + zb[k, q].astype(F32)
            o_ref[q] = total.astype(o_ref.dtype)
            return carry

        lax.fori_loop(0, half // 16, body, 0)
    for copy in sends:
        copy.wait_send()


def scatter(p, cid):
    n = lax.axis_size("ep")
    nz = n // 4
    rows, cols = p.shape[1:]
    half = rows // 2
    p = p.reshape(nz, 2, 2, rows, cols)

    def room(*shape):
        return pltpu.VMEM(shape, p.dtype)

    return pl.pallas_call(
        functools.partial(scatter_kernel, n),
        out_shape=jax.ShapeDtypeStruct((rows, cols), F32),
        in_specs=[ANY],
        out_specs=pl.BlockSpec(memory_space=pltpu.VMEM),
        scratch_shapes=[room(nz, 2, half, cols)] * 4
        + [room(nz, half, cols)] * 2
        + [room(nz, rows, cols)]
        + [DMA((nz,))] * 2
        + [DMA((2 * nz,))] * 6,
        compiler_params=pltpu.CompilerParams(
            collective_id=cid, has_side_effects=True, vmem_limit_bytes=40 << 20
        ),
        name="scatter",
    )(p)


def swap_kernel(n, m, *refs):
    ins, outs, (own, ss, rs) = refs[:m], refs[m : 2 * m], refs[2 * m :]
    me = lax.axis_index("ep")
    to = [(me + k) % n for k in range(n)]
    back = [(me + n - k) % n for k in range(n)]
    greet(to[1:])
    copies = []
    for j in range(m):
        local = pltpu.make_async_copy(ins[j].at[me], outs[j].at[me], own.at[j])
        local.start()
        copies.append(local)
    sends = []
    for k in range(1, n):
        for j in range(m):
            c = remote(ins[j].at[to[k]], outs[j].at[me], ss.at[j, k], rs.at[j, k], to[k])
            c.start()
            sends.append(c)
    for k in range(1, n):
        for j in range(m):
            remote(
                ins[j].at[back[k]], outs[j].at[back[k]], ss.at[j, k], rs.at[j, k], to[k]
            ).wait_recv()
    for c in sends:
        c.wait_send()
    for c in copies:
        c.wait()


def swap(cid, *arrays):
    n = lax.axis_size("ep")
    m = len(arrays)
    return pl.pallas_call(
        functools.partial(swap_kernel, n, m),
        out_shape=[jax.ShapeDtypeStruct(a.shape, a.dtype) for a in arrays],
        in_specs=[ANY] * m,
        out_specs=[ANY] * m,
        scratch_shapes=[DMA((m,)), DMA((m, n)), DMA((m, n))],
        compiler_params=pltpu.CompilerParams(collective_id=cid, has_side_effects=True),
        name="swap",
    )(*arrays)


def over_groups(p):
    groups = lax.axis_size("grp")
    if groups == 2:
        g = lax.axis_index("grp")
        mine = lax.dynamic_index_in_dim(p, g, 0, keepdims=False)
        theirs = lax.dynamic_index_in_dim(p, 1 - g, 0, keepdims=False).astype(BF16)
        return mine.astype(F32) + lax.ppermute(theirs, "grp", [(0, 1), (1, 0)]).astype(F32)
    return lax.psum_scatter(p.astype(BF16), "grp", scatter_dimension=0, tiled=False).astype(F32)


def to_row_owner(block):
    groups, n = lax.axis_size("grp"), lax.axis_size("ep")
    pairs = [(h * n + e, e * groups + h) for h in range(groups) for e in range(n)]
    return lax.ppermute(block.astype(BF16), ("grp", "ep"), pairs).astype(F32)


def product(form, left, right):
    return jnp.einsum(form, left, right, preferred_element_type=F32)


def rms_scale(values):
    return lax.rsqrt(jnp.mean(values * values, axis=-1, keepdims=True) + EPSILON)


def rotary_tables(positions):
    halfway = ROPE // 2
    inverse = 10000.0 ** (-(jnp.arange(halfway, dtype=F32) * 2.0 / ROPE))
    angles = positions[:, None] * inverse[None, :]
    return (jnp.cos(angles), jnp.sin(angles))


def rotate(values, cos_table, sin_table):
    halfway = values.shape[-1] // 2
    first = values[..., :halfway]
    second = values[..., halfway:]
    return jnp.concatenate(
        [first * cos_table - second * sin_table, second * cos_table + first * sin_table], axis=-1
    )


def unrotate(grads, cos_table, sin_table):
    halfway = grads.shape[-1] // 2
    first = grads[..., :halfway]
    second = grads[..., halfway:]
    return jnp.concatenate(
        [first * cos_table + second * sin_table, second * cos_table - first * sin_table], axis=-1
    )


def norm_back(grad_unit, unit_values, scale_values):
    return scale_values * (
        grad_unit - unit_values * jnp.mean(grad_unit * unit_values, axis=-1, keepdims=True)
    )


def silu_back(grad_hidden, gate_value, up_value):
    sigmoid = jax.nn.sigmoid(gate_value)
    grad_gate = grad_hidden * up_value * sigmoid * (1.0 + gate_value * (1.0 - sigmoid))
    grad_up = grad_hidden * gate_value * sigmoid
    return (grad_gate.astype(BF16), grad_up.astype(BF16))


def columns_out(weight, n):
    return weight.T.reshape(n, weight.shape[1] // n, weight.shape[0])


def columns_in(blocks):
    n, width, rows = blocks.shape
    return blocks.transpose(1, 0, 2).reshape(width, n * rows)


def per_device(
    layer_input,
    attention_gain,
    query_weight,
    latent_weight,
    latent_gain,
    expand_weight,
    output_weight,
    feedforward_gain,
    router_weight,
    shared_gate,
    shared_up,
    shared_down,
    expert_gate,
    expert_up,
    expert_down,
    expert_routes,
    prefix_length,
    output_grad,
):
    n = lax.axis_size("ep")
    groups = lax.axis_size("grp")
    e = lax.axis_index("ep")
    tokens = layer_input.shape[0]
    length = tokens * n
    capacity = tokens * TOPK * 4 // (3 * n)
    scale = 1.0 / math.sqrt(NOPE + ROPE)
    rows_dev = attention_gain.shape[0]
    latent_rows = latent_gain.shape[0]

    pad = jnp.zeros((rows_dev - latent_rows,), BF16)
    first_block = jnp.concatenate(
        [
            layer_input,
            latent_weight,
            router_weight,
            attention_gain[:, None],
            feedforward_gain[:, None],
            jnp.concatenate([latent_gain, pad])[:, None],
            expert_routes.astype(BF16),
        ],
        axis=1,
    )
    width = first_block.shape[1]
    first_block = jnp.pad(first_block, ((0, 0), (0, -width % 128)))
    first_all = gather(first_block, 0)
    c0 = D
    c1 = c0 + LATENT + ROPE
    c2 = c1 + n
    all_input = first_all[:, :, :c0].reshape(length, D)
    latent_w = first_all[:, :, c0:c1].reshape(D, LATENT + ROPE)
    router_w = first_all[:, :, c1:c2].reshape(D, n)
    attn_gain = first_all[:, :, c2].reshape(D).astype(F32)
    ffn_gain = first_all[:, :, c2 + 1].reshape(D).astype(F32)
    lat_gain = first_all[:, :latent_rows, c2 + 2].reshape(LATENT).astype(F32)
    routes = first_all[:, :, c2 + 3 : c2 + 3 + TOPK].astype(jnp.int32)

    q_blocks, x_blocks, g_blocks, u_blocks = swap(
        1,
        columns_out(query_weight, n),
        columns_out(expand_weight, n),
        columns_out(shared_gate, n),
        columns_out(shared_up, n),
    )
    query_t = columns_in(q_blocks)
    expand_t = columns_in(x_blocks)
    gate_t = columns_in(g_blocks)
    up_t = columns_in(u_blocks)

    output_w = lax.all_gather(output_weight, "ep", axis=0, tiled=True)
    all_out_grad = lax.all_gather(output_grad, "ep", axis=0, tiled=True)

    def own(values):
        return lax.dynamic_slice_in_dim(values, e * tokens, tokens, 0)

    residual_all = all_input.astype(F32)
    unit_all = residual_all * rms_scale(residual_all)
    normed = (unit_all * attn_gain).astype(BF16)
    places = jnp.arange(length, dtype=jnp.int32)
    cos_table, sin_table = rotary_tables(places.astype(F32))
    query_raw = product("td,cd->tc", normed, query_t)
    query_n = query_raw[:, :NOPE].astype(BF16)
    query_r = rotate(query_raw[:, NOPE:], cos_table, sin_table).astype(BF16)
    compressed = product("td,dc->tc", normed, latent_w)
    latent_raw = compressed[:, :LATENT]
    latent = (latent_raw * rms_scale(latent_raw) * lat_gain).astype(BF16)
    key_rope = rotate(compressed[:, LATENT:], cos_table, sin_table).astype(BF16)
    expanded = product("tl,cl->tc", latent, expand_t).astype(BF16)
    key_nope = expanded[:, :NOPE]
    values = expanded[:, NOPE:]
    visible = (places[None, :] <= places[:, None]) | (places[None, :] < prefix_length[0])

    def attention_scores():
        scores = product("qd,kd->qk", query_n, key_nope)
        scores = scores + product("qd,kd->qk", query_r, key_rope)
        return jnp.where(visible, scores * scale, MASKED)

    scores = attention_scores()
    row_max = jnp.max(scores, axis=-1, keepdims=True)
    log_total = row_max + jnp.log(jnp.sum(jnp.exp(scores - row_max), axis=-1, keepdims=True))
    weights = jnp.exp(scores - log_total).astype(BF16)
    attended_head = product("qk,kd->qd", weights, values).astype(BF16)
    (attended_blocks,) = swap(2, attended_head.reshape(n, tokens, VH))
    attended = attended_blocks.transpose(1, 0, 2).reshape(tokens, HEADS * VH)

    residual_in = layer_input.astype(F32)
    input_scale = rms_scale(residual_in)
    input_unit = residual_in * input_scale
    residual_mid = residual_in + product("ta,ad->td", attended, output_w)
    mid_scale = rms_scale(residual_mid)
    mid_unit = residual_mid * mid_scale
    own_ffn_in = (mid_unit * ffn_gain).astype(BF16)
    ffn_blocks = gather(own_ffn_in, 3)
    ffn_in = ffn_blocks.reshape(length, D)

    out_blocks = all_out_grad.reshape(n, tokens, D)
    router_all = jax.nn.softmax(product("td,de->te", ffn_in, router_w), axis=-1)
    gate_values = jnp.sum(
        jnp.where(jnp.arange(n, dtype=jnp.int32) == e, router_all, 0.0), axis=-1
    ).reshape(n, tokens)
    chosen = jnp.any(routes == e, axis=-1)
    chosen_int = chosen.astype(jnp.int32)
    place = jnp.cumsum(chosen_int, axis=1) - chosen_int
    kept = chosen & (place < capacity)
    dispatch = (
        (place[:, None, :] == jnp.arange(capacity, dtype=jnp.int32)[None, :, None])
        & kept[:, None, :]
    )
    slot_gate = jnp.sum(jnp.where(dispatch, gate_values[:, None, :], 0.0), axis=-1)
    dispatch = dispatch.astype(BF16)
    kept_gate = jnp.where(kept, gate_values, 0.0)

    def to_slots(blocks):
        return product("bst,btd->bsd", dispatch, blocks)

    def to_tokens(slots):
        return product("bst,bsd->btd", dispatch, slots.reshape(n, capacity, D))

    incoming = to_slots(ffn_blocks).astype(BF16).reshape(n * capacity, D)
    out_slots = to_slots(out_blocks)
    slot_grad = (out_slots * slot_gate[:, :, None]).astype(BF16).reshape(n * capacity, D)
    gate_m, up_m, down_m = expert_gate[0], expert_up[0], expert_down[0]
    expert_g = product("rd,df->rf", incoming, gate_m)
    expert_u = product("rd,df->rf", incoming, up_m)
    expert_hidden = (jax.nn.silu(expert_g) * expert_u).astype(BF16)
    expert_out = product("rf,fd->rd", expert_hidden, down_m).astype(BF16)
    slot_dot = jnp.sum(
        out_slots * expert_out.astype(F32).reshape(n, capacity, D), axis=-1
    )
    token_dot = jnp.sum(dispatch.astype(F32) * slot_dot[:, :, None], axis=1)
    shared_g = product("td,fd->tf", ffn_in, gate_t)
    shared_u = product("td,fd->tf", ffn_in, up_t)
    shared_hidden = (jax.nn.silu(shared_g) * shared_u).astype(BF16)
    out_partial = product("tf,fd->td", shared_hidden, shared_down).reshape(n, tokens, D)
    out_partial = (out_partial + to_tokens(expert_out) * kept_gate[:, :, None]).astype(BF16)
    out_sum = lax.psum_scatter(out_partial, "ep", scatter_dimension=0)
    layer_output = (residual_mid + out_sum.astype(F32)).astype(BF16)

    grad_shared_hidden = product("td,fd->tf", all_out_grad, shared_down)
    grad_shared_g, grad_shared_u = silu_back(grad_shared_hidden, shared_g, shared_u)
    grad_expert_hidden = product("rd,fd->rf", slot_grad, down_m)
    grad_expert_g, grad_expert_u = silu_back(grad_expert_hidden, expert_g, expert_u)
    row_grad = (
        product("rf,df->rd", grad_expert_g, gate_m) + product("rf,df->rd", grad_expert_u, up_m)
    ).astype(BF16)
    ffn_partial = product("tf,fd->td", grad_shared_g, gate_t) + product(
        "tf,fd->td", grad_shared_u, up_t
    )
    ffn_partial = (ffn_partial.reshape(n, tokens, D) + to_tokens(row_grad)).astype(BF16)
    own_column = (jnp.arange(128, dtype=jnp.int32) == e).astype(F32)
    dot_partial = (token_dot[:, :, None] * own_column).astype(BF16)
    ffn_sum = scatter(jnp.concatenate([ffn_partial, dot_partial], axis=2), 4)

    grad_down_matrix = product("rf,rd->fd", expert_hidden, slot_grad)
    grad_gate_matrix = product("rd,rf->df", incoming, grad_expert_g)
    grad_up_matrix = product("rd,rf->df", incoming, grad_expert_u)
    expert_gate_grad = over_groups(grad_gate_matrix.reshape(groups, D // groups, -1))[None]
    expert_up_grad = over_groups(grad_up_matrix.reshape(groups, D // groups, -1))[None]
    expert_down_grad = over_groups(
        grad_down_matrix.reshape(groups, grad_down_matrix.shape[0] // groups, D)
    )[None]
    grad_shared_down = product("tf,td->fd", shared_hidden, all_out_grad)
    shared_down_grad = to_row_owner(
        over_groups(grad_shared_down.reshape(groups, grad_shared_down.shape[0] // groups, D))
    )
    grad_shared_gate = product("td,tf->df", ffn_in, grad_shared_g)
    grad_shared_up = product("td,tf->df", ffn_in, grad_shared_u)

    router_own = own(router_all)
    grad_probs = ffn_sum[:, D : D + n]
    grad_logits = (
        router_own * (grad_probs - jnp.sum(router_own * grad_probs, axis=-1, keepdims=True))
    ).astype(BF16)
    grad_ffn_in = ffn_sum[:, :D] + product("te,de->td", grad_logits, router_w)
    grad_ffn_gain = jnp.sum(grad_ffn_in * mid_unit, axis=0)
    grad_mid = output_grad.astype(F32) + norm_back(grad_ffn_in * ffn_gain, mid_unit, mid_scale)
    grad_mid_b = grad_mid.astype(BF16)
    grad_attended = product("td,ad->ta", grad_mid_b, output_w).astype(BF16)
    (grad_att_blocks,) = swap(
        5, grad_attended.reshape(tokens, HEADS, VH).transpose(1, 0, 2)
    )
    grad_att = grad_att_blocks.reshape(length, VH)
    mid_all = lax.all_gather(
        jnp.concatenate([grad_mid_b, jnp.pad(grad_logits, ((0, 0), (0, 128 - n)))], axis=1),
        "ep", axis=0, tiled=True,
    )

    probs = jnp.exp(attention_scores() - log_total)
    grad_weights = product("qd,kd->qk", grad_att, values)
    delta = jnp.sum(probs * grad_weights, axis=-1, keepdims=True)
    grad_scores = (probs * (grad_weights - delta)).astype(BF16)
    grad_query_n = product("qk,kd->qd", grad_scores, key_nope) * scale
    grad_query_r = product("qk,kd->qd", grad_scores, key_rope) * scale
    grad_key_n = product("qk,qd->kd", grad_scores, query_n) * scale
    grad_key_r = product("qk,qd->kd", grad_scores, query_r) * scale
    grad_values = product("qk,qd->kd", probs.astype(BF16), grad_att)
    grad_expanded = jnp.concatenate([grad_key_n, grad_values], axis=1).astype(BF16)
    latent_partial = product("tc,cl->tl", grad_expanded, expand_t)
    latent_partial = jnp.concatenate([latent_partial, grad_key_r], axis=1).astype(BF16)
    latent_sum = scatter(latent_partial.reshape(n, tokens, LATENT + ROPE), 6)
    grad_expand = product("tl,tc->lc", latent, grad_expanded)
    grad_query = jnp.concatenate(
        [grad_query_n, unrotate(grad_query_r, cos_table, sin_table)], axis=1
    ).astype(BF16)
    normed_partial = product("tc,cd->td", grad_query, query_t).astype(BF16)
    normed_sum = scatter(normed_partial.reshape(n, tokens, D), 7)
    grad_query_matrix = product("td,tc->dc", normed, grad_query)

    own_compressed = own(compressed)
    latent_scale = rms_scale(own_compressed[:, :LATENT])
    latent_unit = own_compressed[:, :LATENT] * latent_scale
    grad_latent = latent_sum[:, :LATENT]
    grad_latent_gain = jnp.sum(grad_latent * latent_unit, axis=0)
    grad_compressed = jnp.concatenate(
        [
            norm_back(grad_latent * lat_gain, latent_unit, latent_scale),
            unrotate(latent_sum[:, LATENT:], own(cos_table), own(sin_table)),
        ],
        axis=-1,
    ).astype(BF16)
    compressed_all = gather(grad_compressed, 8).reshape(length, LATENT + ROPE)
    grad_normed = normed_sum + product("tc,dc->td", grad_compressed, latent_w)
    grad_attn_gain = jnp.sum(grad_normed * input_unit, axis=0)
    input_grad = (
        grad_mid + norm_back(grad_normed * attn_gain, input_unit, input_scale)
    ).astype(BF16)

    rows_out = D // (groups * n)

    def own_rows(values):
        blocks = values.reshape(length, groups, n, rows_out)
        return lax.dynamic_index_in_dim(blocks, e, 2, keepdims=False).reshape(
            length, groups * rows_out
        )

    latent_weight_grad = over_groups(
        product("tr,tc->rc", own_rows(normed), compressed_all).reshape(
            groups, rows_out, LATENT + ROPE
        )
    )
    router_weight_grad = over_groups(
        product("tr,te->re", own_rows(ffn_in), mid_all[:, D : D + n]).reshape(groups, rows_out, n)
    )
    grad_output = product("ta,td->ad", attended_head, mid_all[:, :D])
    output_weight_grad = to_row_owner(
        over_groups(grad_output.reshape(groups, grad_output.shape[0] // groups, D))
    )
    side = jnp.concatenate([grad_query_matrix, grad_shared_gate, grad_shared_up], axis=1)
    side = over_groups(side.reshape(groups, D // groups, -1)).astype(BF16)
    expand_rows = LATENT // (groups * n)
    grad_expand = over_groups(grad_expand.reshape(groups, LATENT // groups, -1)).astype(BF16)
    gains = jnp.concatenate(
        [
            grad_attn_gain.reshape(groups, n, rows_out),
            grad_ffn_gain.reshape(groups, n, rows_out),
            grad_latent_gain.reshape(groups, n, expand_rows),
        ],
        axis=2,
    ).transpose(1, 0, 2)
    side_all, expand_all, gain_all = swap(
        9,
        side.reshape(n, rows_out, -1),
        grad_expand.reshape(n, expand_rows, -1),
        gains,
    )
    side_all = side_all.transpose(1, 0, 2).astype(F32)
    query_width = query_t.shape[0]
    shared_width = gate_t.shape[0]
    query_weight_grad = side_all[:, :, :query_width].reshape(rows_out, -1)
    shared_gate_grad = side_all[:, :, query_width : query_width + shared_width].reshape(
        rows_out, -1
    )
    shared_up_grad = side_all[:, :, query_width + shared_width :].reshape(rows_out, -1)
    expand_weight_grad = expand_all.transpose(1, 0, 2).reshape(expand_rows, -1).astype(F32)
    gain_sum = jnp.sum(gain_all, axis=0)
    gain_sum = lax.psum_scatter(gain_sum, "grp", scatter_dimension=0) if groups != 2 else (
        lax.dynamic_index_in_dim(gain_sum, lax.axis_index("grp"), 0, keepdims=False)
        + lax.ppermute(
            lax.dynamic_index_in_dim(gain_sum, 1 - lax.axis_index("grp"), 0, keepdims=False),
            "grp", [(0, 1), (1, 0)],
        )
    )
    attention_gain_grad = gain_sum[:rows_out]
    feedforward_gain_grad = gain_sum[rows_out : 2 * rows_out]
    latent_gain_grad = gain_sum[2 * rows_out :]
    return (
        layer_output,
        input_grad,
        attention_gain_grad,
        query_weight_grad,
        latent_weight_grad,
        latent_gain_grad,
        expand_weight_grad,
        output_weight_grad,
        feedforward_gain_grad,
        router_weight_grad,
        shared_gate_grad,
        shared_up_grad,
        shared_down_grad,
        expert_gate_grad,
        expert_up_grad,
        expert_down_grad,
    )


def solution(mesh):
    return jax.shard_map(
        per_device,
        mesh=mesh,
        in_specs=(
            P(("grp", "ep"), None),
            P("ep"),
            P("ep", None),
            P("ep", None),
            P("ep"),
            P("ep", None),
            P("ep", None),
            P("ep"),
            P("ep", None),
            P("ep", None),
            P("ep", None),
            P("ep", None),
            P("ep", None, None),
            P("ep", None, None),
            P("ep", None, None),
            P(("grp", "ep"), None),
            P("grp"),
            P(("grp", "ep"), None),
        ),
        out_specs=(
            P(("grp", "ep"), None),
            P(("grp", "ep"), None),
            P(("grp", "ep")),
            P(("grp", "ep"), None),
            P(("grp", "ep"), None),
            P(("grp", "ep")),
            P(("grp", "ep"), None),
            P(("grp", "ep"), None),
            P(("grp", "ep")),
            P(("grp", "ep"), None),
            P(("grp", "ep"), None),
            P(("grp", "ep"), None),
            P(("grp", "ep"), None),
            P("ep", "grp", None),
            P("ep", "grp", None),
            P("ep", "grp", None),
        ),
        check_vma=False,
    )
```

time: 4080 us -> 1480 us (0.36)
  waiting for transfers between devices: 2780 us -> 1.47 us
  Pallas kernels: 0 us -> 862 us
  blocking collectives: 682 us -> 0 us
  matrix products: 423 us -> 285 us
  local copies, waits for them, and re-layouts: 77.8 us -> 165 us
  other arithmetic: 79.5 us -> 124 us
    reduce_scatter x10 -> x1, waiting for transfers between devices: 2420 us -> 0.01 us  [per_device(): out_sum = lax.psum_scatter(out_partial, 'ep', scatter_dimension=0)]
    pallas_call x0 -> x10, Pallas kernels: none -> 862 us  [the longest x3 318 us: scatter(): pl.pallas_call(functools.partial(scatter_kernel, n), out_shape=jax.ShapeD...]
    all_to_all x2 -> x0, blocking collectives: 357 us -> none  [the longest x1 186 us: per_device(): lax.all_to_all(grad_slots, 'ep', split_axis=0, concat_axis=0, tiled=True)]
    all_gather x8 -> x3, waiting for transfers between devices: 298 us -> 0.02 us  [the longest x1 0.02 us: per_device(): all_out_grad = lax.all_gather(output_grad, 'ep', axis=0, tiled=True)]
    all_gather x4 -> x0, blocking collectives: 236 us -> none  [the longest x1 125 us: per_device(): lax.all_gather(router_weight, 'ep', axis=0, tiled=True)]
    dot_general x44 -> x46, matrix products: 422 us -> 285 us  [product(): return jnp.einsum(form, left, right, preferred_element_type=F32)]
    unnamed x2 -> x0, blocking collectives: 88.7 us -> none
    unnamed x24 -> x4, waiting for transfers between devices: 63.2 us -> 1.41 us
  transfers between devices with their start and end apart: 23 -> 16, of which waited for: 16 -> 0; matrix products, arithmetic and copies ran while one was open for 13% -> 31% of each run, Pallas kernels for 0% -> 52%
where the time goes in v1:
time: 1480 us; the launch traced here: 1460 us
  Pallas kernels  862 us (58%)
  matrix products  285 us (19%)
  local copies, waits for them, and re-layouts  165 us (11%)
  other arithmetic  124 us (8%)
  between operations  16.7 us (1%)
    pallas_call x3, Pallas kernels, scatter(): pl.pallas_call(functools.partial(scatter_kernel, n), out_shape=jax.ShapeD...  318 us
    pallas_call x3, Pallas kernels, gather(): pl.pallas_call(functools.partial(gather_kernel, n), out_shape=jax.ShapeDt...  317 us
    dot_general x46, matrix products, product(): return jnp.einsum(form, left, right, preferred_element_type=F32)  285 us
    pallas_call x4, Pallas kernels, swap(): pl.pallas_call(functools.partial(swap_kernel, n, m), out_shape=[jax.Shape...  227 us
    convert_element_type x2, local copies, waits for them, and re-layouts, per_device(): residual_all = all_input.astype(F32)  36.3 us
    unnamed x240, local copies, waits for them, and re-layouts  32.9 us
  transfers between devices with their start and end apart: 16, of which 0 were waited for; matrix products, arithmetic and copies ran while one was open for 31% of the time, Pallas kernels for 52%

profile of v1, /device:TPU:0, one launch (start us, length us, event | category | flops | bytes accessed | tf_op | source)
XLA Modules:
  0.0 1461.3 jit_solution(5366252192807913683)
XLA Ops:
  15.9 162.2 %gather.3 = bf16[16,128,2688]{2,1,0:T(8,128)(2,1)} custom-call(bf16[128,2688]{1,0:T(8,128)(2,1)} %pad.9.x_ref), custom_call_target="tpu_custom_call" | custom-call | tf_op jit(solution)/shard_map/gather/pallas_call | solution.py:110
  212.1 99.3 %swap.4 = (bf16[16,192,128]{2,1,0:T(8,128)(2,1)}, bf16[16,256,32]{2,1,0:T(8,128)(2,1)}, bf16[16,176,128]{2,1,0:T(8,128)(2,1)}, bf16[16,176,128]{2,1,0:T(8,128)(2,1)}) custom-call(bf16[16,192,128]{2,1,0:T(8,128)(2,1)} %bitcast.339, bf16[16,256,32]{2,1,0:T(8,128)(2,1)} %bitcast.332, bf16[16,176,128]{2,1,0:T(8,128)(2,1)} %bitcast.342, ...), custom_call_target="tpu_custom_call" | custom-call | tf_op jit(solution)/shard_map/swap/pallas_call | solution.py:266
  339.3 10.5 fusion.165
  349.7 8.1 exponential_reduce_fusion
  357.9 9.5 convolution_convert_fusion.5
  367.4 60.3 %swap.5 = bf16[16,128,128]{2,1,0:T(8,128)(2,1)} custom-call(bf16[16,128,128]{2,1,0:T(8,128)(2,1)} %bitcast.340), custom_call_target="tpu_custom_call" | custom-call | tf_op jit(solution)/shard_map/swap/pallas_call | solution.py:266
  438.2 86.7 %gather.4 = bf16[16,128,2048]{2,1,0:T(8,128)(2,1)} custom-call(bf16[128,2048]{1,0:T(8,128)(2,1)} %multiply_convert_fusion.12.x_ref), custom_call_target="tpu_custom_call" | custom-call | tf_op jit(solution)/shard_map/gather/pallas_call | solution.py:110
  545.6 8.6 fusion.7
  556.8 8.6 fusion.25
  575.1 15.3 %multiply_convert_fusion.4 = (bf16[1024,1408]{1,0:T(8,128)(2,1)}, bf16[1024,1408]{1,0:T(8,128)(2,1)S(1)}) fusion(f32[1024,1408]{1,0:T(8,128)} %copy-done.94, f32[1024,1408]{1,0:T(8,128)} %copy-done.95, bf16[1024,2048]{1,0:T(8,128)(2,1)} %bitcast.335, bf16[1,1408,2048]{2,1,0:T(8,128)(2,1)} %param.32), kind=kOutput, calls=%fused_computation.52 | convolution fusion | flops 5924323328 | bytes 27262976 | tf_op jit(solution)/shard_map/rd,fd->rf/dot_general | solution.py:294
  590.5 11.9 fusion.17
  615.0 12.5 add_convert_fusion.2
  627.5 8.2 convolution_add_fusion
  635.7 12.7 add_convert_fusion
  660.3 103.8 %scatter.3 = f32[128,2176]{1,0:T(8,128)S(1)} custom-call(bf16[4,2,2,128,2176]{4,3,2,1,0:T(8,128)(2,1)S(1)} %bitcast.296), custom_call_target="tpu_custom_call" | custom-call | tf_op jit(solution)/shard_map/scatter/pallas_call | solution.py:218
  770.1 11.3 slice_convert_fusion
  781.4 18.2 %copy.197 = f32[16,128,2048]{1,0,2:T(8,128)} copy(f32[16,128,2048]{2,1,0:T(8,128)} %slice_convert_fusion) | data formatting | bytes 33554432 | tf_op jit(solution)/shard_map/convert_element_type | solution.py:423
  799.6 18.1 %reshape.418 = f32[2048,2,16,64]{0,3,2,1:T(8,128)} reshape(f32[16,128,2048]{1,0,2:T(8,128)} %copy.197) | data formatting | bytes 33554432 | tf_op jit(solution)/shard_map/convert_element_type | solution.py:423
  818.6 8.0 fusion.1
  826.6 12.4 copy.200
  850.3 9.5 fusion.33
  876.8 13.4 reshape_reshape.8
  897.8 21.5 %swap.6 = bf16[16,128,128]{2,1,0:T(8,128)(2,1)} custom-call(bf16[16,128,128]{2,1,0:T(8,128)(2,1)} %bitcast.345), custom_call_target="tpu_custom_call" | custom-call | tf_op jit(solution)/shard_map/swap/pallas_call | solution.py:266
  919.3 15.6 %multiply_reduce_fusion = (f32[2048]{0:T(1024)S(1)}, f32[2048,2048]{0,1:T(8,128)}) fusion(f32[2048,2048]{0,1:T(8,128)} %get-tuple-element.78, f32[2048]{0:T(1024)S(1)} %copy-done.50, bf16[2048,128]{1,0:T(8,128)(2,1)} %bitcast.325, bf16[2048,256]{1,0:T(8,128)(2,1)} %convolution_convert_fusion.2), kind=kOutput, calls=%fused_computation.4 | convolution fusion | flops 1086322688 | bytes 34619392 | tf_op jit(solution)/shard_map/qd,kd->qk/dot_general | solution.py:294
  935.0 8.8 multiply_convert_fusion
  951.8 8.7 convolution_convert_fusion.3
  968.2 8.2 fusion.168
  976.4 9.2 add_convert_fusion.1
  989.0 68.3 %scatter.5 = f32[128,576]{1,0:T(8,128)S(1)} custom-call(bf16[4,2,2,128,576]{4,3,2,1,0:T(8,128)(2,1)S(1)} %pad_maximum_fusion.2.p_ref), custom_call_target="tpu_custom_call" | custom-call | tf_op jit(solution)/shard_map/scatter/pallas_call | solution.py:218
  1069.8 67.7 %gather.5 = bf16[16,128,576]{2,1,0:T(8,128)(2,1)} custom-call(bf16[128,576]{1,0:T(8,128)(2,1)} %pad_maximum_fusion.8.x_ref), custom_call_target="tpu_custom_call" | custom-call | tf_op jit(solution)/shard_map/gather/pallas_call | solution.py:110
  1149.3 145.8 %scatter.4 = f32[128,2048]{1,0:T(8,128)S(1)} custom-call(bf16[4,2,2,128,2048]{4,3,2,1,0:T(8,128)(2,1)S(1)} %bitcast.295), custom_call_target="tpu_custom_call" | custom-call | tf_op jit(solution)/shard_map/scatter/pallas_call | solution.py:218
  1356.2 46.1 %swap.7 = (bf16[16,64,544]{2,1,0:T(8,128)(2,1)}, bf16[16,16,256]{2,1,0:T(8,128)(2,1)}, f32[16,2,144]{2,1,0:T(2,128)}) custom-call(bf16[16,64,544]{2,1,0:T(8,128)(2,1)} %bitcast.329, bf16[16,16,256]{2,1,0:T(8,128)(2,1)} %bitcast.361, f32[16,2,144]{2,1,0:T(2,128)} %maximum_bitcast_fusion.refs_2_), custom_call_target="tpu_custom_call" | custom-call | tf_op jit(solution)/shard_map/swap/pallas_call | solution.py:266
  (441 shorter events, 335.6 us)
Async XLA Ops:
  7.2 601.2 %copy-start = (bf16[176,2048]{1,0:T(8,128)(2,1)S(1)}, bf16[176,2048]{1,0:T(8,128)(2,1)}, u32[]{:S(2)}) copy-start(bf16[176,2048]{1,0:T(8,128)(2,1)} %param.29) | copy-start | bytes 2162692
  7.2 424.3 %all-gather.4.cloned.1.call-start = ((), (), s32[]{:S(2)}) async-start(), calls=%async_computation.1 | async-start | bytes 8912896 | tf_op jit(solution)/shard_map/all_gather | solution.py:417
  7.9 557.5 %all-gather.6.cloned.1.call-start = ((), (), s32[]{:S(2)}) async-start(), calls=%async_computation.3 | async-start | bytes 8912896 | tf_op jit(solution)/shard_map/all_gather | solution.py:418
  8.7 1421.7 %all-gather.8.cloned.1.call-start = ((), (), s32[]{:S(2)}) async-start(), calls=%async_computation.4 | async-start | bytes 9469952 | tf_op jit(solution)/shard_map/all_gather | solution.py:550
  180.1 256.2 %copy-start.65 = (f32[16,128]{1,0:T(8,128)}, f32[16,128]{1,0:T(8,128)S(1)}, u32[]{:S(2)}) copy-start(f32[16,128]{1,0:T(8,128)S(1)} %get-tuple-element.30) | copy-start | bytes 24580
  187.9 140.7 %copy-start.70 = (f32[2048]{0:T(1024)}, f32[2048]{0:T(1024)S(1)}, u32[]{:S(2)}) copy-start(f32[2048]{0:T(1024)S(1)} %iota_convert_fusion) | copy-start | bytes 24580
  188.0 140.7 %copy-start.87 = (f32[32]{0:T(128)}, f32[32]{0:T(128)S(1)}, u32[]{:S(2)}) copy-start(f32[32]{0:T(128)S(1)} %negate_power_fusion) | copy-start | bytes 388
  202.3 322.5 %copy-start.21 = (bf16[16,128,16]{2,1,0:T(8,128)(2,1)}, bf16[16,128,16]{2,1,0:T(8,128)(2,1)S(1)}, u32[]{:S(2)}) copy-start(bf16[16,128,16]{2,1,0:T(8,128)(2,1)S(1)} %slice.118) | copy-start | bytes 196612
  656.7 109.2 %copy-start.81 = (f32[128]{0:T(128)S(1)}, f32[128]{0:T(128)}, u32[]{:S(2)}) copy-start(f32[128]{0:T(128)} %copy-done.80) | copy-start | bytes 1540
  660.3 105.7 %copy-start.6 = (f32[128,2048]{1,0:T(8,128)S(1)}, f32[128,2048]{1,0:T(8,128)}, u32[]{:S(2)}) copy-start(f32[128,2048]{1,0:T(8,128)} %copy-done.5) | copy-start | bytes 3145732
  660.3 105.7 %copy-start.22 = (bf16[16,128,16]{2,1,0:T(8,128)(2,1)S(1)}, bf16[16,128,16]{2,1,0:T(8,128)(2,1)}, u32[]{:S(2)}) copy-start(bf16[16,128,16]{2,1,0:T(8,128)(2,1)} %copy-done.21) | copy-start | bytes 196612
  660.3 105.7 %copy-start.66 = (f32[16,128]{1,0:T(8,128)S(1)}, f32[16,128]{1,0:T(8,128)}, u32[]{:S(2)}) copy-start(f32[16,128]{1,0:T(8,128)} %copy-done.65) | copy-start | bytes 24580
  660.3 106.8 %copy-start.23 = (bf16[128,2048]{1,0:T(8,128)(2,1)S(1)}, bf16[128,2048]{1,0:T(8,128)(2,1)}, u32[]{:S(2)}) copy-start(bf16[128,2048]{1,0:T(8,128)(2,1)} %param.35) | copy-start | bytes 1572868
  768.9 680.9 %reduce-scatter.2.cloned.1.call-start = ((), (), s32[]{:S(2)}) async-start(), calls=%async_computation.2 | async-start | bytes 8912896 | tf_op jit(solution)/shard_map/reduce_scatter | solution.py:503
  861.7 555.6 %collective-permute-start.10 = (bf16[1024,1408]{1,0:T(8,128)(2,1)}, bf16[1024,1408]{1,0:T(8,128)(2,1)}, u32[]{:S(2)}, u32[]{:S(2)}) collective-permute-start(bf16[1024,1408]{1,0:T(8,128)(2,1)} %fusion.31), channel_id=1, source_target_pairs={{0,16},{16,0},{1,17},{17,1},{2,18},{18,2},{3,19},{19,3},{4,20},{20... | collective-permute-start | bytes 8650760 | tf_op jit(solution)/shard_map/ppermute | solution.py:283
  876.8 547.0 %collective-permute-start.9 = (bf16[1024,1408]{1,0:T(8,128)(2,1)}, bf16[1024,1408]{1,0:T(8,128)(2,1)}, u32[]{:S(2)}, u32[]{:S(2)}) collective-permute-start(bf16[1024,1408]{1,0:T(8,128)(2,1)} %fusion.30), channel_id=1, source_target_pairs={{0,16},{16,0},{1,17},{17,1},{2,18},{18,2},{3,19},{19,3},{4,20},{20... | collective-permute-start | bytes 8650760 | tf_op jit(solution)/shard_map/ppermute | solution.py:283
  1140.9 206.3 %collective-permute-start.3 = (bf16[64,576]{1,0:T(8,128)(2,1)}, bf16[64,576]{1,0:T(8,128)(2,1)}, u32[]{:S(2)}, u32[]{:S(2)}) collective-permute-start(bf16[64,576]{1,0:T(8,128)(2,1)} %fusion.145), channel_id=1, source_target_pairs={{0,16},{16,0},{1,17},{17,1},{2,18},{18,2},{3,19},{19,3},{4,20},{20... | collective-permute-start | bytes 221192 | tf_op jit(solution)/shard_map/ppermute | solution.py:283
  1149.2 145.9 %copy-start.12 = (bf16[16,128,576]{2,1,0:T(8,128)(2,1)S(1)}, bf16[16,128,576]{2,1,0:T(8,128)(2,1)}, u32[]{:S(2)}) copy-start(bf16[16,128,576]{2,1,0:T(8,128)(2,1)} %copy-done.11) | copy-start | bytes 7077892
  1149.2 145.9 %copy-start.44 = (bf16[128,576]{1,0:T(8,128)(2,1)S(1)}, bf16[128,576]{1,0:T(8,128)(2,1)}, u32[]{:S(2)}) copy-start(bf16[128,576]{1,0:T(8,128)(2,1)} %pad_maximum_fusion.8.x_ref) | copy-start | bytes 442372
  1149.2 145.9 %copy-start.85 = (f32[128]{0:T(128)S(1)}, f32[128]{0:T(128)}, u32[]{:S(2)}) copy-start(f32[128]{0:T(128)} %add_rsqrt_fusion.3) | copy-start | bytes 1540
  1149.2 148.5 %copy-start.77 = (f32[512]{0:T(512)S(1)}, f32[512]{0:T(512)}, u32[]{:S(2)}) copy-start(f32[512]{0:T(512)} %get-tuple-element.36) | copy-start | bytes 6148
  1149.3 148.6 %copy-start.72 = (f32[2048]{0:T(1024)S(1)}, f32[2048]{0:T(1024)}, u32[]{:S(2)}) copy-start(f32[2048]{0:T(1024)} %get-tuple-element.32) | copy-start | bytes 24580
  1149.3 148.7 %copy-start.48 = (bf16[2048,176]{0,1:T(8,128)(2,1)S(1)}, bf16[2048,176]{0,1:T(8,128)(2,1)}, u32[]{:S(2)}) copy-start(bf16[2048,176]{0,1:T(8,128)(2,1)} %copy-done.47) | copy-start | bytes 2162692
  1324.7 28.2 %collective-permute-start = (bf16[1024,544]{0,1:T(8,128)(2,1)S(1)}, bf16[1024,544]{0,1:T(8,128)(2,1)}, u32[]{:S(2)}, u32[]{:S(2)}) collective-permute-start(bf16[1024,544]{0,1:T(8,128)(2,1)S(1)} %bitcast.349), channel_id=1, source_target_pairs={{0,16},{16,0},{1,17},{17,1},{2,18},{18,2},{3,19},{19,3},{4,20},{20... | collective-permute-start | bytes 3342344 | tf_op jit(solution)/shard_map/ppermute | solution.py:283
  1330.1 16.9 %collective-permute-start.7 = (bf16[88,2048]{1,0:T(8,128)(2,1)S(1)}, bf16[88,2048]{1,0:T(8,128)(2,1)S(1)}, u32[]{:S(2)}, u32[]{:S(2)}) collective-permute-start(bf16[88,2048]{1,0:T(8,128)(2,1)S(1)} %fusion.132), channel_id=1, source_target_pairs={{0,16},{16,0},{1,17},{17,1},{2,18},{18,2},{3,19},{19,3},{4,20},{20... | collective-permute-start | bytes 1081352 | tf_op jit(solution)/shard_map/ppermute | solution.py:283
  1346.9 2.5 collective-permute-start.1
  1347.1 4.8 collective-permute-start.8
  1349.4 88.0 %collective-permute-start.11 = (bf16[704,2048]{1,0:T(8,128)(2,1)}, bf16[704,2048]{1,0:T(8,128)(2,1)}, u32[]{:S(2)}, u32[]{:S(2)}) collective-permute-start(bf16[704,2048]{1,0:T(8,128)(2,1)} %fusion.32), channel_id=1, source_target_pairs={{0,16},{16,0},{1,17},{17,1},{2,18},{18,2},{3,19},{19,3},{4,20},{20... | collective-permute-start | bytes 8650760 | tf_op jit(solution)/shard_map/ppermute | solution.py:283
  1403.1 13.1 collective-permute-start.2
  1431.9 12.9 collective-permute-start.6
  1437.3 8.2 collective-permute-start.4
  1446.2 6.6 collective-permute-start.5
  (101 other events, 1182.1 us)
Sparse Core Ops, SparseCore 0:
  10.8 185.3 all-gather.3
  199.0 178.3 all-gather.5
  769.0 124.7 all-gather.7
  985.8 267.3 reduce-scatter.1

commit v2 on v1

v2 whole, which is shorter than its diff:
```python
import functools
import math

import jax
import jax.numpy as jnp
from jax import lax
from jax.experimental import pallas as pl
from jax.experimental.pallas import tpu as pltpu
from jax.sharding import PartitionSpec as P

D = 2048
HEADS = 16
NOPE = 128
ROPE = 64
VH = 128
LATENT = 512
TOPK = 6

EPSILON = 1e-06
MASKED = -1e30

MESH = pl.DeviceIdType.MESH
ANY = pl.BlockSpec(memory_space=pl.ANY)
DMA = pltpu.SemaphoreType.DMA
F32 = jnp.float32
BF16 = jnp.bfloat16


def remote(src, dst, send, recv, peer):
    return pltpu.make_async_remote_copy(
        src_ref=src,
        dst_ref=dst,
        send_sem=send,
        recv_sem=recv,
        device_id={"ep": peer},
        device_id_type=MESH,
    )


def greet(peers):
    barrier = pltpu.get_barrier_semaphore()
    for peer in peers:
        pl.semaphore_signal(barrier, inc=1, device_id={"ep": peer}, device_id_type=MESH)
    pl.semaphore_wait(barrier, len(peers))


def around(n):
    me = lax.axis_index("ep")
    x, y = me % 2, (me // 2) % 2
    return me, me // 4, y, x, me + 1 - 2 * x, me + 2 - 4 * y


def near(z, nz, below, above):
    for s in range(nz - 1):
        pl.when(z - 1 - s >= 0)(functools.partial(below, s, z - 1 - s))
        pl.when(z + 1 + s < nz)(functools.partial(above, s, z + 1 + s))


def gather_kernel(n, x_ref, o_ref, own, us, ur, ds, dr, xs, xr, ys, yr):
    me, z, y, x, px, py = around(n)
    nz = n // 4
    low = me % 4
    half = x_ref.shape[0] // 2
    top, bottom = pl.ds(0, half), pl.ds(half, half)
    up, down = (me + 4) % n, (me + n - 4) % n
    barrier = pltpu.get_barrier_semaphore()
    greeted = [(px, None), (py, None), (up, z + 1 < nz), (down, z > 0)]
    for peer, there in greeted:

        def hello(peer=peer):
            pl.semaphore_signal(barrier, inc=1, device_id={"ep": peer}, device_id_type=MESH)

        hello() if there is None else pl.when(there)(hello)
    on_line = (z + 1 < nz).astype(jnp.int32) + (z > 0).astype(jnp.int32)
    pl.semaphore_wait(barrier, 2 + on_line)
    local = pltpu.make_async_copy(x_ref, o_ref.at[me], own)
    local.start()

    def over_x(src, b, part, i):
        return remote(src.at[part], o_ref.at[b, part], xs.at[i], xr.at[i], px)

    def over_y(src, b, part, i):
        return remote(src.at[part], o_ref.at[b, part], ys.at[i], yr.at[i], py)

    def upward(src, b, s):
        return remote(src, o_ref.at[b], us.at[s], ur.at[s], up)

    def downward(src, b, s):
        return remote(src, o_ref.at[b], ds.at[s], dr.at[s], down)

    def spread(src, t):
        b = t * 4 + low
        over_x(src, b, top, t).start()
        over_y(src, b, bottom, t).start()
        over_y(src, b, top, nz + t).start()
        over_x(src, b, bottom, nz + t).start()

    pl.when(z + 1 < nz)(lambda: upward(x_ref, me, 0).start())
    pl.when(z > 0)(lambda: downward(x_ref, me, 0).start())
    spread(x_ref, z)

    def from_below(s, t):
        b = t * 4 + low
        upward(o_ref.at[b], b, s).wait_recv()
        pl.when(z + 1 < nz)(lambda: upward(o_ref.at[b], b, s + 1).start())
        spread(o_ref.at[b], t)

    def from_above(s, t):
        b = t * 4 + low
        downward(o_ref.at[b], b, s).wait_recv()
        pl.when(z > 0)(lambda: downward(o_ref.at[b], b, s + 1).start())
        spread(o_ref.at[b], t)

    def turn(s, t):
        bx = t * 4 + low + px - me
        by = t * 4 + low + py - me
        over_x(o_ref.at[bx], bx, top, t).wait_recv()
        over_y(o_ref.at[bx], bx, top, 2 * nz + t).start()
        over_y(o_ref.at[by], by, bottom, t).wait_recv()
        over_x(o_ref.at[by], by, bottom, 2 * nz + t).start()

    for s in range(nz - 1):
        pl.when(z - 1 - s >= 0)(functools.partial(from_below, s, z - 1 - s))
        pl.when(z + 1 + s < nz)(functools.partial(from_above, s, z + 1 + s))
        if s == 0:
            turn(0, z)
        else:
            pl.when(z - s >= 0)(functools.partial(turn, s, z - s))
            pl.when(z + s < nz)(functools.partial(turn, s, z + s))
    pl.when(z - (nz - 1) >= 0)(functools.partial(turn, 0, z - (nz - 1)))
    pl.when(z + (nz - 1) < nz)(functools.partial(turn, 0, z + (nz - 1)))

    def finish(s, t):
        bx = t * 4 + low + px - me
        by = t * 4 + low + py - me
        bxy = bx + py - me
        over_y(o_ref.at[by], by, top, nz + t).wait_recv()
        over_x(o_ref.at[bx], bx, bottom, nz + t).wait_recv()
        over_y(o_ref.at[bxy], bxy, top, 2 * nz + t).wait_recv()
        over_x(o_ref.at[bxy], bxy, bottom, 2 * nz + t).wait_recv()
        for i in range(3):
            over_x(x_ref, me, top, i * nz + t).wait_send()
            over_y(x_ref, me, top, i * nz + t).wait_send()

    finish(0, z)
    near(z, nz, finish, finish)

    def sent_up(s, t):
        upward(x_ref, me, s).wait_send()

    def sent_down(s, t):
        downward(x_ref, me, s).wait_send()

    for s in range(nz - 1):
        pl.when((z + 1 < nz) & (z - s >= 0))(functools.partial(sent_up, s, z))
        pl.when((z > 0) & (z + s < nz))(functools.partial(sent_down, s, z))
    local.wait()


def gather(x, cid):
    n = lax.axis_size("ep")
    nz = n // 4
    return pl.pallas_call(
        functools.partial(gather_kernel, n),
        out_shape=jax.ShapeDtypeStruct((n,) + x.shape, x.dtype),
        in_specs=[ANY],
        out_specs=ANY,
        scratch_shapes=[DMA] + [DMA((nz,))] * 4 + [DMA((3 * nz,))] * 4,
        compiler_params=pltpu.CompilerParams(collective_id=cid, has_side_effects=True),
        name="gather",
    )(x)


def add_rows(dst, left, right, rows):
    step = 16

    def body(i, carry):
        r = pl.ds(pl.multiple_of(i * step, step), step)
        dst[r] = (left[r].astype(F32) + right[r].astype(F32)).astype(dst.dtype)
        return carry

    lax.fori_loop(0, rows // step, body, 0)


def exchange_kernel(n, m, w, *refs):
    refs = list(refs)

    def take(count):
        out = refs[:count]
        del refs[:count]
        return out

    sums_in, swaps_in = take(m), take(w)
    sums_out, swaps_out = take(m), take(w)
    room = [take(7) for _ in range(m)]
    sems = [take(8) for _ in range(m)]
    swap_sems = take(3) if w else None
    me, z, y, x, px, py = around(n)
    nz = n // 4
    low = me % 4
    to = [(z + k) % nz for k in range(nz)]
    at = [t * 4 + low for t in to]
    everyone = [(me + k) % n for k in range(n)]
    back = [(me + n - k) % n for k in range(n)]
    if w:
        greet(everyone[1:])
    else:
        greet([px, py] + at[1:])
    order = [2, 1, 3, 0] if nz == 4 else list(range(1, nz)) + [0]
    sends, copies = [], []

    def halves(j):
        half = sums_in[j].shape[3] // 2
        return half, pl.ds(0, half), pl.ds(half, half)

    first, second, third = {}, {}, {}

    def stage_one(j, k):
        p = sums_in[j]
        half, top, bottom = halves(j)
        la, lb, a1, b1, a2, b2, zb = room[j]
        lsa, lsb, xs, xr, ys, yr, zs, zr = sems[j]
        t = to[k]
        c = remote(p.at[t, 1 - y, :, top], a1.at[k], ys.at[k], yr.at[k], py)
        d = remote(p.at[t, :, 1 - x, bottom], b1.at[k], xs.at[k], xr.at[k], px)
        c.start()
        d.start()
        e = pltpu.make_async_copy(p.at[t, y, :, top], la.at[k], lsa.at[k])
        f = pltpu.make_async_copy(p.at[t, :, x, bottom], lb.at[k], lsb.at[k])
        e.start()
        f.start()
        first[j, k] = (c, d, e, f)
        sends.extend([c, d])

    def stage_two(j, k):
        half, top, bottom = halves(j)
        la, lb, a1, b1, a2, b2, zb = room[j]
        lsa, lsb, xs, xr, ys, yr, zs, zr = sems[j]
        c, d, e, f = first[j, k]
        e.wait()
        c.wait_recv()
        for i in range(2):
            add_rows(la.at[k, i], la.at[k, i], a1.at[k, i], half)
        g = remote(la.at[k, 1 - x], a2.at[k], xs.at[nz + k], xr.at[nz + k], px)
        g.start()
        f.wait()
        d.wait_recv()
        for i in range(2):
            add_rows(lb.at[k, i], lb.at[k, i], b1.at[k, i], half)
        h = remote(lb.at[k, 1 - y], b2.at[k], ys.at[nz + k], yr.at[nz + k], py)
        h.start()
        second[j, k] = (g, h)
        sends.extend([g, h])

    def stage_three(j, k):
        half, top, bottom = halves(j)
        la, lb, a1, b1, a2, b2, zb = room[j]
        lsa, lsb, xs, xr, ys, yr, zs, zr = sems[j]
        g, h = second[j, k]
        g.wait_recv()
        add_rows(a2.at[k], la.at[k, x], a2.at[k], half)
        if k:
            c = remote(a2.at[k], zb.at[k, top], zs.at[k], zr.at[k], at[k])
            c.start()
        h.wait_recv()
        add_rows(b2.at[k], lb.at[k, y], b2.at[k], half)
        if k:
            d = remote(b2.at[k], zb.at[k, bottom], zs.at[nz + k], zr.at[nz + k], at[k])
            d.start()
            third[j, k] = (c, d)
            sends.extend([c, d])

    def start_swaps():
        own, ss, rs = swap_sems
        for j in range(w):
            local = pltpu.make_async_copy(swaps_in[j].at[me], swaps_out[j].at[me], own.at[j])
            local.start()
            copies.append(local)
        for k in range(1, n):
            for j in range(w):
                c = remote(
                    swaps_in[j].at[everyone[k]],
                    swaps_out[j].at[me],
                    ss.at[j, k],
                    rs.at[j, k],
                    everyone[k],
                )
                c.start()
                sends.append(c)

    steps = [(j, k) for j in range(m) for k in order]
    for i in range(min(2, len(steps))):
        stage_one(*steps[i])
    if w:
        start_swaps()
    for i, step in enumerate(steps):
        stage_two(*step)
        if i + 2 < len(steps):
            stage_one(*steps[i + 2])
        if i:
            stage_three(*steps[i - 1])
    if steps:
        stage_three(*steps[-1])
    for j in range(m):
        half, top, bottom = halves(j)
        la, lb, a1, b1, a2, b2, zb = room[j]
        o_ref = sums_out[j]
        for k in range(1, nz):
            c, d = third[j, k]
            c.wait_recv()
            d.wait_recv()
        for part, offset in ((a2, 0), (b2, half)):

            def body(i, carry, part=part, offset=offset, zb=zb, o_ref=o_ref):
                r = pl.ds(pl.multiple_of(i * 16, 16), 16)
                q = pl.ds(pl.multiple_of(i * 16 + offset, 16), 16)
                total = part[0, r].astype(F32)
                for k in range(1, nz):
                    total = total + zb[k, q].astype(F32)
                o_ref[q] = total.astype(o_ref.dtype)
                return carry

            lax.fori_loop(0, half // 16, body, 0)
    if w:
        own, ss, rs = swap_sems
        for k in range(1, n):
            for j in range(w):
                remote(
                    swaps_in[j].at[back[k]],
                    swaps_out[j].at[back[k]],
                    ss.at[j, k],
                    rs.at[j, k],
                    everyone[k],
                ).wait_recv()
    for copy in sends:
        copy.wait_send()
    for copy in copies:
        copy.wait()


def exchange(cid, sums=(), swaps=()):
    n = lax.axis_size("ep")
    nz = n // 4
    m, w = len(sums), len(swaps)
    kept_rows = [p.shape[1] for p in sums]
    sums = [jnp.pad(p, ((0, 0), (0, -p.shape[1] % 32), (0, 0))) for p in sums]
    views = [p.reshape((nz, 2, 2) + p.shape[1:]) for p in sums]
    scratch = []
    for p in sums:
        rows, cols = p.shape[1:]
        half = rows // 2
        scratch += [pltpu.VMEM((nz, 2, half, cols), p.dtype)] * 4
        scratch += [pltpu.VMEM((nz, half, cols), p.dtype)] * 2
        scratch += [pltpu.VMEM((nz, rows, cols), p.dtype)]
    for p in sums:
        scratch += [DMA((nz,))] * 2 + [DMA((2 * nz,))] * 6
    if w:
        scratch += [DMA((w,)), DMA((w, n)), DMA((w, n))]
    out = pl.pallas_call(
        functools.partial(exchange_kernel, n, m, w),
        out_shape=[jax.ShapeDtypeStruct(p.shape[1:], F32) for p in sums]
        + [jax.ShapeDtypeStruct(a.shape, a.dtype) for a in swaps],
        in_specs=[ANY] * (m + w),
        out_specs=[pl.BlockSpec(memory_space=pltpu.VMEM)] * m + [ANY] * w,
        scratch_shapes=scratch,
        compiler_params=pltpu.CompilerParams(
            collective_id=cid, has_side_effects=True, vmem_limit_bytes=(40 << 20) if m else None
        ),
        name="exchange",
    )(*views, *swaps)
    return [a[:rows] for a, rows in zip(out, kept_rows)] + list(out[m:])


def both(p):
    g = lax.axis_index("grp")
    mine = lax.dynamic_index_in_dim(p, g, 0, keepdims=False)
    theirs = lax.dynamic_index_in_dim(p, 1 - g, 0, keepdims=False)
    return mine, lax.ppermute(theirs.astype(BF16), "grp", [(0, 1), (1, 0)])


def over_groups(p):
    if lax.axis_size("grp") == 2:
        mine, other = both(p)
        return mine.astype(F32) + other.astype(F32)
    return lax.psum_scatter(p.astype(BF16), "grp", scatter_dimension=0, tiled=False).astype(F32)


def product_over_groups(left, right):
    groups = lax.axis_size("grp")
    rows = left.shape[1] // groups
    if groups != 2:
        whole = product("km,kn->mn", left, right)
        return over_groups(whole.reshape(groups, rows, -1))
    g = lax.axis_index("grp")
    mine = lax.dynamic_slice_in_dim(left, g * rows, rows, 1)
    theirs = lax.dynamic_slice_in_dim(left, (1 - g) * rows, rows, 1)
    sent = product("km,kn->mn", theirs, right).astype(BF16)
    other = lax.ppermute(sent, "grp", [(0, 1), (1, 0)])
    return product("km,kn->mn", mine, right) + other.astype(F32)


def from_partner(values):
    groups = lax.axis_size("grp")
    return lax.ppermute(values, "grp", [(g, g + 1 - 2 * (g % 2)) for g in range(groups)])


def to_row_owner(block):
    groups, n = lax.axis_size("grp"), lax.axis_size("ep")
    pairs = [(h * n + e, e * groups + h) for h in range(groups) for e in range(n)]
    return lax.ppermute(block.astype(BF16), ("grp", "ep"), pairs).astype(F32)


def product(form, left, right):
    return jnp.einsum(form, left, right, preferred_element_type=F32)


def rms_scale(values):
    return lax.rsqrt(jnp.mean(values * values, axis=-1, keepdims=True) + EPSILON)


def rotary_tables(positions):
    halfway = ROPE // 2
    inverse = 10000.0 ** (-(jnp.arange(halfway, dtype=F32) * 2.0 / ROPE))
    angles = positions[:, None] * inverse[None, :]
    return (jnp.cos(angles), jnp.sin(angles))


def rotate(values, cos_table, sin_table):
    halfway = values.shape[-1] // 2
    first = values[..., :halfway]
    second = values[..., halfway:]
    return jnp.concatenate(
        [first * cos_table - second * sin_table, second * cos_table + first * sin_table], axis=-1
    )


def unrotate(grads, cos_table, sin_table):
    halfway = grads.shape[-1] // 2
    first = grads[..., :halfway]
    second = grads[..., halfway:]
    return jnp.concatenate(
        [first * cos_table + second * sin_table, second * cos_table - first * sin_table], axis=-1
    )


def norm_back(grad_unit, unit_values, scale_values):
    return scale_values * (
        grad_unit - unit_values * jnp.mean(grad_unit * unit_values, axis=-1, keepdims=True)
    )


def silu_back(grad_hidden, gate_value, up_value):
    sigmoid = jax.nn.sigmoid(gate_value)
    grad_gate = grad_hidden * up_value * sigmoid * (1.0 + gate_value * (1.0 - sigmoid))
    grad_up = grad_hidden * gate_value * sigmoid
    return (grad_gate.astype(BF16), grad_up.astype(BF16))


def column_halves(weight, n, half):
    rows, width = weight.shape[0], weight.shape[1] // n
    parts = weight.T.reshape(n, 2, width // 2, rows)
    return lax.dynamic_index_in_dim(parts, half, 1, keepdims=False)


def columns_in(blocks):
    n, width, rows = blocks.shape
    return blocks.transpose(1, 0, 2).reshape(width, n * rows)


def both_halves(mine, other, even):
    return jnp.concatenate([jnp.where(even, mine, other), jnp.where(even, other, mine)], axis=0)


def per_device(
    layer_input,
    attention_gain,
    query_weight,
    latent_weight,
    latent_gain,
    expand_weight,
    output_weight,
    feedforward_gain,
    router_weight,
    shared_gate,
    shared_up,
    shared_down,
    expert_gate,
    expert_up,
    expert_down,
    expert_routes,
    prefix_length,
    output_grad,
):
    n = lax.axis_size("ep")
    groups = lax.axis_size("grp")
    e = lax.axis_index("ep")
    half = lax.axis_index("grp") % 2
    even = half == 0
    tokens = layer_input.shape[0]
    length = tokens * n
    capacity = tokens * TOPK * 4 // (3 * n)
    scale = 1.0 / math.sqrt(NOPE + ROPE)
    rows_dev = attention_gain.shape[0]
    latent_rows = latent_gain.shape[0]
    rows_out = D // (groups * n)
    expand_rows = LATENT // (groups * n)

    pad = jnp.zeros((rows_dev - latent_rows,), BF16)
    first_block = jnp.concatenate(
        [
            layer_input,
            latent_weight,
            router_weight,
            attention_gain[:, None],
            feedforward_gain[:, None],
            jnp.concatenate([latent_gain, pad])[:, None],
            expert_routes.astype(BF16),
        ],
        axis=1,
    )
    width = first_block.shape[1]
    first_block = jnp.pad(first_block, ((0, 0), (0, -width % 128)))
    first_all = gather(first_block, 0)
    c0 = D
    c1 = c0 + LATENT + ROPE
    c2 = c1 + n
    all_input = first_all[:, :, :c0].reshape(length, D)
    latent_w = first_all[:, :, c0:c1].reshape(D, LATENT + ROPE)
    router_w = first_all[:, :, c1:c2].reshape(D, n)
    attn_gain = first_all[:, :, c2].reshape(D).astype(F32)
    ffn_gain = first_all[:, :, c2 + 1].reshape(D).astype(F32)
    lat_gain = first_all[:, :latent_rows, c2 + 2].reshape(LATENT).astype(F32)
    routes = first_all[:, :, c2 + 3 : c2 + 3 + TOPK].astype(jnp.int32)

    q_half, x_half = (
        column_halves(query_weight, n, half),
        column_halves(expand_weight, n, half),
    )
    q_half, x_half, first_all = lax.optimization_barrier((q_half, x_half, first_all))
    q_blocks, x_blocks = exchange(1, swaps=(q_half, x_half))
    q_mine, x_mine = columns_in(q_blocks), columns_in(x_blocks)
    query_t = both_halves(q_mine, from_partner(q_mine), even)
    expand_t = both_halves(x_mine, from_partner(x_mine), even)
    shared_half = jnp.where(even, shared_gate, shared_up)
    shared_half = shared_half.T.reshape(n, shared_half.shape[1] // n, rows_dev)

    out_w_half = lax.dynamic_slice_in_dim(output_weight, half * (D // 2), D // 2, 1)
    out_w_half, later_grad, q_blocks = lax.optimization_barrier(
        (out_w_half, output_grad, q_blocks)
    )
    out_w_mine = lax.all_gather(out_w_half, "ep", axis=0, tiled=True)
    out_w_other = from_partner(out_w_mine)
    all_out_grad = lax.all_gather(later_grad, "ep", axis=0, tiled=True)

    def own(values):
        return lax.dynamic_slice_in_dim(values, e * tokens, tokens, 0)

    residual_all = all_input.astype(F32)
    unit_all = residual_all * rms_scale(residual_all)
    normed = (unit_all * attn_gain).astype(BF16)
    places = jnp.arange(length, dtype=jnp.int32)
    cos_table, sin_table = rotary_tables(places.astype(F32))
    query_raw = product("td,cd->tc", normed, query_t)
    query_n = query_raw[:, :NOPE].astype(BF16)
    query_r = rotate(query_raw[:, NOPE:], cos_table, sin_table).astype(BF16)
    compressed = product("td,dc->tc", normed, latent_w)
    latent_raw = compressed[:, :LATENT]
    latent = (latent_raw * rms_scale(latent_raw) * lat_gain).astype(BF16)
    key_rope = rotate(compressed[:, LATENT:], cos_table, sin_table).astype(BF16)
    expanded = product("tl,cl->tc", latent, expand_t).astype(BF16)
    key_nope = expanded[:, :NOPE]
    values = expanded[:, NOPE:]
    visible = (places[None, :] <= places[:, None]) | (places[None, :] < prefix_length[0])

    def attention_scores():
        scores = product("qd,kd->qk", query_n, key_nope)
        scores = scores + product("qd,kd->qk", query_r, key_rope)
        return jnp.where(visible, scores * scale, MASKED)

    scores = attention_scores()
    row_max = jnp.max(scores, axis=-1, keepdims=True)
    log_total = row_max + jnp.log(jnp.sum(jnp.exp(scores - row_max), axis=-1, keepdims=True))
    weights = jnp.exp(scores - log_total).astype(BF16)
    attended_head = product("qk,kd->qd", weights, values).astype(BF16)
    attended_blocks, shared_blocks = exchange(
        2, swaps=(attended_head.reshape(n, tokens, VH), shared_half)
    )
    attended = attended_blocks.transpose(1, 0, 2).reshape(tokens, HEADS * VH)
    shared_mine = columns_in(shared_blocks)
    shared_other = from_partner(shared_mine)
    gate_t = jnp.where(even, shared_mine, shared_other)
    up_t = jnp.where(even, shared_other, shared_mine)

    residual_in = layer_input.astype(F32)
    input_scale = rms_scale(residual_in)
    input_unit = residual_in * input_scale
    out_mine = product("ta,ad->td", attended, out_w_mine)
    out_other = product("ta,ad->td", attended, out_w_other)
    residual_mid = residual_in + jnp.concatenate(
        [jnp.where(even, out_mine, out_other), jnp.where(even, out_other, out_mine)], axis=1
    )
    mid_scale = rms_scale(residual_mid)
    mid_unit = residual_mid * mid_scale
    own_ffn_in = (mid_unit * ffn_gain).astype(BF16)
    ffn_blocks = gather(own_ffn_in, 3)
    ffn_in = ffn_blocks.reshape(length, D)

    out_blocks = all_out_grad.reshape(n, tokens, D)
    router_all = jax.nn.softmax(product("td,de->te", ffn_in, router_w), axis=-1)
    gate_values = jnp.sum(
        jnp.where(jnp.arange(n, dtype=jnp.int32) == e, router_all, 0.0), axis=-1
    ).reshape(n, tokens)
    chosen = jnp.any(routes == e, axis=-1)
    chosen_int = chosen.astype(jnp.int32)
    place = jnp.cumsum(chosen_int, axis=1) - chosen_int
    kept = chosen & (place < capacity)
    dispatch = (
        (place[:, None, :] == jnp.arange(capacity, dtype=jnp.int32)[None, :, None])
        & kept[:, None, :]
    )
    slot_gate = jnp.sum(jnp.where(dispatch, gate_values[:, None, :], 0.0), axis=-1)
    dispatch = dispatch.astype(BF16)
    kept_gate = jnp.where(kept, gate_values, 0.0)

    def to_slots(blocks):
        return product("bst,btd->bsd", dispatch, blocks)

    def to_tokens(slots):
        return product("bst,bsd->btd", dispatch, slots.reshape(n, capacity, D))

    incoming = to_slots(ffn_blocks).astype(BF16).reshape(n * capacity, D)
    out_slots = to_slots(out_blocks)
    slot_grad = (out_slots * slot_gate[:, :, None]).astype(BF16).reshape(n * capacity, D)
    gate_m, up_m, down_m = expert_gate[0], expert_up[0], expert_down[0]
    expert_g = product("rd,df->rf", incoming, gate_m)
    expert_u = product("rd,df->rf", incoming, up_m)
    expert_hidden = (jax.nn.silu(expert_g) * expert_u).astype(BF16)
    expert_out = product("rf,fd->rd", expert_hidden, down_m).astype(BF16)
    slot_dot = jnp.sum(
        out_slots * expert_out.astype(F32).reshape(n, capacity, D), axis=-1
    )
    token_dot = jnp.sum(dispatch.astype(F32) * slot_dot[:, :, None], axis=1)
    shared_g = product("td,fd->tf", ffn_in, gate_t)
    shared_u = product("td,fd->tf", ffn_in, up_t)
    shared_hidden = (jax.nn.silu(shared_g) * shared_u).astype(BF16)
    out_partial = product("tf,fd->td", shared_hidden, shared_down).reshape(n, tokens, D)
    out_partial = (out_partial + to_tokens(expert_out) * kept_gate[:, :, None]).astype(BF16)
    out_partial, slot_grad, all_out_grad = lax.optimization_barrier(
        (out_partial, slot_grad, all_out_grad)
    )
    out_sum = lax.psum_scatter(out_partial, "ep", scatter_dimension=0)
    layer_output = (residual_mid + out_sum.astype(F32)).astype(BF16)

    grad_shared_hidden = product("td,fd->tf", all_out_grad, shared_down)
    grad_shared_g, grad_shared_u = silu_back(grad_shared_hidden, shared_g, shared_u)
    grad_expert_hidden = product("rd,fd->rf", slot_grad, down_m)
    grad_expert_g, grad_expert_u = silu_back(grad_expert_hidden, expert_g, expert_u)
    row_grad = (
        product("rf,df->rd", grad_expert_g, gate_m) + product("rf,df->rd", grad_expert_u, up_m)
    ).astype(BF16)
    ffn_partial = product("tf,fd->td", grad_shared_g, gate_t) + product(
        "tf,fd->td", grad_shared_u, up_t
    )
    ffn_partial = (ffn_partial.reshape(n, tokens, D) + to_tokens(row_grad)).astype(BF16)
    own_column = (jnp.arange(128, dtype=jnp.int32) == e).astype(F32)
    dot_partial = (token_dot[:, :, None] * own_column).astype(BF16)
    ffn_sum, dot_sum = exchange(4, sums=(ffn_partial, dot_partial))

    expert_down_grad = product_over_groups(expert_hidden, slot_grad)[None]
    expert_gate_grad = product_over_groups(incoming, grad_expert_g)[None]
    expert_up_grad = product_over_groups(incoming, grad_expert_u)[None]
    shared_down_grad = to_row_owner(product_over_groups(shared_hidden, all_out_grad))
    side_shared = product_over_groups(
        ffn_in, jnp.concatenate([grad_shared_g, grad_shared_u], axis=1)
    ).astype(BF16)

    router_own = own(router_all)
    grad_probs = dot_sum[:, :n]
    grad_logits = (
        router_own * (grad_probs - jnp.sum(router_own * grad_probs, axis=-1, keepdims=True))
    ).astype(BF16)
    grad_ffn_in = ffn_sum + product("te,de->td", grad_logits, router_w)
    grad_ffn_gain = jnp.sum(grad_ffn_in * mid_unit, axis=0)
    grad_mid = output_grad.astype(F32) + norm_back(grad_ffn_in * ffn_gain, mid_unit, mid_scale)
    grad_mid_b = grad_mid.astype(BF16)
    mid_left, mid_right = grad_mid_b[:, : D // 2], grad_mid_b[:, D // 2 :]
    grad_attended = (
        product("td,ad->ta", jnp.where(even, mid_left, mid_right), out_w_mine)
        + product("td,ad->ta", jnp.where(even, mid_right, mid_left), out_w_other)
    ).astype(BF16)
    output_w_partial = product_over_groups(attended, grad_mid_b).astype(BF16)
    output_w_partial, grad_attended = lax.optimization_barrier((output_w_partial, grad_attended))
    (grad_att_blocks,) = exchange(
        5, swaps=(grad_attended.reshape(tokens, HEADS, VH).transpose(1, 0, 2),)
    )
    output_w_partial, grad_att_blocks = lax.optimization_barrier(
        (output_w_partial, grad_att_blocks)
    )
    grad_att = grad_att_blocks.reshape(length, VH)
    output_weight_grad = lax.psum_scatter(
        output_w_partial.reshape(n, rows_out, D), "ep", scatter_dimension=0
    ).astype(F32)
    grad_router = product("te,td->ed", grad_logits, own_ffn_in)

    probs = jnp.exp(attention_scores() - log_total)
    grad_weights = product("qd,kd->qk", grad_att, values)
    delta = jnp.sum(probs * grad_weights, axis=-1, keepdims=True)
    grad_scores = (probs * (grad_weights - delta)).astype(BF16)
    grad_query_n = product("qk,kd->qd", grad_scores, key_nope) * scale
    grad_query_r = product("qk,kd->qd", grad_scores, key_rope) * scale
    grad_key_n = product("qk,qd->kd", grad_scores, query_n) * scale
    grad_key_r = product("qk,qd->kd", grad_scores, query_r) * scale
    grad_values = product("qk,qd->kd", probs.astype(BF16), grad_att)
    grad_expanded = jnp.concatenate([grad_key_n, grad_values], axis=1).astype(BF16)
    latent_partial = product("tc,cl->tl", grad_expanded, expand_t).astype(BF16)
    grad_key_r = jnp.pad(grad_key_r, ((0, 0), (0, 128 - ROPE))).astype(BF16)
    latent_sum, rope_sum = exchange(
        6, sums=(latent_partial.reshape(n, tokens, LATENT), grad_key_r.reshape(n, tokens, 128))
    )
    grad_query = jnp.concatenate(
        [grad_query_n, unrotate(grad_query_r, cos_table, sin_table)], axis=1
    ).astype(BF16)
    normed_partial = product("tc,cd->td", grad_query, query_t)
    gain_partial = jnp.sum(normed_partial * unit_all, axis=0)
    normed_partial = normed_partial.astype(BF16).reshape(n, tokens, D)
    side_query = product_over_groups(normed, grad_query).astype(BF16)
    grad_expand = product_over_groups(latent, grad_expanded).astype(BF16)

    own_compressed = own(compressed)
    latent_scale = rms_scale(own_compressed[:, :LATENT])
    latent_unit = own_compressed[:, :LATENT] * latent_scale
    grad_latent_gain = jnp.sum(latent_sum * latent_unit, axis=0)
    grad_compressed = jnp.concatenate(
        [
            norm_back(latent_sum * lat_gain, latent_unit, latent_scale),
            unrotate(rope_sum[:, :ROPE], own(cos_table), own(sin_table)),
        ],
        axis=-1,
    ).astype(BF16)
    own_normed = (input_unit * attn_gain).astype(BF16)
    latent_w_partial = product_over_groups(
        own_normed, jnp.pad(grad_compressed, ((0, 0), (0, 640 - LATENT - ROPE)))
    ).astype(BF16)
    own_part = product("tc,dc->td", grad_compressed, latent_w)
    grad_attn_gain = gain_partial + jnp.sum(own_part * input_unit, axis=0)

    def by_owner(values, rows):
        blocks = values.reshape(-1, groups, n, rows).transpose(2, 1, 0, 3)
        return blocks.reshape(n, groups, -1)

    small = jnp.concatenate(
        [
            by_owner(grad_attn_gain, rows_out),
            by_owner(grad_ffn_gain, rows_out),
            by_owner(grad_router, rows_out),
            by_owner(grad_latent_gain, expand_rows),
        ],
        axis=2,
    )
    normed_sum, latent_weight_sum, query_all, shared_all, expand_all, small_all = exchange(
        7,
        sums=(normed_partial, latent_w_partial.reshape(n, rows_out, -1)),
        swaps=(
            side_query.reshape(n, rows_out, -1),
            side_shared.reshape(n, rows_out, -1),
            grad_expand.reshape(n, expand_rows, -1),
            small,
        ),
    )
    grad_normed = normed_sum + own_part
    input_grad = (
        grad_mid + norm_back(grad_normed * attn_gain, input_unit, input_scale)
    ).astype(BF16)
    latent_weight_grad = latent_weight_sum[:, : LATENT + ROPE]
    query_weight_grad = query_all.transpose(1, 0, 2).reshape(rows_out, -1).astype(F32)
    shared_width = gate_t.shape[0]
    shared_all = shared_all.transpose(1, 0, 2)
    shared_gate_grad = shared_all[:, :, :shared_width].reshape(rows_out, -1).astype(F32)
    shared_up_grad = shared_all[:, :, shared_width:].reshape(rows_out, -1).astype(F32)
    expand_weight_grad = expand_all.transpose(1, 0, 2).reshape(expand_rows, -1).astype(F32)
    small_sum = jnp.sum(small_all, axis=0)
    if groups == 2:
        g = lax.axis_index("grp")
        mine = lax.dynamic_index_in_dim(small_sum, g, 0, keepdims=False)
        theirs = lax.dynamic_index_in_dim(small_sum, 1 - g, 0, keepdims=False)
        small_sum = mine + lax.ppermute(theirs, "grp", [(0, 1), (1, 0)])
    else:
        small_sum = lax.psum_scatter(small_sum, "grp", scatter_dimension=0)
    attention_gain_grad = small_sum[:rows_out]
    feedforward_gain_grad = small_sum[rows_out : 2 * rows_out]
    router_weight_grad = small_sum[2 * rows_out : (2 + n) * rows_out].reshape(n, rows_out).T
    latent_gain_grad = small_sum[(2 + n) * rows_out :]
    return (
        layer_output,
        input_grad,
        attention_gain_grad,
        query_weight_grad,
        latent_weight_grad,
        latent_gain_grad,
        expand_weight_grad,
        output_weight_grad,
        feedforward_gain_grad,
        router_weight_grad,
        shared_gate_grad,
        shared_up_grad,
        shared_down_grad,
        expert_gate_grad,
        expert_up_grad,
        expert_down_grad,
    )


def solution(mesh):
    return jax.shard_map(
        per_device,
        mesh=mesh,
        in_specs=(
            P(("grp", "ep"), None),
            P("ep"),
            P("ep", None),
            P("ep", None),
            P("ep"),
            P("ep", None),
            P("ep", None),
            P("ep"),
            P("ep", None),
            P("ep", None),
            P("ep", None),
            P("ep", None),
            P("ep", None, None),
            P("ep", None, None),
            P("ep", None, None),
            P(("grp", "ep"), None),
            P("grp"),
            P(("grp", "ep"), None),
        ),
        out_specs=(
            P(("grp", "ep"), None),
            P(("grp", "ep"), None),
            P(("grp", "ep")),
            P(("grp", "ep"), None),
            P(("grp", "ep"), None),
            P(("grp", "ep")),
            P(("grp", "ep"), None),
            P(("grp", "ep"), None),
            P(("grp", "ep")),
            P(("grp", "ep"), None),
            P(("grp", "ep"), None),
            P(("grp", "ep"), None),
            P(("grp", "ep"), None),
            P("ep", "grp", None),
            P("ep", "grp", None),
            P("ep", "grp", None),
        ),
        check_vma=False,
    )
```

time: 1480 us -> 1140 us (0.77)
  Pallas kernels: 862 us -> 603 us
  local copies, waits for them, and re-layouts: 165 us -> 71.2 us
  other arithmetic: 124 us -> 92.5 us
  matrix products: 285 us -> 314 us
  starting transfers between devices: 7.89 us -> 25 us
    pallas_call x7 -> x6, Pallas kernels: 545 us -> 397 us  [exchange(): pl.pallas_call(functools.partial(exchange_kernel, n, m, w), out_shape=[ja...]
    pallas_call x3 -> x2, Pallas kernels: 317 us -> 206 us  [gather(): pl.pallas_call(functools.partial(gather_kernel, n), out_shape=jax.ShapeDt...]
    convert_element_type x14 -> x8, local copies, waits for them, and re-layouts: 49.8 us -> 16.9 us  [the longest x2 5.58 us: per_device(): shared_all[:, :, shared_width:].reshape(rows_out, -1).astype(F32)]
    dot_general x46 -> x56, matrix products: 285 us -> 314 us  [product(): return jnp.einsum(form, left, right, preferred_element_type=F32)]
    broadcast_in_dim x3 -> x0, other arithmetic: 20.6 us -> none  [the longest x1 7.46 us: per_device(): over_groups(grad_down_matrix.reshape(groups, grad_down_matrix.shape[0] //...]
    ppermute x10 -> x14, starting transfers between devices: 3.46 us -> 23.2 us  [the longest x9 22.5 us: product_over_groups(): other = lax.ppermute(sent, 'grp', [(0, 1), (1, 0)])]
    unnamed x240 -> x244, local copies, waits for them, and re-layouts: 32.9 us -> 26.5 us
  transfers between devices with their start and end apart: 16 -> 19, of which waited for: 0 -> 2; matrix products, arithmetic and copies ran while one was open for 31% -> 31% of each run, Pallas kernels for 52% -> 34%
where the time goes in v2:
time: 1140 us; the launch traced here: 1130 us
  Pallas kernels  603 us (53%)
  matrix products  314 us (28%)
  other arithmetic  92.5 us (8%)
  local copies, waits for them, and re-layouts  71.2 us (6%)
  starting transfers between devices  25 us (2%)
  between operations  16.5 us (1%)
    pallas_call x6, Pallas kernels, exchange(): pl.pallas_call(functools.partial(exchange_kernel, n, m, w), out_shape=[ja...  397 us
    dot_general x56, matrix products, product(): return jnp.einsum(form, left, right, preferred_element_type=F32)  314 us
    pallas_call x2, Pallas kernels, gather(): pl.pallas_call(functools.partial(gather_kernel, n), out_shape=jax.ShapeDt...  206 us
    unnamed x244, local copies, waits for them, and re-layouts  26.5 us
  transfers between devices with their start and end apart: 19, of which 2 were waited for; matrix products, arithmetic and copies ran while one was open for 31% of the time, Pallas kernels for 34%

profile of v2, /device:TPU:0, one launch (start us, length us, event | category | flops | bytes accessed | tf_op | source)
XLA Modules:
  0.0 1131.9 jit_solution(7994727788201843661)
XLA Ops:
  18.4 96.1 %gather.2 = bf16[16,128,2688]{2,1,0:T(8,128)(2,1)} custom-call(bf16[128,2688]{1,0:T(8,128)(2,1)} %pad.14.x_ref), custom_call_target="tpu_custom_call" | custom-call | tf_op jit(solution)/shard_map/gather/pallas_call | solution.py:163
  115.3 17.5 %exchange.6 = (bf16[16,96,128]{2,1,0:T(8,128)(2,1)}, bf16[16,128,32]{2,1,0:T(8,128)(2,1)}) custom-call(bf16[16,96,128]{2,1,0:T(8,128)(2,1)} %dynamic-slice_bitcast_fusion.refs_0_, bf16[16,128,32]{2,1,0:T(8,128)(2,1)} %bitcast.269), custom_call_target="tpu_custom_call" | custom-call | tf_op jit(solution)/shard_map/exchange/pallas_call | solution.py:359
  154.4 7.7 fusion.198
  165.4 8.4 multiply_convert_fusion.2
  196.9 8.4 fusion.71
  205.3 10.1 all-gather.3.cloned.1.call-done
  219.2 10.6 fusion.195
  229.8 8.2 exponential_reduce_fusion
  238.1 9.4 convolution_convert_fusion.8
  247.5 40.0 %exchange.7 = (bf16[16,128,128]{2,1,0:T(8,128)(2,1)}, bf16[16,176,128]{2,1,0:T(8,128)(2,1)}) custom-call(bf16[16,128,128]{2,1,0:T(8,128)(2,1)} %bitcast.267, bf16[16,176,128]{2,1,0:T(8,128)(2,1)} %bitcast.268), custom_call_target="tpu_custom_call" | custom-call | tf_op jit(solution)/shard_map/exchange/pallas_call | solution.py:359
  299.7 109.6 %gather.3 = bf16[16,128,2048]{2,1,0:T(8,128)(2,1)} custom-call(bf16[128,2048]{1,0:T(8,128)(2,1)} %multiply_convert_fusion.12.x_ref), custom_call_target="tpu_custom_call" | custom-call | tf_op jit(solution)/shard_map/gather/pallas_call | solution.py:163
  431.8 8.1 fusion.200
  439.9 8.4 fusion.12
  448.4 10.8 multiply_convert_fusion.6
  468.3 9.2 add_convert_fusion.1
  485.0 16.2 %multiply_convert_fusion.5 = (bf16[1024,1408]{1,0:T(8,128)(2,1)}, bf16[1024,1408]{1,0:T(8,128)(2,1)}) fusion(f32[1024,1408]{1,0:T(8,128)} %fusion.12, f32[1024,1408]{1,0:T(8,128)} %get-tuple-element.130, bf16[1024,2048]{1,0:T(8,128)(2,1)S(1)} %bitcast.246, bf16[1,1408,2048]{2,1,0:T(8,128)(2,1)} %param.32), kind=kOutput, calls=%fused_computation.36 | convolution fusion | flops 5924323328 | bytes 27262976 | tf_op jit(solution)/shard_map/rd,fd->rf/dot_general | solution.py:414
  501.2 10.5 fusion.6
  511.7 11.2 add_convert_fusion.3
  522.9 8.1 fusion.101
  539.4 8.3 convolution_add_fusion
  547.8 11.5 %add_convert_fusion = bf16[16,128,2048]{2,1,0:T(8,128)(2,1)S(1)} fusion(f32[16,128,2048]{2,1,0:T(8,128)} %bitcast.241, f32[16,128,2048]{2,1,0:T(8,128)} %fusion.101), kind=kLoop, calls=%fused_computation.4 | loop fusion | flops 8388608 | bytes 41943040 | tf_op jit(solution)/shard_map/convert_element_type | solution.py:664
  559.3 87.0 %exchange.8 = (f32[128,2048]{1,0:T(8,128)S(1)}, f32[128,128]{1,0:T(8,128)S(1)}) custom-call(bf16[4,2,2,128,2048]{4,3,2,1,0:T(8,128)(2,1)S(1)} %bitcast.217, bf16[4,2,2,128,128]{4,3,2,1,0:T(8,128)(2,1)S(1)} %multiply_convert_fusion.11.refs_1_), custom_call_target="tpu_custom_call" | custom-call | tf_op jit(solution)/shard_map/exchange/pallas_call | solution.py:359
  667.5 13.0 %exchange.9 = bf16[16,128,128]{2,1,0:T(8,128)(2,1)} custom-call(bf16[16,128,128]{2,1,0:T(8,128)(2,1)} %bitcast.271), custom_call_target="tpu_custom_call" | custom-call | tf_op jit(solution)/shard_map/exchange/pallas_call | solution.py:359
  681.9 7.6 convolution_convert_fusion
  729.1 9.5 add_bitcast_fusion.1
  745.5 7.6 add_bitcast_fusion
  753.2 7.5 multiply_reduce_fusion.1
  760.6 8.8 multiply_convert_fusion
  775.8 9.0 convolution_convert_fusion.7
  786.0 19.8 %collective-permute-start.8 = (bf16[256,256]{1,0:T(8,128)(2,1)}, bf16[256,256]{1,0:T(8,128)(2,1)}, u32[]{:S(2)}, u32[]{:S(2)}) collective-permute-start(bf16[256,256]{1,0:T(8,128)(2,1)} %convolution_convert_fusion.11), channel_id=1, source_target_pairs={{0,16},{16,0},{1,17},{17,1},{2,18},{18,2},{3,19},{19,3},{4,20},{20... | collective-permute-start | bytes 393224 | tf_op jit(solution)/shard_map/ppermute | solution.py:398
  820.5 77.1 %exchange.10 = (f32[128,512]{1,0:T(8,128)S(1)}, f32[128,128]{1,0:T(8,128)S(1)}) custom-call(bf16[4,2,2,128,512]{4,3,2,1,0:T(8,128)(2,1)S(1)} %bitcast.222, bf16[4,2,2,128,128]{4,3,2,1,0:T(8,128)(2,1)S(1)} %bitcast.223), custom_call_target="tpu_custom_call" | custom-call | tf_op jit(solution)/shard_map/exchange/pallas_call | solution.py:359
  930.0 162.7 %exchange.11 = (f32[128,2048]{1,0:T(8,128)S(1)}, f32[64,640]{1,0:T(8,128)S(1)}, bf16[16,64,192]{2,1,0:T(8,128)(2,1)S(1)}, bf16[16,64,352]{2,1,0:T(8,128)(2,1)S(1...) custom-call(bf16[4,2,2,128,2048]{4,3,2,1,0:T(8,128)(2,1)S(1)} %bitcast.218, ...), custom_call_target="tpu_custom_call" | custom-call | tf_op jit(solution)/shard_map/exchange/pallas_call | solution.py:359
  (436 shorter events, 277.6 us)
Async XLA Ops:
  7.2 424.6 %copy-start = (bf16[176,2048]{1,0:T(8,128)(2,1)S(1)}, bf16[176,2048]{1,0:T(8,128)(2,1)}, u32[]{:S(2)}) copy-start(bf16[176,2048]{1,0:T(8,128)(2,1)} %param.29) | copy-start | bytes 2162692
  7.2 208.2 %all-gather.3.cloned.1.call-start = ((), (), s32[]{:S(2)}) async-start(), calls=%async_computation.2 | async-start | bytes 4456448 | tf_op jit(solution)/shard_map/all_gather | solution.py:551
  18.4 96.1 %copy-start.78 = (bf16[128,2048]{1,0:T(8,128)(2,1)S(1)}, bf16[128,2048]{1,0:T(8,128)(2,1)}, u32[]{:S(2)}) copy-start(bf16[128,2048]{1,0:T(8,128)(2,1)} %param.24) | copy-start | bytes 1572868
  132.8 344.7 %all-gather.5.cloned.1.call-start = ((), (), s32[]{:S(2)}) async-start(), calls=%async_computation.3 | async-start | bytes 8912896 | tf_op jit(solution)/shard_map/all_gather | solution.py:553
  134.0 46.8 %collective-permute-start.1 = (bf16[128,512]{0,1:T(8,128)(2,1)S(1)}, bf16[128,512]{0,1:T(8,128)(2,1)S(1)}, u32[]{:S(2)}, u32[]{:S(2)}) collective-permute-start(bf16[128,512]{0,1:T(8,128)(2,1)S(1)} %bitcast.274), channel_id=1, source_target_pairs={{0,16},{16,0},{1,17},{17,1},{2,18},{18,2},{3,19},{19,3},{4,20},{20... | collective-permute-start | bytes 393224 | tf_op jit(solution)/shard_map/ppermute | solution.py:404
  135.9 48.4 %collective-permute-start = (bf16[96,2048]{1,0:T(8,128)(2,1)}, bf16[96,2048]{1,0:T(8,128)(2,1)}, u32[]{:S(2)}, u32[]{:S(2)}) collective-permute-start(bf16[96,2048]{1,0:T(8,128)(2,1)} %copy_bitcast_fusion.1), channel_id=1, source_target_pairs={{0,16},{16,0},{1,17},{17,1},{2,18},{18,2},{3,19},{19,3},{4,20},{20... | collective-permute-start | bytes 1179656 | tf_op jit(solution)/shard_map/ppermute | solution.py:404
  136.4 982.7 %reduce-scatter.5.cloned.1.call-start = ((), (), s32[]{:S(2)}) async-start(), calls=%async_computation.5 | async-start | bytes 4456448 | tf_op jit(solution)/shard_map/reduce_scatter | solution.py:700
  147.3 150.5 %copy-start.70 = (f32[16,128]{1,0:T(8,128)}, f32[16,128]{1,0:T(8,128)S(1)}, u32[]{:S(2)}) copy-start(f32[16,128]{1,0:T(8,128)S(1)} %get-tuple-element.66) | copy-start | bytes 24580
  177.0 232.3 %copy-start.31 = (bf16[16,128,16]{2,1,0:T(8,128)(2,1)}, bf16[16,128,16]{2,1,0:T(8,128)(2,1)S(1)}, u32[]{:S(2)}) copy-start(bf16[16,128,16]{2,1,0:T(8,128)(2,1)S(1)} %slice.115) | copy-start | bytes 196612
  215.4 78.6 %collective-permute-start.2 = (bf16[2048,1024]{1,0:T(8,128)(2,1)}, bf16[2048,1024]{1,0:T(8,128)(2,1)}, u32[]{:S(2)}, u32[]{:S(2)}) collective-permute-start(bf16[2048,1024]{1,0:T(8,128)(2,1)} %all-gather.3.cloned.1.call-done), channel_id=1, source_target_pairs={{0,16},{16,0},{1,17},{17,1},{2,18},{18,2},{3,19},{19,3},{4,20},{20... | collective-permute-start | bytes 12582920 | tf_op jit(solution)/shard_map/ppermute | solution.py:404
  291.1 131.7 %collective-permute-start.3 = (bf16[176,2048]{1,0:T(8,128)(2,1)}, bf16[176,2048]{1,0:T(8,128)(2,1)}, u32[]{:S(2)}, u32[]{:S(2)}) collective-permute-start(bf16[176,2048]{1,0:T(8,128)(2,1)} %copy_bitcast_fusion), channel_id=1, source_target_pairs={{0,16},{16,0},{1,17},{17,1},{2,18},{18,2},{3,19},{19,3},{4,20},{20... | collective-permute-start | bytes 2162696 | tf_op jit(solution)/shard_map/ppermute | solution.py:404
  297.8 111.5 %copy-start.85 = (f32[128]{0:T(128)}, f32[128]{0:T(128)S(1)}, u32[]{:S(2)}) copy-start(f32[128]{0:T(128)S(1)} %add_rsqrt_fusion.4) | copy-start | bytes 1540
  559.3 88.1 %copy-start.10 = (f32[128,2048]{1,0:T(8,128)S(1)}, f32[128,2048]{1,0:T(8,128)}, u32[]{:S(2)}) copy-start(f32[128,2048]{1,0:T(8,128)} %copy-done.9) | copy-start | bytes 3145732
  559.3 88.1 %copy-start.32 = (bf16[16,128,16]{2,1,0:T(8,128)(2,1)S(1)}, bf16[16,128,16]{2,1,0:T(8,128)(2,1)}, u32[]{:S(2)}) copy-start(bf16[16,128,16]{2,1,0:T(8,128)(2,1)} %copy-done.31) | copy-start | bytes 196612
  559.3 88.1 %copy-start.71 = (f32[16,128]{1,0:T(8,128)S(1)}, f32[16,128]{1,0:T(8,128)}, u32[]{:S(2)}) copy-start(f32[16,128]{1,0:T(8,128)} %copy-done.70) | copy-start | bytes 24580
  559.3 88.1 %copy-start.86 = (f32[128]{0:T(128)S(1)}, f32[128]{0:T(128)}, u32[]{:S(2)}) copy-start(f32[128]{0:T(128)} %copy-done.85) | copy-start | bytes 1540
  559.3 90.4 %copy-start.34 = (bf16[128,2048]{1,0:T(8,128)(2,1)S(1)}, bf16[128,2048]{1,0:T(8,128)(2,1)}, u32[]{:S(2)}) copy-start(bf16[128,2048]{1,0:T(8,128)(2,1)} %param.35) | copy-start | bytes 1572868
  653.4 7.5 collective-permute-start.4
  680.5 440.4 %reduce-scatter.3.cloned.1.call-start = ((), (), s32[]{:S(2)}) async-start(), calls=%async_computation.4 | async-start | bytes 8912896 | tf_op jit(solution)/shard_map/reduce_scatter | solution.py:651
  689.4 39.7 %collective-permute-start.13 = (bf16[1024,1408]{1,0:T(8,128)(2,1)}, bf16[1024,1408]{1,0:T(8,128)(2,1)}, u32[]{:S(2)}, u32[]{:S(2)}) collective-permute-start(bf16[1024,1408]{1,0:T(8,128)(2,1)} %convolution_convert_fusion), channel_id=1, source_target_pairs={{0,16},{16,0},{1,17},{17,1},{2,18},{18,2},{3,19},{19,3},{4,20},{20... | collective-permute-start | bytes 8650760 | tf_op jit(solution)/shard_map/ppermute | solution.py:398
  695.4 19.0 %collective-permute-start.10 = (bf16[88,2048]{1,0:T(8,128)(2,1)}, bf16[88,2048]{1,0:T(8,128)(2,1)}, u32[]{:S(2)}, u32[]{:S(2)}) collective-permute-start(bf16[88,2048]{1,0:T(8,128)(2,1)} %convolution_convert_fusion.9), channel_id=1, source_target_pairs={{0,16},{16,0},{1,17},{17,1},{2,18},{18,2},{3,19},{19,3},{4,20},{20... | collective-permute-start | bytes 1081352 | tf_op jit(solution)/shard_map/ppermute | solution.py:398
  701.2 37.4 %collective-permute-start.12 = (bf16[1024,1408]{1,0:T(8,128)(2,1)}, bf16[1024,1408]{1,0:T(8,128)(2,1)}, u32[]{:S(2)}, u32[]{:S(2)}) collective-permute-start(bf16[1024,1408]{1,0:T(8,128)(2,1)} %convolution_convert_fusion.1), channel_id=1, source_target_pairs={{0,16},{16,0},{1,17},{17,1},{2,18},{18,2},{3,19},{19,3},{4,20},{20... | collective-permute-start | bytes 8650760 | tf_op jit(solution)/shard_map/ppermute | solution.py:398
  706.2 39.3 %collective-permute-start.14 = (bf16[704,2048]{1,0:T(8,128)(2,1)}, bf16[704,2048]{1,0:T(8,128)(2,1)}, u32[]{:S(2)}, u32[]{:S(2)}) collective-permute-start(bf16[704,2048]{1,0:T(8,128)(2,1)} %convolution_convert_fusion.4), channel_id=1, source_target_pairs={{0,16},{16,0},{1,17},{17,1},{2,18},{18,2},{3,19},{19,3},{4,20},{20... | collective-permute-start | bytes 8650760 | tf_op jit(solution)/shard_map/ppermute | solution.py:398
  712.3 9.4 collective-permute-start.7
  720.1 8.0 collective-permute-start.11
  786.0 131.7 %collective-permute-start.8 = (bf16[256,256]{1,0:T(8,128)(2,1)}, bf16[256,256]{1,0:T(8,128)(2,1)}, u32[]{:S(2)}, u32[]{:S(2)}) collective-permute-start(bf16[256,256]{1,0:T(8,128)(2,1)} %convolution_convert_fusion.11), channel_id=1, source_target_pairs={{0,16},{16,0},{1,17},{17,1},{2,18},{18,2},{3,19},{19,3},{4,20},{20... | collective-permute-start | bytes 393224 | tf_op jit(solution)/shard_map/ppermute | solution.py:398
  814.5 84.5 %copy-start.17 = (bf16[128,2048]{1,0:T(8,128)(2,1)S(1)}, bf16[128,2048]{1,0:T(8,128)(2,1)}, u32[]{:S(2)}) copy-start(bf16[128,2048]{1,0:T(8,128)(2,1)} %param.18) | copy-start | bytes 1572868
  814.5 84.5 %copy-start.69 = (f32[16,128]{1,0:T(8,128)S(1)}, f32[16,128]{1,0:T(8,128)}, u32[]{:S(2)}) copy-start(f32[16,128]{1,0:T(8,128)} %copy-done.68) | copy-start | bytes 24580
  818.3 89.3 %slice-start.6 = ((s8[11010048]{0:T(1024)(128)(4,1)}), s8[2621440]{0:T(1024)(128)(4,1)S(1)}, s32[]{:S(2)}) async-start(s8[11010048]{0:T(1024)(128)(4,1)} %bitcast.232), calls=%async_computation.12 | async-start | bytes 5242880
  902.6 21.2 %collective-permute-start.5 = (bf16[1024,640]{1,0:T(8,128)(2,1)}, bf16[1024,640]{1,0:T(8,128)(2,1)}, u32[]{:S(2)}, u32[]{:S(2)}) collective-permute-start(bf16[1024,640]{1,0:T(8,128)(2,1)} %convolution_convert_fusion.10), channel_id=1, source_target_pairs={{0,16},{16,0},{1,17},{17,1},{2,18},{18,2},{3,19},{19,3},{4,20},{20... | collective-permute-start | bytes 3932168 | tf_op jit(solution)/shard_map/ppermute | solution.py:398
  916.5 3.7 collective-permute-start.6
  1095.9 21.5 %collective-permute-start.9 = (f32[1168]{0:T(1024)S(1)}, f32[1168]{0:T(1024)S(1)}, u32[]{:S(2)}, u32[]{:S(2)}) collective-permute-start(f32[1168]{0:T(1024)S(1)} %get-tuple-element.72), channel_id=1, source_target_pairs={{0,16},{16,0},{1,17},{17,1},{2,18},{18,2},{3,19},{19,3},{4,20},{20... | collective-permute-start | bytes 14024 | tf_op jit(solution)/shard_map/ppermute | solution.py:786
  (104 other events, 1167.3 us)
Sparse Core Ops, SparseCore 0:
  132.9 82.4 all-gather.2
  218.1 152.8 all-gather.4
  680.7 107.0 reduce-scatter.4
  789.9 267.7 reduce-scatter.2

commit v3 on v2

--- a/solution.py
+++ b/solution.py
@@ -410,6 +410,338 @@
     return lax.ppermute(block.astype(BF16), ("grp", "ep"), pairs).astype(F32)
 
 
+def sum_async(p):
+    n = lax.axis_size("ep")
+    nz = n // 4
+    e = lax.axis_index("ep")
+    z, y, x = e // 4, (e // 2) % 2, e % 2
+    rows, cols = p.shape[1:]
+    p = p.reshape(nz, 2, 2, rows, cols)
+    top, bottom = p[:, :, :, : rows // 2], p[:, :, :, rows // 2 :]
+
+    def fold(part, place, axis, bit):
+        kept = lax.dynamic_index_in_dim(part, place, axis, keepdims=False)
+        sent = lax.dynamic_index_in_dim(part, 1 - place, axis, keepdims=False)
+        got = lax.ppermute(sent, "ep", [(i, i ^ bit) for i in range(n)])
+        return (kept.astype(F32) + got.astype(F32)).astype(p.dtype)
+
+    top = fold(fold(top, y, 1, 2), x, 1, 1)
+    bottom = fold(fold(bottom, x, 2, 1), y, 1, 2)
+    line = jnp.concatenate([top, bottom], axis=1)
+    total = lax.dynamic_index_in_dim(line, z, 0, keepdims=False).astype(F32)
+    for k in range(1, nz):
+        sent = lax.dynamic_index_in_dim(line, (z + k) % nz, 0, keepdims=False)
+        total = total + lax.ppermute(sent, "ep", [(i, (i + 4 * k) % n) for i in range(n)]).astype(F32)
+    return total
+
+
+def dot(left, right):
+    return jnp.dot(left, right, preferred_element_type=F32)
+
+
+def dot_nt(left, right):
+    return lax.dot_general(left, right, (((1,), (1,)), ((), ())), preferred_element_type=F32)
+
+
+KEYS = 512
+
+
+def scores_of(scale, prefix, k, q, first_key, first_query):
+    scores = dot_nt(k, q) * scale
+    key = first_key + lax.broadcasted_iota(jnp.int32, scores.shape, 0)
+    query = first_query + lax.broadcasted_iota(jnp.int32, scores.shape, 1)
+    return jnp.where((key <= query) | (key < prefix), scores, MASKED)
+
+
+def key_blocks(prefix, last_query):
+    return (jnp.maximum(last_query, prefix) + KEYS - 1) // KEYS
+
+
+def attend_kernel(scale, prefix_ref, q_ref, k_ref, v_ref, attended_ref, exact_ref, lse_ref):
+    q = q_ref[...]
+    rows = q.shape[0]
+    start = pl.program_id(0) * rows
+    prefix = prefix_ref[0]
+
+    def step(j, carry):
+        top, total, out = carry
+        s = scores_of(scale, prefix, k_ref[j], q, j * KEYS, start)
+        new_top = jnp.maximum(top, jnp.max(s, axis=0, keepdims=True))
+        p = jnp.exp(s - new_top)
+        shrink = jnp.exp(top - new_top)
+        total = total * shrink + jnp.sum(p, axis=0, keepdims=True)
+        return new_top, total, out * shrink + dot(v_ref[j], p.astype(BF16))
+
+    top, total, out = lax.fori_loop(
+        0,
+        key_blocks(prefix, start + rows),
+        step,
+        (
+            jnp.full((1, rows), MASKED, F32),
+            jnp.zeros((1, rows), F32),
+            jnp.zeros((v_ref.shape[1], rows), F32),
+        ),
+    )
+    lse_ref[...] = top + jnp.log(total)
+    exact = (out / total).T
+    exact_ref[...] = exact
+    attended_ref[...] = exact.astype(BF16)
+
+
+def attend(prefix, q, k, v):
+    length, depth = q.shape
+    values = v.shape[1]
+    rows = 256
+    v = v.reshape(length // KEYS, KEYS, values).transpose(0, 2, 1)
+    k = k.reshape(length // KEYS, KEYS, depth)
+    return pl.pallas_call(
+        functools.partial(attend_kernel, 1.0 / math.sqrt(NOPE + ROPE)),
+        grid=(length // rows,),
+        in_specs=[
+            pl.BlockSpec(memory_space=pltpu.SMEM),
+            pl.BlockSpec((rows, depth), lambda i: (i, 0)),
+            pl.BlockSpec(k.shape, lambda i: (0, 0, 0)),
+            pl.BlockSpec(v.shape, lambda i: (0, 0, 0)),
+        ],
+        out_specs=[
+            pl.BlockSpec((rows, values), lambda i: (i, 0)),
+            pl.BlockSpec((rows, values), lambda i: (i, 0)),
+            pl.BlockSpec((1, rows), lambda i: (0, i)),
+        ],
+        out_shape=[
+            jax.ShapeDtypeStruct((length, values), BF16),
+            jax.ShapeDtypeStruct((length, values), F32),
+            jax.ShapeDtypeStruct((1, length), F32),
+        ],
+        compiler_params=pltpu.CompilerParams(vmem_limit_bytes=32 << 20),
+        name="attend",
+    )(prefix, q, k, v)
+
+
+def attend_back_kernel(
+    scale, prefix_ref, q_ref, g_ref, lse_ref, delta_ref, k_ref, v_ref, dq_ref, dk_ref, dv_ref
+):
+    q, g = q_ref[...], g_ref[...]
+    rows = q.shape[0]
+    start = pl.program_id(0) * rows
+    prefix = prefix_ref[0]
+
+    @pl.when(pl.program_id(0) == 0)
+    def _():
+        dk_ref[...] = jnp.zeros_like(dk_ref)
+        dv_ref[...] = jnp.zeros_like(dv_ref)
+
+    def step(j, dq):
+        k = k_ref[j]
+        p = jnp.exp(scores_of(scale, prefix, k, q, j * KEYS, start) - lse_ref[...])
+        ds = (p * (dot_nt(v_ref[j], g) - delta_ref[...]) * scale).astype(BF16)
+        dv_ref[j] += dot(p.astype(BF16), g)
+        dk_ref[j] += dot(ds, q)
+        return dq + lax.dot_general(
+            ds, k, (((0,), (0,)), ((), ())), preferred_element_type=F32
+        )
+
+    dq_ref[...] = lax.fori_loop(
+        0, key_blocks(prefix, start + rows), step, jnp.zeros(dq_ref.shape, F32)
+    )
+
+
+def attend_back(prefix, q, g, lse, delta, k, v):
+    length, depth = q.shape
+    values = v.shape[1]
+    rows = 256
+    k = k.reshape(length // KEYS, KEYS, depth)
+    v = v.reshape(length // KEYS, KEYS, values)
+    dq, dk, dv = pl.pallas_call(
+        functools.partial(attend_back_kernel, 1.0 / math.sqrt(NOPE + ROPE)),
+        grid=(length // rows,),
+        in_specs=[
+            pl.BlockSpec(memory_space=pltpu.SMEM),
+            pl.BlockSpec((rows, depth), lambda i: (i, 0)),
+            pl.BlockSpec((rows, values), lambda i: (i, 0)),
+            pl.BlockSpec((1, rows), lambda i: (0, i)),
+            pl.BlockSpec((1, rows), lambda i: (0, i)),
+            pl.BlockSpec(k.shape, lambda i: (0, 0, 0)),
+            pl.BlockSpec(v.shape, lambda i: (0, 0, 0)),
+        ],
+        out_specs=[
+            pl.BlockSpec((rows, depth), lambda i: (i, 0)),
+            pl.BlockSpec(k.shape, lambda i: (0, 0, 0)),
+            pl.BlockSpec(v.shape, lambda i: (0, 0, 0)),
+        ],
+        out_shape=[
+            jax.ShapeDtypeStruct((length, depth), F32),
+            jax.ShapeDtypeStruct(k.shape, F32),
+            jax.ShapeDtypeStruct(v.shape, F32),
+        ],
+        compiler_params=pltpu.CompilerParams(vmem_limit_bytes=40 << 20),
+        name="attend_back",
+    )(prefix, q, g, lse, delta, k, v)
+    return dq, dk.reshape(length, depth), dv.reshape(length, values)
+
+
+def ffn_kernel(
+    n,
+    x_ref,
+    y_ref,
+    slots_ref,
+    tokens_ref,
+    own_ref,
+    router_ref,
+    sg_ref,
+    su_ref,
+    sd_ref,
+    eg_ref,
+    eu_ref,
+    ed_ref,
+    out_ref,
+    ffn_ref,
+    dot_ref,
+    probs_ref,
+    rows_ref,
+    hidden_ref,
+    slot_grad_ref,
+    grad_g_ref,
+    grad_u_ref,
+    shared_h_ref,
+    shared_dg_ref,
+    shared_du_ref,
+    expert_out,
+    row_grad,
+):
+    blocks, tokens = x_ref.shape[:2]
+    capacity = slots_ref.shape[1]
+    own = own_ref[...]
+    lanes = lax.broadcasted_iota(jnp.int32, (tokens, own.shape[1]), 1)
+    gates = []
+    for b in range(blocks):
+        x, y = x_ref[b], y_ref[b]
+        logits = jnp.where(lanes < n, dot(x, router_ref[...]), MASKED)
+        raised = jnp.exp(logits - jnp.max(logits, axis=-1, keepdims=True))
+        probs = raised / jnp.sum(raised, axis=-1, keepdims=True)
+        probs_ref[b] = probs
+        gate = jnp.sum(probs * own, axis=-1, keepdims=True)
+        gates.append(gate)
+        part = pl.ds(b * capacity, capacity)
+        rows_ref[part] = dot(slots_ref[b], x).astype(BF16)
+        weighted = (gate * y.astype(F32)).astype(BF16)
+        slot_grad_ref[part] = dot(slots_ref[b], weighted).astype(BF16)
+    rows = rows_ref[...]
+    slot_grad = slot_grad_ref[...]
+    g = dot(rows, eg_ref[...])
+    u = dot(rows, eu_ref[...])
+    sigmoid = 1.0 / (1.0 + jnp.exp(-g))
+    silu = g * sigmoid
+    hidden = (silu * u).astype(BF16)
+    hidden_ref[...] = hidden
+    expert_out[...] = dot(hidden, ed_ref[...]).astype(BF16)
+    grad_hidden = dot_nt(slot_grad, ed_ref[...])
+    grad_g = (grad_hidden * u * sigmoid * (1.0 + g * (1.0 - sigmoid))).astype(BF16)
+    grad_u = (grad_hidden * silu).astype(BF16)
+    grad_g_ref[...] = grad_g
+    grad_u_ref[...] = grad_u
+    row_grad[...] = (dot_nt(grad_g, eg_ref[...]) + dot_nt(grad_u, eu_ref[...])).astype(BF16)
+    x = x_ref[...].reshape(blocks * tokens, -1)
+    y = y_ref[...].reshape(blocks * tokens, -1)
+    g = dot_nt(x, sg_ref[...])
+    u = dot_nt(x, su_ref[...])
+    grad_hidden = dot_nt(y, sd_ref[...])
+    sigmoid = 1.0 / (1.0 + jnp.exp(-g))
+    silu = g * sigmoid
+    hidden = (silu * u).astype(BF16)
+    grad_g = (grad_hidden * u * sigmoid * (1.0 + g * (1.0 - sigmoid))).astype(BF16)
+    grad_u = (grad_hidden * silu).astype(BF16)
+    for ref, value in ((shared_h_ref, hidden), (shared_dg_ref, grad_g), (shared_du_ref, grad_u)):
+        ref[...] = value.reshape(blocks, tokens, -1)
+    width = x.shape[1]
+    chunk = width // 4
+    met = [0.0] * blocks
+    for c in range(width // chunk):
+        cols = pl.ds(c * chunk, chunk)
+        shared_out = dot(hidden, sd_ref[:, cols])
+        shared_ffn = dot(grad_g, sg_ref[:, cols]) + dot(grad_u, su_ref[:, cols])
+        for b in range(blocks):
+            part = pl.ds(b * capacity, capacity)
+            here = slice(b * tokens, (b + 1) * tokens)
+            picked = dot(tokens_ref[b], expert_out[part, cols])
+            met[b] += jnp.sum(picked * y_ref[b, :, cols].astype(F32), axis=-1, keepdims=True)
+            out_ref[b, :, cols] = (shared_out[here] + picked * gates[b]).astype(BF16)
+            back = dot(tokens_ref[b], row_grad[part, cols])
+            ffn_ref[b, :, cols] = (shared_ffn[here] + back).astype(BF16)
+    for b in range(blocks):
+        dot_ref[b] = (met[b] * own).astype(BF16)
+
+
+def ffn(x, y, slots, own_lane, router_w, gate_t, up_t, down, gate_m, up_m, down_m):
+    n, tokens, width = x.shape
+    capacity = slots.shape[1]
+    hidden = gate_m.shape[1]
+    shared = gate_t.shape[0]
+    group = 4
+
+    def whole(a):
+        return pl.BlockSpec(a.shape, lambda i: (0,) * a.ndim, pipeline_mode=pl.Buffered(1))
+
+    def block(*shape):
+        return pl.BlockSpec((group,) + shape, lambda i: (i, 0, 0))
+
+    def slot_rows(cols):
+        return pl.BlockSpec((group * capacity, cols), lambda i: (i, 0))
+
+    def tokens_of(cols, kind=BF16):
+        return jax.ShapeDtypeStruct((n, tokens, cols), kind)
+
+    def slots_of(cols):
+        return jax.ShapeDtypeStruct((n * capacity, cols), BF16)
+
+    weights = (own_lane, router_w, gate_t, up_t, down, gate_m, up_m, down_m)
+    return pl.pallas_call(
+        functools.partial(ffn_kernel, n),
+        grid=(n // group,),
+        in_specs=[
+            block(tokens, width),
+            block(tokens, width),
+            block(capacity, tokens),
+            block(tokens, capacity),
+        ]
+        + [whole(a) for a in weights],
+        out_specs=[
+            block(tokens, width),
+            block(tokens, width),
+            block(tokens, 128),
+            block(tokens, 128),
+            slot_rows(width),
+            slot_rows(hidden),
+            slot_rows(width),
+            slot_rows(hidden),
+            slot_rows(hidden),
+            block(tokens, shared),
+            block(tokens, shared),
+            block(tokens, shared),
+        ],
+        out_shape=[
+            tokens_of(width),
+            tokens_of(width),
+            tokens_of(128),
+            tokens_of(128, F32),
+            slots_of(width),
+            slots_of(hidden),
+            slots_of(width),
+            slots_of(hidden),
+            slots_of(hidden),
+            tokens_of(shared),
+            tokens_of(shared),
+            tokens_of(shared),
+        ],
+        scratch_shapes=[
+            pltpu.VMEM((group * capacity, width), BF16),
+            pltpu.VMEM((group * capacity, width), BF16),
+        ],
+        compiler_params=pltpu.CompilerParams(vmem_limit_bytes=60 << 20),
+        name="ffn",
+    )(x, y, slots, slots.transpose(0, 2, 1), *weights)
+
+
 def product(form, left, right):
     return jnp.einsum(form, left, right, preferred_element_type=F32)
 
@@ -418,20 +750,18 @@
     return lax.rsqrt(jnp.mean(values * values, axis=-1, keepdims=True) + EPSILON)
 
 
-def rotary_tables(positions):
+def rotary_tables(tokens, n):
     halfway = ROPE // 2
     inverse = 10000.0 ** (-(jnp.arange(halfway, dtype=F32) * 2.0 / ROPE))
-    angles = positions[:, None] * inverse[None, :]
-    return (jnp.cos(angles), jnp.sin(angles))
-
-
-def rotate(values, cos_table, sin_table):
-    halfway = values.shape[-1] // 2
-    first = values[..., :halfway]
-    second = values[..., halfway:]
-    return jnp.concatenate(
-        [first * cos_table - second * sin_table, second * cos_table + first * sin_table], axis=-1
-    )
+    inverse = jnp.concatenate([inverse, inverse])
+    sign = jnp.where(jnp.arange(ROPE) < halfway, -1.0, 1.0)
+    base = (jnp.arange(n, dtype=F32) * tokens)[:, None] * inverse
+    step = jnp.arange(tokens, dtype=F32)[:, None] * inverse
+    base_cos, base_sin = jnp.cos(base)[:, None], jnp.sin(base)[:, None]
+    step_cos, step_sin = jnp.cos(step)[None], jnp.sin(step)[None]
+    cos_table = base_cos * step_cos - base_sin * step_sin
+    sin_table = (base_sin * step_cos + base_cos * step_sin) * sign
+    return cos_table.reshape(n * tokens, ROPE), sin_table.reshape(n * tokens, ROPE)
 
 
 def unrotate(grads, cos_table, sin_table):
@@ -447,13 +777,6 @@
     return scale_values * (
         grad_unit - unit_values * jnp.mean(grad_unit * unit_values, axis=-1, keepdims=True)
     )
-
-
-def silu_back(grad_hidden, gate_value, up_value):
-    sigmoid = jax.nn.sigmoid(gate_value)
-    grad_gate = grad_hidden * up_value * sigmoid * (1.0 + gate_value * (1.0 - sigmoid))
-    grad_up = grad_hidden * gate_value * sigmoid
-    return (grad_gate.astype(BF16), grad_up.astype(BF16))
 
 
 def column_halves(weight, n, half):
@@ -499,7 +822,6 @@
     tokens = layer_input.shape[0]
     length = tokens * n
     capacity = tokens * TOPK * 4 // (3 * n)
-    scale = 1.0 / math.sqrt(NOPE + ROPE)
     rows_dev = attention_gain.shape[0]
     latent_rows = latent_gain.shape[0]
     rows_out = D // (groups * n)
@@ -545,9 +867,7 @@
     shared_half = shared_half.T.reshape(n, shared_half.shape[1] // n, rows_dev)
 
     out_w_half = lax.dynamic_slice_in_dim(output_weight, half * (D // 2), D // 2, 1)
-    out_w_half, later_grad, q_blocks = lax.optimization_barrier(
-        (out_w_half, output_grad, q_blocks)
-    )
+    later_grad, q_blocks = lax.optimization_barrier((output_grad, q_blocks))
     out_w_mine = lax.all_gather(out_w_half, "ep", axis=0, tiled=True)
     out_w_other = from_partner(out_w_mine)
     all_out_grad = lax.all_gather(later_grad, "ep", axis=0, tiled=True)
@@ -558,30 +878,34 @@
     residual_all = all_input.astype(F32)
     unit_all = residual_all * rms_scale(residual_all)
     normed = (unit_all * attn_gain).astype(BF16)
-    places = jnp.arange(length, dtype=jnp.int32)
-    cos_table, sin_table = rotary_tables(places.astype(F32))
-    query_raw = product("td,cd->tc", normed, query_t)
-    query_n = query_raw[:, :NOPE].astype(BF16)
-    query_r = rotate(query_raw[:, NOPE:], cos_table, sin_table).astype(BF16)
-    compressed = product("td,dc->tc", normed, latent_w)
+    cos_table, sin_table = rotary_tables(tokens, n)
+    turned = jnp.concatenate(
+        [query_t, query_t[NOPE + ROPE // 2 :], query_t[NOPE : NOPE + ROPE // 2]], axis=0
+    )
+    query_raw = product("td,cd->tc", normed, turned)
+    query_r = query_raw[:, NOPE : NOPE + ROPE] * cos_table + query_raw[:, NOPE + ROPE :] * sin_table
+    query = jnp.concatenate(
+        [query_raw[:, :NOPE], query_r, jnp.zeros((length, ROPE), F32)], axis=1
+    ).astype(BF16)
+    latent_turned = jnp.concatenate(
+        [latent_w, latent_w[:, LATENT + ROPE // 2 :], latent_w[:, LATENT : LATENT + ROPE // 2]],
+        axis=1,
+    )
+    compressed = product("td,dc->tc", normed, latent_turned)
     latent_raw = compressed[:, :LATENT]
     latent = (latent_raw * rms_scale(latent_raw) * lat_gain).astype(BF16)
-    key_rope = rotate(compressed[:, LATENT:], cos_table, sin_table).astype(BF16)
+    rope_raw, rope_swapped = compressed[:, LATENT : LATENT + ROPE], compressed[:, LATENT + ROPE :]
     expanded = product("tl,cl->tc", latent, expand_t).astype(BF16)
-    key_nope = expanded[:, :NOPE]
+    keys = jnp.concatenate(
+        [
+            expanded[:, :NOPE],
+            (rope_raw * cos_table + rope_swapped * sin_table).astype(BF16),
+            (rope_swapped * cos_table - rope_raw * sin_table).astype(BF16),
+        ],
+        axis=1,
+    )
     values = expanded[:, NOPE:]
-    visible = (places[None, :] <= places[:, None]) | (places[None, :] < prefix_length[0])
-
-    def attention_scores():
-        scores = product("qd,kd->qk", query_n, key_nope)
-        scores = scores + product("qd,kd->qk", query_r, key_rope)
-        return jnp.where(visible, scores * scale, MASKED)
-
-    scores = attention_scores()
-    row_max = jnp.max(scores, axis=-1, keepdims=True)
-    log_total = row_max + jnp.log(jnp.sum(jnp.exp(scores - row_max), axis=-1, keepdims=True))
-    weights = jnp.exp(scores - log_total).astype(BF16)
-    attended_head = product("qk,kd->qd", weights, values).astype(BF16)
+    attended_head, attended_exact, lse = attend(prefix_length, query, keys, values)
     attended_blocks, shared_blocks = exchange(
         2, swaps=(attended_head.reshape(n, tokens, VH), shared_half)
     )
@@ -605,11 +929,7 @@
     ffn_blocks = gather(own_ffn_in, 3)
     ffn_in = ffn_blocks.reshape(length, D)
 
-    out_blocks = all_out_grad.reshape(n, tokens, D)
-    router_all = jax.nn.softmax(product("td,de->te", ffn_in, router_w), axis=-1)
-    gate_values = jnp.sum(
-        jnp.where(jnp.arange(n, dtype=jnp.int32) == e, router_all, 0.0), axis=-1
-    ).reshape(n, tokens)
+    own_lane = (jnp.arange(128, dtype=jnp.int32) == e).astype(F32)[None]
     chosen = jnp.any(routes == e, axis=-1)
     chosen_int = chosen.astype(jnp.int32)
     place = jnp.cumsum(chosen_int, axis=1) - chosen_int
@@ -617,64 +937,52 @@
     dispatch = (
         (place[:, None, :] == jnp.arange(capacity, dtype=jnp.int32)[None, :, None])
         & kept[:, None, :]
-    )
-    slot_gate = jnp.sum(jnp.where(dispatch, gate_values[:, None, :], 0.0), axis=-1)
-    dispatch = dispatch.astype(BF16)
-    kept_gate = jnp.where(kept, gate_values, 0.0)
-
-    def to_slots(blocks):
-        return product("bst,btd->bsd", dispatch, blocks)
-
-    def to_tokens(slots):
-        return product("bst,bsd->btd", dispatch, slots.reshape(n, capacity, D))
-
-    incoming = to_slots(ffn_blocks).astype(BF16).reshape(n * capacity, D)
-    out_slots = to_slots(out_blocks)
-    slot_grad = (out_slots * slot_gate[:, :, None]).astype(BF16).reshape(n * capacity, D)
-    gate_m, up_m, down_m = expert_gate[0], expert_up[0], expert_down[0]
-    expert_g = product("rd,df->rf", incoming, gate_m)
-    expert_u = product("rd,df->rf", incoming, up_m)
-    expert_hidden = (jax.nn.silu(expert_g) * expert_u).astype(BF16)
-    expert_out = product("rf,fd->rd", expert_hidden, down_m).astype(BF16)
-    slot_dot = jnp.sum(
-        out_slots * expert_out.astype(F32).reshape(n, capacity, D), axis=-1
-    )
-    token_dot = jnp.sum(dispatch.astype(F32) * slot_dot[:, :, None], axis=1)
-    shared_g = product("td,fd->tf", ffn_in, gate_t)
-    shared_u = product("td,fd->tf", ffn_in, up_t)
-    shared_hidden = (jax.nn.silu(shared_g) * shared_u).astype(BF16)
-    out_partial = product("tf,fd->td", shared_hidden, shared_down).reshape(n, tokens, D)
-    out_partial = (out_partial + to_tokens(expert_out) * kept_gate[:, :, None]).astype(BF16)
-    out_partial, slot_grad, all_out_grad = lax.optimization_barrier(
-        (out_partial, slot_grad, all_out_grad)
+    ).astype(BF16)
+    shared_width = gate_t.shape[0]
+    fill = ((0, -shared_width % 128), (0, 0))
+    (
+        out_partial,
+        ffn_partial,
+        dot_partial,
+        router_all,
+        incoming,
+        expert_hidden,
+        slot_grad,
+        grad_expert_g,
+        grad_expert_u,
+        shared_hidden,
+        grad_shared_g,
+        grad_shared_u,
+    ) = ffn(
+        ffn_blocks,
+        all_out_grad.reshape(n, tokens, D),
+        dispatch,
+        own_lane,
+        jnp.pad(router_w, ((0, 0), (0, 128 - n))),
+        jnp.pad(gate_t, fill),
+        jnp.pad(up_t, fill),
+        jnp.pad(shared_down, fill),
+        expert_gate[0],
+        expert_up[0],
+        expert_down[0],
     )
     out_sum = lax.psum_scatter(out_partial, "ep", scatter_dimension=0)
     layer_output = (residual_mid + out_sum.astype(F32)).astype(BF16)
-
-    grad_shared_hidden = product("td,fd->tf", all_out_grad, shared_down)
-    grad_shared_g, grad_shared_u = silu_back(grad_shared_hidden, shared_g, shared_u)
-    grad_expert_hidden = product("rd,fd->rf", slot_grad, down_m)
-    grad_expert_g, grad_expert_u = silu_back(grad_expert_hidden, expert_g, expert_u)
-    row_grad = (
-        product("rf,df->rd", grad_expert_g, gate_m) + product("rf,df->rd", grad_expert_u, up_m)
-    ).astype(BF16)
-    ffn_partial = product("tf,fd->td", grad_shared_g, gate_t) + product(
-        "tf,fd->td", grad_shared_u, up_t
-    )
-    ffn_partial = (ffn_partial.reshape(n, tokens, D) + to_tokens(row_grad)).astype(BF16)
-    own_column = (jnp.arange(128, dtype=jnp.int32) == e).astype(F32)
-    dot_partial = (token_dot[:, :, None] * own_column).astype(BF16)
     ffn_sum, dot_sum = exchange(4, sums=(ffn_partial, dot_partial))
+
+    def shared_columns(values):
+        return values.reshape(length, -1)[:, :shared_width]
 
     expert_down_grad = product_over_groups(expert_hidden, slot_grad)[None]
     expert_gate_grad = product_over_groups(incoming, grad_expert_g)[None]
     expert_up_grad = product_over_groups(incoming, grad_expert_u)[None]
-    shared_down_grad = to_row_owner(product_over_groups(shared_hidden, all_out_grad))
+    shared_down_grad = to_row_owner(product_over_groups(shared_columns(shared_hidden), all_out_grad))
     side_shared = product_over_groups(
-        ffn_in, jnp.concatenate([grad_shared_g, grad_shared_u], axis=1)
+        ffn_in,
+        jnp.concatenate([shared_columns(grad_shared_g), shared_columns(grad_shared_u)], axis=1),
     ).astype(BF16)
 
-    router_own = own(router_all)
+    router_own = lax.dynamic_index_in_dim(router_all, e, 0, keepdims=False)[:, :n]
     grad_probs = dot_sum[:, :n]
     grad_logits = (
         router_own * (grad_probs - jnp.sum(router_own * grad_probs, axis=-1, keepdims=True))
@@ -697,28 +1005,27 @@
         (output_w_partial, grad_att_blocks)
     )
     grad_att = grad_att_blocks.reshape(length, VH)
-    output_weight_grad = lax.psum_scatter(
-        output_w_partial.reshape(n, rows_out, D), "ep", scatter_dimension=0
-    ).astype(F32)
+    output_weight_grad = sum_async(output_w_partial.reshape(n, rows_out, D))
     grad_router = product("te,td->ed", grad_logits, own_ffn_in)
 
-    probs = jnp.exp(attention_scores() - log_total)
-    grad_weights = product("qd,kd->qk", grad_att, values)
-    delta = jnp.sum(probs * grad_weights, axis=-1, keepdims=True)
-    grad_scores = (probs * (grad_weights - delta)).astype(BF16)
-    grad_query_n = product("qk,kd->qd", grad_scores, key_nope) * scale
-    grad_query_r = product("qk,kd->qd", grad_scores, key_rope) * scale
-    grad_key_n = product("qk,qd->kd", grad_scores, query_n) * scale
-    grad_key_r = product("qk,qd->kd", grad_scores, query_r) * scale
-    grad_values = product("qk,qd->kd", probs.astype(BF16), grad_att)
+    delta = jnp.sum(grad_att.astype(F32) * attended_exact, axis=-1)[None]
+    grad_query_raw, grad_keys, grad_values = attend_back(
+        prefix_length, query, grad_att, lse, delta, keys, values
+    )
+    grad_key_n = grad_keys[:, :NOPE]
     grad_expanded = jnp.concatenate([grad_key_n, grad_values], axis=1).astype(BF16)
     latent_partial = product("tc,cl->tl", grad_expanded, expand_t).astype(BF16)
-    grad_key_r = jnp.pad(grad_key_r, ((0, 0), (0, 128 - ROPE))).astype(BF16)
+    grad_key_r = grad_keys[:, NOPE:].astype(BF16)
     latent_sum, rope_sum = exchange(
         6, sums=(latent_partial.reshape(n, tokens, LATENT), grad_key_r.reshape(n, tokens, 128))
     )
     grad_query = jnp.concatenate(
-        [grad_query_n, unrotate(grad_query_r, cos_table, sin_table)], axis=1
+        [
+            grad_query_raw[:, :NOPE],
+            grad_query_raw[:, NOPE : NOPE + ROPE] * cos_table
+            - grad_query_raw[:, NOPE + ROPE :] * sin_table,
+        ],
+        axis=1,
     ).astype(BF16)
     normed_partial = product("tc,cd->td", grad_query, query_t)
     gain_partial = jnp.sum(normed_partial * unit_all, axis=0)
@@ -733,7 +1040,11 @@
     grad_compressed = jnp.concatenate(
         [
             norm_back(latent_sum * lat_gain, latent_unit, latent_scale),
-            unrotate(rope_sum[:, :ROPE], own(cos_table), own(sin_table)),
+            unrotate(
+                rope_sum[:, :ROPE],
+                own(cos_table)[:, : ROPE // 2],
+                own(sin_table)[:, ROPE // 2 :],
+            ),
         ],
         axis=-1,
     ).astype(BF16)
@@ -773,7 +1084,6 @@
     ).astype(BF16)
     latent_weight_grad = latent_weight_sum[:, : LATENT + ROPE]
     query_weight_grad = query_all.transpose(1, 0, 2).reshape(rows_out, -1).astype(F32)
-    shared_width = gate_t.shape[0]
     shared_all = shared_all.transpose(1, 0, 2)
     shared_gate_grad = shared_all[:, :, :shared_width].reshape(rows_out, -1).astype(F32)
     shared_up_grad = shared_all[:, :, shared_width:].reshape(rows_out, -1).astype(F32)

time: 1140 us -> 1060 us (0.930)
  matrix products: 314 us -> 113 us
  Pallas kernels: 603 us -> 741 us
  other arithmetic: 92.5 us -> 70.3 us
  local copies, waits for them, and re-layouts: 71.2 us -> 91.3 us
    dot_general x56 -> x30, matrix products: 314 us -> 113 us  [product(): return jnp.einsum(form, left, right, preferred_element_type=F32)]
    pallas_call x0 -> x3, Pallas kernels: none -> 116 us  [the longest x1 85.7 us: ffn(): pl.pallas_call(functools.partial(ffn_kernel, n), grid=(n // group,), in_s...]
    ppermute x9, starting transfers between devices: 22.5 us -> 1.63 us  [product_over_groups(): other = lax.ppermute(sent, 'grp', [(0, 1), (1, 0)])]
    ppermute x0 -> x7, starting transfers between devices: none -> 11.9 us  [the longest x4 6.49 us: fold(): got = lax.ppermute(sent, 'ep', [(i, i ^ bit) for i in range(n)])]
    pallas_call x2, Pallas kernels: 206 us -> 217 us  [gather(): pl.pallas_call(functools.partial(gather_kernel, n), out_shape=jax.ShapeDt...]
    unnamed x244 -> x230, local copies, waits for them, and re-layouts: 26.5 us -> 30.2 us
    convert_element_type x7 -> x10, other arithmetic: 23.4 us -> 24.8 us  [the longest x1 14.8 us: per_device(): (rope_swapped * cos_table - rope_raw * sin_table).astype(BF16)]
  transfers between devices with their start and end apart: 19 -> 25, of which waited for: 2 -> 1; matrix products, arithmetic and copies ran while one was open for 31% -> 24% of each run, Pallas kernels for 34% -> 62%
where the time goes in v3:
time: 1060 us; the launch traced here: 1050 us
  Pallas kernels  741 us (70%)
  matrix products  113 us (11%)
  local copies, waits for them, and re-layouts  91.3 us (9%)
  other arithmetic  70.3 us (7%)
  starting transfers between devices  18.7 us (2%)
  between operations  16.4 us (2%)
    pallas_call x6, Pallas kernels, exchange(): pl.pallas_call(functools.partial(exchange_kernel, n, m, w), out_shape=[ja...  408 us
    pallas_call x2, Pallas kernels, gather(): pl.pallas_call(functools.partial(gather_kernel, n), out_shape=jax.ShapeDt...  217 us
    dot_general x30, matrix products, product(): return jnp.einsum(form, left, right, preferred_element_type=F32)  113 us
    pallas_call x1, Pallas kernels, ffn(): pl.pallas_call(functools.partial(ffn_kernel, n), grid=(n // group,), in_s...  85.7 us
    unnamed x230, local copies, waits for them, and re-layouts  30.2 us
  transfers between devices with their start and end apart: 25, of which 1 were waited for; matrix products, arithmetic and copies ran while one was open for 24% of the time, Pallas kernels for 62%

profile of v3, /device:TPU:0, one launch (start us, length us, event | category | flops | bytes accessed | tf_op | source)
XLA Modules:
  0.0 1052.2 jit_solution(11014473550728656277)
XLA Ops:
  20.7 121.4 %gather.2 = bf16[16,128,2688]{2,1,0:T(8,128)(2,1)} custom-call(bf16[128,2688]{1,0:T(8,128)(2,1)} %pad.23.x_ref), custom_call_target="tpu_custom_call" | custom-call | tf_op jit(solution)/shard_map/gather/pallas_call | solution.py:163
  142.9 19.6 %exchange.6 = (bf16[16,96,128]{2,1,0:T(8,128)(2,1)}, bf16[16,128,32]{2,1,0:T(8,128)(2,1)}) custom-call(bf16[16,96,128]{2,1,0:T(8,128)(2,1)} %dynamic-slice_bitcast_fusion.2.refs_0_, bf16[16,128,32]{2,1,0:T(8,128)(2,1)} %bitcast.244), custom_call_target="tpu_custom_call" | custom-call | tf_op jit(solution)/shard_map/exchange/pallas_call | solution.py:359
  175.2 5.1 multiply_reduce_fusion.1
  180.6 5.9 multiply_convert_fusion
  186.5 5.7 fusion.8
  212.2 6.1 fusion.43
  218.4 14.8 %subtract_convert_fusion.1 = (bf16[2048,64]{1,0:T(8,128)(2,1)S(1)}, bf16[2048,64]{1,0:T(8,128)(2,1)S(1)}) fusion(f32[2048,64]{1,0:T(8,128)S(1)} %copy-done.32, f32[2048,64]{1,0:T(8,128)S(1)} %get-tuple-element.105, f32[2048,64]{1,0:T(8,128)S(1)} %copy-done.34, f32[16,128,64]{2,1,0:T(8,128)S(1)} %get-tuple-element.147, f32[2048,256]{1,0:T(8,128)S(1)} %fusion.43), kind=kLoop, calls=%fused_computation.119 | loop fusion | flops 1048576 | bytes 3670016 | tf_op jit(solution)/shard_map/convert_element_type | solution.py:903
  233.9 13.9 %attend.1 = (bf16[2048,128]{1,0:T(8,128)(2,1)S(1)}, f32[2048,128]{1,0:T(8,128)S(1)}, f32[1,2048]{1,0:T(1,128)S(1)}) custom-call(s32[1]{0:T(128)S(6)} %copy.134.prefix_ref, bf16[2048,256]{1,0:T(8,128)(2,1)S(1)} %get-tuple-element.157.q_ref, bf16[4,512,256]{2,1,0:T(8,128)(2,1)S(1)} %bitcast.201, bf16[4,128,512]{2,1,0:T(8,128)(2,1)S(1)} %copy.71.v_ref), custom_call_target="tpu_custom_call" | custom-call | tf_op jit(solution)/shard_map/attend/pallas_call | solution.py:497
  249.6 40.3 %exchange.7 = (bf16[16,128,128]{2,1,0:T(8,128)(2,1)}, bf16[16,176,128]{2,1,0:T(8,128)(2,1)}) custom-call(bf16[16,128,128]{2,1,0:T(8,128)(2,1)} %bitcast.215, bf16[16,176,128]{2,1,0:T(8,128)(2,1)} %bitcast.243), custom_call_target="tpu_custom_call" | custom-call | tf_op jit(solution)/shard_map/exchange/pallas_call | solution.py:359
  310.8 95.7 %gather.3.x_ref = bf16[16,128,2048]{2,1,0:T(8,128)(2,1)} custom-call(bf16[128,2048]{1,0:T(8,128)(2,1)} %multiply_convert_fusion.2.x_ref), custom_call_target="tpu_custom_call" | custom-call | tf_op jit(solution)/shard_map/gather/pallas_call | solution.py:163
  407.1 85.7 %ffn.1 = (bf16[16,128,2048]{2,1,0:T(8,128)(2,1)}, bf16[16,128,2048]{2,1,0:T(8,128)(2,1)}, bf16[16,128,128]{2,1,0:T(8,128)(2,1)}, f32[16,128,128]{2,1,0:T(8,128)}...) custom-call(bf16[16,128,2048]{2,1,0:T(8,128)(2,1)} %gather.3.x_ref, ...), custom_call_target="tpu_custom_call" | custom-call | tf_op jit(solution)/shard_map/ffn/pallas_call | solution.py:698
  493.9 3.5 copy-done.3
  497.3 182.8 %exchange.8 = (f32[128,2048]{1,0:T(8,128)S(1)}, f32[128,128]{1,0:T(8,128)S(1)}) custom-call(bf16[4,2,2,128,2048]{4,3,2,1,0:T(8,128)(2,1)S(1)} %bitcast.204, bf16[4,2,2,128,128]{4,3,2,1,0:T(8,128)(2,1)S(1)} %bitcast.214), custom_call_target="tpu_custom_call" | custom-call | tf_op jit(solution)/shard_map/exchange/pallas_call | solution.py:359
  681.9 6.1 convolution_convert_fusion.6
  688.1 4.8 convolution_convert_fusion.1
  692.9 4.8 convolution_convert_fusion
  698.2 5.1 convolution_convert_fusion.3
  709.8 4.7 fusion.14
  718.6 6.2 add_convert_fusion.5
  724.8 4.4 collective-permute-start.18
  729.2 5.1 add_convert_fusion.2
  737.6 9.5 add_bitcast_fusion.1
  747.2 7.1 add_bitcast_fusion.2
  754.3 6.8 add_bitcast_fusion
  761.1 5.4 add_convert_fusion
  770.5 22.6 %exchange.9 = bf16[16,128,128]{2,1,0:T(8,128)(2,1)} custom-call(bf16[16,128,128]{2,1,0:T(8,128)(2,1)} %bitcast.246), custom_call_target="tpu_custom_call" | custom-call | tf_op jit(solution)/shard_map/exchange/pallas_call | solution.py:359
  805.4 16.6 %attend_back.1 = (f32[2048,256]{1,0:T(8,128)S(1)}, f32[4,512,256]{2,1,0:T(8,128)S(1)}, f32[4,512,128]{2,1,0:T(8,128)S(1)}) custom-call(s32[1]{0:T(128)S(6)} %copy.134.prefix_ref, bf16[2048,256]{1,0:T(8,128)(2,1)S(1)} %get-tuple-element.157.q_ref, bf16[2048,128]{1,0:T(8,128)(2,1)S(1)} %bitcast.206, f32[1,2048]{1,0:T(1,128)S(1)} %get-tuple-element.72.lse_ref, ...), custom_call_target="tpu_custom_call" | custom-call | tf_op jit(solution)/shard_map/attend_back/pallas_call | solution.py:555
  823.9 4.1 fusion.30
  831.8 33.6 %exchange.10 = (f32[128,512]{1,0:T(8,128)S(1)}, f32[128,128]{1,0:T(8,128)S(1)}) custom-call(bf16[4,2,2,128,512]{4,3,2,1,0:T(8,128)(2,1)S(1)} %bitcast.211, bf16[4,2,2,128,128]{4,3,2,1,0:T(8,128)(2,1)S(1)} %bitcast.212), custom_call_target="tpu_custom_call" | custom-call | tf_op jit(solution)/shard_map/exchange/pallas_call | solution.py:359
  865.9 5.0 multiply_reduce_fusion
  877.0 4.0 add_convert_fusion.4
  894.9 109.4 %exchange.11 = (f32[128,2048]{1,0:T(8,128)S(1)}, f32[64,640]{1,0:T(8,128)S(1)}, bf16[16,64,192]{2,1,0:T(8,128)(2,1)S(1)}, bf16[16,64,352]{2,1,0:T(8,128)(2,1)S(1...) custom-call(bf16[4,2,2,128,2048]{4,3,2,1,0:T(8,128)(2,1)S(1)} %bitcast.203, ...), custom_call_target="tpu_custom_call" | custom-call | tf_op jit(solution)/shard_map/exchange/pallas_call | solution.py:359
  (427 shorter events, 170.2 us)
Async XLA Ops:
  7.2 204.0 %all-gather.3.cloned.1.call-start = ((), (), s32[]{:S(2)}) async-start(), calls=%async_computation.1 | async-start | bytes 4456448 | tf_op jit(solution)/shard_map/all_gather | solution.py:871
  9.0 398.1 %all-gather.5.cloned.1.call-start = ((), (), s32[]{:S(2)}) async-start(), calls=%async_computation.2 | async-start | bytes 8912896 | tf_op jit(solution)/shard_map/all_gather | solution.py:873
  163.7 41.7 %collective-permute-start.1 = (bf16[128,512]{0,1:T(8,128)(2,1)S(1)}, bf16[128,512]{0,1:T(8,128)(2,1)}, u32[]{:S(2)}, u32[]{:S(2)}) collective-permute-start(bf16[128,512]{0,1:T(8,128)(2,1)S(1)} %bitcast.254), channel_id=1, source_target_pairs={{0,16},{16,0},{1,17},{17,1},{2,18},{18,2},{3,19},{19,3},{4,20},{20... | collective-permute-start | bytes 393224 | tf_op jit(solution)/shard_map/ppermute | solution.py:404
  165.6 43.5 %collective-permute-start = (bf16[96,2048]{1,0:T(8,128)(2,1)}, bf16[96,2048]{1,0:T(8,128)(2,1)}, u32[]{:S(2)}, u32[]{:S(2)}) collective-permute-start(bf16[96,2048]{1,0:T(8,128)(2,1)} %copy_bitcast_fusion.5), channel_id=1, source_target_pairs={{0,16},{16,0},{1,17},{17,1},{2,18},{18,2},{3,19},{19,3},{4,20},{20... | collective-permute-start | bytes 1179656 | tf_op jit(solution)/shard_map/ppermute | solution.py:404
  166.1 875.3 %reduce-scatter.2.cloned.1.call-start = ((), (), s32[]{:S(2)}) async-start(), calls=%async_computation.3 | async-start | bytes 8912896 | tf_op jit(solution)/shard_map/reduce_scatter | solution.py:969
  170.8 533.1 %copy-start.70 = (f32[16,128]{1,0:T(8,128)}, f32[16,128]{1,0:T(8,128)S(1)}, u32[]{:S(2)}) copy-start(f32[16,128]{1,0:T(8,128)S(1)} %get-tuple-element.94) | copy-start | bytes 24580
  211.2 94.2 %collective-permute-start.2 = (bf16[2048,1024]{1,0:T(8,128)(2,1)}, bf16[2048,1024]{1,0:T(8,128)(2,1)}, u32[]{:S(2)}, u32[]{:S(2)}) collective-permute-start(bf16[2048,1024]{1,0:T(8,128)(2,1)} %all-gather.3.cloned.1.call-done), channel_id=1, source_target_pairs={{0,16},{16,0},{1,17},{17,1},{2,18},{18,2},{3,19},{19,3},{4,20},{20... | collective-permute-start | bytes 12582920 | tf_op jit(solution)/shard_map/ppermute | solution.py:404
  292.0 8.6 collective-permute-start.3
  308.9 395.0 %copy-start.86 = (f32[128]{0:T(128)}, f32[128]{0:T(128)S(1)}, u32[]{:S(2)}) copy-start(f32[128]{0:T(128)S(1)} %add_rsqrt_fusion.3) | copy-start | bytes 1540
  497.3 184.0 %copy-start.15 = (f32[128,2048]{1,0:T(8,128)S(1)}, f32[128,2048]{1,0:T(8,128)}, u32[]{:S(2)}) copy-start(f32[128,2048]{1,0:T(8,128)} %copy-done.14) | copy-start | bytes 3145732
  497.3 184.0 %copy-start.46 = (bf16[16,128,16]{2,1,0:T(8,128)(2,1)S(1)}, bf16[16,128,16]{2,1,0:T(8,128)(2,1)}, u32[]{:S(2)}) copy-start(bf16[16,128,16]{2,1,0:T(8,128)(2,1)} %copy-done.45) | copy-start | bytes 196612
  688.0 29.7 %collective-permute-start.17 = (bf16[88,2048]{1,0:T(8,128)(2,1)}, bf16[88,2048]{1,0:T(8,128)(2,1)}, u32[]{:S(2)}, u32[]{:S(2)}) collective-permute-start(bf16[88,2048]{1,0:T(8,128)(2,1)} %convolution_convert_fusion.6), channel_id=1, source_target_pairs={{0,16},{16,0},{1,17},{17,1},{2,18},{18,2},{3,19},{19,3},{4,20},{20... | collective-permute-start | bytes 1081352 | tf_op jit(solution)/shard_map/ppermute | solution.py:398
  697.7 39.9 %collective-permute-start.20 = (bf16[1024,1408]{1,0:T(8,128)(2,1)}, bf16[1024,1408]{1,0:T(8,128)(2,1)}, u32[]{:S(2)}, u32[]{:S(2)}) collective-permute-start(bf16[1024,1408]{1,0:T(8,128)(2,1)} %convolution_convert_fusion), channel_id=1, source_target_pairs={{0,16},{16,0},{1,17},{17,1},{2,18},{18,2},{3,19},{19,3},{4,20},{20... | collective-permute-start | bytes 8650760 | tf_op jit(solution)/shard_map/ppermute | solution.py:398
  698.2 48.9 %collective-permute-start.19 = (bf16[1024,1408]{1,0:T(8,128)(2,1)}, bf16[1024,1408]{1,0:T(8,128)(2,1)}, u32[]{:S(2)}, u32[]{:S(2)}) collective-permute-start(bf16[1024,1408]{1,0:T(8,128)(2,1)} %convolution_convert_fusion.1), channel_id=1, source_target_pairs={{0,16},{16,0},{1,17},{17,1},{2,18},{18,2},{3,19},{19,3},{4,20},{20... | collective-permute-start | bytes 8650760 | tf_op jit(solution)/shard_map/ppermute | solution.py:398
  703.4 50.8 %collective-permute-start.21 = (bf16[704,2048]{1,0:T(8,128)(2,1)}, bf16[704,2048]{1,0:T(8,128)(2,1)}, u32[]{:S(2)}, u32[]{:S(2)}) collective-permute-start(bf16[704,2048]{1,0:T(8,128)(2,1)} %convolution_convert_fusion.3), channel_id=1, source_target_pairs={{0,16},{16,0},{1,17},{17,1},{2,18},{18,2},{3,19},{19,3},{4,20},{20... | collective-permute-start | bytes 8650760 | tf_op jit(solution)/shard_map/ppermute | solution.py:398
  707.8 53.2 %collective-permute-start.4 = (bf16[1024,2048]{1,0:T(8,128)(2,1)}, bf16[1024,2048]{1,0:T(8,128)(2,1)}, u32[]{:S(2)}, u32[]{:S(2)}) collective-permute-start(bf16[1024,2048]{1,0:T(8,128)(2,1)} %convolution_convert_fusion.2), channel_id=1, source_target_pairs={{0,16},{16,0},{1,17},{17,1},{2,18},{18,2},{3,19},{19,3},{4,20},{20... | collective-permute-start | bytes 12582920 | tf_op jit(solution)/shard_map/ppermute | solution.py:398
  717.8 7.0 collective-permute-start.7
  724.8 10.9 %collective-permute-start.18 = (bf16[88,2048]{1,0:T(8,128)(2,1)}, bf16[88,2048]{1,0:T(8,128)(2,1)}, u32[]{:S(2)}, u32[]{:S(2)}) collective-permute-start(bf16[88,2048]{1,0:T(8,128)(2,1)} %add_convert_fusion.5), channel_id=1, source_target_pairs={{0,0},{1,2},{2,4},{3,6},{4,8},{5,10},{6,12},{7,14},{8,16},{9,18},{... | collective-permute-start | bytes 1081352 | tf_op jit(solution)/shard_map/ppermute | solution.py:410
  798.1 84.2 %collective-permute-start.12 = (bf16[4,2,32,2048]{3,2,0,1:T(8,128)(2,1)}, bf16[4,2,32,2048]{3,2,0,1:T(8,128)(2,1)}, u32[]{:S(2)}, u32[]{:S(2)}) collective-permute-start(bf16[4,2,32,2048]{3,2,0,1:T(8,128)(2,1)} %bitcast.191), channel_id=1, source_target_pairs={{0,1},{1,0},{2,3},{3,2},{4,5},{5,4},{6,7},{7,6},{8,9},{9,8},{10,11... | collective-permute-start | bytes 3145736 | tf_op jit(solution)/shard_map/ppermute | solution.py:425
  801.9 84.4 %collective-permute-start.10 = (bf16[4,2,32,2048]{3,2,0,1:T(8,128)(2,1)}, bf16[4,2,32,2048]{3,2,0,1:T(8,128)(2,1)}, u32[]{:S(2)}, u32[]{:S(2)}) collective-permute-start(bf16[4,2,32,2048]{3,2,0,1:T(8,128)(2,1)} %bitcast.192), channel_id=1, source_target_pairs={{0,2},{1,3},{2,0},{3,1},{4,6},{5,7},{6,4},{7,5},{8,10},{9,11},{10,... | collective-permute-start | bytes 3145736 | tf_op jit(solution)/shard_map/ppermute | solution.py:425
  823.8 42.0 %slice-start = ((s8[11010048]{0:T(1024)(128)(4,1)}), s8[4194304]{0:T(1024)(128)(4,1)S(1)}, s32[]{:S(2)}) async-start(s8[11010048]{0:T(1024)(128)(4,1)} %bitcast.220), calls=%async_computation.4 | async-start | bytes 8388608
  823.8 42.0 %slice-start.1 = ((s8[11010048]{0:T(1024)(128)(4,1)}), s8[4194304]{0:T(1024)(128)(4,1)S(1)}, s32[]{:S(2)}) async-start(s8[11010048]{0:T(1024)(128)(4,1)} %bitcast.220), calls=%async_computation.5 | async-start | bytes 8388608
  828.0 49.0 %collective-permute-start.6 = (bf16[1024,192]{0,1:T(8,128)(2,1)}, bf16[1024,192]{0,1:T(8,128)(2,1)}, u32[]{:S(2)}, u32[]{:S(2)}) collective-permute-start(bf16[1024,192]{0,1:T(8,128)(2,1)} %fusion.30), channel_id=1, source_target_pairs={{0,16},{16,0},{1,17},{17,1},{2,18},{18,2},{3,19},{19,3},{4,20},{20... | collective-permute-start | bytes 1179656 | tf_op jit(solution)/shard_map/ppermute | solution.py:398
  830.9 35.0 %slice-start.2 = ((s8[11010048]{0:T(1024)(128)(4,1)}), s8[2621440]{0:T(1024)(128)(4,1)S(1)}, s32[]{:S(2)}) async-start(s8[11010048]{0:T(1024)(128)(4,1)} %bitcast.220), calls=%async_computation.6 | async-start | bytes 5242880
  830.9 44.2 %collective-permute-start.8 = (bf16[256,256]{1,0:T(8,128)(2,1)}, bf16[256,256]{1,0:T(8,128)(2,1)}, u32[]{:S(2)}, u32[]{:S(2)}) collective-permute-start(bf16[256,256]{1,0:T(8,128)(2,1)} %convolution_convert_fusion.8), channel_id=1, source_target_pairs={{0,16},{16,0},{1,17},{17,1},{2,18},{18,2},{3,19},{19,3},{4,20},{20... | collective-permute-start | bytes 393224 | tf_op jit(solution)/shard_map/ppermute | solution.py:398
  874.9 14.8 %collective-permute-start.5 = (bf16[1024,640]{1,0:T(8,128)(2,1)}, bf16[1024,640]{1,0:T(8,128)(2,1)}, u32[]{:S(2)}, u32[]{:S(2)}) collective-permute-start(bf16[1024,640]{1,0:T(8,128)(2,1)} %convolution_convert_fusion.7), channel_id=1, source_target_pairs={{0,16},{16,0},{1,17},{17,1},{2,18},{18,2},{3,19},{19,3},{4,20},{20... | collective-permute-start | bytes 3932168 | tf_op jit(solution)/shard_map/ppermute | solution.py:398
  885.2 128.4 %collective-permute-start.13 = (bf16[4,32,2048]{2,1,0:T(8,128)(2,1)}, bf16[4,32,2048]{2,1,0:T(8,128)(2,1)}, u32[]{:S(2)}, u32[]{:S(2)}) collective-permute-start(bf16[4,32,2048]{2,1,0:T(8,128)(2,1)} %dynamic-slice_bitcast_fusion), channel_id=1, source_target_pairs={{0,2},{1,3},{2,0},{3,1},{4,6},{5,7},{6,4},{7,5},{8,10},{9,11},{10,... | collective-permute-start | bytes 1572872 | tf_op jit(solution)/shard_map/ppermute | solution.py:425
  888.9 125.9 %collective-permute-start.11 = (bf16[4,32,2048]{2,1,0:T(8,128)(2,1)}, bf16[4,32,2048]{2,1,0:T(8,128)(2,1)}, u32[]{:S(2)}, u32[]{:S(2)}) collective-permute-start(bf16[4,32,2048]{2,1,0:T(8,128)(2,1)} %dynamic-slice_bitcast_fusion.1), channel_id=1, source_target_pairs={{0,1},{1,0},{2,3},{3,2},{4,5},{5,4},{6,7},{7,6},{8,9},{9,8},{10,11... | collective-permute-start | bytes 1572872 | tf_op jit(solution)/shard_map/ppermute | solution.py:425
  1008.1 27.9 %collective-permute-start.9 = (f32[1168]{0:T(1024)S(1)}, f32[1168]{0:T(1024)S(1)}, u32[]{:S(2)}, u32[]{:S(2)}) collective-permute-start(f32[1168]{0:T(1024)S(1)} %get-tuple-element.100), channel_id=1, source_target_pairs={{0,16},{16,0},{1,17},{17,1},{2,18},{18,2},{3,19},{19,3},{4,20},{20... | collective-permute-start | bytes 14024 | tf_op jit(solution)/shard_map/ppermute | solution.py:1096
  1017.0 20.8 %collective-permute-start.14 = (bf16[64,2048]{1,0:T(8,128)(2,1)}, bf16[64,2048]{1,0:T(8,128)(2,1)}, u32[]{:S(2)}, u32[]{:S(2)}) collective-permute-start(bf16[64,2048]{1,0:T(8,128)(2,1)} %get-tuple-element.124), channel_id=1, source_target_pairs={{0,4},{1,5},{2,6},{3,7},{4,8},{5,9},{6,10},{7,11},{8,12},{9,13},{1... | collective-permute-start | bytes 786440 | tf_op jit(solution)/shard_map/ppermute | solution.py:434
  1018.1 21.1 %collective-permute-start.15 = (bf16[64,2048]{1,0:T(8,128)(2,1)S(1)}, bf16[64,2048]{1,0:T(8,128)(2,1)}, u32[]{:S(2)}, u32[]{:S(2)}) collective-permute-start(bf16[64,2048]{1,0:T(8,128)(2,1)S(1)} %get-tuple-element.125), channel_id=1, source_target_pairs={{0,8},{1,9},{2,10},{3,11},{4,12},{5,13},{6,14},{7,15},{8,0},{9,1},... | collective-permute-start | bytes 786440 | tf_op jit(solution)/shard_map/ppermute | solution.py:434
  1020.0 19.2 %collective-permute-start.16 = (bf16[64,2048]{1,0:T(8,128)(2,1)S(1)}, bf16[64,2048]{1,0:T(8,128)(2,1)}, u32[]{:S(2)}, u32[]{:S(2)}) collective-permute-start(bf16[64,2048]{1,0:T(8,128)(2,1)S(1)} %get-tuple-element.126), channel_id=1, source_target_pairs={{0,12},{1,13},{2,14},{3,15},{4,0},{5,1},{6,2},{7,3},{8,4},{9,5},{1... | collective-permute-start | bytes 786440 | tf_op jit(solution)/shard_map/ppermute | solution.py:434
  (103 other events, 857.0 us)
Sparse Core Ops, SparseCore 0:
  11.4 102.6 all-gather.2
  166.2 140.9 all-gather.4
  493.0 255.0 reduce-scatter.1

commit v4 on v3

--- a/solution.py
+++ b/solution.py
@@ -182,7 +182,7 @@
     lax.fori_loop(0, rows // step, body, 0)
 
 
-def exchange_kernel(n, m, w, *refs):
+def exchange_kernel(n, m, w, laid, *refs):
     refs = list(refs)
 
     def take(count):
@@ -195,6 +195,8 @@
     room = [take(7) for _ in range(m)]
     sems = [take(8) for _ in range(m)]
     swap_sems = take(3) if w else None
+    side_by_side = swaps_out[w - laid :]
+    swaps_out = swaps_out[: w - laid] + take(laid)
     me, z, y, x, px, py = around(n)
     nz = n // 4
     low = me % 4
@@ -301,26 +303,6 @@
             stage_three(*steps[i - 1])
     if steps:
         stage_three(*steps[-1])
-    for j in range(m):
-        half, top, bottom = halves(j)
-        la, lb, a1, b1, a2, b2, zb = room[j]
-        o_ref = sums_out[j]
-        for k in range(1, nz):
-            c, d = third[j, k]
-            c.wait_recv()
-            d.wait_recv()
-        for part, offset in ((a2, 0), (b2, half)):
-
-            def body(i, carry, part=part, offset=offset, zb=zb, o_ref=o_ref):
-                r = pl.ds(pl.multiple_of(i * 16, 16), 16)
-                q = pl.ds(pl.multiple_of(i * 16 + offset, 16), 16)
-                total = part[0, r].astype(F32)
-                for k in range(1, nz):
-                    total = total + zb[k, q].astype(F32)
-                o_ref[q] = total.astype(o_ref.dtype)
-                return carry
-
-            lax.fori_loop(0, half // 16, body, 0)
     if w:
         own, ss, rs = swap_sems
         for k in range(1, n):
@@ -332,13 +314,37 @@
                     rs.at[j, k],
                     everyone[k],
                 ).wait_recv()
+        for copy in copies:
+            copy.wait()
+        for wide, got in zip(side_by_side, swaps_out[w - laid :]):
+            width = got.shape[2]
+            for k in range(n):
+                wide[:, k * width : (k + 1) * width] = got[k].astype(F32)
+    for j in range(m):
+        half, top, bottom = halves(j)
+        la, lb, a1, b1, a2, b2, zb = room[j]
+        o_ref = sums_out[j]
+        for k in range(1, nz):
+            c, d = third[j, k]
+            c.wait_recv()
+            d.wait_recv()
+        for part, offset in ((a2, 0), (b2, half)):
+
+            def body(i, carry, part=part, offset=offset, zb=zb, o_ref=o_ref):
+                r = pl.ds(pl.multiple_of(i * 16, 16), 16)
+                q = pl.ds(pl.multiple_of(i * 16 + offset, 16), 16)
+                total = part[0, r].astype(F32)
+                for k in range(1, nz):
+                    total = total + zb[k, q].astype(F32)
+                o_ref[q] = total.astype(o_ref.dtype)
+                return carry
+
+            lax.fori_loop(0, half // 16, body, 0)
     for copy in sends:
         copy.wait_send()
-    for copy in copies:
-        copy.wait()
-
-
-def exchange(cid, sums=(), swaps=()):
+
+
+def exchange(cid, sums=(), swaps=(), laid=0):
     n = lax.axis_size("ep")
     nz = n // 4
     m, w = len(sums), len(swaps)
@@ -356,12 +362,17 @@
         scratch += [DMA((nz,))] * 2 + [DMA((2 * nz,))] * 6
     if w:
         scratch += [DMA((w,)), DMA((w, n)), DMA((w, n))]
+    plain, wide = swaps[: w - laid], swaps[w - laid :]
+    scratch += [pltpu.VMEM(a.shape, a.dtype) for a in wide]
     out = pl.pallas_call(
-        functools.partial(exchange_kernel, n, m, w),
+        functools.partial(exchange_kernel, n, m, w, laid),
         out_shape=[jax.ShapeDtypeStruct(p.shape[1:], F32) for p in sums]
-        + [jax.ShapeDtypeStruct(a.shape, a.dtype) for a in swaps],
+        + [jax.ShapeDtypeStruct(a.shape, a.dtype) for a in plain]
+        + [jax.ShapeDtypeStruct((a.shape[1], n * a.shape[2]), F32) for a in wide],
         in_specs=[ANY] * (m + w),
-        out_specs=[pl.BlockSpec(memory_space=pltpu.VMEM)] * m + [ANY] * w,
+        out_specs=[pl.BlockSpec(memory_space=pltpu.VMEM)] * m
+        + [ANY] * (w - laid)
+        + [pl.BlockSpec(memory_space=pltpu.VMEM)] * laid,
         scratch_shapes=scratch,
         compiler_params=pltpu.CompilerParams(
             collective_id=cid, has_side_effects=True, vmem_limit_bytes=(40 << 20) if m else None
@@ -441,6 +452,135 @@
 
 def dot_nt(left, right):
     return lax.dot_general(left, right, (((1,), (1,)), ((), ())), preferred_element_type=F32)
+
+
+def front_kernel(
+    x_ref, cos_ref, sin_ref, gain_ref, lat_gain_ref, wq_ref, wl_ref, we_ref,
+    normed_ref, query_ref, keys_ref, values_ref, latent_ref,
+):
+    blocks, tokens = x_ref.shape[:2]
+    rows = blocks * tokens
+    width = gain_ref.shape[1]
+    x = x_ref[:, :, :width].reshape(rows, width).astype(F32)
+    normed = (x * rms_scale(x) * gain_ref[...]).astype(BF16)
+    normed_ref[...] = normed
+    cos, sin = cos_ref[...], sin_ref[...]
+    own_half = lax.broadcasted_iota(jnp.int32, cos.shape, 1) < ROPE
+
+    def turn(pair):
+        return pair * cos + pltpu.roll(pair, ROPE, 1) * sin
+
+    query = dot_nt(normed, wq_ref[...])
+    query_ref[:, :NOPE] = query[:, :NOPE].astype(BF16)
+    query_ref[:, NOPE:] = jnp.where(own_half, turn(query[:, NOPE:]), 0.0).astype(BF16)
+    compressed = dot(normed, wl_ref[...])
+    raw = compressed[:, :LATENT]
+    latent = (raw * rms_scale(raw) * lat_gain_ref[...]).astype(BF16)
+    latent_ref[...] = latent
+    expanded = dot_nt(latent, we_ref[...])
+    keys_ref[:, :NOPE] = expanded[:, :NOPE].astype(BF16)
+    keys_ref[:, NOPE:] = turn(compressed[:, LATENT:]).astype(BF16)
+    values_ref[...] = expanded[:, NOPE:].astype(BF16)
+
+
+def front(x, cos, sin, gain, lat_gain, wq, wl, we):
+    n, tokens, width = x.shape
+    length = n * tokens
+    blocks = 2
+    rows = blocks * tokens
+
+    def whole(a):
+        return pl.BlockSpec(a.shape, lambda i: (0,) * a.ndim, pipeline_mode=pl.Buffered(1))
+
+    def rows_of(cols):
+        return pl.BlockSpec((rows, cols), lambda i: (i, 0))
+
+    def out(cols):
+        return jax.ShapeDtypeStruct((length, cols), BF16)
+
+    cols = (gain.shape[1], wq.shape[0], NOPE + 2 * ROPE, VH, LATENT)
+    return pl.pallas_call(
+        front_kernel,
+        grid=(n // blocks,),
+        in_specs=[
+            pl.BlockSpec((blocks, tokens, width), lambda i: (i, 0, 0)),
+            rows_of(2 * ROPE),
+            rows_of(2 * ROPE),
+        ]
+        + [whole(a) for a in (gain, lat_gain, wq, wl, we)],
+        out_specs=[rows_of(c) for c in cols],
+        out_shape=[out(c) for c in cols],
+        compiler_params=pltpu.CompilerParams(vmem_limit_bytes=48 << 20),
+        name="front",
+    )(x, cos, sin, gain, lat_gain, wq, wl, we)
+
+
+def back_kernel(
+    x_ref, cos_ref, sin_ref, dq_ref, dk_ref, dv_ref, wq_ref, we_ref,
+    query_ref, expanded_ref, latent_ref, rope_ref, normed_ref, gain_ref,
+):
+    blocks, tokens = x_ref.shape[:2]
+    rows = blocks * tokens
+    width = gain_ref.shape[1]
+    own_half = lax.broadcasted_iota(jnp.int32, cos_ref.shape, 1) < ROPE
+    pair = dq_ref[:, NOPE:] * jnp.where(own_half, cos_ref[...], sin_ref[...])
+    pair = jnp.where(own_half, pair + pltpu.roll(pair, ROPE, 1), 0.0)
+    query_ref[:, :NOPE] = dq_ref[:, :NOPE].astype(BF16)
+    query_ref[:, NOPE:] = pair.astype(BF16)
+    part = dot(query_ref[...], wq_ref[...])
+    normed_ref[...] = part.astype(BF16)
+    x = x_ref[:, :, :width].reshape(rows, width).astype(F32)
+    gain = jnp.sum(part * (x * rms_scale(x)), axis=0, keepdims=True)
+
+    @pl.when(pl.program_id(0) == 0)
+    def _():
+        gain_ref[...] = gain
+
+    @pl.when(pl.program_id(0) > 0)
+    def _():
+        gain_ref[...] += gain
+
+    expanded_ref[:, :NOPE] = dk_ref[:, :NOPE].astype(BF16)
+    expanded_ref[:, NOPE:] = dv_ref[...].astype(BF16)
+    latent_ref[...] = dot(expanded_ref[...], we_ref[...]).astype(BF16)
+    rope_ref[...] = dk_ref[:, NOPE:].astype(BF16)
+
+
+def back(x, cos, sin, dq, dk, dv, wq, we):
+    n, tokens, width = x.shape
+    length = n * tokens
+    blocks = 2
+    rows = blocks * tokens
+    model = wq.shape[1]
+
+    def whole(a):
+        return pl.BlockSpec(a.shape, lambda i: (0,) * a.ndim, pipeline_mode=pl.Buffered(1))
+
+    def rows_of(cols):
+        return pl.BlockSpec((rows, cols), lambda i: (i, 0))
+
+    def out(cols):
+        return jax.ShapeDtypeStruct((length, cols), BF16)
+
+    cols = (NOPE + 2 * ROPE, NOPE + VH, LATENT, 2 * ROPE, model)
+    return pl.pallas_call(
+        back_kernel,
+        grid=(n // blocks,),
+        in_specs=[
+            pl.BlockSpec((blocks, tokens, width), lambda i: (i, 0, 0)),
+            rows_of(2 * ROPE),
+            rows_of(2 * ROPE),
+            rows_of(dq.shape[1]),
+            rows_of(dk.shape[1]),
+            rows_of(dv.shape[1]),
+            whole(wq),
+            whole(we),
+        ],
+        out_specs=[rows_of(c) for c in cols] + [pl.BlockSpec((1, model), lambda i: (0, 0))],
+        out_shape=[out(c) for c in cols] + [jax.ShapeDtypeStruct((1, model), F32)],
+        compiler_params=pltpu.CompilerParams(vmem_limit_bytes=48 << 20),
+        name="back",
+    )(x, cos, sin, dq, dk, dv, wq, we)
 
 
 KEYS = 512
@@ -753,15 +893,16 @@
 def rotary_tables(tokens, n):
     halfway = ROPE // 2
     inverse = 10000.0 ** (-(jnp.arange(halfway, dtype=F32) * 2.0 / ROPE))
-    inverse = jnp.concatenate([inverse, inverse])
-    sign = jnp.where(jnp.arange(ROPE) < halfway, -1.0, 1.0)
+    inverse = jnp.concatenate([inverse] * 4)
+    lane = jnp.arange(2 * ROPE)
+    sign = jnp.where((lane < halfway) | (lane >= 3 * halfway), -1.0, 1.0)
     base = (jnp.arange(n, dtype=F32) * tokens)[:, None] * inverse
     step = jnp.arange(tokens, dtype=F32)[:, None] * inverse
     base_cos, base_sin = jnp.cos(base)[:, None], jnp.sin(base)[:, None]
     step_cos, step_sin = jnp.cos(step)[None], jnp.sin(step)[None]
     cos_table = base_cos * step_cos - base_sin * step_sin
     sin_table = (base_sin * step_cos + base_cos * step_sin) * sign
-    return cos_table.reshape(n * tokens, ROPE), sin_table.reshape(n * tokens, ROPE)
+    return cos_table.reshape(n * tokens, -1), sin_table.reshape(n * tokens, -1)
 
 
 def unrotate(grads, cos_table, sin_table):
@@ -846,7 +987,6 @@
     c0 = D
     c1 = c0 + LATENT + ROPE
     c2 = c1 + n
-    all_input = first_all[:, :, :c0].reshape(length, D)
     latent_w = first_all[:, :, c0:c1].reshape(D, LATENT + ROPE)
     router_w = first_all[:, :, c1:c2].reshape(D, n)
     attn_gain = first_all[:, :, c2].reshape(D).astype(F32)
@@ -875,36 +1015,17 @@
     def own(values):
         return lax.dynamic_slice_in_dim(values, e * tokens, tokens, 0)
 
-    residual_all = all_input.astype(F32)
-    unit_all = residual_all * rms_scale(residual_all)
-    normed = (unit_all * attn_gain).astype(BF16)
     cos_table, sin_table = rotary_tables(tokens, n)
     turned = jnp.concatenate(
         [query_t, query_t[NOPE + ROPE // 2 :], query_t[NOPE : NOPE + ROPE // 2]], axis=0
     )
-    query_raw = product("td,cd->tc", normed, turned)
-    query_r = query_raw[:, NOPE : NOPE + ROPE] * cos_table + query_raw[:, NOPE + ROPE :] * sin_table
-    query = jnp.concatenate(
-        [query_raw[:, :NOPE], query_r, jnp.zeros((length, ROPE), F32)], axis=1
-    ).astype(BF16)
     latent_turned = jnp.concatenate(
         [latent_w, latent_w[:, LATENT + ROPE // 2 :], latent_w[:, LATENT : LATENT + ROPE // 2]],
         axis=1,
     )
-    compressed = product("td,dc->tc", normed, latent_turned)
-    latent_raw = compressed[:, :LATENT]
-    latent = (latent_raw * rms_scale(latent_raw) * lat_gain).astype(BF16)
-    rope_raw, rope_swapped = compressed[:, LATENT : LATENT + ROPE], compressed[:, LATENT + ROPE :]
-    expanded = product("tl,cl->tc", latent, expand_t).astype(BF16)
-    keys = jnp.concatenate(
-        [
-            expanded[:, :NOPE],
-            (rope_raw * cos_table + rope_swapped * sin_table).astype(BF16),
-            (rope_swapped * cos_table - rope_raw * sin_table).astype(BF16),
-        ],
-        axis=1,
-    )
-    values = expanded[:, NOPE:]
+    normed, query, keys, values, latent = front(
+        first_all, cos_table, sin_table, attn_gain[None], lat_gain[None], turned, latent_turned, expand_t
+    )
     attended_head, attended_exact, lse = attend(prefix_length, query, keys, values)
     attended_blocks, shared_blocks = exchange(
         2, swaps=(attended_head.reshape(n, tokens, VH), shared_half)
@@ -966,9 +1087,10 @@
         expert_up[0],
         expert_down[0],
     )
+    ffn_sum, dot_sum = exchange(4, sums=(ffn_partial, dot_partial))
+    out_partial, ffn_sum = lax.optimization_barrier((out_partial, ffn_sum))
     out_sum = lax.psum_scatter(out_partial, "ep", scatter_dimension=0)
     layer_output = (residual_mid + out_sum.astype(F32)).astype(BF16)
-    ffn_sum, dot_sum = exchange(4, sums=(ffn_partial, dot_partial))
 
     def shared_columns(values):
         return values.reshape(length, -1)[:, :shared_width]
@@ -1012,30 +1134,30 @@
     grad_query_raw, grad_keys, grad_values = attend_back(
         prefix_length, query, grad_att, lse, delta, keys, values
     )
-    grad_key_n = grad_keys[:, :NOPE]
-    grad_expanded = jnp.concatenate([grad_key_n, grad_values], axis=1).astype(BF16)
-    latent_partial = product("tc,cl->tl", grad_expanded, expand_t).astype(BF16)
-    grad_key_r = grad_keys[:, NOPE:].astype(BF16)
+    (
+        grad_query,
+        grad_expanded,
+        latent_partial,
+        rope_partial,
+        normed_partial,
+        gain_partial,
+    ) = back(
+        first_all, cos_table, sin_table, grad_query_raw, grad_keys, grad_values, turned, expand_t
+    )
     latent_sum, rope_sum = exchange(
-        6, sums=(latent_partial.reshape(n, tokens, LATENT), grad_key_r.reshape(n, tokens, 128))
-    )
-    grad_query = jnp.concatenate(
-        [
-            grad_query_raw[:, :NOPE],
-            grad_query_raw[:, NOPE : NOPE + ROPE] * cos_table
-            - grad_query_raw[:, NOPE + ROPE :] * sin_table,
-        ],
-        axis=1,
-    ).astype(BF16)
-    normed_partial = product("tc,cd->td", grad_query, query_t)
-    gain_partial = jnp.sum(normed_partial * unit_all, axis=0)
-    normed_partial = normed_partial.astype(BF16).reshape(n, tokens, D)
-    side_query = product_over_groups(normed, grad_query).astype(BF16)
+        6,
+        sums=(
+            latent_partial.reshape(n, tokens, LATENT),
+            rope_partial.reshape(n, tokens, 2 * ROPE),
+        ),
+    )
+    side_query = product_over_groups(normed, grad_query)[:, : query_t.shape[0]].astype(BF16)
     grad_expand = product_over_groups(latent, grad_expanded).astype(BF16)
 
-    own_compressed = own(compressed)
-    latent_scale = rms_scale(own_compressed[:, :LATENT])
-    latent_unit = own_compressed[:, :LATENT] * latent_scale
+    own_normed = (input_unit * attn_gain).astype(BF16)
+    own_raw = product("td,dc->tc", own_normed, latent_w[:, :LATENT])
+    latent_scale = rms_scale(own_raw)
+    latent_unit = own_raw * latent_scale
     grad_latent_gain = jnp.sum(latent_sum * latent_unit, axis=0)
     grad_compressed = jnp.concatenate(
         [
@@ -1043,17 +1165,16 @@
             unrotate(
                 rope_sum[:, :ROPE],
                 own(cos_table)[:, : ROPE // 2],
-                own(sin_table)[:, ROPE // 2 :],
+                own(sin_table)[:, ROPE // 2 : ROPE],
             ),
         ],
         axis=-1,
     ).astype(BF16)
-    own_normed = (input_unit * attn_gain).astype(BF16)
     latent_w_partial = product_over_groups(
         own_normed, jnp.pad(grad_compressed, ((0, 0), (0, 640 - LATENT - ROPE)))
     ).astype(BF16)
     own_part = product("tc,dc->td", grad_compressed, latent_w)
-    grad_attn_gain = gain_partial + jnp.sum(own_part * input_unit, axis=0)
+    grad_attn_gain = gain_partial[0] + jnp.sum(own_part * input_unit, axis=0)
 
     def by_owner(values, rows):
         blocks = values.reshape(-1, groups, n, rows).transpose(2, 1, 0, 3)
@@ -1068,34 +1189,40 @@
         ],
         axis=2,
     )
-    normed_sum, latent_weight_sum, query_all, shared_all, expand_all, small_all = exchange(
+    small = small.transpose(1, 0, 2)
+    if groups == 2:
+        g = lax.axis_index("grp")
+        mine = lax.dynamic_index_in_dim(small, g, 0, keepdims=False)
+        theirs = lax.dynamic_index_in_dim(small, 1 - g, 0, keepdims=False)
+        small = mine + lax.ppermute(theirs, "grp", [(0, 1), (1, 0)])
+    else:
+        small = lax.psum_scatter(small, "grp", scatter_dimension=0)
+    (
+        normed_sum,
+        latent_weight_sum,
+        small_all,
+        query_weight_grad,
+        shared_gate_grad,
+        shared_up_grad,
+        expand_weight_grad,
+    ) = exchange(
         7,
-        sums=(normed_partial, latent_w_partial.reshape(n, rows_out, -1)),
+        sums=(normed_partial.reshape(n, tokens, D), latent_w_partial.reshape(n, rows_out, -1)),
         swaps=(
+            small[:, None],
             side_query.reshape(n, rows_out, -1),
-            side_shared.reshape(n, rows_out, -1),
+            side_shared[:, :shared_width].reshape(n, rows_out, -1),
+            side_shared[:, shared_width:].reshape(n, rows_out, -1),
             grad_expand.reshape(n, expand_rows, -1),
-            small,
         ),
+        laid=4,
     )
     grad_normed = normed_sum + own_part
     input_grad = (
         grad_mid + norm_back(grad_normed * attn_gain, input_unit, input_scale)
     ).astype(BF16)
     latent_weight_grad = latent_weight_sum[:, : LATENT + ROPE]
-    query_weight_grad = query_all.transpose(1, 0, 2).reshape(rows_out, -1).astype(F32)
-    shared_all = shared_all.transpose(1, 0, 2)
-    shared_gate_grad = shared_all[:, :, :shared_width].reshape(rows_out, -1).astype(F32)
-    shared_up_grad = shared_all[:, :, shared_width:].reshape(rows_out, -1).astype(F32)
-    expand_weight_grad = expand_all.transpose(1, 0, 2).reshape(expand_rows, -1).astype(F32)
-    small_sum = jnp.sum(small_all, axis=0)
-    if groups == 2:
-        g = lax.axis_index("grp")
-        mine = lax.dynamic_index_in_dim(small_sum, g, 0, keepdims=False)
-        theirs = lax.dynamic_index_in_dim(small_sum, 1 - g, 0, keepdims=False)
-        small_sum = mine + lax.ppermute(theirs, "grp", [(0, 1), (1, 0)])
-    else:
-        small_sum = lax.psum_scatter(small_sum, "grp", scatter_dimension=0)
+    small_sum = jnp.sum(small_all[:, 0], axis=0)
     attention_gain_grad = small_sum[:rows_out]
     feedforward_gain_grad = small_sum[rows_out : 2 * rows_out]
     router_weight_grad = small_sum[2 * rows_out : (2 + n) * rows_out].reshape(n, rows_out).T

time: 1060 us -> 1000 us (0.943)
  other arithmetic: 70.3 us -> 33.5 us
  waiting for transfers between devices: 1.47 us -> 36.5 us
  Pallas kernels: 741 us -> 723 us
  matrix products: 113 us -> 96.2 us
  local copies, waits for them, and re-layouts: 91.3 us -> 74.8 us
    convert_element_type x6 -> x0, other arithmetic: 24.9 us -> none  [the longest x1 14.8 us: per_device(): (rope_swapped * cos_table - rope_raw * sin_table).astype(BF16)]
    ppermute x4, waiting for transfers between devices: 0.01 us -> 20.3 us  [fold(): got = lax.ppermute(sent, 'ep', [(i, i ^ bit) for i in range(n)])]
    pallas_call x6 -> x8, Pallas kernels: 408 us -> 389 us  [the longest x6 358 us: exchange(): pl.pallas_call(functools.partial(exchange_kernel, n, m, w, laid), out_sha...]
    dot_general x30 -> x26, matrix products: 113 us -> 96.2 us  [product(): return jnp.einsum(form, left, right, preferred_element_type=F32)]
    convert_element_type x9 -> x0, local copies, waits for them, and re-layouts: 16.3 us -> none  [the longest x2 5.54 us: per_device(): shared_all[:, :, :shared_width].reshape(rows_out, -1).astype(F32)]
    ppermute x3, waiting for transfers between devices: 1.36 us -> 16.2 us  [sum_async(): lax.ppermute(sent, 'ep', [(i, (i + 4 * k) % n) for i in range(n)])]
    unnamed x230 -> x181, local copies, waits for them, and re-layouts: 30.2 us -> 33.2 us
  transfers between devices with their start and end apart: 25 -> 25, of which waited for: 1 -> 4; matrix products, arithmetic and copies ran while one was open for 24% -> 17% of each run, Pallas kernels for 62% -> 56%
where the time goes in v4:
time: 1000 us; the launch traced here: 997 us
  Pallas kernels  723 us (72%)
  matrix products  96.2 us (10%)
  local copies, waits for them, and re-layouts  74.8 us (7%)
  waiting for transfers between devices  36.5 us (4%)
  other arithmetic  33.5 us (3%)
  starting transfers between devices  16.1 us (2%)
  between operations  15.9 us (2%)
    pallas_call x6, Pallas kernels, exchange(): pl.pallas_call(functools.partial(exchange_kernel, n, m, w, laid), out_sha...  358 us
    pallas_call x2, Pallas kernels, gather(): pl.pallas_call(functools.partial(gather_kernel, n), out_shape=jax.ShapeDt...  218 us
    dot_general x26, matrix products, product(): return jnp.einsum(form, left, right, preferred_element_type=F32)  96.2 us
    pallas_call x1, Pallas kernels, ffn(): pl.pallas_call(functools.partial(ffn_kernel, n), grid=(n // group,), in_s...  85.9 us
    unnamed x181, local copies, waits for them, and re-layouts  33.2 us
    ppermute x4, waiting for transfers between devices, fold(): got = lax.ppermute(sent, 'ep', [(i, i ^ bit) for i in range(n)])  20.3 us
  transfers between devices with their start and end apart: 25, of which 4 were waited for; matrix products, arithmetic and copies ran while one was open for 17% of the time, Pallas kernels for 56%

profile of v4, /device:TPU:0, one launch (start us, length us, event | category | flops | bytes accessed | tf_op | source)
XLA Modules:
  0.0 996.6 jit_solution(17247490709626589709)
XLA Ops:
  16.2 124.0 %gather.2.x_ref = bf16[16,128,2688]{2,1,0:T(8,128)(2,1)} custom-call(bf16[128,2688]{1,0:T(8,128)(2,1)} %pad.23.x_ref), custom_call_target="tpu_custom_call" | custom-call | tf_op jit(solution)/shard_map/gather/pallas_call | solution.py:163
  142.9 17.5 %exchange.6 = (bf16[16,96,128]{2,1,0:T(8,128)(2,1)}, bf16[16,128,32]{2,1,0:T(8,128)(2,1)}) custom-call(bf16[16,96,128]{2,1,0:T(8,128)(2,1)} %dynamic-slice_bitcast_fusion.2.refs_0_, bf16[16,128,32]{2,1,0:T(8,128)(2,1)} %bitcast.227), custom_call_target="tpu_custom_call" | custom-call | tf_op jit(solution)/shard_map/exchange/pallas_call | solution.py:367
  164.4 3.7 slice.104
  182.5 17.7 %front.1 = (bf16[2048,2048]{1,0:T(8,128)(2,1)}, bf16[2048,256]{1,0:T(8,128)(2,1)S(1)}, bf16[2048,256]{1,0:T(8,128)(2,1)S(1)}, bf16[2048,128]{1,0:T(8,128)(2,1)S(1)}, bf16[2048,512]{1,0:T(8,128)(2,1)}) custom-call(bf16[16,128,2688]{2,1,0:T(8,128)(2,1)} %gather.2.x_ref, f32[2048,128]{1,0:T(8,128)S(1)} %bitcast.182, ...), custom_call_target="tpu_custom_call" | custom-call | tf_op jit(solution)/shard_map/front/pallas_call | solution.py:502
  204.9 13.8 %attend.1 = (bf16[2048,128]{1,0:T(8,128)(2,1)S(1)}, f32[2048,128]{1,0:T(8,128)S(1)}, f32[1,2048]{1,0:T(1,128)S(1)}) custom-call(s32[1]{0:T(128)S(6)} %copy.115.prefix_ref, bf16[2048,256]{1,0:T(8,128)(2,1)S(1)} %copy-done.6, bf16[4,512,256]{2,1,0:T(8,128)(2,1)S(1)} %bitcast.188, bf16[4,128,512]{2,1,0:T(8,128)(2,1)S(1)} %copy.67.v_ref), custom_call_target="tpu_custom_call" | custom-call | tf_op jit(solution)/shard_map/attend/pallas_call | solution.py:637
  220.5 52.6 %exchange.7 = (bf16[16,128,128]{2,1,0:T(8,128)(2,1)}, bf16[16,176,128]{2,1,0:T(8,128)(2,1)}) custom-call(bf16[16,128,128]{2,1,0:T(8,128)(2,1)} %bitcast.201, bf16[16,176,128]{2,1,0:T(8,128)(2,1)} %bitcast.226), custom_call_target="tpu_custom_call" | custom-call | tf_op jit(solution)/shard_map/exchange/pallas_call | solution.py:367
  293.0 94.4 %gather.3.x_ref = bf16[16,128,2048]{2,1,0:T(8,128)(2,1)} custom-call(bf16[128,2048]{1,0:T(8,128)(2,1)} %multiply_convert_fusion.x_ref), custom_call_target="tpu_custom_call" | custom-call | tf_op jit(solution)/shard_map/gather/pallas_call | solution.py:163
  390.7 85.9 %ffn.1 = (bf16[16,128,2048]{2,1,0:T(8,128)(2,1)}, bf16[16,128,2048]{2,1,0:T(8,128)(2,1)}, bf16[16,128,128]{2,1,0:T(8,128)(2,1)}, f32[16,128,128]{2,1,0:T(8,128)}...) custom-call(bf16[16,128,2048]{2,1,0:T(8,128)(2,1)} %gather.3.x_ref, ...), custom_call_target="tpu_custom_call" | custom-call | tf_op jit(solution)/shard_map/ffn/pallas_call | solution.py:838
  481.0 80.4 %exchange.8 = (f32[128,2048]{1,0:T(8,128)S(1)}, f32[128,128]{1,0:T(8,128)S(1)}) custom-call(bf16[4,2,2,128,2048]{4,3,2,1,0:T(8,128)(2,1)S(1)} %bitcast.185, bf16[4,2,2,128,128]{4,3,2,1,0:T(8,128)(2,1)S(1)} %bitcast.199), custom_call_target="tpu_custom_call" | custom-call | tf_op jit(solution)/shard_map/exchange/pallas_call | solution.py:367
  569.2 4.8 fusion.23
  574.6 5.4 convolution_convert_fusion.4
  580.8 4.8 convolution_convert_fusion.1
  585.6 4.9 convolution_convert_fusion
  590.9 5.1 convolution_convert_fusion.3
  597.6 4.6 fusion.8
  605.2 6.2 add_convert_fusion.3
  611.4 4.4 collective-permute-start.18
  615.8 4.2 add_convert_fusion.2
  625.6 9.5 add_bitcast_fusion.2
  635.1 7.3 add_bitcast_fusion.1
  642.4 6.8 add_bitcast_fusion
  649.2 5.4 add_convert_fusion
  658.8 37.9 %exchange.9 = bf16[16,128,128]{2,1,0:T(8,128)(2,1)} custom-call(bf16[16,128,128]{2,1,0:T(8,128)(2,1)} %bitcast.229), custom_call_target="tpu_custom_call" | custom-call | tf_op jit(solution)/shard_map/exchange/pallas_call | solution.py:367
  701.7 16.5 %attend_back.1 = (f32[2048,256]{1,0:T(8,128)S(1)}, f32[4,512,256]{2,1,0:T(8,128)S(1)}, f32[4,512,128]{2,1,0:T(8,128)S(1)}) custom-call(s32[1]{0:T(128)S(6)} %copy.115.prefix_ref, bf16[2048,256]{1,0:T(8,128)(2,1)S(1)} %copy-done.7, bf16[2048,128]{1,0:T(8,128)(2,1)S(1)} %bitcast.187, f32[1,2048]{1,0:T(1,128)S(1)} %get-tuple-element.93.lse_ref, ...), custom_call_target="tpu_custom_call" | custom-call | tf_op jit(solution)/shard_map/attend_back/pallas_call | solution.py:695
  720.9 13.5 %back.1 = (bf16[2048,256]{1,0:T(8,128)(2,1)S(1)}, bf16[2048,256]{1,0:T(8,128)(2,1)S(1)}, bf16[2048,512]{1,0:T(8,128)(2,1)}, bf16[2048,128]{1,0:T(8,128)(2,1)S(1)...) custom-call(bf16[16,128,2688]{2,1,0:T(8,128)(2,1)} %gather.2.x_ref, f32[2048,128]{1,0:T(8,128)S(1)} %bitcast.183, ...), custom_call_target="tpu_custom_call" | custom-call | tf_op jit(solution)/shard_map/back/pallas_call | solution.py:566
  736.4 55.9 %exchange.10 = (f32[128,512]{1,0:T(8,128)S(1)}, f32[128,128]{1,0:T(8,128)S(1)}) custom-call(bf16[4,2,2,128,512]{4,3,2,1,0:T(8,128)(2,1)S(1)} %bitcast.194, bf16[4,2,2,128,128]{4,3,2,1,0:T(8,128)(2,1)S(1)} %bitcast.200), custom_call_target="tpu_custom_call" | custom-call | tf_op jit(solution)/shard_map/exchange/pallas_call | solution.py:367
  795.7 3.8 fusion.30
  814.5 17.8 %collective-permute-done.10 = bf16[4,2,32,2048]{3,2,0,1:T(8,128)(2,1)} collective-permute-done((bf16[4,2,32,2048]{3,2,0,1:T(8,128)(2,1)}, bf16[4,2,32,2048]{3,2,0,1:T(8,128)(2,1)}, u32[]{:S(2)}, u32[]{:S(2)}) %collective-permute-start.10) | collective-permute-done | bytes 1048608 | tf_op jit(solution)/shard_map/ppermute | solution.py:436
  842.5 113.4 %exchange.11 = (f32[128,2048]{1,0:T(8,128)S(1)}, f32[64,640]{1,0:T(8,128)S(1)}, f32[16,1,1168]{2,1,0:T(1,128)S(1)}, f32[64,3072]{1,0:T(8,128)S(1)}, f32[64,2816]...) custom-call(bf16[4,2,2,128,2048]{4,3,2,1,0:T(8,128)(2,1)} %bitcast.220, ...), custom_call_target="tpu_custom_call" | custom-call | tf_op jit(solution)/shard_map/exchange/pallas_call | solution.py:367
  963.9 4.8 collective-permute-done.16
  968.7 11.3 %collective-permute-done.15 = bf16[64,2048]{1,0:T(8,128)(2,1)} collective-permute-done((bf16[64,2048]{1,0:T(8,128)(2,1)}, bf16[64,2048]{1,0:T(8,128)(2,1)}, u32[]{:S(2)}, u32[]{:S(2)}) %collective-permute-start.15) | collective-permute-done | bytes 262176 | tf_op jit(solution)/shard_map/ppermute | solution.py:445
  982.1 3.7 fusion.35
  (354 shorter events, 138.7 us)
Async XLA Ops:
  7.2 167.8 %all-gather.3.cloned.1.call-start = ((), (), s32[]{:S(2)}) async-start(), calls=%async_computation.1 | async-start | bytes 4456448 | tf_op jit(solution)/shard_map/all_gather | solution.py:1011
  9.0 381.7 %all-gather.5.cloned.1.call-start = ((), (), s32[]{:S(2)}) async-start(), calls=%async_computation.2 | async-start | bytes 8912896 | tf_op jit(solution)/shard_map/all_gather | solution.py:1013
  16.2 124.0 %copy-start.58 = (bf16[128,3072]{1,0:T(8,128)(2,1)S(1)}, bf16[128,3072]{1,0:T(8,128)(2,1)}, u32[]{:S(2)}) copy-start(bf16[128,3072]{1,0:T(8,128)(2,1)} %param.20) | copy-start | bytes 2359300
  16.2 124.4 %copy-start.66 = (bf16[32,4096]{1,0:T(8,128)(2,1)S(1)}, bf16[32,4096]{1,0:T(8,128)(2,1)}, u32[]{:S(2)}) copy-start(bf16[32,4096]{1,0:T(8,128)(2,1)} %param.23) | copy-start | bytes 786436
  160.4 821.7 %reduce-scatter.2.cloned.1.call-start = ((), (), s32[]{:S(2)}) async-start(), calls=%async_computation.3 | async-start | bytes 8912896 | tf_op jit(solution)/shard_map/reduce_scatter | solution.py:1092
  162.4 18.8 %collective-permute-start = (bf16[96,2048]{1,0:T(8,128)(2,1)}, bf16[96,2048]{1,0:T(8,128)(2,1)}, u32[]{:S(2)}, u32[]{:S(2)}) collective-permute-start(bf16[96,2048]{1,0:T(8,128)(2,1)} %copy_bitcast_fusion.5), channel_id=1, source_target_pairs={{0,16},{16,0},{1,17},{17,1},{2,18},{18,2},{3,19},{19,3},{4,20},{20... | collective-permute-start | bytes 1179656 | tf_op jit(solution)/shard_map/ppermute | solution.py:415
  163.8 17.4 %collective-permute-start.1 = (bf16[128,512]{1,0:T(8,128)(2,1)S(1)}, bf16[128,512]{1,0:T(8,128)(2,1)S(1)}, u32[]{:S(2)}, u32[]{:S(2)}) collective-permute-start(bf16[128,512]{1,0:T(8,128)(2,1)S(1)} %copy.65), channel_id=1, source_target_pairs={{0,16},{16,0},{1,17},{17,1},{2,18},{18,2},{3,19},{19,3},{4,20},{20... | collective-permute-start | bytes 393224 | tf_op jit(solution)/shard_map/ppermute | solution.py:415
  175.0 112.6 %collective-permute-start.2 = (bf16[2048,1024]{1,0:T(8,128)(2,1)}, bf16[2048,1024]{1,0:T(8,128)(2,1)}, u32[]{:S(2)}, u32[]{:S(2)}) collective-permute-start(bf16[2048,1024]{1,0:T(8,128)(2,1)} %all-gather.3.cloned.1.call-done), channel_id=1, source_target_pairs={{0,16},{16,0},{1,17},{17,1},{2,18},{18,2},{3,19},{19,3},{4,20},{20... | collective-permute-start | bytes 12582920 | tf_op jit(solution)/shard_map/ppermute | solution.py:415
  175.1 620.6 %copy-start.67 = (f32[128]{0:T(128)}, f32[128]{0:T(128)S(1)}, u32[]{:S(2)}) copy-start(f32[128]{0:T(128)S(1)} %add_rsqrt_fusion.1) | copy-start | bytes 1540
  275.3 7.5 collective-permute-start.3
  291.0 273.6 %copy-start.69 = (f32[128]{0:T(128)}, f32[128]{0:T(128)S(1)}, u32[]{:S(2)}) copy-start(f32[128]{0:T(128)S(1)} %add_rsqrt_fusion.2) | copy-start | bytes 1540
  569.2 80.0 %collective-permute-start.4 = (bf16[1024,2048]{1,0:T(8,128)(2,1)}, bf16[1024,2048]{1,0:T(8,128)(2,1)}, u32[]{:S(2)}, u32[]{:S(2)}) collective-permute-start(bf16[1024,2048]{1,0:T(8,128)(2,1)} %convolution_convert_fusion.2), channel_id=1, source_target_pairs={{0,16},{16,0},{1,17},{17,1},{2,18},{18,2},{3,19},{19,3},{4,20},{20... | collective-permute-start | bytes 12582920 | tf_op jit(solution)/shard_map/ppermute | solution.py:409
  574.1 37.3 %collective-permute-start.8 = (bf16[1024,352]{0,1:T(8,128)(2,1)}, bf16[1024,352]{0,1:T(8,128)(2,1)}, u32[]{:S(2)}, u32[]{:S(2)}) collective-permute-start(bf16[1024,352]{0,1:T(8,128)(2,1)} %fusion.23), channel_id=1, source_target_pairs={{0,16},{16,0},{1,17},{17,1},{2,18},{18,2},{3,19},{19,3},{4,20},{20... | collective-permute-start | bytes 2162696 | tf_op jit(solution)/shard_map/ppermute | solution.py:409
  580.1 22.2 %collective-permute-start.17 = (bf16[88,2048]{1,0:T(8,128)(2,1)S(1)}, bf16[88,2048]{1,0:T(8,128)(2,1)S(1)}, u32[]{:S(2)}, u32[]{:S(2)}) collective-permute-start(bf16[88,2048]{1,0:T(8,128)(2,1)S(1)} %convolution_convert_fusion.4), channel_id=1, source_target_pairs={{0,16},{16,0},{1,17},{17,1},{2,18},{18,2},{3,19},{19,3},{4,20},{20... | collective-permute-start | bytes 1081352 | tf_op jit(solution)/shard_map/ppermute | solution.py:409
  585.6 40.1 %collective-permute-start.19 = (bf16[1024,1408]{1,0:T(8,128)(2,1)}, bf16[1024,1408]{1,0:T(8,128)(2,1)}, u32[]{:S(2)}, u32[]{:S(2)}) collective-permute-start(bf16[1024,1408]{1,0:T(8,128)(2,1)} %convolution_convert_fusion.1), channel_id=1, source_target_pairs={{0,16},{16,0},{1,17},{17,1},{2,18},{18,2},{3,19},{19,3},{4,20},{20... | collective-permute-start | bytes 8650760 | tf_op jit(solution)/shard_map/ppermute | solution.py:409
  590.4 44.7 %collective-permute-start.20 = (bf16[1024,1408]{1,0:T(8,128)(2,1)}, bf16[1024,1408]{1,0:T(8,128)(2,1)}, u32[]{:S(2)}, u32[]{:S(2)}) collective-permute-start(bf16[1024,1408]{1,0:T(8,128)(2,1)} %convolution_convert_fusion), channel_id=1, source_target_pairs={{0,16},{16,0},{1,17},{17,1},{2,18},{18,2},{3,19},{19,3},{4,20},{20... | collective-permute-start | bytes 8650760 | tf_op jit(solution)/shard_map/ppermute | solution.py:409
  602.2 40.2 %collective-permute-start.21 = (bf16[704,2048]{1,0:T(8,128)(2,1)}, bf16[704,2048]{1,0:T(8,128)(2,1)}, u32[]{:S(2)}, u32[]{:S(2)}) collective-permute-start(bf16[704,2048]{1,0:T(8,128)(2,1)} %convolution_convert_fusion.3), channel_id=1, source_target_pairs={{0,16},{16,0},{1,17},{17,1},{2,18},{18,2},{3,19},{19,3},{4,20},{20... | collective-permute-start | bytes 8650760 | tf_op jit(solution)/shard_map/ppermute | solution.py:409
  611.4 12.3 %collective-permute-start.18 = (bf16[88,2048]{1,0:T(8,128)(2,1)}, bf16[88,2048]{1,0:T(8,128)(2,1)}, u32[]{:S(2)}, u32[]{:S(2)}) collective-permute-start(bf16[88,2048]{1,0:T(8,128)(2,1)} %add_convert_fusion.3), channel_id=1, source_target_pairs={{0,0},{1,2},{2,4},{3,6},{4,8},{5,10},{6,12},{7,14},{8,16},{9,18},{... | collective-permute-start | bytes 1081352 | tf_op jit(solution)/shard_map/ppermute | solution.py:421
  794.4 46.2 %collective-permute-start.5 = (bf16[1024,640]{1,0:T(8,128)(2,1)}, bf16[1024,640]{1,0:T(8,128)(2,1)}, u32[]{:S(2)}, u32[]{:S(2)}) collective-permute-start(bf16[1024,640]{1,0:T(8,128)(2,1)} %convolution_convert_fusion.5), channel_id=1, source_target_pairs={{0,16},{16,0},{1,17},{17,1},{2,18},{18,2},{3,19},{19,3},{4,20},{20... | collective-permute-start | bytes 3932168 | tf_op jit(solution)/shard_map/ppermute | solution.py:409
  799.7 11.7 %collective-permute-start.6 = (f32[16,1168]{1,0:T(8,128)S(1)}, f32[16,1168]{1,0:T(8,128)S(1)}, u32[]{:S(2)}, u32[]{:S(2)}) collective-permute-start(f32[16,1168]{1,0:T(8,128)S(1)} %dynamic-slice_bitcast_fusion.3), channel_id=1, source_target_pairs={{0,16},{16,0},{1,17},{17,1},{2,18},{18,2},{3,19},{19,3},{4,20},{20... | collective-permute-start | bytes 224264 | tf_op jit(solution)/shard_map/ppermute | solution.py:1197
  804.0 10.3 %collective-permute-start.7 = (bf16[1024,256]{0,1:T(8,128)(2,1)S(1)}, bf16[1024,256]{0,1:T(8,128)(2,1)S(1)}, u32[]{:S(2)}, u32[]{:S(2)}) collective-permute-start(bf16[1024,256]{0,1:T(8,128)(2,1)S(1)} %fusion.26), channel_id=1, source_target_pairs={{0,16},{16,0},{1,17},{17,1},{2,18},{18,2},{3,19},{19,3},{4,20},{20... | collective-permute-start | bytes 1572872 | tf_op jit(solution)/shard_map/ppermute | solution.py:409
  804.6 9.2 collective-permute-start.9
  807.0 25.4 %collective-permute-start.10 = (bf16[4,2,32,2048]{3,2,0,1:T(8,128)(2,1)}, bf16[4,2,32,2048]{3,2,0,1:T(8,128)(2,1)}, u32[]{:S(2)}, u32[]{:S(2)}) collective-permute-start(bf16[4,2,32,2048]{3,2,0,1:T(8,128)(2,1)} %bitcast.177), channel_id=1, source_target_pairs={{0,2},{1,3},{2,0},{3,1},{4,6},{5,7},{6,4},{7,5},{8,10},{9,11},{10,... | collective-permute-start | bytes 3145736 | tf_op jit(solution)/shard_map/ppermute | solution.py:436
  811.4 26.2 %collective-permute-start.12 = (bf16[4,2,32,2048]{3,2,0,1:T(8,128)(2,1)}, bf16[4,2,32,2048]{3,2,0,1:T(8,128)(2,1)}, u32[]{:S(2)}, u32[]{:S(2)}) collective-permute-start(bf16[4,2,32,2048]{3,2,0,1:T(8,128)(2,1)} %bitcast.176), channel_id=1, source_target_pairs={{0,1},{1,0},{2,3},{3,2},{4,5},{5,4},{6,7},{7,6},{8,9},{9,8},{10,11... | collective-permute-start | bytes 3145736 | tf_op jit(solution)/shard_map/ppermute | solution.py:436
  834.1 122.3 %collective-permute-start.11 = (bf16[4,32,2048]{2,1,0:T(8,128)(2,1)S(1)}, bf16[4,32,2048]{2,1,0:T(8,128)(2,1)S(1)}, u32[]{:S(2)}, u32[]{:S(2)}) collective-permute-start(bf16[4,32,2048]{2,1,0:T(8,128)(2,1)S(1)} %dynamic-slice_bitcast_fusion.1), channel_id=1, source_target_pairs={{0,1},{1,0},{2,3},{3,2},{4,5},{5,4},{6,7},{7,6},{8,9},{9,8},{10,11... | collective-permute-start | bytes 1572872 | tf_op jit(solution)/shard_map/ppermute | solution.py:436
  839.4 117.1 %collective-permute-start.13 = (bf16[4,32,2048]{2,1,0:T(8,128)(2,1)S(1)}, bf16[4,32,2048]{2,1,0:T(8,128)(2,1)S(1)}, u32[]{:S(2)}, u32[]{:S(2)}) collective-permute-start(bf16[4,32,2048]{2,1,0:T(8,128)(2,1)S(1)} %dynamic-slice_bitcast_fusion), channel_id=1, source_target_pairs={{0,2},{1,3},{2,0},{3,1},{4,6},{5,7},{6,4},{7,5},{8,10},{9,11},{10,... | collective-permute-start | bytes 1572872 | tf_op jit(solution)/shard_map/ppermute | solution.py:436
  842.5 113.5 %copy-start.33 = (bf16[128,2048]{1,0:T(8,128)(2,1)S(1)}, bf16[128,2048]{1,0:T(8,128)(2,1)}, u32[]{:S(2)}) copy-start(bf16[128,2048]{1,0:T(8,128)(2,1)} %param.18) | copy-start | bytes 1572868
  842.5 113.5 %copy-start.38 = (f32[128,2048]{1,0:T(8,128)S(1)}, f32[128,2048]{1,0:T(8,128)}, u32[]{:S(2)}) copy-start(f32[128,2048]{1,0:T(8,128)} %get-tuple-element.172) | copy-start | bytes 3145732
  842.5 113.5 %copy-start.68 = (f32[128]{0:T(128)S(1)}, f32[128]{0:T(128)}, u32[]{:S(2)}) copy-start(f32[128]{0:T(128)} %copy-done.67) | copy-start | bytes 1540
  958.1 10.6 %collective-permute-start.16 = (bf16[64,2048]{1,0:T(8,128)(2,1)}, bf16[64,2048]{1,0:T(8,128)(2,1)}, u32[]{:S(2)}, u32[]{:S(2)}) collective-permute-start(bf16[64,2048]{1,0:T(8,128)(2,1)} %get-tuple-element.146), channel_id=1, source_target_pairs={{0,12},{1,13},{2,14},{3,15},{4,0},{5,1},{6,2},{7,3},{8,4},{9,5},{1... | collective-permute-start | bytes 786440 | tf_op jit(solution)/shard_map/ppermute | solution.py:445
  960.3 19.7 %collective-permute-start.15 = (bf16[64,2048]{1,0:T(8,128)(2,1)}, bf16[64,2048]{1,0:T(8,128)(2,1)}, u32[]{:S(2)}, u32[]{:S(2)}) collective-permute-start(bf16[64,2048]{1,0:T(8,128)(2,1)} %get-tuple-element.145), channel_id=1, source_target_pairs={{0,8},{1,9},{2,10},{3,11},{4,12},{5,13},{6,14},{7,15},{8,0},{9,1},... | collective-permute-start | bytes 786440 | tf_op jit(solution)/shard_map/ppermute | solution.py:445
  960.9 19.1 %collective-permute-start.14 = (bf16[64,2048]{1,0:T(8,128)(2,1)}, bf16[64,2048]{1,0:T(8,128)(2,1)}, u32[]{:S(2)}, u32[]{:S(2)}) collective-permute-start(bf16[64,2048]{1,0:T(8,128)(2,1)} %get-tuple-element.144), channel_id=1, source_target_pairs={{0,4},{1,5},{2,6},{3,7},{4,8},{5,9},{6,10},{7,11},{8,12},{9,13},{1... | collective-permute-start | bytes 786440 | tf_op jit(solution)/shard_map/ppermute | solution.py:445
  (78 other events, 872.2 us)
Sparse Core Ops, SparseCore 0:
  11.4 105.9 all-gather.2
  160.6 143.3 all-gather.4
  574.7 209.5 reduce-scatter.1

commit v5 on v4

--- a/solution.py
+++ b/solution.py
@@ -56,23 +56,63 @@
         pl.when(z + 1 + s < nz)(functools.partial(above, s, z + 1 + s))
 
 
-def gather_kernel(n, x_ref, o_ref, own, us, ur, ds, dr, xs, xr, ys, yr):
+def greet_near(px, py, up, down, z, nz):
+    barrier = pltpu.get_barrier_semaphore()
+    for peer, there in ((px, None), (py, None), (up, z + 1 < nz), (down, z > 0)):
+
+        def hello(peer=peer):
+            pl.semaphore_signal(barrier, inc=1, device_id={"ep": peer}, device_id_type=MESH)
+
+        hello() if there is None else pl.when(there)(hello)
+    on_line = (z + 1 < nz).astype(jnp.int32) + (z > 0).astype(jnp.int32)
+    pl.semaphore_wait(barrier, 2 + on_line)
+
+
+def start_swaps(n, ins, outs, sems):
+    own, ss, rs = sems
+    me = lax.axis_index("ep")
+    sends, copies = [], []
+    for j in range(len(ins)):
+        local = pltpu.make_async_copy(ins[j].at[me], outs[j].at[me], own.at[j])
+        local.start()
+        copies.append(local)
+    for k in range(1, n):
+        to = (me + k) % n
+        for j in range(len(ins)):
+            c = remote(ins[j].at[to], outs[j].at[me], ss.at[j, k], rs.at[j, k], to)
+            c.start()
+            sends.append(c)
+    return sends, copies
+
+
+def end_swaps(n, ins, outs, sems, started):
+    own, ss, rs = sems
+    me = lax.axis_index("ep")
+    sends, copies = started
+    for k in range(1, n):
+        to, back = (me + k) % n, (me + n - k) % n
+        for j in range(len(ins)):
+            remote(ins[j].at[back], outs[j].at[back], ss.at[j, k], rs.at[j, k], to).wait_recv()
+    for copy in sends:
+        copy.wait_send()
+    for copy in copies:
+        copy.wait()
+
+
+def gather_kernel(n, w, x_ref, *refs):
+    swaps_in, o_ref, swaps_out = refs[:w], refs[w], refs[w + 1 : 2 * w + 1]
+    own, us, ur, ds, dr, xs, xr, ys, yr, *swap_sems = refs[2 * w + 1 :]
     me, z, y, x, px, py = around(n)
     nz = n // 4
     low = me % 4
     half = x_ref.shape[0] // 2
     top, bottom = pl.ds(0, half), pl.ds(half, half)
     up, down = (me + 4) % n, (me + n - 4) % n
-    barrier = pltpu.get_barrier_semaphore()
-    greeted = [(px, None), (py, None), (up, z + 1 < nz), (down, z > 0)]
-    for peer, there in greeted:
-
-        def hello(peer=peer):
-            pl.semaphore_signal(barrier, inc=1, device_id={"ep": peer}, device_id_type=MESH)
-
-        hello() if there is None else pl.when(there)(hello)
-    on_line = (z + 1 < nz).astype(jnp.int32) + (z > 0).astype(jnp.int32)
-    pl.semaphore_wait(barrier, 2 + on_line)
+    everyone = [(me + k) % n for k in range(n)]
+    if w:
+        greet(everyone[1:])
+    else:
+        greet_near(px, py, up, down, z, nz)
     local = pltpu.make_async_copy(x_ref, o_ref.at[me], own)
     local.start()
 
@@ -98,6 +138,7 @@
     pl.when(z + 1 < nz)(lambda: upward(x_ref, me, 0).start())
     pl.when(z > 0)(lambda: downward(x_ref, me, 0).start())
     spread(x_ref, z)
+    swapping = start_swaps(n, swaps_in, swaps_out, swap_sems) if w else None
 
     def from_below(s, t):
         b = t * 4 + low
@@ -155,20 +196,27 @@
         pl.when((z + 1 < nz) & (z - s >= 0))(functools.partial(sent_up, s, z))
         pl.when((z > 0) & (z + s < nz))(functools.partial(sent_down, s, z))
     local.wait()
-
-
-def gather(x, cid):
+    if w:
+        end_swaps(n, swaps_in, swaps_out, swap_sems, swapping)
+
+
+def gather(x, cid, swaps=()):
     n = lax.axis_size("ep")
+    w = len(swaps)
     nz = n // 4
     return pl.pallas_call(
-        functools.partial(gather_kernel, n),
-        out_shape=jax.ShapeDtypeStruct((n,) + x.shape, x.dtype),
-        in_specs=[ANY],
-        out_specs=ANY,
-        scratch_shapes=[DMA] + [DMA((nz,))] * 4 + [DMA((3 * nz,))] * 4,
+        functools.partial(gather_kernel, n, w),
+        out_shape=[jax.ShapeDtypeStruct((n,) + x.shape, x.dtype)]
+        + [jax.ShapeDtypeStruct(a.shape, a.dtype) for a in swaps],
+        in_specs=[ANY] * (1 + w),
+        out_specs=[ANY] * (1 + w),
+        scratch_shapes=[DMA]
+        + [DMA((nz,))] * 4
+        + [DMA((3 * nz,))] * 4
+        + ([DMA((w,)), DMA((w, n)), DMA((w, n))] if w else []),
         compiler_params=pltpu.CompilerParams(collective_id=cid, has_side_effects=True),
         name="gather",
-    )(x)
+    )(x, *swaps)
 
 
 def add_rows(dst, left, right, rows):
@@ -182,7 +230,10 @@
     lax.fori_loop(0, rows // step, body, 0)
 
 
-def exchange_kernel(n, m, w, laid, *refs):
+TILE = 128
+
+
+def exchange_kernel(n, m, w, laid, jobs, *refs):
     refs = list(refs)
 
     def take(count):
@@ -191,25 +242,25 @@
         return out
 
     sums_in, swaps_in = take(m), take(w)
-    sums_out, swaps_out = take(m), take(w)
+    jobs_in = [take(2) for _ in range(jobs)]
+    sums_out, swaps_out, jobs_out = take(m), take(w), take(jobs)
     room = [take(7) for _ in range(m)]
     sems = [take(8) for _ in range(m)]
     swap_sems = take(3) if w else None
     side_by_side = swaps_out[w - laid :]
     swaps_out = swaps_out[: w - laid] + take(laid)
+    desks = [take(5) for _ in range(jobs)]
     me, z, y, x, px, py = around(n)
     nz = n // 4
     low = me % 4
     to = [(z + k) % nz for k in range(nz)]
     at = [t * 4 + low for t in to]
-    everyone = [(me + k) % n for k in range(n)]
-    back = [(me + n - k) % n for k in range(n)]
     if w:
-        greet(everyone[1:])
+        greet([(me + k) % n for k in range(1, n)])
     else:
         greet([px, py] + at[1:])
     order = [2, 1, 3, 0] if nz == 4 else list(range(1, nz)) + [0]
-    sends, copies = [], []
+    sends = []
 
     def halves(j):
         half = sums_in[j].shape[3] // 2
@@ -272,50 +323,64 @@
             third[j, k] = (c, d)
             sends.extend([c, d])
 
-    def start_swaps():
-        own, ss, rs = swap_sems
-        for j in range(w):
-            local = pltpu.make_async_copy(swaps_in[j].at[me], swaps_out[j].at[me], own.at[j])
-            local.start()
-            copies.append(local)
-        for k in range(1, n):
-            for j in range(w):
-                c = remote(
-                    swaps_in[j].at[everyone[k]],
-                    swaps_out[j].at[me],
-                    ss.at[j, k],
-                    rs.at[j, k],
-                    everyone[k],
-                )
-                c.start()
-                sends.append(c)
+    loads = []
+    for (left, right), (left_v, right_v, page, in_sem, out_sem) in zip(jobs_in, desks):
+        for i, (src, dst) in enumerate(((left, left_v), (right, right_v))):
+            loads.append(pltpu.make_async_copy(src, dst, in_sem.at[i]))
+
+    def tile(j, i):
+        left_v, right_v, page, in_sem, out_sem = desks[j]
+        slot = i % 2
+        write = pltpu.make_async_copy(
+            page.at[slot],
+            jobs_out[j].at[pl.ds(pl.multiple_of(i * TILE, TILE), TILE)],
+            out_sem.at[slot],
+        )
+        value = lax.dot_general(
+            left_v[:, pl.ds(pl.multiple_of(i * TILE, TILE), TILE)],
+            right_v[...],
+            (((0,), (0,)), ((), ())),
+            preferred_element_type=F32,
+        )
+        pl.when(i >= 2)(write.wait)
+        page[slot] = value.astype(page.dtype)
+        write.start()
+
+    tiles = [desk[0].shape[1] // TILE for desk in desks]
+    loaded = []
+
+    def work(step, of):
+        first, last = sum(tiles) * step // of, sum(tiles) * (step + 1) // of
+        for j in range(jobs):
+            start = sum(tiles[:j])
+            low, high = max(first - start, 0), min(last - start, tiles[j])
+            if low >= high:
+                continue
+            if j not in loaded:
+                loaded.append(j)
+                loads[2 * j].wait()
+                loads[2 * j + 1].wait()
+            lax.fori_loop(low, high, lambda i, c, j=j: (tile(j, i), c)[1], 0)
 
     steps = [(j, k) for j in range(m) for k in order]
-    for i in range(min(2, len(steps))):
+    ahead = 3 if jobs else 2
+    for i in range(min(ahead, len(steps))):
         stage_one(*steps[i])
+    for copy in loads:
+        copy.start()
     if w:
-        start_swaps()
+        swapping = start_swaps(n, swaps_in, swaps_out, swap_sems)
     for i, step in enumerate(steps):
         stage_two(*step)
-        if i + 2 < len(steps):
-            stage_one(*steps[i + 2])
+        if i + ahead < len(steps):
+            stage_one(*steps[i + ahead])
         if i:
             stage_three(*steps[i - 1])
+        work(i, len(steps))
     if steps:
         stage_three(*steps[-1])
     if w:
-        own, ss, rs = swap_sems
-        for k in range(1, n):
-            for j in range(w):
-                remote(
-                    swaps_in[j].at[back[k]],
-                    swaps_out[j].at[back[k]],
-                    ss.at[j, k],
-                    rs.at[j, k],
-                    everyone[k],
-                ).wait_recv()
-        for copy in copies:
-            copy.wait()
+        end_swaps(n, swaps_in, swaps_out, swap_sems, swapping)
         for wide, got in zip(side_by_side, swaps_out[w - laid :]):
             width = got.shape[2]
             for k in range(n):
@@ -342,9 +407,14 @@
             lax.fori_loop(0, half // 16, body, 0)
     for copy in sends:
         copy.wait_send()
-
-
-def exchange(cid, sums=(), swaps=(), laid=0):
+    for j in range(jobs):
+        left_v, right_v, page, in_sem, out_sem = desks[j]
+        for slot in range(2):
+            rows = jobs_out[j].at[pl.ds(0, TILE)]
+            pltpu.make_async_copy(page.at[slot], rows, out_sem.at[slot]).wait()
+
+
+def exchange(cid, sums=(), swaps=(), laid=0, jobs=()):
     n = lax.axis_size("ep")
     nz = n // 4
     m, w = len(sums), len(swaps)
@@ -364,21 +434,26 @@
         scratch += [DMA((w,)), DMA((w, n)), DMA((w, n))]
     plain, wide = swaps[: w - laid], swaps[w - laid :]
     scratch += [pltpu.VMEM(a.shape, a.dtype) for a in wide]
+    for left, right in jobs:
+        scratch += [pltpu.VMEM(left.shape, left.dtype), pltpu.VMEM(right.shape, right.dtype)]
+        scratch += [pltpu.VMEM((2, TILE, right.shape[1]), BF16), DMA((2,)), DMA((2,))]
     out = pl.pallas_call(
-        functools.partial(exchange_kernel, n, m, w, laid),
+        functools.partial(exchange_kernel, n, m, w, laid, len(jobs)),
         out_shape=[jax.ShapeDtypeStruct(p.shape[1:], F32) for p in sums]
         + [jax.ShapeDtypeStruct(a.shape, a.dtype) for a in plain]
-        + [jax.ShapeDtypeStruct((a.shape[1], n * a.shape[2]), F32) for a in wide],
-        in_specs=[ANY] * (m + w),
+        + [jax.ShapeDtypeStruct((a.shape[1], n * a.shape[2]), F32) for a in wide]
+        + [jax.ShapeDtypeStruct((a.shape[1], b.shape[1]), BF16) for a, b in jobs],
+        in_specs=[ANY] * (m + w + 2 * len(jobs)),
         out_specs=[pl.BlockSpec(memory_space=pltpu.VMEM)] * m
         + [ANY] * (w - laid)
-        + [pl.BlockSpec(memory_space=pltpu.VMEM)] * laid,
+        + [pl.BlockSpec(memory_space=pltpu.VMEM)] * laid
+        + [ANY] * len(jobs),
         scratch_shapes=scratch,
         compiler_params=pltpu.CompilerParams(
-            collective_id=cid, has_side_effects=True, vmem_limit_bytes=(40 << 20) if m else None
+            collective_id=cid, has_side_effects=True, vmem_limit_bytes=(60 if jobs else 40) << 20 if m else None
         ),
         name="exchange",
-    )(*views, *swaps)
+    )(*views, *swaps, *(a for job in jobs for a in job))
     return [a[:rows] for a, rows in zip(out, kept_rows)] + list(out[m:])
 
 
@@ -419,31 +494,6 @@
     groups, n = lax.axis_size("grp"), lax.axis_size("ep")
     pairs = [(h * n + e, e * groups + h) for h in range(groups) for e in range(n)]
     return lax.ppermute(block.astype(BF16), ("grp", "ep"), pairs).astype(F32)
-
-
-def sum_async(p):
-    n = lax.axis_size("ep")
-    nz = n // 4
-    e = lax.axis_index("ep")
-    z, y, x = e // 4, (e // 2) % 2, e % 2
-    rows, cols = p.shape[1:]
-    p = p.reshape(nz, 2, 2, rows, cols)
-    top, bottom = p[:, :, :, : rows // 2], p[:, :, :, rows // 2 :]
-
-    def fold(part, place, axis, bit):
-        kept = lax.dynamic_index_in_dim(part, place, axis, keepdims=False)
-        sent = lax.dynamic_index_in_dim(part, 1 - place, axis, keepdims=False)
-        got = lax.ppermute(sent, "ep", [(i, i ^ bit) for i in range(n)])
-        return (kept.astype(F32) + got.astype(F32)).astype(p.dtype)
-
-    top = fold(fold(top, y, 1, 2), x, 1, 1)
-    bottom = fold(fold(bottom, x, 2, 1), y, 1, 2)
-    line = jnp.concatenate([top, bottom], axis=1)
-    total = lax.dynamic_index_in_dim(line, z, 0, keepdims=False).astype(F32)
-    for k in range(1, nz):
-        sent = lax.dynamic_index_in_dim(line, (z + k) % nz, 0, keepdims=False)
-        total = total + lax.ppermute(sent, "ep", [(i, (i + 4 * k) % n) for i in range(n)]).astype(F32)
-    return total
 
 
 def dot(left, right):
@@ -741,8 +791,7 @@
     rows_ref,
     hidden_ref,
     slot_grad_ref,
-    grad_g_ref,
-    grad_u_ref,
+    grad_gu_ref,
     shared_h_ref,
     shared_dg_ref,
     shared_du_ref,
@@ -778,8 +827,8 @@
     grad_hidden = dot_nt(slot_grad, ed_ref[...])
     grad_g = (grad_hidden * u * sigmoid * (1.0 + g * (1.0 - sigmoid))).astype(BF16)
     grad_u = (grad_hidden * silu).astype(BF16)
-    grad_g_ref[...] = grad_g
-    grad_u_ref[...] = grad_u
+    grad_gu_ref[:, : grad_g.shape[1]] = grad_g
+    grad_gu_ref[:, grad_g.shape[1] :] = grad_u
     row_grad[...] = (dot_nt(grad_g, eg_ref[...]) + dot_nt(grad_u, eu_ref[...])).astype(BF16)
     x = x_ref[...].reshape(blocks * tokens, -1)
     y = y_ref[...].reshape(blocks * tokens, -1)
@@ -853,8 +902,7 @@
             slot_rows(width),
             slot_rows(hidden),
             slot_rows(width),
-            slot_rows(hidden),
-            slot_rows(hidden),
+            slot_rows(2 * hidden),
             block(tokens, shared),
             block(tokens, shared),
             block(tokens, shared),
@@ -867,8 +915,7 @@
             slots_of(width),
             slots_of(hidden),
             slots_of(width),
-            slots_of(hidden),
-            slots_of(hidden),
+            slots_of(2 * hidden),
             tokens_of(shared),
             tokens_of(shared),
             tokens_of(shared),
@@ -983,7 +1030,16 @@
     )
     width = first_block.shape[1]
     first_block = jnp.pad(first_block, ((0, 0), (0, -width % 128)))
-    first_all = gather(first_block, 0)
+    shared_half = jnp.where(even, shared_gate, shared_up)
+    first_all, q_blocks, x_blocks, shared_blocks = gather(
+        first_block,
+        0,
+        swaps=(
+            column_halves(query_weight, n, half),
+            column_halves(expand_weight, n, half),
+            shared_half.T.reshape(n, shared_half.shape[1] // n, rows_dev),
+        ),
+    )
     c0 = D
     c1 = c0 + LATENT + ROPE
     c2 = c1 + n
@@ -994,47 +1050,37 @@
     lat_gain = first_all[:, :latent_rows, c2 + 2].reshape(LATENT).astype(F32)
     routes = first_all[:, :, c2 + 3 : c2 + 3 + TOPK].astype(jnp.int32)
 
-    q_half, x_half = (
-        column_halves(query_weight, n, half),
-        column_halves(expand_weight, n, half),
-    )
-    q_half, x_half, first_all = lax.optimization_barrier((q_half, x_half, first_all))
-    q_blocks, x_blocks = exchange(1, swaps=(q_half, x_half))
+    out_w_half = lax.dynamic_slice_in_dim(output_weight, half * (D // 2), D // 2, 1)
+    all_out_grad = lax.all_gather(output_grad, "ep", axis=0, tiled=True)
+    out_w_half, q_blocks = lax.optimization_barrier((out_w_half, q_blocks))
+    out_w_mine = lax.all_gather(out_w_half, "ep", axis=0, tiled=True)
+    out_w_other = from_partner(out_w_mine)
+
     q_mine, x_mine = columns_in(q_blocks), columns_in(x_blocks)
     query_t = both_halves(q_mine, from_partner(q_mine), even)
     expand_t = both_halves(x_mine, from_partner(x_mine), even)
-    shared_half = jnp.where(even, shared_gate, shared_up)
-    shared_half = shared_half.T.reshape(n, shared_half.shape[1] // n, rows_dev)
-
-    out_w_half = lax.dynamic_slice_in_dim(output_weight, half * (D // 2), D // 2, 1)
-    later_grad, q_blocks = lax.optimization_barrier((output_grad, q_blocks))
-    out_w_mine = lax.all_gather(out_w_half, "ep", axis=0, tiled=True)
-    out_w_other = from_partner(out_w_mine)
-    all_out_grad = lax.all_gather(later_grad, "ep", axis=0, tiled=True)
-
-    def own(values):
-        return lax.dynamic_slice_in_dim(values, e * tokens, tokens, 0)
-
-    cos_table, sin_table = rotary_tables(tokens, n)
-    turned = jnp.concatenate(
-        [query_t, query_t[NOPE + ROPE // 2 :], query_t[NOPE : NOPE + ROPE // 2]], axis=0
-    )
-    latent_turned = jnp.concatenate(
-        [latent_w, latent_w[:, LATENT + ROPE // 2 :], latent_w[:, LATENT : LATENT + ROPE // 2]],
-        axis=1,
-    )
-    normed, query, keys, values, latent = front(
-        first_all, cos_table, sin_table, attn_gain[None], lat_gain[None], turned, latent_turned, expand_t
-    )
-    attended_head, attended_exact, lse = attend(prefix_length, query, keys, values)
-    attended_blocks, shared_blocks = exchange(
-        2, swaps=(attended_head.reshape(n, tokens, VH), shared_half)
-    )
-    attended = attended_blocks.transpose(1, 0, 2).reshape(tokens, HEADS * VH)
     shared_mine = columns_in(shared_blocks)
     shared_other = from_partner(shared_mine)
     gate_t = jnp.where(even, shared_mine, shared_other)
     up_t = jnp.where(even, shared_other, shared_mine)
+
+    def own(values):
+        return lax.dynamic_slice_in_dim(values, e * tokens, tokens, 0)
+
+    cos_table, sin_table = rotary_tables(tokens, n)
+    turned = jnp.concatenate(
+        [query_t, query_t[NOPE + ROPE // 2 :], query_t[NOPE : NOPE + ROPE // 2]], axis=0
+    )
+    latent_turned = jnp.concatenate(
+        [latent_w, latent_w[:, LATENT + ROPE // 2 :], latent_w[:, LATENT : LATENT + ROPE // 2]],
+        axis=1,
+    )
+    normed, query, keys, values, latent = front(
+        first_all, cos_table, sin_table, attn_gain[None], lat_gain[None], turned, latent_turned, expand_t
+    )
+    attended_head, attended_exact, lse = attend(prefix_length, query, keys, values)
+    (attended_blocks,) = exchange(2, swaps=(attended_head.reshape(n, tokens, VH),))
+    attended = attended_blocks.transpose(1, 0, 2).reshape(tokens, HEADS * VH)
 
     residual_in = layer_input.astype(F32)
     input_scale = rms_scale(residual_in)
@@ -1047,7 +1093,7 @@
     mid_scale = rms_scale(residual_mid)
     mid_unit = residual_mid * mid_scale
     own_ffn_in = (mid_unit * ffn_gain).astype(BF16)
-    ffn_blocks = gather(own_ffn_in, 3)
+    (ffn_blocks,) = gather(own_ffn_in, 3)
     ffn_in = ffn_blocks.reshape(length, D)
 
     own_lane = (jnp.arange(128, dtype=jnp.int32) == e).astype(F32)[None]
@@ -1069,8 +1115,7 @@
         incoming,
         expert_hidden,
         slot_grad,
-        grad_expert_g,
-        grad_expert_u,
+        grad_expert_gu,
         shared_hidden,
         grad_shared_g,
         grad_shared_u,
@@ -1087,17 +1132,24 @@
         expert_up[0],
         expert_down[0],
     )
-    ffn_sum, dot_sum = exchange(4, sums=(ffn_partial, dot_partial))
-    out_partial, ffn_sum = lax.optimization_barrier((out_partial, ffn_sum))
-    out_sum = lax.psum_scatter(out_partial, "ep", scatter_dimension=0)
-    layer_output = (residual_mid + out_sum.astype(F32)).astype(BF16)
+    ffn_sum, dot_sum, out_sum, grad_down_m, grad_gate_up_m = exchange(
+        4,
+        sums=(ffn_partial, dot_partial, out_partial),
+        jobs=((expert_hidden, slot_grad), (incoming, grad_expert_gu)),
+    )
+    layer_output = (residual_mid + out_sum).astype(BF16)
 
     def shared_columns(values):
         return values.reshape(length, -1)[:, :shared_width]
 
-    expert_down_grad = product_over_groups(expert_hidden, slot_grad)[None]
-    expert_gate_grad = product_over_groups(incoming, grad_expert_g)[None]
-    expert_up_grad = product_over_groups(incoming, grad_expert_u)[None]
+    hidden = expert_down.shape[1]
+
+    def by_group(values):
+        return over_groups(values.reshape(groups, values.shape[0] // groups, -1))[None]
+
+    expert_down_grad = by_group(grad_down_m)
+    expert_gate_grad = by_group(grad_gate_up_m[:, :hidden])
+    expert_up_grad = by_group(grad_gate_up_m[:, hidden:])
     shared_down_grad = to_row_owner(product_over_groups(shared_columns(shared_hidden), all_out_grad))
     side_shared = product_over_groups(
         ffn_in,
@@ -1127,7 +1179,9 @@
         (output_w_partial, grad_att_blocks)
     )
     grad_att = grad_att_blocks.reshape(length, VH)
-    output_weight_grad = sum_async(output_w_partial.reshape(n, rows_out, D))
+    output_weight_grad = lax.psum_scatter(
+        output_w_partial.reshape(n, rows_out, D), "ep", scatter_dimension=0
+    ).astype(F32)
     grad_router = product("te,td->ed", grad_logits, own_ffn_in)
 
     delta = jnp.sum(grad_att.astype(F32) * attended_exact, axis=-1)[None]

time: 1000 us -> 1010 us (1.010)
  matrix products: 96.2 us -> 59.4 us
  waiting for transfers between devices: 36.5 us -> 62.8 us
  other arithmetic: 33.5 us -> 47.5 us
  local copies, waits for them, and re-layouts: 74.8 us -> 85.3 us
    all_gather x1, waiting for transfers between devices: 0.01 us -> 61.7 us  [per_device(): out_w_mine = lax.all_gather(out_w_half, 'ep', axis=0, tiled=True)]
    dot_general x26 -> x20, matrix products: 96.2 us -> 59.4 us  [product(): return jnp.einsum(form, left, right, preferred_element_type=F32)]
    ppermute x7 -> x3, waiting for transfers between devices: 36.4 us -> 0.01 us  [both(): return (mine, lax.ppermute(theirs.astype(BF16), 'grp', [(0, 1), (1, 0)]))]
    broadcast_in_dim x0 -> x3, other arithmetic: none -> 16.7 us  [by_group(): over_groups(values.reshape(groups, values.shape[0] // groups, -1))[None]]
    pallas_call x8 -> x7, Pallas kernels: 576 us -> 584 us  [the longest x5 359 us: exchange(): pl.pallas_call(functools.partial(exchange_kernel, n, m, w, laid, len(jobs...]
    unnamed x181 -> x157, local copies, waits for them, and re-layouts: 33.2 us -> 27.3 us
  transfers between devices with their start and end apart: 25 -> 18, of which waited for: 4 -> 3; matrix products, arithmetic and copies ran while one was open for 17% -> 15% of each run, Pallas kernels for 56% -> 36%
where the time goes in v5:
time: 1010 us
  Pallas kernels  728 us (72%)
  local copies, waits for them, and re-layouts  85.3 us (8%)
  waiting for transfers between devices  62.8 us (6%)
  matrix products  59.4 us (6%)
  other arithmetic  47.5 us (5%)
  between operations  15.8 us (2%)
    pallas_call x5, Pallas kernels, exchange(): pl.pallas_call(functools.partial(exchange_kernel, n, m, w, laid, len(jobs...  359 us
    pallas_call x2, Pallas kernels, gather(): pl.pallas_call(functools.partial(gather_kernel, n, w), out_shape=[jax.Sha...  224 us
    pallas_call x1, Pallas kernels, ffn(): pl.pallas_call(functools.partial(ffn_kernel, n), grid=(n // group,), in_s...  85.8 us
    all_gather x1, waiting for transfers between devices, per_device(): out_w_mine = lax.all_gather(out_w_half, 'ep', axis=0, tiled=True)  61.7 us
    dot_general x20, matrix products, product(): return jnp.einsum(form, left, right, preferred_element_type=F32)  59.4 us
    unnamed x157, local copies, waits for them, and re-layouts  27.3 us
  transfers between devices with their start and end apart: 18, of which 3 were waited for; matrix products, arithmetic and copies ran while one was open for 15% of the time, Pallas kernels for 36%

profile of v5, /device:TPU:0, one launch (start us, length us, event | category | flops | bytes accessed | tf_op | source)
XLA Modules:
  0.0 1006.6 jit_solution(6509026771768459794)
XLA Ops:
  16.3 120.0 %gather.2 = (bf16[16,128,2688]{2,1,0:T(8,128)(2,1)}, bf16[16,96,128]{2,1,0:T(8,128)(2,1)}, bf16[16,128,32]{2,1,0:T(8,128)(2,1)}, bf16[16,176,128]{2,1,0:T(8,128)(2,1)}) custom-call(bf16[128,2688]{1,0:T(8,128)(2,1)} %pad.23.x_ref, bf16[16,96,128]{2,1,0:T(8,128)(2,1)} %dynamic-slice_bitcast_fusion.3.refs_0_, bf16[16,128,32]{2,1,0:T(8,128)(2,1)} %bitcast.218, ...), custom_call_target="tpu_custom_call" | custom-call | tf_op jit(solution)/shard_map/gather/pallas_call | solution.py:207
  149.3 61.7 %all-gather.3.cloned.1.call-done = bf16[2048,1024]{1,0:T(8,128)(2,1)} async-done(((bf16[128,1024]{1,0:T(8,128)(2,1)}), bf16[2048,1024]{1,0:T(8,128)(2,1)}) %all-gather.3.cloned.1.call-update) | async-done | bytes 4194320 | tf_op jit(solution)/shard_map/all_gather | solution.py:1056
  226.5 17.4 %front.1 = (bf16[2048,2048]{1,0:T(8,128)(2,1)}, bf16[2048,256]{1,0:T(8,128)(2,1)S(1)}, bf16[2048,256]{1,0:T(8,128)(2,1)S(1)}, bf16[2048,128]{1,0:T(8,128)(2,1)S(1)}, bf16[2048,512]{1,0:T(8,128)(2,1)}) custom-call(bf16[16,128,2688]{2,1,0:T(8,128)(2,1)} %get-tuple-element.68.x_ref, f32[2048,128]{1,0:T(8,128)S(1)} %bitcast.158, ...), custom_call_target="tpu_custom_call" | custom-call | tf_op jit(solution)/shard_map/front/pallas_call | solution.py:552
  248.6 12.7 %attend.1 = (bf16[2048,128]{1,0:T(8,128)(2,1)S(1)}, f32[2048,128]{1,0:T(8,128)S(1)}, f32[1,2048]{1,0:T(1,128)S(1)}) custom-call(s32[1]{0:T(128)S(6)} %copy.95.prefix_ref, bf16[2048,256]{1,0:T(8,128)(2,1)S(1)} %copy-done.5, bf16[4,512,256]{2,1,0:T(8,128)(2,1)S(1)} %bitcast.163, bf16[4,128,512]{2,1,0:T(8,128)(2,1)S(1)} %copy.66.v_ref), custom_call_target="tpu_custom_call" | custom-call | tf_op jit(solution)/shard_map/attend/pallas_call | solution.py:687
  263.1 13.5 %exchange.5 = bf16[16,128,128]{2,1,0:T(8,128)(2,1)} custom-call(bf16[16,128,128]{2,1,0:T(8,128)(2,1)} %bitcast.175), custom_call_target="tpu_custom_call" | custom-call | tf_op jit(solution)/shard_map/exchange/pallas_call | solution.py:440
  282.9 3.1 broadcast_select_fusion.5
  289.1 104.5 %gather.3.x_ref = bf16[16,128,2048]{2,1,0:T(8,128)(2,1)} custom-call(bf16[128,2048]{1,0:T(8,128)(2,1)} %multiply_convert_fusion.x_ref), custom_call_target="tpu_custom_call" | custom-call | tf_op jit(solution)/shard_map/gather/pallas_call | solution.py:207
  396.9 85.8 %ffn.1 = (bf16[16,128,2048]{2,1,0:T(8,128)(2,1)}, bf16[16,128,2048]{2,1,0:T(8,128)(2,1)}, bf16[16,128,128]{2,1,0:T(8,128)(2,1)}, f32[16,128,128]{2,1,0:T(8,128)}...) custom-call(bf16[16,128,2048]{2,1,0:T(8,128)(2,1)} %gather.3.x_ref, ...), custom_call_target="tpu_custom_call" | custom-call | tf_op jit(solution)/shard_map/ffn/pallas_call | solution.py:887
  482.7 162.9 %exchange.6 = (f32[128,2048]{1,0:T(8,128)}, f32[128,128]{1,0:T(8,128)}, f32[128,2048]{1,0:T(8,128)}, bf16[1408,2048]{1,0:T(8,128)(2,1)}, bf16[2048,2816]{1,0:T(8,128)(2,1)}) custom-call(bf16[4,2,2,128,2048]{4,3,2,1,0:T(8,128)(2,1)} %bitcast.206, bf16[4,2,2,128,128]{4,3,2,1,0:T(8,128)(2,1)} %bitcast.223, bf16[4,2,2,128,2048]{4,3,2,1,0:T(8,128)(2,1)} %bitcast.205, ...), custom_call_target="tpu_custom_call" | custom-call | tf_op jit(solution)/shard_map/exchange/pallas_call | solution.py:440
  645.7 3.9 dynamic-slice_bitcast_fusion
  653.4 3.3 convolution_convert_fusion
  657.1 9.6 fusion.94
  666.7 3.7 dynamic-slice_bitcast_fusion.1
  673.0 5.8 convolution_convert_fusion.1
  685.4 4.0 fusion.60
  689.4 5.3 fusion.18
  694.7 4.6 fusion.11
  699.4 3.3 add_convert_fusion.4
  702.7 4.5 collective-permute-start.11
  707.2 5.4 add_convert_fusion
  715.0 10.7 %exchange.7 = bf16[16,128,128]{2,1,0:T(8,128)(2,1)} custom-call(bf16[16,128,128]{2,1,0:T(8,128)(2,1)} %bitcast.217), custom_call_target="tpu_custom_call" | custom-call | tf_op jit(solution)/shard_map/exchange/pallas_call | solution.py:440
  725.7 4.8 add_convert_fusion.2
  736.4 6.6 fusion
  743.0 5.0 fusion.1
  748.1 5.1 fusion.2
  753.6 15.2 %attend_back.1 = (f32[2048,256]{1,0:T(8,128)S(1)}, f32[4,512,256]{2,1,0:T(8,128)S(1)}, f32[4,512,128]{2,1,0:T(8,128)S(1)}) custom-call(s32[1]{0:T(128)S(6)} %copy.95.prefix_ref, bf16[2048,256]{1,0:T(8,128)(2,1)S(1)} %copy-done.6, bf16[2048,128]{1,0:T(8,128)(2,1)S(1)} %bitcast.162, f32[1,2048]{1,0:T(1,128)S(1)} %get-tuple-element.92.lse_ref, ...), custom_call_target="tpu_custom_call" | custom-call | tf_op jit(solution)/shard_map/attend_back/pallas_call | solution.py:745
  771.5 13.6 %back.1 = (bf16[2048,256]{1,0:T(8,128)(2,1)S(1)}, bf16[2048,256]{1,0:T(8,128)(2,1)S(1)}, bf16[2048,512]{1,0:T(8,128)(2,1)}, bf16[2048,128]{1,0:T(8,128)(2,1)S(1)...) custom-call(bf16[16,128,2688]{2,1,0:T(8,128)(2,1)} %get-tuple-element.68.x_ref, f32[2048,128]{1,0:T(8,128)S(1)} %bitcast.159, ...), custom_call_target="tpu_custom_call" | custom-call | tf_op jit(solution)/shard_map/back/pallas_call | solution.py:616
  787.0 62.5 %exchange.8 = (f32[128,512]{1,0:T(8,128)S(1)}, f32[128,128]{1,0:T(8,128)S(1)}) custom-call(bf16[4,2,2,128,512]{4,3,2,1,0:T(8,128)(2,1)S(1)} %bitcast.169, bf16[4,2,2,128,128]{4,3,2,1,0:T(8,128)(2,1)S(1)} %bitcast.174), custom_call_target="tpu_custom_call" | custom-call | tf_op jit(solution)/shard_map/exchange/pallas_call | solution.py:440
  857.1 3.9 fusion.21
  861.0 3.6 fusion.9
  871.0 109.6 %exchange.9 = (f32[128,2048]{1,0:T(8,128)S(1)}, f32[64,640]{1,0:T(8,128)S(1)}, f32[16,1,1168]{2,1,0:T(1,128)S(1)}, f32[64,3072]{1,0:T(8,128)S(1)}, f32[64,2816]{...) custom-call(bf16[4,2,2,128,2048]{4,3,2,1,0:T(8,128)(2,1)} %bitcast.204, ...), custom_call_target="tpu_custom_call" | custom-call | tf_op jit(solution)/shard_map/exchange/pallas_call | solution.py:440
  988.8 4.1 fusion.30
  (308 shorter events, 111.3 us)
Async XLA Ops:
  7.3 203.7 %all-gather.3.cloned.1.call-start = ((), (), s32[]{:S(2)}) async-start(), calls=%async_computation.1 | async-start | bytes 4456448 | tf_op jit(solution)/shard_map/all_gather | solution.py:1056
  136.3 260.6 %all-gather.5.cloned.1.call-start = ((), (), s32[]{:S(2)}) async-start(), calls=%async_computation.2 | async-start | bytes 8912896 | tf_op jit(solution)/shard_map/all_gather | solution.py:1054
  137.1 855.8 %reduce-scatter.2.cloned.1.call-start = ((), (), s32[]{:S(2)}) async-start(), calls=%async_computation.3 | async-start | bytes 4456448 | tf_op jit(solution)/shard_map/reduce_scatter | solution.py:1182
  139.3 84.8 %collective-permute-start.1 = (bf16[128,512]{1,0:T(8,128)(2,1)}, bf16[128,512]{1,0:T(8,128)(2,1)}, u32[]{:S(2)}, u32[]{:S(2)}) collective-permute-start(bf16[128,512]{1,0:T(8,128)(2,1)} %copy.64), channel_id=1, source_target_pairs={{0,16},{16,0},{1,17},{17,1},{2,18},{18,2},{3,19},{19,3},{4,20},{20... | collective-permute-start | bytes 393224 | tf_op jit(solution)/shard_map/ppermute | solution.py:490
  141.1 84.0 %collective-permute-start = (bf16[96,2048]{1,0:T(8,128)(2,1)}, bf16[96,2048]{1,0:T(8,128)(2,1)}, u32[]{:S(2)}, u32[]{:S(2)}) collective-permute-start(bf16[96,2048]{1,0:T(8,128)(2,1)} %copy_bitcast_fusion.1), channel_id=1, source_target_pairs={{0,16},{16,0},{1,17},{17,1},{2,18},{18,2},{3,19},{19,3},{4,20},{20... | collective-permute-start | bytes 1179656 | tf_op jit(solution)/shard_map/ppermute | solution.py:490
  143.7 134.2 %collective-permute-start.3 = (bf16[176,2048]{1,0:T(8,128)(2,1)}, bf16[176,2048]{1,0:T(8,128)(2,1)}, u32[]{:S(2)}, u32[]{:S(2)}) collective-permute-start(bf16[176,2048]{1,0:T(8,128)(2,1)} %copy_bitcast_fusion), channel_id=1, source_target_pairs={{0,16},{16,0},{1,17},{17,1},{2,18},{18,2},{3,19},{19,3},{4,20},{20... | collective-permute-start | bytes 2162696 | tf_op jit(solution)/shard_map/ppermute | solution.py:490
  147.8 702.4 %copy-start.58 = (f32[128]{0:T(128)}, f32[128]{0:T(128)S(1)}, u32[]{:S(2)}) copy-start(f32[128]{0:T(128)S(1)} %add_rsqrt_fusion.1) | copy-start | bytes 1540
  211.0 71.9 %collective-permute-start.2 = (bf16[2048,1024]{1,0:T(8,128)(2,1)}, bf16[2048,1024]{1,0:T(8,128)(2,1)}, u32[]{:S(2)}, u32[]{:S(2)}) collective-permute-start(bf16[2048,1024]{1,0:T(8,128)(2,1)} %all-gather.3.cloned.1.call-done), channel_id=1, source_target_pairs={{0,16},{16,0},{1,17},{17,1},{2,18},{18,2},{3,19},{19,3},{4,20},{20... | collective-permute-start | bytes 12582920 | tf_op jit(solution)/shard_map/ppermute | solution.py:490
  220.0 23.9 %copy-start.44 = (bf16[16,128,16]{2,1,0:T(8,128)(2,1)}, bf16[16,128,16]{2,1,0:T(8,128)(2,1)S(1)}, u32[]{:S(2)}) copy-start(bf16[16,128,16]{2,1,0:T(8,128)(2,1)S(1)} %slice.109) | copy-start | bytes 196612
  226.5 17.4 %copy-start.2 = (bf16[256,2048]{1,0:T(8,128)(2,1)}, bf16[256,2048]{1,0:T(8,128)(2,1)S(1)}, u32[]{:S(2)}) copy-start(bf16[256,2048]{1,0:T(8,128)(2,1)S(1)} %pad_maximum_fusion.2.wq_ref) | copy-start | bytes 3145732
  287.2 364.1 %copy-start.59 = (f32[128]{0:T(128)}, f32[128]{0:T(128)S(1)}, u32[]{:S(2)}) copy-start(f32[128]{0:T(128)S(1)} %add_rsqrt_fusion.2) | copy-start | bytes 1540
  289.1 104.5 %copy-start.48 = (bf16[128,2048]{1,0:T(8,128)(2,1)S(1)}, bf16[128,2048]{1,0:T(8,128)(2,1)}, u32[]{:S(2)}) copy-start(bf16[128,2048]{1,0:T(8,128)(2,1)} %get-tuple-element.144) | copy-start | bytes 1572868
  649.6 86.8 %collective-permute-start.14 = (bf16[704,2048]{1,0:T(8,128)(2,1)}, bf16[704,2048]{1,0:T(8,128)(2,1)}, u32[]{:S(2)}, u32[]{:S(2)}) collective-permute-start(bf16[704,2048]{1,0:T(8,128)(2,1)} %dynamic-slice_bitcast_fusion), channel_id=1, source_target_pairs={{0,16},{16,0},{1,17},{17,1},{2,18},{18,2},{3,19},{19,3},{4,20},{20... | collective-permute-start | bytes 8650760 | tf_op jit(solution)/shard_map/ppermute | solution.py:464
  656.7 46.0 %collective-permute-start.4 = (bf16[1024,2048]{1,0:T(8,128)(2,1)}, bf16[1024,2048]{1,0:T(8,128)(2,1)}, u32[]{:S(2)}, u32[]{:S(2)}) collective-permute-start(bf16[1024,2048]{1,0:T(8,128)(2,1)} %convolution_convert_fusion), channel_id=1, source_target_pairs={{0,16},{16,0},{1,17},{17,1},{2,18},{18,2},{3,19},{19,3},{4,20},{20... | collective-permute-start | bytes 12582920 | tf_op jit(solution)/shard_map/ppermute | solution.py:484
  670.4 72.5 %collective-permute-start.13 = (bf16[1024,1408]{1,0:T(8,128)(2,1)}, bf16[1024,1408]{1,0:T(8,128)(2,1)}, u32[]{:S(2)}, u32[]{:S(2)}) collective-permute-start(bf16[1024,1408]{1,0:T(8,128)(2,1)} %dynamic-slice_bitcast_fusion.1), channel_id=1, source_target_pairs={{0,16},{16,0},{1,17},{17,1},{2,18},{18,2},{3,19},{19,3},{4,20},{20... | collective-permute-start | bytes 8650760 | tf_op jit(solution)/shard_map/ppermute | solution.py:464
  672.9 75.1 %collective-permute-start.12 = (bf16[1024,1408]{1,0:T(8,128)(2,1)}, bf16[1024,1408]{1,0:T(8,128)(2,1)}, u32[]{:S(2)}, u32[]{:S(2)}) collective-permute-start(bf16[1024,1408]{1,0:T(8,128)(2,1)} %dynamic-slice_bitcast_fusion.2), channel_id=1, source_target_pairs={{0,16},{16,0},{1,17},{17,1},{2,18},{18,2},{3,19},{19,3},{4,20},{20... | collective-permute-start | bytes 8650760 | tf_op jit(solution)/shard_map/ppermute | solution.py:464
  678.7 20.5 %collective-permute-start.10 = (bf16[88,2048]{1,0:T(8,128)(2,1)}, bf16[88,2048]{1,0:T(8,128)(2,1)}, u32[]{:S(2)}, u32[]{:S(2)}) collective-permute-start(bf16[88,2048]{1,0:T(8,128)(2,1)} %convolution_convert_fusion.1), channel_id=1, source_target_pairs={{0,16},{16,0},{1,17},{17,1},{2,18},{18,2},{3,19},{19,3},{4,20},{20... | collective-permute-start | bytes 1081352 | tf_op jit(solution)/shard_map/ppermute | solution.py:484
  685.4 14.0 %slice-start = ((s8[8388608]{0:T(1024)(128)(4,1)}), s8[4194304]{0:T(1024)(128)(4,1)S(1)}, s32[]{:S(2)}) async-start(s8[8388608]{0:T(1024)(128)(4,1)} %bitcast.183), calls=%async_computation.4 | async-start | bytes 8388608
  689.4 10.0 slice-start.1
  699.3 26.5 %collective-permute-start.8 = (bf16[1024,352]{0,1:T(8,128)(2,1)}, bf16[1024,352]{0,1:T(8,128)(2,1)}, u32[]{:S(2)}, u32[]{:S(2)}) collective-permute-start(bf16[1024,352]{0,1:T(8,128)(2,1)} %fusion.18), channel_id=1, source_target_pairs={{0,16},{16,0},{1,17},{17,1},{2,18},{18,2},{3,19},{19,3},{4,20},{20... | collective-permute-start | bytes 2162696 | tf_op jit(solution)/shard_map/ppermute | solution.py:484
  702.7 31.6 %collective-permute-start.11 = (bf16[88,2048]{1,0:T(8,128)(2,1)}, bf16[88,2048]{1,0:T(8,128)(2,1)}, u32[]{:S(2)}, u32[]{:S(2)}) collective-permute-start(bf16[88,2048]{1,0:T(8,128)(2,1)} %add_convert_fusion.4), channel_id=1, source_target_pairs={{0,0},{1,2},{2,4},{3,6},{4,8},{5,10},{6,12},{7,14},{8,16},{9,18},{... | collective-permute-start | bytes 1081352 | tf_op jit(solution)/shard_map/ppermute | solution.py:496
  736.4 11.7 %slice-start.2 = ((s8[5767168]{0:T(1024)(128)(4,1)}), s8[4194304]{0:T(1024)(128)(4,1)S(1)}, s32[]{:S(2)}) async-start(s8[5767168]{0:T(1024)(128)(4,1)} %bitcast.192), calls=%async_computation.6 | async-start | bytes 8388608
  771.4 78.1 %copy-start.52 = (f32[128,512]{1,0:T(8,128)S(1)}, f32[128,512]{1,0:T(8,128)}, u32[]{:S(2)}) copy-start(f32[128,512]{1,0:T(8,128)} %get-tuple-element.159) | copy-start | bytes 786436
  771.4 78.1 %copy-start.63 = (f32[128]{0:T(128)S(1)}, f32[128]{0:T(128)}, u32[]{:S(2)}) copy-start(f32[128]{0:T(128)} %add_rsqrt_fusion) | copy-start | bytes 1540
  771.5 78.7 %copy-start.30 = (bf16[16,128,576]{2,1,0:T(8,128)(2,1)S(1)}, bf16[16,128,576]{2,1,0:T(8,128)(2,1)}, u32[]{:S(2)}) copy-start(bf16[16,128,576]{2,1,0:T(8,128)(2,1)} %copy-done.29) | copy-start | bytes 7077892
  771.5 78.7 %copy-start.36 = (bf16[128,2048]{1,0:T(8,128)(2,1)S(1)}, bf16[128,2048]{1,0:T(8,128)(2,1)}, u32[]{:S(2)}) copy-start(bf16[128,2048]{1,0:T(8,128)(2,1)} %param.18) | copy-start | bytes 1572868
  785.0 67.1 %copy-start.27 = (bf16[2048,256]{1,0:T(8,128)(2,1)}, bf16[2048,256]{1,0:T(8,128)(2,1)S(1)}, u32[]{:S(2)}) copy-start(bf16[2048,256]{1,0:T(8,128)(2,1)S(1)} %get-tuple-element.104) | copy-start | bytes 3145732
  856.1 12.1 %collective-permute-start.5 = (bf16[1024,640]{1,0:T(8,128)(2,1)}, bf16[1024,640]{1,0:T(8,128)(2,1)}, u32[]{:S(2)}, u32[]{:S(2)}) collective-permute-start(bf16[1024,640]{1,0:T(8,128)(2,1)} %convolution_convert_fusion.2), channel_id=1, source_target_pairs={{0,16},{16,0},{1,17},{17,1},{2,18},{18,2},{3,19},{19,3},{4,20},{20... | collective-permute-start | bytes 3932168 | tf_op jit(solution)/shard_map/ppermute | solution.py:484
  864.7 1.7 collective-permute-start.6
  865.8 1.4 collective-permute-start.9
  865.9 2.1 collective-permute-start.7
  988.8 11.1 %copy-start.1 = (bf16[128,2048]{1,0:T(8,128)(2,1)S(1)}, bf16[128,2048]{1,0:T(8,128)(2,1)}, u32[]{:S(2)}) copy-start(bf16[128,2048]{1,0:T(8,128)(2,1)} %param.24) | copy-start | bytes 1572868
  (60 other events, 236.9 us)
Sparse Core Ops, SparseCore 0:
  136.4 74.4 all-gather.2
  213.7 136.7 all-gather.4
  725.9 119.0 reduce-scatter.1

commit v6 on v5

--- a/solution.py
+++ b/solution.py
@@ -242,14 +242,14 @@
         return out
 
     sums_in, swaps_in = take(m), take(w)
-    jobs_in = [take(2) for _ in range(jobs)]
-    sums_out, swaps_out, jobs_out = take(m), take(w), take(jobs)
+    jobs_in = [take(2) for _ in jobs]
+    sums_out, swaps_out, jobs_out = take(m), take(w), [take(parts) for parts in jobs]
     room = [take(7) for _ in range(m)]
     sems = [take(8) for _ in range(m)]
     swap_sems = take(3) if w else None
     side_by_side = swaps_out[w - laid :]
     swaps_out = swaps_out[: w - laid] + take(laid)
-    desks = [take(5) for _ in range(jobs)]
+    desks = [take(5) for _ in jobs]
     me, z, y, x, px, py = around(n)
     nz = n // 4
     low = me % 4
@@ -328,30 +328,35 @@
         for i, (src, dst) in enumerate(((left, left_v), (right, right_v))):
             loads.append(pltpu.make_async_copy(src, dst, in_sem.at[i]))
 
+    def writes(j, i):
+        left_v, right_v, page, in_sem, out_sem = desks[j]
+        slot = i % 2
+        rows = pl.ds(pl.multiple_of(i * TILE, TILE), TILE)
+        return [
+            pltpu.make_async_copy(page.at[slot, part], out.at[rows], out_sem.at[slot, part])
+            for part, out in enumerate(jobs_out[j])
+        ]
+
     def tile(j, i):
         left_v, right_v, page, in_sem, out_sem = desks[j]
-        slot = i % 2
-        write = pltpu.make_async_copy(
-            page.at[slot],
-            jobs_out[j].at[pl.ds(pl.multiple_of(i * TILE, TILE), TILE)],
-            out_sem.at[slot],
-        )
         value = lax.dot_general(
             left_v[:, pl.ds(pl.multiple_of(i * TILE, TILE), TILE)],
             right_v[...],
             (((0,), (0,)), ((), ())),
             preferred_element_type=F32,
-        )
-        pl.when(i >= 2)(write.wait)
-        page[slot] = value.astype(page.dtype)
-        write.start()
+        ).astype(page.dtype)
+        width = page.shape[3]
+        for part, write in enumerate(writes(j, i)):
+            pl.when(i >= 2)(write.wait)
+            page[i % 2, part] = value[:, part * width : (part + 1) * width]
+            write.start()
 
     tiles = [desk[0].shape[1] // TILE for desk in desks]
     loaded = []
 
     def work(step, of):
         first, last = sum(tiles) * step // of, sum(tiles) * (step + 1) // of
-        for j in range(jobs):
+        for j in range(len(jobs)):
             start = sum(tiles[:j])
             low, high = max(first - start, 0), min(last - start, tiles[j])
             if low >= high:
@@ -407,11 +412,10 @@
             lax.fori_loop(0, half // 16, body, 0)
     for copy in sends:
         copy.wait_send()
-    for j in range(jobs):
-        left_v, right_v, page, in_sem, out_sem = desks[j]
-        for slot in range(2):
-            rows = jobs_out[j].at[pl.ds(0, TILE)]
-            pltpu.make_async_copy(page.at[slot], rows, out_sem.at[slot]).wait()
+    for j in range(len(jobs)):
+        for i in range(min(2, tiles[j])):
+            for write in writes(j, i):
+                write.wait()
 
 
 def exchange(cid, sums=(), swaps=(), laid=0, jobs=()):
@@ -434,26 +438,31 @@
         scratch += [DMA((w,)), DMA((w, n)), DMA((w, n))]
     plain, wide = swaps[: w - laid], swaps[w - laid :]
     scratch += [pltpu.VMEM(a.shape, a.dtype) for a in wide]
-    for left, right in jobs:
+    for left, right, parts in jobs:
         scratch += [pltpu.VMEM(left.shape, left.dtype), pltpu.VMEM(right.shape, right.dtype)]
-        scratch += [pltpu.VMEM((2, TILE, right.shape[1]), BF16), DMA((2,)), DMA((2,))]
+        scratch += [pltpu.VMEM((2, parts, TILE, right.shape[1] // parts), BF16)]
+        scratch += [DMA((2,)), DMA((2, parts))]
     out = pl.pallas_call(
-        functools.partial(exchange_kernel, n, m, w, laid, len(jobs)),
+        functools.partial(exchange_kernel, n, m, w, laid, [parts for _, _, parts in jobs]),
         out_shape=[jax.ShapeDtypeStruct(p.shape[1:], F32) for p in sums]
         + [jax.ShapeDtypeStruct(a.shape, a.dtype) for a in plain]
         + [jax.ShapeDtypeStruct((a.shape[1], n * a.shape[2]), F32) for a in wide]
-        + [jax.ShapeDtypeStruct((a.shape[1], b.shape[1]), BF16) for a, b in jobs],
+        + [
+            jax.ShapeDtypeStruct((a.shape[1], b.shape[1] // parts), BF16)
+            for a, b, parts in jobs
+            for _ in range(parts)
+        ],
         in_specs=[ANY] * (m + w + 2 * len(jobs)),
         out_specs=[pl.BlockSpec(memory_space=pltpu.VMEM)] * m
         + [ANY] * (w - laid)
         + [pl.BlockSpec(memory_space=pltpu.VMEM)] * laid
-        + [ANY] * len(jobs),
+        + [ANY] * sum(parts for _, _, parts in jobs),
         scratch_shapes=scratch,
         compiler_params=pltpu.CompilerParams(
             collective_id=cid, has_side_effects=True, vmem_limit_bytes=(60 if jobs else 40) << 20 if m else None
         ),
         name="exchange",
-    )(*views, *swaps, *(a for job in jobs for a in job))
+    )(*views, *swaps, *(a for job in jobs for a in job[:2]))
     return [a[:rows] for a, rows in zip(out, kept_rows)] + list(out[m:])
 
 
@@ -510,8 +519,7 @@
 ):
     blocks, tokens = x_ref.shape[:2]
     rows = blocks * tokens
-    width = gain_ref.shape[1]
-    x = x_ref[:, :, :width].reshape(rows, width).astype(F32)
+    x = x_ref[...].reshape(rows, gain_ref.shape[1]).astype(F32)
     normed = (x * rms_scale(x) * gain_ref[...]).astype(BF16)
     normed_ref[...] = normed
     cos, sin = cos_ref[...], sin_ref[...]
@@ -534,7 +542,8 @@
 
 
 def front(x, cos, sin, gain, lat_gain, wq, wl, we):
-    n, tokens, width = x.shape
+    n, tokens = x.shape[:2]
+    model = gain.shape[1]
     length = n * tokens
     blocks = 2
     rows = blocks * tokens
@@ -548,12 +557,12 @@
     def out(cols):
         return jax.ShapeDtypeStruct((length, cols), BF16)
 
-    cols = (gain.shape[1], wq.shape[0], NOPE + 2 * ROPE, VH, LATENT)
+    cols = (model, wq.shape[0], NOPE + 2 * ROPE, VH, LATENT)
     return pl.pallas_call(
         front_kernel,
         grid=(n // blocks,),
         in_specs=[
-            pl.BlockSpec((blocks, tokens, width), lambda i: (i, 0, 0)),
+            pl.BlockSpec((blocks, tokens, model), lambda i: (i, 0, 0)),
             rows_of(2 * ROPE),
             rows_of(2 * ROPE),
         ]
@@ -571,7 +580,6 @@
 ):
     blocks, tokens = x_ref.shape[:2]
     rows = blocks * tokens
-    width = gain_ref.shape[1]
     own_half = lax.broadcasted_iota(jnp.int32, cos_ref.shape, 1) < ROPE
     pair = dq_ref[:, NOPE:] * jnp.where(own_half, cos_ref[...], sin_ref[...])
     pair = jnp.where(own_half, pair + pltpu.roll(pair, ROPE, 1), 0.0)
@@ -579,7 +587,7 @@
     query_ref[:, NOPE:] = pair.astype(BF16)
     part = dot(query_ref[...], wq_ref[...])
     normed_ref[...] = part.astype(BF16)
-    x = x_ref[:, :, :width].reshape(rows, width).astype(F32)
+    x = x_ref[...].reshape(rows, gain_ref.shape[1]).astype(F32)
     gain = jnp.sum(part * (x * rms_scale(x)), axis=0, keepdims=True)
 
     @pl.when(pl.program_id(0) == 0)
@@ -597,7 +605,7 @@
 
 
 def back(x, cos, sin, dq, dk, dv, wq, we):
-    n, tokens, width = x.shape
+    n, tokens = x.shape[:2]
     length = n * tokens
     blocks = 2
     rows = blocks * tokens
@@ -617,7 +625,7 @@
         back_kernel,
         grid=(n // blocks,),
         in_specs=[
-            pl.BlockSpec((blocks, tokens, width), lambda i: (i, 0, 0)),
+            pl.BlockSpec((blocks, tokens, model), lambda i: (i, 0, 0)),
             rows_of(2 * ROPE),
             rows_of(2 * ROPE),
             rows_of(dq.shape[1]),
@@ -793,8 +801,7 @@
     slot_grad_ref,
     grad_gu_ref,
     shared_h_ref,
-    shared_dg_ref,
-    shared_du_ref,
+    shared_gu_ref,
     expert_out,
     row_grad,
 ):
@@ -840,8 +847,10 @@
     hidden = (silu * u).astype(BF16)
     grad_g = (grad_hidden * u * sigmoid * (1.0 + g * (1.0 - sigmoid))).astype(BF16)
     grad_u = (grad_hidden * silu).astype(BF16)
-    for ref, value in ((shared_h_ref, hidden), (shared_dg_ref, grad_g), (shared_du_ref, grad_u)):
-        ref[...] = value.reshape(blocks, tokens, -1)
+    shared = hidden.shape[1]
+    shared_h_ref[...] = hidden.reshape(blocks, tokens, shared)
+    shared_gu_ref[:, :, :shared] = grad_g.reshape(blocks, tokens, shared)
+    shared_gu_ref[:, :, shared:] = grad_u.reshape(blocks, tokens, shared)
     width = x.shape[1]
     chunk = width // 4
     met = [0.0] * blocks
@@ -904,8 +913,7 @@
             slot_rows(width),
             slot_rows(2 * hidden),
             block(tokens, shared),
-            block(tokens, shared),
-            block(tokens, shared),
+            block(tokens, 2 * shared),
         ],
         out_shape=[
             tokens_of(width),
@@ -917,8 +925,7 @@
             slots_of(width),
             slots_of(2 * hidden),
             tokens_of(shared),
-            tokens_of(shared),
-            tokens_of(shared),
+            tokens_of(2 * shared),
         ],
         scratch_shapes=[
             pltpu.VMEM((group * capacity, width), BF16),
@@ -1029,7 +1036,10 @@
         axis=1,
     )
     width = first_block.shape[1]
-    first_block = jnp.pad(first_block, ((0, 0), (0, -width % 128)))
+    out_w_half = lax.dynamic_slice_in_dim(output_weight, half * (D // 2), D // 2, 1)
+    first_block = jnp.concatenate(
+        [first_block, jnp.zeros((tokens, -width % 128), BF16), out_w_half], axis=1
+    )
     shared_half = jnp.where(even, shared_gate, shared_up)
     first_all, q_blocks, x_blocks, shared_blocks = gather(
         first_block,
@@ -1050,11 +1060,10 @@
     lat_gain = first_all[:, :latent_rows, c2 + 2].reshape(LATENT).astype(F32)
     routes = first_all[:, :, c2 + 3 : c2 + 3 + TOPK].astype(jnp.int32)
 
-    out_w_half = lax.dynamic_slice_in_dim(output_weight, half * (D // 2), D // 2, 1)
-    all_out_grad = lax.all_gather(output_grad, "ep", axis=0, tiled=True)
-    out_w_half, q_blocks = lax.optimization_barrier((out_w_half, q_blocks))
-    out_w_mine = lax.all_gather(out_w_half, "ep", axis=0, tiled=True)
+    out_w_mine = first_all[:, :, -(D // 2) :].reshape(D, D // 2)
     out_w_other = from_partner(out_w_mine)
+    later_grad, q_blocks = lax.optimization_barrier((output_grad, q_blocks))
+    all_out_grad = lax.all_gather(later_grad, "ep", axis=0, tiled=True)
 
     q_mine, x_mine = columns_in(q_blocks), columns_in(x_blocks)
     query_t = both_halves(q_mine, from_partner(q_mine), even)
@@ -1117,8 +1126,7 @@
         slot_grad,
         grad_expert_gu,
         shared_hidden,
-        grad_shared_g,
-        grad_shared_u,
+        grad_shared_gu,
     ) = ffn(
         ffn_blocks,
         all_out_grad.reshape(n, tokens, D),
@@ -1132,29 +1140,19 @@
         expert_up[0],
         expert_down[0],
     )
-    ffn_sum, dot_sum, out_sum, grad_down_m, grad_gate_up_m = exchange(
+    ffn_sum, dot_sum, out_sum, grad_down_m, grad_gate_m, grad_up_m = exchange(
         4,
         sums=(ffn_partial, dot_partial, out_partial),
-        jobs=((expert_hidden, slot_grad), (incoming, grad_expert_gu)),
+        jobs=((expert_hidden, slot_grad, 1), (incoming, grad_expert_gu, 2)),
     )
     layer_output = (residual_mid + out_sum).astype(BF16)
 
-    def shared_columns(values):
-        return values.reshape(length, -1)[:, :shared_width]
-
-    hidden = expert_down.shape[1]
-
     def by_group(values):
-        return over_groups(values.reshape(groups, values.shape[0] // groups, -1))[None]
-
-    expert_down_grad = by_group(grad_down_m)
-    expert_gate_grad = by_group(grad_gate_up_m[:, :hidden])
-    expert_up_grad = by_group(grad_gate_up_m[:, hidden:])
-    shared_down_grad = to_row_owner(product_over_groups(shared_columns(shared_hidden), all_out_grad))
-    side_shared = product_over_groups(
-        ffn_in,
-        jnp.concatenate([shared_columns(grad_shared_g), shared_columns(grad_shared_u)], axis=1),
-    ).astype(BF16)
+        return over_groups(values.reshape(groups, values.shape[0] // groups, -1))
+
+    expert_down_grad = by_group(grad_down_m)[None]
+    expert_gate_grad = by_group(grad_gate_m)[None]
+    expert_up_grad = by_group(grad_up_m)[None]
 
     router_own = lax.dynamic_index_in_dim(router_all, e, 0, keepdims=False)[:, :n]
     grad_probs = dot_sum[:, :n]
@@ -1198,15 +1196,24 @@
     ) = back(
         first_all, cos_table, sin_table, grad_query_raw, grad_keys, grad_values, turned, expand_t
     )
-    latent_sum, rope_sum = exchange(
+    latent_sum, rope_sum, side_gate, side_up, side_down, side_query, side_expand = exchange(
         6,
         sums=(
             latent_partial.reshape(n, tokens, LATENT),
             rope_partial.reshape(n, tokens, 2 * ROPE),
         ),
-    )
-    side_query = product_over_groups(normed, grad_query)[:, : query_t.shape[0]].astype(BF16)
-    grad_expand = product_over_groups(latent, grad_expanded).astype(BF16)
+        jobs=(
+            (ffn_in, grad_shared_gu.reshape(length, -1), 2),
+            (shared_hidden.reshape(length, -1), all_out_grad, 1),
+            (normed, grad_query, 1),
+            (latent, grad_expanded, 1),
+        ),
+    )
+    shared_down_grad = to_row_owner(by_group(side_down[:shared_width]))
+    side_gate = by_group(side_gate)[:, :shared_width].astype(BF16)
+    side_up = by_group(side_up)[:, :shared_width].astype(BF16)
+    side_query = by_group(side_query)[:, : query_t.shape[0]].astype(BF16)
+    grad_expand = by_group(side_expand).astype(BF16)
 
     own_normed = (input_unit * attn_gain).astype(BF16)
     own_raw = product("td,dc->tc", own_normed, latent_w[:, :LATENT])
@@ -1265,8 +1272,8 @@
         swaps=(
             small[:, None],
             side_query.reshape(n, rows_out, -1),
-            side_shared[:, :shared_width].reshape(n, rows_out, -1),
-            side_shared[:, shared_width:].reshape(n, rows_out, -1),
+            side_gate.reshape(n, rows_out, -1),
+            side_up.reshape(n, rows_out, -1),
             grad_expand.reshape(n, expand_rows, -1),
         ),
         laid=4,

time: 1010 us -> 967 us (0.957)
  waiting for transfers between devices: 62.8 us -> 0.1 us
  Pallas kernels: 728 us -> 766 us
  matrix products: 59.4 us -> 32 us
    all_gather x2 -> x1, waiting for transfers between devices: 61.7 us -> 0.02 us  [per_device(): all_out_grad = lax.all_gather(later_grad, 'ep', axis=0, tiled=True)]
    dot_general x20 -> x12, matrix products: 59.4 us -> 32 us  [product(): return jnp.einsum(form, left, right, preferred_element_type=F32)]
    pallas_call x5, Pallas kernels: 359 us -> 385 us  [exchange(): pl.pallas_call(functools.partial(exchange_kernel, n, m, w, laid, [parts f...]
    unnamed x157 -> x137, local copies, waits for them, and re-layouts: 27.3 us -> 27.5 us
  transfers between devices with their start and end apart: 18 -> 18, of which waited for: 3 -> 0; matrix products, arithmetic and copies ran while one was open for 15% -> 13% of each run, Pallas kernels for 36% -> 38%
where the time goes in v6:
time: 967 us; the launch traced here: 962 us
  Pallas kernels  766 us (79%)
  local copies, waits for them, and re-layouts  89.5 us (9%)
  other arithmetic  52.8 us (5%)
  matrix products  32 us (3%)
  between operations  16 us (2%)
    pallas_call x5, Pallas kernels, exchange(): pl.pallas_call(functools.partial(exchange_kernel, n, m, w, laid, [parts f...  385 us
    pallas_call x2, Pallas kernels, gather(): pl.pallas_call(functools.partial(gather_kernel, n, w), out_shape=[jax.Sha...  234 us
    pallas_call x1, Pallas kernels, ffn(): pl.pallas_call(functools.partial(ffn_kernel, n), grid=(n // group,), in_s...  85.9 us
    dot_general x12, matrix products, product(): return jnp.einsum(form, left, right, preferred_element_type=F32)  32 us
    unnamed x137, local copies, waits for them, and re-layouts  27.5 us
  transfers between devices with their start and end apart: 18, of which 0 were waited for; matrix products, arithmetic and copies ran while one was open for 13% of the time, Pallas kernels for 38%

profile of v6, /device:TPU:0, one launch (start us, length us, event | category | flops | bytes accessed | tf_op | source)
XLA Modules:
  0.0 961.6 jit_solution(11707642570741961890)
XLA Ops:
  23.5 150.1 %gather.2 = (bf16[16,128,3712]{2,1,0:T(8,128)(2,1)}, bf16[16,96,128]{2,1,0:T(8,128)(2,1)}, bf16[16,128,32]{2,1,0:T(8,128)(2,1)}, bf16[16,176,128]{2,1,0:T(8,128)(2,1)}) custom-call(bf16[128,3712]{1,0:T(8,128)(2,1)} %concatenate.29.x_ref, bf16[16,96,128]{2,1,0:T(8,128)(2,1)} %dynamic-slice_bitcast_fusion.9.refs_0_, bf16[16,128,32]{2,1,0:T(8,128)(2,1)} %bitcast.235, ...), custom_call_target="tpu_custom_call" | custom-call | tf_op jit(solution)/shard_map/gather/pallas_call | solution.py:207
  178.2 5.2 slice.100
  184.9 3.6 slice.97
  196.2 2.1 pad_maximum_fusion.wl_ref
  203.2 2.2 pad.22.sd_ref
  207.7 17.3 %front.1 = (bf16[2048,2048]{1,0:T(8,128)(2,1)}, bf16[2048,256]{1,0:T(8,128)(2,1)S(1)}, bf16[2048,256]{1,0:T(8,128)(2,1)S(1)}, bf16[2048,128]{1,0:T(8,128)(2,1)S(1)}, bf16[2048,512]{1,0:T(8,128)(2,1)}) custom-call(bf16[16,128,3712]{2,1,0:T(8,128)(2,1)} %get-tuple-element.73.x_ref, f32[2048,128]{1,0:T(8,128)S(1)} %bitcast.181, ...), custom_call_target="tpu_custom_call" | custom-call | tf_op jit(solution)/shard_map/front/pallas_call | solution.py:561
  231.6 13.8 %attend.1 = (bf16[2048,128]{1,0:T(8,128)(2,1)S(1)}, f32[2048,128]{1,0:T(8,128)S(1)}, f32[1,2048]{1,0:T(1,128)S(1)}) custom-call(s32[1]{0:T(128)S(6)} %copy.86.prefix_ref, bf16[2048,256]{1,0:T(8,128)(2,1)S(1)} %copy-done.5, bf16[4,512,256]{2,1,0:T(8,128)(2,1)S(1)} %bitcast.186, bf16[4,128,512]{2,1,0:T(8,128)(2,1)S(1)} %copy-done.12), custom_call_target="tpu_custom_call" | custom-call | tf_op jit(solution)/shard_map/attend/pallas_call | solution.py:695
  247.2 20.2 %exchange.5 = bf16[16,128,128]{2,1,0:T(8,128)(2,1)} custom-call(bf16[16,128,128]{2,1,0:T(8,128)(2,1)} %bitcast.197), custom_call_target="tpu_custom_call" | custom-call | tf_op jit(solution)/shard_map/exchange/pallas_call | solution.py:445
  269.5 3.1 convolution_bitcast_fusion
  276.3 3.0 broadcast_select_fusion.5
  282.3 84.3 %gather.3.x_ref = bf16[16,128,2048]{2,1,0:T(8,128)(2,1)} custom-call(bf16[128,2048]{1,0:T(8,128)(2,1)} %multiply_convert_fusion.x_ref), custom_call_target="tpu_custom_call" | custom-call | tf_op jit(solution)/shard_map/gather/pallas_call | solution.py:207
  366.7 85.9 %ffn.1 = (bf16[16,128,2048]{2,1,0:T(8,128)(2,1)}, bf16[16,128,2048]{2,1,0:T(8,128)(2,1)}, bf16[16,128,128]{2,1,0:T(8,128)(2,1)}, f32[16,128,128]{2,1,0:T(8,128)}...) custom-call(bf16[16,128,2048]{2,1,0:T(8,128)(2,1)} %gather.3.x_ref, ...), custom_call_target="tpu_custom_call" | custom-call | tf_op jit(solution)/shard_map/ffn/pallas_call | solution.py:896
  453.5 160.7 %exchange.6 = (f32[128,2048]{1,0:T(8,128)}, f32[128,128]{1,0:T(8,128)}, f32[128,2048]{1,0:T(8,128)}, bf16[1408,2048]{1,0:T(8,128)(2,1)}, bf16[2048,1408]{1,0:T(8,128)(2,1)}, /*index=5*/bf16[2048,1408]{1,0:T(8,128)(2,1)}) custom-call(bf16[4,2,2,128,2048]{4,3,2,1,0:T(8,128)(2,1)} %bitcast.213, bf16[4,2,2,128,128]{4,3,2,1,0:T(8,128)(2,1)} %bitcast.245, ...), custom_call_target="tpu_custom_call" | custom-call | tf_op jit(solution)/shard_map/exchange/pallas_call | solution.py:445
  616.2 2.1 multiply_reduce_fusion
  620.4 3.3 convolution_convert_fusion
  623.7 3.8 dynamic-slice_bitcast_fusion
  628.1 3.8 dynamic-slice_bitcast_fusion.1
  631.9 2.3 multiply_reduce_fusion.6
  634.1 3.6 dynamic-slice_bitcast_fusion.2
  640.5 3.9 fusion.34
  644.4 4.7 fusion.3
  649.2 5.5 add_convert_fusion
  658.8 13.0 %exchange.7 = bf16[16,128,128]{2,1,0:T(8,128)(2,1)} custom-call(bf16[16,128,128]{2,1,0:T(8,128)(2,1)} %bitcast.238), custom_call_target="tpu_custom_call" | custom-call | tf_op jit(solution)/shard_map/exchange/pallas_call | solution.py:445
  671.8 6.6 fusion
  678.4 6.1 fusion.1
  684.5 5.1 fusion.2
  690.0 16.6 %attend_back.1 = (f32[2048,256]{1,0:T(8,128)S(1)}, f32[4,512,256]{2,1,0:T(8,128)S(1)}, f32[4,512,128]{2,1,0:T(8,128)S(1)}) custom-call(s32[1]{0:T(128)S(6)} %copy.86.prefix_ref, bf16[2048,256]{1,0:T(8,128)(2,1)S(1)} %copy-done.6, bf16[2048,128]{1,0:T(8,128)(2,1)S(1)} %bitcast.185, f32[1,2048]{1,0:T(1,128)S(1)} %get-tuple-element.97.lse_ref, ...), custom_call_target="tpu_custom_call" | custom-call | tf_op jit(solution)/shard_map/attend_back/pallas_call | solution.py:753
  709.3 13.1 %back.1 = (bf16[2048,256]{1,0:T(8,128)(2,1)S(1)}, bf16[2048,256]{1,0:T(8,128)(2,1)S(1)}, bf16[2048,512]{1,0:T(8,128)(2,1)}, bf16[2048,128]{1,0:T(8,128)(2,1)S(1)...) custom-call(bf16[16,128,3712]{2,1,0:T(8,128)(2,1)} %get-tuple-element.73.x_ref, f32[2048,128]{1,0:T(8,128)S(1)} %bitcast.182, ...), custom_call_target="tpu_custom_call" | custom-call | tf_op jit(solution)/shard_map/back/pallas_call | solution.py:624
  725.2 70.4 %exchange.8 = (f32[128,512]{1,0:T(8,128)}, f32[128,128]{1,0:T(8,128)}, bf16[2048,256]{1,0:T(8,128)(2,1)}, bf16[2048,256]{1,0:T(8,128)(2,1)}, bf16[256,2048]{1,0:...) custom-call(bf16[4,2,2,128,512]{4,3,2,1,0:T(8,128)(2,1)} %bitcast.234, ...), custom_call_target="tpu_custom_call" | custom-call | tf_op jit(solution)/shard_map/exchange/pallas_call | solution.py:445
  799.8 2.2 dynamic-slice_bitcast_fusion.3
  818.3 120.7 %exchange.9 = (f32[128,2048]{1,0:T(8,128)S(1)}, f32[64,640]{1,0:T(8,128)S(1)}, f32[16,1,1168]{2,1,0:T(1,128)S(1)}, f32[64,3072]{1,0:T(8,128)S(1)}, f32[64,2816]{...) custom-call(bf16[4,2,2,128,2048]{4,3,2,1,0:T(8,128)(2,1)} %bitcast.211, ...), custom_call_target="tpu_custom_call" | custom-call | tf_op jit(solution)/shard_map/exchange/pallas_call | solution.py:445
  943.5 4.1 fusion.16
  (283 shorter events, 103.4 us)
Async XLA Ops:
  7.2 15.0 %copy-start = (bf16[128,2048]{1,0:T(8,128)(2,1)S(1)}, bf16[128,2048]{1,0:T(8,128)(2,1)}, u32[]{:S(2)}) copy-start(bf16[128,2048]{1,0:T(8,128)(2,1)} %param.24) | copy-start | bytes 1572868
  7.2 13.8 %copy-start.47 = (bf16[128,2816]{1,0:T(8,128)(2,1)S(1)}, bf16[128,2816]{1,0:T(8,128)(2,1)}, u32[]{:S(2)}) copy-start(bf16[128,2816]{1,0:T(8,128)(2,1)} %param.27) | copy-start | bytes 2162692
  7.2 13.8 %copy-start.48 = (bf16[128,2816]{1,0:T(8,128)(2,1)S(1)}, bf16[128,2816]{1,0:T(8,128)(2,1)}, u32[]{:S(2)}) copy-start(bf16[128,2816]{1,0:T(8,128)(2,1)} %param.28) | copy-start | bytes 2162692
  7.2 359.5 %all-gather.2.cloned.1.call-start = ((), (), s32[]{:S(2)}) async-start(), calls=%async_computation.1 | async-start | bytes 8912896 | tf_op jit(solution)/shard_map/all_gather | solution.py:1066
  173.6 774.1 %reduce-scatter.2.cloned.1.call-start = ((), (), s32[]{:S(2)}) async-start(), calls=%async_computation.2 | async-start | bytes 4456448 | tf_op jit(solution)/shard_map/reduce_scatter | solution.py:1180
  175.9 29.4 %collective-permute-start.1 = (bf16[128,512]{1,0:T(8,128)(2,1)}, bf16[128,512]{1,0:T(8,128)(2,1)}, u32[]{:S(2)}, u32[]{:S(2)}) collective-permute-start(bf16[128,512]{1,0:T(8,128)(2,1)} %copy.60), channel_id=1, source_target_pairs={{0,16},{16,0},{1,17},{17,1},{2,18},{18,2},{3,19},{19,3},{4,20},{20... | collective-permute-start | bytes 393224 | tf_op jit(solution)/shard_map/ppermute | solution.py:499
  177.7 28.7 %collective-permute-start = (bf16[96,2048]{1,0:T(8,128)(2,1)}, bf16[96,2048]{1,0:T(8,128)(2,1)}, u32[]{:S(2)}, u32[]{:S(2)}) collective-permute-start(bf16[96,2048]{1,0:T(8,128)(2,1)} %copy_bitcast_fusion.1), channel_id=1, source_target_pairs={{0,16},{16,0},{1,17},{17,1},{2,18},{18,2},{3,19},{19,3},{4,20},{20... | collective-permute-start | bytes 1179656 | tf_op jit(solution)/shard_map/ppermute | solution.py:499
  183.4 92.9 %collective-permute-start.2 = (bf16[2048,1024]{1,0:T(8,128)(2,1)}, bf16[2048,1024]{1,0:T(8,128)(2,1)}, u32[]{:S(2)}, u32[]{:S(2)}) collective-permute-start(bf16[2048,1024]{1,0:T(8,128)(2,1)} %bitcast.23), channel_id=1, source_target_pairs={{0,16},{16,0},{1,17},{17,1},{2,18},{18,2},{3,19},{19,3},{4,20},{20... | collective-permute-start | bytes 12582920 | tf_op jit(solution)/shard_map/ppermute | solution.py:499
  184.3 88.3 %collective-permute-start.3 = (bf16[176,2048]{1,0:T(8,128)(2,1)}, bf16[176,2048]{1,0:T(8,128)(2,1)}, u32[]{:S(2)}, u32[]{:S(2)}) collective-permute-start(bf16[176,2048]{1,0:T(8,128)(2,1)} %copy_bitcast_fusion), channel_id=1, source_target_pairs={{0,16},{16,0},{1,17},{17,1},{2,18},{18,2},{3,19},{19,3},{4,20},{20... | collective-permute-start | bytes 2162696 | tf_op jit(solution)/shard_map/ppermute | solution.py:499
  207.7 17.4 %copy-start.2 = (bf16[256,2048]{1,0:T(8,128)(2,1)}, bf16[256,2048]{1,0:T(8,128)(2,1)S(1)}, u32[]{:S(2)}) copy-start(bf16[256,2048]{1,0:T(8,128)(2,1)S(1)} %pad_maximum_fusion.1.wq_ref) | copy-start | bytes 3145732
  280.4 337.9 %copy-start.58 = (f32[128]{0:T(128)}, f32[128]{0:T(128)S(1)}, u32[]{:S(2)}) copy-start(f32[128]{0:T(128)S(1)} %add_rsqrt_fusion.2) | copy-start | bytes 1540
  453.5 162.7 %copy-start.36 = (bf16[16,128,16]{2,1,0:T(8,128)(2,1)S(1)}, bf16[16,128,16]{2,1,0:T(8,128)(2,1)}, u32[]{:S(2)}) copy-start(bf16[16,128,16]{2,1,0:T(8,128)(2,1)} %copy-done.35) | copy-start | bytes 196612
  623.7 25.5 %collective-permute-start.4 = (bf16[1024,2048]{1,0:T(8,128)(2,1)}, bf16[1024,2048]{1,0:T(8,128)(2,1)}, u32[]{:S(2)}, u32[]{:S(2)}) collective-permute-start(bf16[1024,2048]{1,0:T(8,128)(2,1)} %convolution_convert_fusion), channel_id=1, source_target_pairs={{0,16},{16,0},{1,17},{17,1},{2,18},{18,2},{3,19},{19,3},{4,20},{20... | collective-permute-start | bytes 12582920 | tf_op jit(solution)/shard_map/ppermute | solution.py:493
  627.5 44.3 %collective-permute-start.15 = (bf16[704,2048]{1,0:T(8,128)(2,1)}, bf16[704,2048]{1,0:T(8,128)(2,1)}, u32[]{:S(2)}, u32[]{:S(2)}) collective-permute-start(bf16[704,2048]{1,0:T(8,128)(2,1)} %dynamic-slice_bitcast_fusion), channel_id=1, source_target_pairs={{0,16},{16,0},{1,17},{17,1},{2,18},{18,2},{3,19},{19,3},{4,20},{20... | collective-permute-start | bytes 8650760 | tf_op jit(solution)/shard_map/ppermute | solution.py:473
  631.8 46.5 %collective-permute-start.14 = (bf16[1024,1408]{1,0:T(8,128)(2,1)}, bf16[1024,1408]{1,0:T(8,128)(2,1)}, u32[]{:S(2)}, u32[]{:S(2)}) collective-permute-start(bf16[1024,1408]{1,0:T(8,128)(2,1)} %dynamic-slice_bitcast_fusion.1), channel_id=1, source_target_pairs={{0,16},{16,0},{1,17},{17,1},{2,18},{18,2},{3,19},{19,3},{4,20},{20... | collective-permute-start | bytes 8650760 | tf_op jit(solution)/shard_map/ppermute | solution.py:473
  637.7 46.7 %collective-permute-start.13 = (bf16[1024,1408]{1,0:T(8,128)(2,1)}, bf16[1024,1408]{1,0:T(8,128)(2,1)}, u32[]{:S(2)}, u32[]{:S(2)}) collective-permute-start(bf16[1024,1408]{1,0:T(8,128)(2,1)} %dynamic-slice_bitcast_fusion.2), channel_id=1, source_target_pairs={{0,16},{16,0},{1,17},{17,1},{2,18},{18,2},{3,19},{19,3},{4,20},{20... | collective-permute-start | bytes 8650760 | tf_op jit(solution)/shard_map/ppermute | solution.py:473
  671.8 12.7 %slice-start = ((s8[5767168]{0:T(1024)(128)(4,1)}), s8[4194304]{0:T(1024)(128)(4,1)S(1)}, s32[]{:S(2)}) async-start(s8[5767168]{0:T(1024)(128)(4,1)} %bitcast.218), calls=%async_computation.3 | async-start | bytes 8388608
  795.7 8.5 copy-start.22
  795.7 8.5 copy-start.27
  797.8 14.6 %collective-permute-start.11 = (bf16[88,2048]{1,0:T(8,128)(2,1)}, bf16[88,2048]{1,0:T(8,128)(2,1)}, u32[]{:S(2)}, u32[]{:S(2)}) collective-permute-start(bf16[88,2048]{1,0:T(8,128)(2,1)} %dynamic-slice_bitcast_fusion.10), channel_id=1, source_target_pairs={{0,16},{16,0},{1,17},{17,1},{2,18},{18,2},{3,19},{19,3},{4,20},{20... | collective-permute-start | bytes 1081352 | tf_op jit(solution)/shard_map/ppermute | solution.py:473
  799.3 11.9 %collective-permute-start.10 = (bf16[256,256]{1,0:T(8,128)(2,1)}, bf16[256,256]{1,0:T(8,128)(2,1)}, u32[]{:S(2)}, u32[]{:S(2)}) collective-permute-start(bf16[256,256]{1,0:T(8,128)(2,1)} %dynamic-slice_bitcast_fusion.11), channel_id=1, source_target_pairs={{0,16},{16,0},{1,17},{17,1},{2,18},{18,2},{3,19},{19,3},{4,20},{20... | collective-permute-start | bytes 393224 | tf_op jit(solution)/shard_map/ppermute | solution.py:473
  802.1 12.1 %collective-permute-start.9 = (bf16[1024,256]{1,0:T(8,128)(2,1)}, bf16[1024,256]{1,0:T(8,128)(2,1)}, u32[]{:S(2)}, u32[]{:S(2)}) collective-permute-start(bf16[1024,256]{1,0:T(8,128)(2,1)} %get-tuple-element.146), channel_id=1, source_target_pairs={{0,16},{16,0},{1,17},{17,1},{2,18},{18,2},{3,19},{19,3},{4,20},{20... | collective-permute-start | bytes 1572872 | tf_op jit(solution)/shard_map/ppermute | solution.py:473
  803.1 12.3 %collective-permute-start.8 = (bf16[1024,256]{1,0:T(8,128)(2,1)}, bf16[1024,256]{1,0:T(8,128)(2,1)}, u32[]{:S(2)}, u32[]{:S(2)}) collective-permute-start(bf16[1024,256]{1,0:T(8,128)(2,1)} %get-tuple-element.148), channel_id=1, source_target_pairs={{0,16},{16,0},{1,17},{17,1},{2,18},{18,2},{3,19},{19,3},{4,20},{20... | collective-permute-start | bytes 1572872 | tf_op jit(solution)/shard_map/ppermute | solution.py:473
  806.3 9.1 copy-start.42
  807.8 2.9 collective-permute-start.6
  810.6 6.0 collective-permute-start.7
  811.3 6.4 collective-permute-start.5
  813.5 3.3 collective-permute-start.12
  818.3 125.3 %copy-start.57 = (f32[128]{0:T(128)S(1)}, f32[128]{0:T(128)}, u32[]{:S(2)}) copy-start(f32[128]{0:T(128)} %add_rsqrt_fusion.1) | copy-start | bytes 1540
  818.3 125.3 %copy-start.59 = (f32[128]{0:T(128)S(1)}, f32[128]{0:T(128)}, u32[]{:S(2)}) copy-start(f32[128]{0:T(128)} %copy-done.58) | copy-start | bytes 1540
  818.3 125.3 %copy-start.61 = (f32[128]{0:T(128)S(1)}, f32[128]{0:T(128)}, u32[]{:S(2)}) copy-start(f32[128]{0:T(128)} %copy-done.60) | copy-start | bytes 1540
  943.5 11.0 %copy-start.1 = (bf16[128,2048]{1,0:T(8,128)(2,1)S(1)}, bf16[128,2048]{1,0:T(8,128)(2,1)}, u32[]{:S(2)}) copy-start(bf16[128,2048]{1,0:T(8,128)(2,1)} %param.24) | copy-start | bytes 1572868
  (50 other events, 192.9 us)
Sparse Core Ops, SparseCore 0:
  173.7 119.4 all-gather.1
  671.9 118.3 reduce-scatter.1

commit v7 on v6

--- a/solution.py
+++ b/solution.py
@@ -535,7 +535,7 @@
     raw = compressed[:, :LATENT]
     latent = (raw * rms_scale(raw) * lat_gain_ref[...]).astype(BF16)
     latent_ref[...] = latent
-    expanded = dot_nt(latent, we_ref[...])
+    expanded = dot(latent, we_ref[...])
     keys_ref[:, :NOPE] = expanded[:, :NOPE].astype(BF16)
     keys_ref[:, NOPE:] = turn(compressed[:, LATENT:]).astype(BF16)
     values_ref[...] = expanded[:, NOPE:].astype(BF16)
@@ -575,44 +575,22 @@
 
 
 def back_kernel(
-    x_ref, cos_ref, sin_ref, dq_ref, dk_ref, dv_ref, wq_ref, we_ref,
-    query_ref, expanded_ref, latent_ref, rope_ref, normed_ref, gain_ref,
+    cos_ref, sin_ref, dq_ref, dk_ref, dv_ref, we_ref, query_ref, expanded_ref, latent_ref, rope_ref
 ):
-    blocks, tokens = x_ref.shape[:2]
-    rows = blocks * tokens
     own_half = lax.broadcasted_iota(jnp.int32, cos_ref.shape, 1) < ROPE
     pair = dq_ref[:, NOPE:] * jnp.where(own_half, cos_ref[...], sin_ref[...])
     pair = jnp.where(own_half, pair + pltpu.roll(pair, ROPE, 1), 0.0)
     query_ref[:, :NOPE] = dq_ref[:, :NOPE].astype(BF16)
     query_ref[:, NOPE:] = pair.astype(BF16)
-    part = dot(query_ref[...], wq_ref[...])
-    normed_ref[...] = part.astype(BF16)
-    x = x_ref[...].reshape(rows, gain_ref.shape[1]).astype(F32)
-    gain = jnp.sum(part * (x * rms_scale(x)), axis=0, keepdims=True)
-
-    @pl.when(pl.program_id(0) == 0)
-    def _():
-        gain_ref[...] = gain
-
-    @pl.when(pl.program_id(0) > 0)
-    def _():
-        gain_ref[...] += gain
-
     expanded_ref[:, :NOPE] = dk_ref[:, :NOPE].astype(BF16)
     expanded_ref[:, NOPE:] = dv_ref[...].astype(BF16)
-    latent_ref[...] = dot(expanded_ref[...], we_ref[...]).astype(BF16)
+    latent_ref[...] = dot_nt(expanded_ref[...], we_ref[...]).astype(BF16)
     rope_ref[...] = dk_ref[:, NOPE:].astype(BF16)
 
 
-def back(x, cos, sin, dq, dk, dv, wq, we):
-    n, tokens = x.shape[:2]
-    length = n * tokens
-    blocks = 2
-    rows = blocks * tokens
-    model = wq.shape[1]
-
-    def whole(a):
-        return pl.BlockSpec(a.shape, lambda i: (0,) * a.ndim, pipeline_mode=pl.Buffered(1))
+def back(cos, sin, dq, dk, dv, we):
+    length = dq.shape[0]
+    rows = 512
 
     def rows_of(cols):
         return pl.BlockSpec((rows, cols), lambda i: (i, 0))
@@ -620,25 +598,17 @@
     def out(cols):
         return jax.ShapeDtypeStruct((length, cols), BF16)
 
-    cols = (NOPE + 2 * ROPE, NOPE + VH, LATENT, 2 * ROPE, model)
+    cols = (NOPE + 2 * ROPE, NOPE + VH, LATENT, 2 * ROPE)
     return pl.pallas_call(
         back_kernel,
-        grid=(n // blocks,),
-        in_specs=[
-            pl.BlockSpec((blocks, tokens, model), lambda i: (i, 0, 0)),
-            rows_of(2 * ROPE),
-            rows_of(2 * ROPE),
-            rows_of(dq.shape[1]),
-            rows_of(dk.shape[1]),
-            rows_of(dv.shape[1]),
-            whole(wq),
-            whole(we),
-        ],
-        out_specs=[rows_of(c) for c in cols] + [pl.BlockSpec((1, model), lambda i: (0, 0))],
-        out_shape=[out(c) for c in cols] + [jax.ShapeDtypeStruct((1, model), F32)],
-        compiler_params=pltpu.CompilerParams(vmem_limit_bytes=48 << 20),
+        grid=(length // rows,),
+        in_specs=[rows_of(a.shape[1]) for a in (cos, sin, dq, dk, dv)]
+        + [pl.BlockSpec(we.shape, lambda i: (0, 0))],
+        out_specs=[rows_of(c) for c in cols],
+        out_shape=[out(c) for c in cols],
+        compiler_params=pltpu.CompilerParams(vmem_limit_bytes=40 << 20),
         name="back",
-    )(x, cos, sin, dq, dk, dv, wq, we)
+    )(cos, sin, dq, dk, dv, we)
 
 
 KEYS = 512
@@ -985,8 +955,8 @@
     return blocks.transpose(1, 0, 2).reshape(width, n * rows)
 
 
-def both_halves(mine, other, even):
-    return jnp.concatenate([jnp.where(even, mine, other), jnp.where(even, other, mine)], axis=0)
+def both_halves(mine, other, even, axis=0):
+    return jnp.concatenate([jnp.where(even, mine, other), jnp.where(even, other, mine)], axis=axis)
 
 
 def per_device(
@@ -1041,12 +1011,15 @@
         [first_block, jnp.zeros((tokens, -width % 128), BF16), out_w_half], axis=1
     )
     shared_half = jnp.where(even, shared_gate, shared_up)
+    expand_half = lax.dynamic_index_in_dim(
+        expand_weight.reshape(latent_rows, n, 2, -1), half, 2, keepdims=False
+    ).transpose(1, 0, 2)
     first_all, q_blocks, x_blocks, shared_blocks = gather(
         first_block,
         0,
         swaps=(
             column_halves(query_weight, n, half),
-            column_halves(expand_weight, n, half),
+            expand_half,
             shared_half.T.reshape(n, shared_half.shape[1] // n, rows_dev),
         ),
     )
@@ -1065,9 +1038,9 @@
     later_grad, q_blocks = lax.optimization_barrier((output_grad, q_blocks))
     all_out_grad = lax.all_gather(later_grad, "ep", axis=0, tiled=True)
 
-    q_mine, x_mine = columns_in(q_blocks), columns_in(x_blocks)
+    q_mine, x_mine = columns_in(q_blocks), x_blocks.reshape(LATENT, -1)
     query_t = both_halves(q_mine, from_partner(q_mine), even)
-    expand_t = both_halves(x_mine, from_partner(x_mine), even)
+    expand_w = both_halves(x_mine, from_partner(x_mine), even, 1)
     shared_mine = columns_in(shared_blocks)
     shared_other = from_partner(shared_mine)
     gate_t = jnp.where(even, shared_mine, shared_other)
@@ -1085,7 +1058,7 @@
         axis=1,
     )
     normed, query, keys, values, latent = front(
-        first_all, cos_table, sin_table, attn_gain[None], lat_gain[None], turned, latent_turned, expand_t
+        first_all, cos_table, sin_table, attn_gain[None], lat_gain[None], turned, latent_turned, expand_w
     )
     attended_head, attended_exact, lse = attend(prefix_length, query, keys, values)
     (attended_blocks,) = exchange(2, swaps=(attended_head.reshape(n, tokens, VH),))
@@ -1103,6 +1076,11 @@
     mid_unit = residual_mid * mid_scale
     own_ffn_in = (mid_unit * ffn_gain).astype(BF16)
     (ffn_blocks,) = gather(own_ffn_in, 3)
+    query_cols = query_weight.shape[1] // 2
+    query_w_half = lax.dynamic_slice_in_dim(query_weight, half * query_cols, query_cols, 1)
+    query_w_half, ffn_blocks = lax.optimization_barrier((query_w_half, ffn_blocks))
+    query_w_mine = lax.all_gather(query_w_half, "ep", axis=0, tiled=True)
+    query_w_other = from_partner(query_w_mine)
     ffn_in = ffn_blocks.reshape(length, D)
 
     own_lane = (jnp.arange(128, dtype=jnp.int32) == e).astype(F32)[None]
@@ -1186,22 +1164,25 @@
     grad_query_raw, grad_keys, grad_values = attend_back(
         prefix_length, query, grad_att, lse, delta, keys, values
     )
+    grad_query, grad_expanded, latent_partial, rope_partial = back(
+        cos_table, sin_table, grad_query_raw, grad_keys, grad_values, expand_w
+    )
     (
-        grad_query,
-        grad_expanded,
-        latent_partial,
-        rope_partial,
-        normed_partial,
-        gain_partial,
-    ) = back(
-        first_all, cos_table, sin_table, grad_query_raw, grad_keys, grad_values, turned, expand_t
-    )
-    latent_sum, rope_sum, side_gate, side_up, side_down, side_query, side_expand = exchange(
+        latent_sum,
+        rope_sum,
+        query_blocks,
+        side_gate,
+        side_up,
+        side_down,
+        side_query,
+        side_expand,
+    ) = exchange(
         6,
         sums=(
             latent_partial.reshape(n, tokens, LATENT),
             rope_partial.reshape(n, tokens, 2 * ROPE),
         ),
+        swaps=(grad_query.reshape(n, tokens, -1),),
         jobs=(
             (ffn_in, grad_shared_gu.reshape(length, -1), 2),
             (shared_hidden.reshape(length, -1), all_out_grad, 1),
@@ -1235,7 +1216,17 @@
         own_normed, jnp.pad(grad_compressed, ((0, 0), (0, 640 - LATENT - ROPE)))
     ).astype(BF16)
     own_part = product("tc,dc->td", grad_compressed, latent_w)
-    grad_attn_gain = gain_partial[0] + jnp.sum(own_part * input_unit, axis=0)
+
+    def of_heads(part):
+        heads = lax.dynamic_slice_in_dim(query_blocks, part * (n // 2), n // 2, 0)
+        return heads[:, :, : NOPE + ROPE].transpose(1, 0, 2).reshape(tokens, -1)
+
+    grad_normed = (
+        product("tc,dc->td", of_heads(half), query_w_mine)
+        + product("tc,dc->td", of_heads(1 - half), query_w_other)
+        + own_part
+    )
+    grad_attn_gain = jnp.sum(grad_normed * input_unit, axis=0)
 
     def by_owner(values, rows):
         blocks = values.reshape(-1, groups, n, rows).transpose(2, 1, 0, 3)
@@ -1259,7 +1250,6 @@
     else:
         small = lax.psum_scatter(small, "grp", scatter_dimension=0)
     (
-        normed_sum,
         latent_weight_sum,
         small_all,
         query_weight_grad,
@@ -1268,7 +1258,7 @@
         expand_weight_grad,
     ) = exchange(
         7,
-        sums=(normed_partial.reshape(n, tokens, D), latent_w_partial.reshape(n, rows_out, -1)),
+        sums=(latent_w_partial.reshape(n, rows_out, -1),),
         swaps=(
             small[:, None],
             side_query.reshape(n, rows_out, -1),
@@ -1278,7 +1268,6 @@
         ),
         laid=4,
     )
-    grad_normed = normed_sum + own_part
     input_grad = (
         grad_mid + norm_back(grad_normed * attn_gain, input_unit, input_scale)
     ).astype(BF16)

time: 967 us -> 961 us (level)
  Pallas kernels: 766 us -> 719 us
  local copies, waits for them, and re-layouts: 89.5 us -> 108 us
    pallas_call x5, Pallas kernels: 385 us -> 342 us  [exchange(): pl.pallas_call(functools.partial(exchange_kernel, n, m, w, laid, [parts f...]
    pallas_call x1, Pallas kernels: 13.1 us -> 1.42 us  [back(): pl.pallas_call(back_kernel, grid=(length // rows,), in_specs=[rows_of(a.s...]
    dot_general x12 -> x14, matrix products: 32 us -> 41.3 us  [product(): return jnp.einsum(form, left, right, preferred_element_type=F32)]
    unnamed x137 -> x149, local copies, waits for them, and re-layouts: 27.5 us -> 31.4 us
  transfers between devices with their start and end apart: 18 -> 20, of which waited for: 0 -> 0; matrix products, arithmetic and copies ran while one was open for 13% -> 17% of each run, Pallas kernels for 38% -> 60%
where the time goes in v7:
time: 961 us; the launch traced here: 950 us
  Pallas kernels  719 us (75%)
  local copies, waits for them, and re-layouts  108 us (11%)
  other arithmetic  52.8 us (5%)
  matrix products  41.3 us (4%)
  between operations  15.7 us (2%)
  starting transfers between devices  12.6 us (1%)
    pallas_call x5, Pallas kernels, exchange(): pl.pallas_call(functools.partial(exchange_kernel, n, m, w, laid, [parts f...  342 us
    pallas_call x2, Pallas kernels, gather(): pl.pallas_call(functools.partial(gather_kernel, n, w), out_shape=[jax.Sha...  241 us
    pallas_call x1, Pallas kernels, ffn(): pl.pallas_call(functools.partial(ffn_kernel, n), grid=(n // group,), in_s...  85.8 us
    dot_general x14, matrix products, product(): return jnp.einsum(form, left, right, preferred_element_type=F32)  41.3 us
    unnamed x149, local copies, waits for them, and re-layouts  31.4 us
  transfers between devices with their start and end apart: 20, of which 0 were waited for; matrix products, arithmetic and copies ran while one was open for 17% of the time, Pallas kernels for 60%

profile of v7, /device:TPU:0, one launch (start us, length us, event | category | flops | bytes accessed | tf_op | source)
XLA Modules:
  0.0 950.0 jit_solution(10653503717241124753)
XLA Ops:
  23.1 145.4 %gather.2 = (bf16[16,128,3712]{2,1,0:T(8,128)(2,1)}, bf16[16,96,128]{2,1,0:T(8,128)(2,1)}, bf16[16,32,128]{2,1,0:T(8,128)(2,1)}, bf16[16,176,128]{2,1,0:T(8,128)(2,1)}) custom-call(bf16[128,3712]{1,0:T(8,128)(2,1)} %concatenate.29.x_ref, bf16[16,96,128]{2,1,0:T(8,128)(2,1)} %dynamic-slice_bitcast_fusion.11.refs_0_, bf16[16,32,128]{2,1,0:T(8,128)(2,1)} %bitcast.256, ...), custom_call_target="tpu_custom_call" | custom-call | tf_op jit(solution)/shard_map/gather/pallas_call | solution.py:207
  170.5 4.8 slice.106
  175.3 3.7 slice.103
  190.1 17.5 %front.1 = (bf16[2048,2048]{1,0:T(8,128)(2,1)}, bf16[2048,256]{1,0:T(8,128)(2,1)S(1)}, bf16[2048,256]{1,0:T(8,128)(2,1)S(1)}, bf16[2048,128]{1,0:T(8,128)(2,1)S(1)}, bf16[2048,512]{1,0:T(8,128)(2,1)}) custom-call(bf16[16,128,3712]{2,1,0:T(8,128)(2,1)} %get-tuple-element.73.x_ref, f32[2048,128]{1,0:T(8,128)S(1)} %bitcast.192, ...), custom_call_target="tpu_custom_call" | custom-call | tf_op jit(solution)/shard_map/front/pallas_call | solution.py:561
  213.6 13.8 %attend.1 = (bf16[2048,128]{1,0:T(8,128)(2,1)S(1)}, f32[2048,128]{1,0:T(8,128)S(1)}, f32[1,2048]{1,0:T(1,128)S(1)}) custom-call(s32[1]{0:T(128)S(6)} %copy.85.prefix_ref, bf16[2048,256]{1,0:T(8,128)(2,1)S(1)} %get-tuple-element.77.q_ref, bf16[4,512,256]{2,1,0:T(8,128)(2,1)S(1)} %bitcast.198, bf16[4,128,512]{2,1,0:T(8,128)(2,1)S(1)} %copy-done.10), custom_call_target="tpu_custom_call" | custom-call | tf_op jit(solution)/shard_map/attend/pallas_call | solution.py:665
  229.3 20.2 %exchange.5 = bf16[16,128,128]{2,1,0:T(8,128)(2,1)} custom-call(bf16[16,128,128]{2,1,0:T(8,128)(2,1)} %bitcast.210), custom_call_target="tpu_custom_call" | custom-call | tf_op jit(solution)/shard_map/exchange/pallas_call | solution.py:445
  251.5 3.1 convolution_bitcast_fusion
  254.7 3.0 broadcast_select_fusion.5
  260.8 96.0 %gather.3.x_ref = bf16[16,128,2048]{2,1,0:T(8,128)(2,1)} custom-call(bf16[128,2048]{1,0:T(8,128)(2,1)} %multiply_convert_fusion.x_ref), custom_call_target="tpu_custom_call" | custom-call | tf_op jit(solution)/shard_map/gather/pallas_call | solution.py:207
  365.3 2.3 pad.22.sd_ref
  373.6 85.8 %ffn.1 = (bf16[16,128,2048]{2,1,0:T(8,128)(2,1)}, bf16[16,128,2048]{2,1,0:T(8,128)(2,1)}, bf16[16,128,128]{2,1,0:T(8,128)(2,1)}, f32[16,128,128]{2,1,0:T(8,128)}...) custom-call(bf16[16,128,2048]{2,1,0:T(8,128)(2,1)} %gather.3.x_ref, ...), custom_call_target="tpu_custom_call" | custom-call | tf_op jit(solution)/shard_map/ffn/pallas_call | solution.py:866
  459.4 166.1 %exchange.6 = (f32[128,2048]{1,0:T(8,128)}, f32[128,128]{1,0:T(8,128)}, f32[128,2048]{1,0:T(8,128)}, bf16[1408,2048]{1,0:T(8,128)(2,1)}, bf16[2048,1408]{1,0:T(8,128)(2,1)}, /*index=5*/bf16[2048,1408]{1,0:T(8,128)(2,1)}) custom-call(bf16[4,2,2,128,2048]{4,3,2,1,0:T(8,128)(2,1)} %bitcast.225, bf16[4,2,2,128,128]{4,3,2,1,0:T(8,128)(2,1)} %bitcast.255, ...), custom_call_target="tpu_custom_call" | custom-call | tf_op jit(solution)/shard_map/exchange/pallas_call | solution.py:445
  632.7 3.3 convolution_convert_fusion
  636.0 3.6 dynamic-slice_bitcast_fusion.1
  640.2 3.9 dynamic-slice_bitcast_fusion
  645.3 3.6 dynamic-slice_bitcast_fusion.2
  656.2 3.9 fusion.34
  660.1 4.5 fusion.3
  664.6 5.9 fusion.1
  670.5 5.4 add_convert_fusion
  680.0 13.1 %exchange.7 = bf16[16,128,128]{2,1,0:T(8,128)(2,1)} custom-call(bf16[16,128,128]{2,1,0:T(8,128)(2,1)} %bitcast.246), custom_call_target="tpu_custom_call" | custom-call | tf_op jit(solution)/shard_map/exchange/pallas_call | solution.py:445
  693.1 6.4 fusion
  699.5 5.9 fusion.2
  705.8 17.0 %attend_back.1 = (f32[2048,256]{1,0:T(8,128)S(1)}, f32[4,512,256]{2,1,0:T(8,128)S(1)}, f32[4,512,128]{2,1,0:T(8,128)S(1)}) custom-call(s32[1]{0:T(128)S(6)} %copy.85.prefix_ref, bf16[2048,256]{1,0:T(8,128)(2,1)S(1)} %get-tuple-element.77.q_ref, bf16[2048,128]{1,0:T(8,128)(2,1)S(1)} %bitcast.196, f32[1,2048]{1,0:T(1,128)S(1)} %get-tuple-element.98.lse_ref, ...), custom_call_target="tpu_custom_call" | custom-call | tf_op jit(solution)/shard_map/attend_back/pallas_call | solution.py:723
  728.4 88.2 %exchange.8 = (f32[128,512]{1,0:T(8,128)}, f32[128,128]{1,0:T(8,128)}, bf16[16,128,256]{2,1,0:T(8,128)(2,1)}, bf16[2048,256]{1,0:T(8,128)(2,1)}, bf16[2048,256]{...) custom-call(bf16[4,2,2,128,512]{4,3,2,1,0:T(8,128)(2,1)} %bitcast.200, ...), custom_call_target="tpu_custom_call" | custom-call | tf_op jit(solution)/shard_map/exchange/pallas_call | solution.py:445
  820.8 2.3 dynamic-slice_bitcast_fusion.5
  833.5 5.2 fusion.63
  846.5 5.2 convolution_add_fusion.3
  851.8 2.6 fusion.16
  858.4 8.2 collective-permute-start.7
  867.2 3.8 fusion.15
  871.1 54.7 %exchange.9 = (f32[64,640]{1,0:T(8,128)S(1)}, f32[16,1,1168]{2,1,0:T(1,128)S(1)}, f32[64,3072]{1,0:T(8,128)S(1)}, f32[64,2816]{1,0:T(8,128)S(1)}, f32[64,2816]{1,0:T(8,128)S(1)}, /*index=5*/f32[16,4096]{1,0:T(8,128)S(1)}) custom-call(bf16[4,2,2,64,640]{4,3,2,1,0:T(8,128)(2,1)S(1)} %bitcast.195, f32[16,1,1168]{2,1,0:T(1,128)S(1)} %broadcast_in_dim.33.refs_1_, ...), custom_call_target="tpu_custom_call" | custom-call | tf_op jit(solution)/shard_map/exchange/pallas_call | solution.py:445
  (298 shorter events, 125.9 us)
Async XLA Ops:
  7.2 14.7 %copy-start = (bf16[128,2048]{1,0:T(8,128)(2,1)S(1)}, bf16[128,2048]{1,0:T(8,128)(2,1)}, u32[]{:S(2)}) copy-start(bf16[128,2048]{1,0:T(8,128)(2,1)} %param.24) | copy-start | bytes 1572868
  7.2 13.5 %copy-start.51 = (bf16[128,2816]{1,0:T(8,128)(2,1)S(1)}, bf16[128,2816]{1,0:T(8,128)(2,1)}, u32[]{:S(2)}) copy-start(bf16[128,2816]{1,0:T(8,128)(2,1)} %param.27) | copy-start | bytes 2162692
  7.2 13.5 %copy-start.52 = (bf16[128,2816]{1,0:T(8,128)(2,1)S(1)}, bf16[128,2816]{1,0:T(8,128)(2,1)}, u32[]{:S(2)}) copy-start(bf16[128,2816]{1,0:T(8,128)(2,1)} %param.28) | copy-start | bytes 2162692
  7.2 366.4 %all-gather.3.cloned.1.call-start = ((), (), s32[]{:S(2)}) async-start(), calls=%async_computation.1 | async-start | bytes 8912896 | tf_op jit(solution)/shard_map/all_gather | solution.py:1039
  7.3 14.6 %copy-start.28 = (bf16[128,2048]{1,0:T(8,128)(2,1)S(1)}, bf16[128,2048]{1,0:T(8,128)(2,1)}, u32[]{:S(2)}) copy-start(bf16[128,2048]{1,0:T(8,128)(2,1)} %param.18) | copy-start | bytes 1572868
  168.6 496.0 %all-gather.5.cloned.1.call-start = ((), (), s32[]{:S(2)}) async-start(), calls=%async_computation.2 | async-start | bytes 6684672 | tf_op jit(solution)/shard_map/all_gather | solution.py:1082
  168.8 19.8 %collective-permute-start.1 = (bf16[512,128]{1,0:T(8,128)(2,1)}, bf16[512,128]{1,0:T(8,128)(2,1)S(1)}, u32[]{:S(2)}, u32[]{:S(2)}) collective-permute-start(bf16[512,128]{1,0:T(8,128)(2,1)} %bitcast.263), channel_id=1, source_target_pairs={{0,16},{16,0},{1,17},{17,1},{2,18},{18,2},{3,19},{19,3},{4,20},{20... | collective-permute-start | bytes 393224 | tf_op jit(solution)/shard_map/ppermute | solution.py:499
  169.9 18.8 %collective-permute-start = (bf16[96,2048]{1,0:T(8,128)(2,1)S(1)}, bf16[96,2048]{1,0:T(8,128)(2,1)}, u32[]{:S(2)}, u32[]{:S(2)}) collective-permute-start(bf16[96,2048]{1,0:T(8,128)(2,1)S(1)} %copy_bitcast_fusion.1), channel_id=1, source_target_pairs={{0,16},{16,0},{1,17},{17,1},{2,18},{18,2},{3,19},{19,3},{4,20},{20... | collective-permute-start | bytes 1179656 | tf_op jit(solution)/shard_map/ppermute | solution.py:499
  175.3 79.4 %collective-permute-start.2 = (bf16[2048,1024]{1,0:T(8,128)(2,1)}, bf16[2048,1024]{1,0:T(8,128)(2,1)}, u32[]{:S(2)}, u32[]{:S(2)}) collective-permute-start(bf16[2048,1024]{1,0:T(8,128)(2,1)} %bitcast.22), channel_id=1, source_target_pairs={{0,16},{16,0},{1,17},{17,1},{2,18},{18,2},{3,19},{19,3},{4,20},{20... | collective-permute-start | bytes 12582920 | tf_op jit(solution)/shard_map/ppermute | solution.py:499
  179.7 77.9 %copy-start.66 = (f32[128]{0:T(128)}, f32[128]{0:T(128)S(1)}, u32[]{:S(2)}) copy-start(f32[128]{0:T(128)S(1)} %add_rsqrt_fusion.1) | copy-start | bytes 1540
  258.8 98.0 %copy-start.64 = (f32[128]{0:T(128)}, f32[128]{0:T(128)S(1)}, u32[]{:S(2)}) copy-start(f32[128]{0:T(128)S(1)} %add_rsqrt_fusion.2) | copy-start | bytes 1540
  356.8 576.5 %reduce-scatter.2.cloned.1.call-start = ((), (), s32[]{:S(2)}) async-start(), calls=%async_computation.3 | async-start | bytes 4456448 | tf_op jit(solution)/shard_map/reduce_scatter | solution.py:1158
  358.9 10.8 %collective-permute-start.3 = (bf16[176,2048]{1,0:T(8,128)(2,1)}, bf16[176,2048]{1,0:T(8,128)(2,1)}, u32[]{:S(2)}, u32[]{:S(2)}) collective-permute-start(bf16[176,2048]{1,0:T(8,128)(2,1)} %copy_bitcast_fusion), channel_id=1, source_target_pairs={{0,16},{16,0},{1,17},{17,1},{2,18},{18,2},{3,19},{19,3},{4,20},{20... | collective-permute-start | bytes 2162696 | tf_op jit(solution)/shard_map/ppermute | solution.py:499
  459.4 169.1 %copy-start.40 = (bf16[16,128,16]{2,1,0:T(8,128)(2,1)S(1)}, bf16[16,128,16]{2,1,0:T(8,128)(2,1)}, u32[]{:S(2)}) copy-start(bf16[16,128,16]{2,1,0:T(8,128)(2,1)} %slice.109) | copy-start | bytes 196612
  459.4 169.0 %copy-start.65 = (f32[128]{0:T(128)S(1)}, f32[128]{0:T(128)}, u32[]{:S(2)}) copy-start(f32[128]{0:T(128)} %copy-done.64) | copy-start | bytes 1540
  636.0 34.6 %collective-permute-start.4 = (bf16[1024,2048]{1,0:T(8,128)(2,1)}, bf16[1024,2048]{1,0:T(8,128)(2,1)}, u32[]{:S(2)}, u32[]{:S(2)}) collective-permute-start(bf16[1024,2048]{1,0:T(8,128)(2,1)} %convolution_convert_fusion), channel_id=1, source_target_pairs={{0,16},{16,0},{1,17},{17,1},{2,18},{18,2},{3,19},{19,3},{4,20},{20... | collective-permute-start | bytes 12582920 | tf_op jit(solution)/shard_map/ppermute | solution.py:493
  639.6 25.1 %collective-permute-start.15 = (bf16[1024,1408]{1,0:T(8,128)(2,1)}, bf16[1024,1408]{1,0:T(8,128)(2,1)}, u32[]{:S(2)}, u32[]{:S(2)}) collective-permute-start(bf16[1024,1408]{1,0:T(8,128)(2,1)} %dynamic-slice_bitcast_fusion.1), channel_id=1, source_target_pairs={{0,16},{16,0},{1,17},{17,1},{2,18},{18,2},{3,19},{19,3},{4,20},{20... | collective-permute-start | bytes 8650760 | tf_op jit(solution)/shard_map/ppermute | solution.py:473
  640.1 189.5 %copy-start.63 = (f32[512]{0:T(512)}, f32[512]{0:T(512)S(1)}, u32[]{:S(2)}) copy-start(f32[512]{0:T(512)S(1)} %reshape.481) | copy-start | bytes 6148
  644.1 49.0 %collective-permute-start.16 = (bf16[704,2048]{1,0:T(8,128)(2,1)}, bf16[704,2048]{1,0:T(8,128)(2,1)}, u32[]{:S(2)}, u32[]{:S(2)}) collective-permute-start(bf16[704,2048]{1,0:T(8,128)(2,1)} %dynamic-slice_bitcast_fusion), channel_id=1, source_target_pairs={{0,16},{16,0},{1,17},{17,1},{2,18},{18,2},{3,19},{19,3},{4,20},{20... | collective-permute-start | bytes 8650760 | tf_op jit(solution)/shard_map/ppermute | solution.py:473
  648.9 50.6 %collective-permute-start.14 = (bf16[1024,1408]{1,0:T(8,128)(2,1)}, bf16[1024,1408]{1,0:T(8,128)(2,1)}, u32[]{:S(2)}, u32[]{:S(2)}) collective-permute-start(bf16[1024,1408]{1,0:T(8,128)(2,1)} %dynamic-slice_bitcast_fusion.2), channel_id=1, source_target_pairs={{0,16},{16,0},{1,17},{17,1},{2,18},{18,2},{3,19},{19,3},{4,20},{20... | collective-permute-start | bytes 8650760 | tf_op jit(solution)/shard_map/ppermute | solution.py:473
  649.4 180.2 %copy-start.69 = (f32[128]{0:T(128)}, f32[128]{0:T(128)S(1)}, u32[]{:S(2)}) copy-start(f32[128]{0:T(128)S(1)} %add_rsqrt_fusion) | copy-start | bytes 1540
  664.6 181.9 %collective-permute-start.5 = (bf16[2048,1536]{1,0:T(8,128)(2,1)}, bf16[2048,1536]{1,0:T(8,128)(2,1)}, u32[]{:S(2)}, u32[]{:S(2)}) collective-permute-start(bf16[2048,1536]{1,0:T(8,128)(2,1)} %all-gather.5.cloned.1.call-done), channel_id=1, source_target_pairs={{0,16},{16,0},{1,17},{17,1},{2,18},{18,2},{3,19},{19,3},{4,20},{20... | collective-permute-start | bytes 18874376 | tf_op jit(solution)/shard_map/ppermute | solution.py:499
  818.7 21.3 %collective-permute-start.12 = (bf16[88,2048]{1,0:T(8,128)(2,1)}, bf16[88,2048]{1,0:T(8,128)(2,1)}, u32[]{:S(2)}, u32[]{:S(2)}) collective-permute-start(bf16[88,2048]{1,0:T(8,128)(2,1)} %dynamic-slice_bitcast_fusion.12), channel_id=1, source_target_pairs={{0,16},{16,0},{1,17},{17,1},{2,18},{18,2},{3,19},{19,3},{4,20},{20... | collective-permute-start | bytes 1081352 | tf_op jit(solution)/shard_map/ppermute | solution.py:473
  820.3 18.6 %collective-permute-start.11 = (bf16[256,256]{1,0:T(8,128)(2,1)}, bf16[256,256]{1,0:T(8,128)(2,1)}, u32[]{:S(2)}, u32[]{:S(2)}) collective-permute-start(bf16[256,256]{1,0:T(8,128)(2,1)} %dynamic-slice_bitcast_fusion.13), channel_id=1, source_target_pairs={{0,16},{16,0},{1,17},{17,1},{2,18},{18,2},{3,19},{19,3},{4,20},{20... | collective-permute-start | bytes 393224 | tf_op jit(solution)/shard_map/ppermute | solution.py:473
  823.0 18.5 %collective-permute-start.10 = (bf16[1024,256]{1,0:T(8,128)(2,1)}, bf16[1024,256]{1,0:T(8,128)(2,1)}, u32[]{:S(2)}, u32[]{:S(2)}) collective-permute-start(bf16[1024,256]{1,0:T(8,128)(2,1)} %get-tuple-element.146), channel_id=1, source_target_pairs={{0,16},{16,0},{1,17},{17,1},{2,18},{18,2},{3,19},{19,3},{4,20},{20... | collective-permute-start | bytes 1572872 | tf_op jit(solution)/shard_map/ppermute | solution.py:473
  824.1 19.6 %collective-permute-start.9 = (bf16[1024,256]{1,0:T(8,128)(2,1)}, bf16[1024,256]{1,0:T(8,128)(2,1)}, u32[]{:S(2)}, u32[]{:S(2)}) collective-permute-start(bf16[1024,256]{1,0:T(8,128)(2,1)} %get-tuple-element.148), channel_id=1, source_target_pairs={{0,16},{16,0},{1,17},{17,1},{2,18},{18,2},{3,19},{19,3},{4,20},{20... | collective-permute-start | bytes 1572872 | tf_op jit(solution)/shard_map/ppermute | solution.py:473
  838.9 7.1 collective-permute-start.6
  840.0 4.9 collective-permute-start.8
  841.5 3.5 collective-permute-start.13
  857.4 13.6 %copy-start.54 = (f32[16,2,1168]{2,0,1:T(8,128)S(1)}, f32[16,2,1168]{2,0,1:T(8,128)}, u32[]{:S(2)}) copy-start(f32[16,2,1168]{2,0,1:T(8,128)} %concatenate.36) | copy-start | bytes 448516
  858.4 12.6 %collective-permute-start.7 = (f32[16,1168]{1,0:T(8,128)S(1)}, f32[16,1168]{1,0:T(8,128)S(1)}, u32[]{:S(2)}, u32[]{:S(2)}) collective-permute-start(f32[16,1168]{1,0:T(8,128)S(1)} %dynamic-slice_bitcast_fusion.14), channel_id=1, source_target_pairs={{0,16},{16,0},{1,17},{17,1},{2,18},{18,2},{3,19},{19,3},{4,20},{20... | collective-permute-start | bytes 224264 | tf_op jit(solution)/shard_map/ppermute | solution.py:1249
  871.1 72.1 %copy-start.1 = (bf16[128,2048]{1,0:T(8,128)(2,1)S(1)}, bf16[128,2048]{1,0:T(8,128)(2,1)}, u32[]{:S(2)}) copy-start(bf16[128,2048]{1,0:T(8,128)(2,1)} %param.24) | copy-start | bytes 1572868
  (58 other events, 225.0 us)
Sparse Core Ops, SparseCore 0:
  168.7 127.2 all-gather.2
  356.9 93.4 all-gather.4
  693.2 131.3 reduce-scatter.1

commit v8 on v7

--- a/solution.py
+++ b/solution.py
@@ -233,7 +233,7 @@
 TILE = 128
 
 
-def exchange_kernel(n, m, w, laid, jobs, *refs):
+def exchange_kernel(n, m, w, laid, groups, jobs, *refs):
     refs = list(refs)
 
     def take(count):
@@ -243,7 +243,7 @@
 
     sums_in, swaps_in = take(m), take(w)
     jobs_in = [take(2) for _ in jobs]
-    sums_out, swaps_out, jobs_out = take(m), take(w), [take(parts) for parts in jobs]
+    sums_out, swaps_out, jobs_out = take(m), take(w), [take(parts * blocks) for parts, blocks in jobs]
     room = [take(7) for _ in range(m)]
     sems = [take(8) for _ in range(m)]
     swap_sems = take(3) if w else None
@@ -328,14 +328,35 @@
         for i, (src, dst) in enumerate(((left, left_v), (right, right_v))):
             loads.append(pltpu.make_async_copy(src, dst, in_sem.at[i]))
 
-    def writes(j, i):
+    def pieces(j):
+        parts, blocks = jobs[j]
+        rows = jobs_out[j][0].shape[0]
+        piece = math.gcd(TILE, rows)
+        return [(q * piece, piece) for q in range(TILE // piece)]
+
+    def start_write(j, i, part):
         left_v, right_v, page, in_sem, out_sem = desks[j]
-        slot = i % 2
-        rows = pl.ds(pl.multiple_of(i * TILE, TILE), TILE)
-        return [
-            pltpu.make_async_copy(page.at[slot, part], out.at[rows], out_sem.at[slot, part])
-            for part, out in enumerate(jobs_out[j])
-        ]
+        parts, blocks = jobs[j]
+        outs = jobs_out[j][part * blocks : (part + 1) * blocks]
+        rows = outs[0].shape[0]
+        for q, (offset, piece) in enumerate(pieces(j)):
+            row = i * TILE + offset
+            src = page.at[i % 2, part, pl.ds(offset, piece)]
+            owner = (row // rows + blocks - (lax.axis_index("grp") if blocks > 1 else 0)) % blocks
+            inside = pl.ds(pl.multiple_of(row % rows, piece), piece)
+            for k, out in enumerate(outs):
+                copy = pltpu.make_async_copy(src, out.at[inside], out_sem.at[i % 2, part, q])
+                if blocks > 1:
+                    pl.when(owner == k)(copy.start)
+                else:
+                    copy.start()
+
+    def wait_write(j, i, part):
+        left_v, right_v, page, in_sem, out_sem = desks[j]
+        for q, (offset, piece) in enumerate(pieces(j)):
+            src = page.at[i % 2, part, pl.ds(offset, piece)]
+            out = jobs_out[j][part * jobs[j][1]].at[pl.ds(0, piece)]
+            pltpu.make_async_copy(src, out, out_sem.at[i % 2, part, q]).wait()
 
     def tile(j, i):
         left_v, right_v, page, in_sem, out_sem = desks[j]
@@ -346,10 +367,10 @@
             preferred_element_type=F32,
         ).astype(page.dtype)
         width = page.shape[3]
-        for part, write in enumerate(writes(j, i)):
-            pl.when(i >= 2)(write.wait)
+        for part in range(jobs[j][0]):
+            pl.when(i >= 2)(functools.partial(wait_write, j, i, part))
             page[i % 2, part] = value[:, part * width : (part + 1) * width]
-            write.start()
+            start_write(j, i, part)
 
     tiles = [desk[0].shape[1] // TILE for desk in desks]
     loaded = []
@@ -414,13 +435,14 @@
         copy.wait_send()
     for j in range(len(jobs)):
         for i in range(min(2, tiles[j])):
-            for write in writes(j, i):
-                write.wait()
+            for part in range(jobs[j][0]):
+                wait_write(j, i, part)
 
 
 def exchange(cid, sums=(), swaps=(), laid=0, jobs=()):
     n = lax.axis_size("ep")
     nz = n // 4
+    groups = lax.axis_size("grp")
     m, w = len(sums), len(swaps)
     kept_rows = [p.shape[1] for p in sums]
     sums = [jnp.pad(p, ((0, 0), (0, -p.shape[1] % 32), (0, 0))) for p in sums]
@@ -438,25 +460,24 @@
         scratch += [DMA((w,)), DMA((w, n)), DMA((w, n))]
     plain, wide = swaps[: w - laid], swaps[w - laid :]
     scratch += [pltpu.VMEM(a.shape, a.dtype) for a in wide]
-    for left, right, parts in jobs:
+    jobs_out = []
+    for left, right, parts, blocks in jobs:
+        rows, cols = left.shape[1] // blocks, right.shape[1] // parts
+        jobs_out += [jax.ShapeDtypeStruct((rows, cols), BF16)] * (parts * blocks)
         scratch += [pltpu.VMEM(left.shape, left.dtype), pltpu.VMEM(right.shape, right.dtype)]
-        scratch += [pltpu.VMEM((2, parts, TILE, right.shape[1] // parts), BF16)]
-        scratch += [DMA((2,)), DMA((2, parts))]
+        scratch += [pltpu.VMEM((2, parts, TILE, cols), BF16), DMA((2,))]
+        scratch += [DMA((2, parts, TILE // math.gcd(TILE, rows)))]
     out = pl.pallas_call(
-        functools.partial(exchange_kernel, n, m, w, laid, [parts for _, _, parts in jobs]),
+        functools.partial(exchange_kernel, n, m, w, laid, groups, [job[2:] for job in jobs]),
         out_shape=[jax.ShapeDtypeStruct(p.shape[1:], F32) for p in sums]
         + [jax.ShapeDtypeStruct(a.shape, a.dtype) for a in plain]
         + [jax.ShapeDtypeStruct((a.shape[1], n * a.shape[2]), F32) for a in wide]
-        + [
-            jax.ShapeDtypeStruct((a.shape[1], b.shape[1] // parts), BF16)
-            for a, b, parts in jobs
-            for _ in range(parts)
-        ],
+        + jobs_out,
         in_specs=[ANY] * (m + w + 2 * len(jobs)),
         out_specs=[pl.BlockSpec(memory_space=pltpu.VMEM)] * m
         + [ANY] * (w - laid)
         + [pl.BlockSpec(memory_space=pltpu.VMEM)] * laid
-        + [ANY] * sum(parts for _, _, parts in jobs),
+        + [ANY] * len(jobs_out),
         scratch_shapes=scratch,
         compiler_params=pltpu.CompilerParams(
             collective_id=cid, has_side_effects=True, vmem_limit_bytes=(60 if jobs else 40) << 20 if m else None
@@ -1035,8 +1056,7 @@
 
     out_w_mine = first_all[:, :, -(D // 2) :].reshape(D, D // 2)
     out_w_other = from_partner(out_w_mine)
-    later_grad, q_blocks = lax.optimization_barrier((output_grad, q_blocks))
-    all_out_grad = lax.all_gather(later_grad, "ep", axis=0, tiled=True)
+    all_out_grad = lax.all_gather(output_grad, "ep", axis=0, tiled=True)
 
     q_mine, x_mine = columns_in(q_blocks), x_blocks.reshape(LATENT, -1)
     query_t = both_halves(q_mine, from_partner(q_mine), even)
@@ -1118,19 +1138,26 @@
         expert_up[0],
         expert_down[0],
     )
-    ffn_sum, dot_sum, out_sum, grad_down_m, grad_gate_m, grad_up_m = exchange(
+    ffn_sum, dot_sum, out_sum, *products = exchange(
         4,
         sums=(ffn_partial, dot_partial, out_partial),
-        jobs=((expert_hidden, slot_grad, 1), (incoming, grad_expert_gu, 2)),
+        jobs=((expert_hidden, slot_grad, 1, groups), (incoming, grad_expert_gu, 2, groups)),
     )
     layer_output = (residual_mid + out_sum).astype(BF16)
 
     def by_group(values):
         return over_groups(values.reshape(groups, values.shape[0] // groups, -1))
 
-    expert_down_grad = by_group(grad_down_m)[None]
-    expert_gate_grad = by_group(grad_gate_m)[None]
-    expert_up_grad = by_group(grad_up_m)[None]
+    def blocks_over_groups(blocks):
+        total = blocks[0].astype(F32)
+        for k in range(1, groups):
+            shift = [(g, (g + k) % groups) for g in range(groups)]
+            total = total + lax.ppermute(blocks[k], "grp", shift).astype(F32)
+        return total
+
+    expert_down_grad, expert_gate_grad, expert_up_grad = (
+        blocks_over_groups(products[k * groups : (k + 1) * groups])[None] for k in range(3)
+    )
 
     router_own = lax.dynamic_index_in_dim(router_all, e, 0, keepdims=False)[:, :n]
     grad_probs = dot_sum[:, :n]
@@ -1151,9 +1178,6 @@
     (grad_att_blocks,) = exchange(
         5, swaps=(grad_attended.reshape(tokens, HEADS, VH).transpose(1, 0, 2),)
     )
-    output_w_partial, grad_att_blocks = lax.optimization_barrier(
-        (output_w_partial, grad_att_blocks)
-    )
     grad_att = grad_att_blocks.reshape(length, VH)
     output_weight_grad = lax.psum_scatter(
         output_w_partial.reshape(n, rows_out, D), "ep", scatter_dimension=0
@@ -1171,11 +1195,8 @@
         latent_sum,
         rope_sum,
         query_blocks,
-        side_gate,
-        side_up,
         side_down,
-        side_query,
-        side_expand,
+        *products,
     ) = exchange(
         6,
         sums=(
@@ -1184,17 +1205,18 @@
         ),
         swaps=(grad_query.reshape(n, tokens, -1),),
         jobs=(
-            (ffn_in, grad_shared_gu.reshape(length, -1), 2),
-            (shared_hidden.reshape(length, -1), all_out_grad, 1),
-            (normed, grad_query, 1),
-            (latent, grad_expanded, 1),
+            (shared_hidden.reshape(length, -1), all_out_grad, 1, 1),
+            (ffn_in, grad_shared_gu.reshape(length, -1), 2, groups),
+            (normed, grad_query, 1, groups),
+            (latent, grad_expanded, 1, groups),
         ),
     )
     shared_down_grad = to_row_owner(by_group(side_down[:shared_width]))
-    side_gate = by_group(side_gate)[:, :shared_width].astype(BF16)
-    side_up = by_group(side_up)[:, :shared_width].astype(BF16)
-    side_query = by_group(side_query)[:, : query_t.shape[0]].astype(BF16)
-    grad_expand = by_group(side_expand).astype(BF16)
+    side_gate, side_up, side_query, grad_expand = (
+        blocks_over_groups(products[k * groups : (k + 1) * groups]).astype(BF16) for k in range(4)
+    )
+    side_gate, side_up = side_gate[:, :shared_width], side_up[:, :shared_width]
+    side_query = side_query[:, : query_t.shape[0]]
 
     own_normed = (input_unit * attn_gain).astype(BF16)
     own_raw = product("td,dc->tc", own_normed, latent_w[:, :LATENT])

time: 961 us -> 996 us (1.036)
  Pallas kernels: 719 us -> 758 us
  local copies, waits for them, and re-layouts: 108 us -> 94.4 us
    pallas_call x2, Pallas kernels: 241 us -> 296 us  [gather(): pl.pallas_call(functools.partial(gather_kernel, n, w), out_shape=[jax.Sha...]
    squeeze x8 -> x1, local copies, waits for them, and re-layouts: 16.9 us -> 0.77 us  [both(): theirs = lax.dynamic_index_in_dim(p, 1 - g, 0, keepdims=False)]
    pallas_call x5, Pallas kernels: 342 us -> 329 us  [exchange(): pl.pallas_call(functools.partial(exchange_kernel, n, m, w, laid, groups,...]
    unnamed x149 -> x121, local copies, waits for them, and re-layouts: 31.4 us -> 33.9 us
  transfers between devices with their start and end apart: 20 -> 20, of which waited for: 0 -> 0; matrix products, arithmetic and copies ran while one was open for 17% -> 16% of each run, Pallas kernels for 60% -> 77%
where the time goes in v8:
time: 996 us; the launch traced here: 980 us
  Pallas kernels  758 us (76%)
  local copies, waits for them, and re-layouts  94.4 us (9%)
  other arithmetic  53.1 us (5%)
  matrix products  44.4 us (4%)
  between operations  15.6 us (2%)
  starting transfers between devices  13.8 us (1%)
    pallas_call x5, Pallas kernels, exchange(): pl.pallas_call(functools.partial(exchange_kernel, n, m, w, laid, groups,...  329 us
    pallas_call x2, Pallas kernels, gather(): pl.pallas_call(functools.partial(gather_kernel, n, w), out_shape=[jax.Sha...  296 us
    pallas_call x1, Pallas kernels, ffn(): pl.pallas_call(functools.partial(ffn_kernel, n), grid=(n // group,), in_s...  85.4 us
    dot_general x14, matrix products, product(): return jnp.einsum(form, left, right, preferred_element_type=F32)  44.4 us
    unnamed x121, local copies, waits for them, and re-layouts  33.9 us
  transfers between devices with their start and end apart: 20, of which 0 were waited for; matrix products, arithmetic and copies ran while one was open for 16% of the time, Pallas kernels for 77%

profile of v8, /device:TPU:0, one launch (start us, length us, event | category | flops | bytes accessed | tf_op | source)
XLA Modules:
  0.0 980.1 jit_solution(17810335674799611008)
XLA Ops:
  21.8 218.3 %gather.2 = (bf16[16,128,3712]{2,1,0:T(8,128)(2,1)}, bf16[16,96,128]{2,1,0:T(8,128)(2,1)}, bf16[16,32,128]{2,1,0:T(8,128)(2,1)}, bf16[16,176,128]{2,1,0:T(8,128)(2,1)}) custom-call(bf16[128,3712]{1,0:T(8,128)(2,1)} %concatenate.29.x_ref, bf16[16,96,128]{2,1,0:T(8,128)(2,1)} %dynamic-slice_bitcast_fusion.2.refs_0_, bf16[16,32,128]{2,1,0:T(8,128)(2,1)} %bitcast.205, ...), custom_call_target="tpu_custom_call" | custom-call | tf_op jit(solution)/shard_map/gather/pallas_call | solution.py:207
  241.8 4.8 slice.103
  246.6 3.7 slice.100
  253.9 2.1 pad_maximum_fusion.wl_ref
  261.5 17.5 %front.1 = (bf16[2048,2048]{1,0:T(8,128)(2,1)}, bf16[2048,256]{1,0:T(8,128)(2,1)S(1)}, bf16[2048,256]{1,0:T(8,128)(2,1)S(1)}, bf16[2048,128]{1,0:T(8,128)(2,1)S(1)}, bf16[2048,512]{1,0:T(8,128)(2,1)}) custom-call(bf16[16,128,3712]{2,1,0:T(8,128)(2,1)} %get-tuple-element.76.x_ref, f32[2048,128]{1,0:T(8,128)S(1)} %bitcast.150, ...), custom_call_target="tpu_custom_call" | custom-call | tf_op jit(solution)/shard_map/front/pallas_call | solution.py:582
  285.2 12.7 %attend.1 = (bf16[2048,128]{1,0:T(8,128)(2,1)S(1)}, f32[2048,128]{1,0:T(8,128)S(1)}, f32[1,2048]{1,0:T(1,128)S(1)}) custom-call(s32[1]{0:T(128)S(6)} %copy.85.prefix_ref, bf16[2048,256]{1,0:T(8,128)(2,1)S(1)} %get-tuple-element.79.q_ref, bf16[4,512,256]{2,1,0:T(8,128)(2,1)S(1)} %bitcast.156, bf16[4,128,512]{2,1,0:T(8,128)(2,1)S(1)} %copy-done.10), custom_call_target="tpu_custom_call" | custom-call | tf_op jit(solution)/shard_map/attend/pallas_call | solution.py:686
  299.7 12.1 %exchange.5 = bf16[16,128,128]{2,1,0:T(8,128)(2,1)} custom-call(bf16[16,128,128]{2,1,0:T(8,128)(2,1)} %bitcast.168), custom_call_target="tpu_custom_call" | custom-call | tf_op jit(solution)/shard_map/exchange/pallas_call | solution.py:470
  313.8 3.1 convolution_bitcast_fusion
  317.0 3.0 broadcast_select_fusion.5
  323.1 78.1 %gather.3.x_ref = bf16[16,128,2048]{2,1,0:T(8,128)(2,1)} custom-call(bf16[128,2048]{1,0:T(8,128)(2,1)} %multiply_convert_fusion.x_ref), custom_call_target="tpu_custom_call" | custom-call | tf_op jit(solution)/shard_map/gather/pallas_call | solution.py:207
  409.7 2.2 pad.22.sd_ref
  417.9 85.4 %ffn.1 = (bf16[16,128,2048]{2,1,0:T(8,128)(2,1)}, bf16[16,128,2048]{2,1,0:T(8,128)(2,1)}, bf16[16,128,128]{2,1,0:T(8,128)(2,1)}, f32[16,128,128]{2,1,0:T(8,128)}...) custom-call(bf16[16,128,2048]{2,1,0:T(8,128)(2,1)} %gather.3.x_ref, ...), custom_call_target="tpu_custom_call" | custom-call | tf_op jit(solution)/shard_map/ffn/pallas_call | solution.py:887
  503.3 166.3 %exchange.6 = (f32[128,2048]{1,0:T(8,128)}, f32[128,128]{1,0:T(8,128)}, f32[128,2048]{1,0:T(8,128)}, bf16[704,2048]{1,0:T(8,128)(2,1)}, bf16[704,2048]{1,0:T(8,1...) custom-call(bf16[4,2,2,128,2048]{4,3,2,1,0:T(8,128)(2,1)} %bitcast.1, ...), custom_call_target="tpu_custom_call" | custom-call | tf_op jit(solution)/shard_map/exchange/pallas_call | solution.py:470
  676.7 3.2 convolution_convert_fusion
  681.1 2.9 multiply_reduce_fusion.6
  692.9 3.9 fusion.27
  696.8 4.5 fusion
  701.4 5.7 add_convert_fusion
  707.1 6.6 add_bitcast_fusion
  713.6 5.1 add_bitcast_fusion.1
  718.7 4.9 add_bitcast_fusion.2
  727.7 16.4 %exchange.7 = bf16[16,128,128]{2,1,0:T(8,128)(2,1)} custom-call(bf16[16,128,128]{2,1,0:T(8,128)(2,1)} %bitcast.198), custom_call_target="tpu_custom_call" | custom-call | tf_op jit(solution)/shard_map/exchange/pallas_call | solution.py:470
  749.2 15.1 %attend_back.1 = (f32[2048,256]{1,0:T(8,128)S(1)}, f32[4,512,256]{2,1,0:T(8,128)S(1)}, f32[4,512,128]{2,1,0:T(8,128)S(1)}) custom-call(s32[1]{0:T(128)S(6)} %copy.85.prefix_ref, bf16[2048,256]{1,0:T(8,128)(2,1)S(1)} %get-tuple-element.79.q_ref, bf16[2048,128]{1,0:T(8,128)(2,1)S(1)} %bitcast.154, f32[1,2048]{1,0:T(1,128)S(1)} %get-tuple-element.97.lse_ref, ...), custom_call_target="tpu_custom_call" | custom-call | tf_op jit(solution)/shard_map/attend_back/pallas_call | solution.py:744
  770.2 79.0 %exchange.8 = (f32[128,512]{1,0:T(8,128)}, f32[128,128]{1,0:T(8,128)}, bf16[16,128,256]{2,1,0:T(8,128)(2,1)}, bf16[256,2048]{1,0:T(8,128)(2,1)}, bf16[1024,256]{...) custom-call(bf16[4,2,2,128,512]{4,3,2,1,0:T(8,128)(2,1)} %bitcast.15, ...), custom_call_target="tpu_custom_call" | custom-call | tf_op jit(solution)/shard_map/exchange/pallas_call | solution.py:470
  852.2 2.1 dynamic-slice_bitcast_fusion
  860.5 5.2 fusion.56
  874.1 5.2 convolution_add_fusion.3
  879.3 2.6 fusion.13
  886.0 10.0 %collective-permute-start.7 = (f32[16,1168]{1,0:T(8,128)S(1)}, f32[16,1168]{1,0:T(8,128)S(1)}, u32[]{:S(2)}, u32[]{:S(2)}) collective-permute-start(f32[16,1168]{1,0:T(8,128)S(1)} %dynamic-slice_bitcast_fusion.4), channel_id=1, source_target_pairs={{0,16},{16,0},{1,17},{17,1},{2,18},{18,2},{3,19},{19,3},{4,20},{20... | collective-permute-start | bytes 224264 | tf_op jit(solution)/shard_map/ppermute | solution.py:1271
  896.7 3.8 fusion.12
  900.6 55.3 %exchange.9 = (f32[64,640]{1,0:T(8,128)S(1)}, f32[16,1,1168]{2,1,0:T(1,128)S(1)}, f32[64,3072]{1,0:T(8,128)S(1)}, f32[64,2816]{1,0:T(8,128)S(1)}, f32[64,2816]{1,0:T(8,128)S(1)}, /*index=5*/f32[16,4096]{1,0:T(8,128)S(1)}) custom-call(bf16[4,2,2,64,640]{4,3,2,1,0:T(8,128)(2,1)S(1)} %bitcast.153, f32[16,1,1168]{2,1,0:T(1,128)S(1)} %broadcast_in_dim.33.refs_1_, ...), custom_call_target="tpu_custom_call" | custom-call | tf_op jit(solution)/shard_map/exchange/pallas_call | solution.py:470
  965.1 2.1 copy.86
  (263 shorter events, 121.7 us)
Async XLA Ops:
  7.2 12.0 %copy-start = (bf16[128,2048]{1,0:T(8,128)(2,1)S(1)}, bf16[128,2048]{1,0:T(8,128)(2,1)}, u32[]{:S(2)}) copy-start(bf16[128,2048]{1,0:T(8,128)(2,1)} %param.24) | copy-start | bytes 1572868
  7.2 10.8 %copy-start.41 = (bf16[128,2816]{1,0:T(8,128)(2,1)S(1)}, bf16[128,2816]{1,0:T(8,128)(2,1)}, u32[]{:S(2)}) copy-start(bf16[128,2816]{1,0:T(8,128)(2,1)} %param.27) | copy-start | bytes 2162692
  7.2 12.0 %copy-start.26 = (bf16[128,2048]{1,0:T(8,128)(2,1)S(1)}, bf16[128,2048]{1,0:T(8,128)(2,1)}, u32[]{:S(2)}) copy-start(bf16[128,2048]{1,0:T(8,128)(2,1)} %param.18) | copy-start | bytes 1572868
  7.2 410.7 %all-gather.3.cloned.1.call-start = ((), (), s32[]{:S(2)}) async-start(), calls=%async_computation.1 | async-start | bytes 8912896 | tf_op jit(solution)/shard_map/all_gather | solution.py:1059
  8.0 693.4 %all-gather.5.cloned.1.call-start = ((), (), s32[]{:S(2)}) async-start(), calls=%async_computation.2 | async-start | bytes 6684672 | tf_op jit(solution)/shard_map/all_gather | solution.py:1102
  240.2 19.8 %collective-permute-start.1 = (bf16[512,128]{1,0:T(8,128)(2,1)}, bf16[512,128]{1,0:T(8,128)(2,1)S(1)}, u32[]{:S(2)}, u32[]{:S(2)}) collective-permute-start(bf16[512,128]{1,0:T(8,128)(2,1)} %bitcast.210), channel_id=1, source_target_pairs={{0,16},{16,0},{1,17},{17,1},{2,18},{18,2},{3,19},{19,3},{4,20},{20... | collective-permute-start | bytes 393224 | tf_op jit(solution)/shard_map/ppermute | solution.py:520
  241.3 18.8 %collective-permute-start = (bf16[96,2048]{1,0:T(8,128)(2,1)S(1)}, bf16[96,2048]{1,0:T(8,128)(2,1)}, u32[]{:S(2)}, u32[]{:S(2)}) collective-permute-start(bf16[96,2048]{1,0:T(8,128)(2,1)S(1)} %copy_bitcast_fusion.1), channel_id=1, source_target_pairs={{0,16},{16,0},{1,17},{17,1},{2,18},{18,2},{3,19},{19,3},{4,20},{20... | collective-permute-start | bytes 1179656 | tf_op jit(solution)/shard_map/ppermute | solution.py:520
  246.6 70.3 %collective-permute-start.2 = (bf16[2048,1024]{1,0:T(8,128)(2,1)}, bf16[2048,1024]{1,0:T(8,128)(2,1)}, u32[]{:S(2)}, u32[]{:S(2)}) collective-permute-start(bf16[2048,1024]{1,0:T(8,128)(2,1)} %bitcast.22), channel_id=1, source_target_pairs={{0,16},{16,0},{1,17},{17,1},{2,18},{18,2},{3,19},{19,3},{4,20},{20... | collective-permute-start | bytes 12582920 | tf_op jit(solution)/shard_map/ppermute | solution.py:520
  251.0 69.0 %copy-start.52 = (f32[128]{0:T(128)}, f32[128]{0:T(128)S(1)}, u32[]{:S(2)}) copy-start(f32[128]{0:T(128)S(1)} %add_rsqrt_fusion.1) | copy-start | bytes 1540
  321.1 80.0 %copy-start.50 = (f32[128]{0:T(128)}, f32[128]{0:T(128)S(1)}, u32[]{:S(2)}) copy-start(f32[128]{0:T(128)S(1)} %add_rsqrt_fusion.2) | copy-start | bytes 1540
  401.2 562.2 %reduce-scatter.2.cloned.1.call-start = ((), (), s32[]{:S(2)}) async-start(), calls=%async_computation.3 | async-start | bytes 4456448 | tf_op jit(solution)/shard_map/reduce_scatter | solution.py:1182
  403.3 10.8 %collective-permute-start.3 = (bf16[176,2048]{1,0:T(8,128)(2,1)}, bf16[176,2048]{1,0:T(8,128)(2,1)}, u32[]{:S(2)}, u32[]{:S(2)}) collective-permute-start(bf16[176,2048]{1,0:T(8,128)(2,1)} %copy_bitcast_fusion), channel_id=1, source_target_pairs={{0,16},{16,0},{1,17},{17,1},{2,18},{18,2},{3,19},{19,3},{4,20},{20... | collective-permute-start | bytes 2162696 | tf_op jit(solution)/shard_map/ppermute | solution.py:520
  503.3 169.2 %copy-start.35 = (bf16[16,128,16]{2,1,0:T(8,128)(2,1)S(1)}, bf16[16,128,16]{2,1,0:T(8,128)(2,1)}, u32[]{:S(2)}) copy-start(bf16[16,128,16]{2,1,0:T(8,128)(2,1)} %slice.106) | copy-start | bytes 196612
  503.3 169.2 %copy-start.51 = (f32[128]{0:T(128)S(1)}, f32[128]{0:T(128)}, u32[]{:S(2)}) copy-start(f32[128]{0:T(128)} %copy-done.50) | copy-start | bytes 1540
  680.0 21.4 %collective-permute-start.4 = (bf16[1024,2048]{1,0:T(8,128)(2,1)}, bf16[1024,2048]{1,0:T(8,128)(2,1)}, u32[]{:S(2)}, u32[]{:S(2)}) collective-permute-start(bf16[1024,2048]{1,0:T(8,128)(2,1)} %convolution_convert_fusion), channel_id=1, source_target_pairs={{0,16},{16,0},{1,17},{17,1},{2,18},{18,2},{3,19},{19,3},{4,20},{20... | collective-permute-start | bytes 12582920 | tf_op jit(solution)/shard_map/ppermute | solution.py:514
  680.0 27.1 %collective-permute-start.16 = (bf16[704,2048]{1,0:T(8,128)(2,1)}, bf16[704,2048]{1,0:T(8,128)(2,1)}, u32[]{:S(2)}, u32[]{:S(2)}) collective-permute-start(bf16[704,2048]{1,0:T(8,128)(2,1)} %get-tuple-element.135), channel_id=1, source_target_pairs={{0,16},{16,0},{1,17},{17,1},{2,18},{18,2},{3,19},{19,3},{4,20},{20... | collective-permute-start | bytes 8650760 | tf_op jit(solution)/shard_map/ppermute | solution.py:1155
  680.5 33.2 %collective-permute-start.15 = (bf16[1024,1408]{1,0:T(8,128)(2,1)}, bf16[1024,1408]{1,0:T(8,128)(2,1)}, u32[]{:S(2)}, u32[]{:S(2)}) collective-permute-start(bf16[1024,1408]{1,0:T(8,128)(2,1)} %get-tuple-element.133), channel_id=1, source_target_pairs={{0,16},{16,0},{1,17},{17,1},{2,18},{18,2},{3,19},{19,3},{4,20},{20... | collective-permute-start | bytes 8650760 | tf_op jit(solution)/shard_map/ppermute | solution.py:1155
  684.6 34.1 %collective-permute-start.14 = (bf16[1024,1408]{1,0:T(8,128)(2,1)}, bf16[1024,1408]{1,0:T(8,128)(2,1)}, u32[]{:S(2)}, u32[]{:S(2)}) collective-permute-start(bf16[1024,1408]{1,0:T(8,128)(2,1)} %get-tuple-element.131), channel_id=1, source_target_pairs={{0,16},{16,0},{1,17},{17,1},{2,18},{18,2},{3,19},{19,3},{4,20},{20... | collective-permute-start | bytes 8650760 | tf_op jit(solution)/shard_map/ppermute | solution.py:1155
  701.3 172.7 %collective-permute-start.5 = (bf16[2048,1536]{1,0:T(8,128)(2,1)}, bf16[2048,1536]{1,0:T(8,128)(2,1)}, u32[]{:S(2)}, u32[]{:S(2)}) collective-permute-start(bf16[2048,1536]{1,0:T(8,128)(2,1)} %all-gather.5.cloned.1.call-done), channel_id=1, source_target_pairs={{0,16},{16,0},{1,17},{17,1},{2,18},{18,2},{3,19},{19,3},{4,20},{20... | collective-permute-start | bytes 18874376 | tf_op jit(solution)/shard_map/ppermute | solution.py:520
  849.2 9.9 %copy-start.46 = (f32[128,128]{1,0:T(8,128)S(1)}, f32[128,128]{1,0:T(8,128)}, u32[]{:S(2)}) copy-start(f32[128,128]{1,0:T(8,128)} %get-tuple-element.113) | copy-start | bytes 196612
  851.2 16.8 %collective-permute-start.12 = (bf16[88,2048]{1,0:T(8,128)(2,1)}, bf16[88,2048]{1,0:T(8,128)(2,1)}, u32[]{:S(2)}, u32[]{:S(2)}) collective-permute-start(bf16[88,2048]{1,0:T(8,128)(2,1)} %dynamic-slice_bitcast_fusion.3), channel_id=1, source_target_pairs={{0,16},{16,0},{1,17},{17,1},{2,18},{18,2},{3,19},{19,3},{4,20},{20... | collective-permute-start | bytes 1081352 | tf_op jit(solution)/shard_map/ppermute | solution.py:494
  851.2 15.1 %collective-permute-start.11 = (bf16[256,256]{1,0:T(8,128)(2,1)}, bf16[256,256]{1,0:T(8,128)(2,1)S(1)}, u32[]{:S(2)}, u32[]{:S(2)}) collective-permute-start(bf16[256,256]{1,0:T(8,128)(2,1)} %get-tuple-element.121), channel_id=1, source_target_pairs={{0,16},{16,0},{1,17},{17,1},{2,18},{18,2},{3,19},{19,3},{4,20},{20... | collective-permute-start | bytes 393224 | tf_op jit(solution)/shard_map/ppermute | solution.py:1155
  851.7 17.4 %collective-permute-start.10 = (bf16[1024,256]{1,0:T(8,128)(2,1)}, bf16[1024,256]{1,0:T(8,128)(2,1)}, u32[]{:S(2)}, u32[]{:S(2)}) collective-permute-start(bf16[1024,256]{1,0:T(8,128)(2,1)} %get-tuple-element.119), channel_id=1, source_target_pairs={{0,16},{16,0},{1,17},{17,1},{2,18},{18,2},{3,19},{19,3},{4,20},{20... | collective-permute-start | bytes 1572872 | tf_op jit(solution)/shard_map/ppermute | solution.py:1155
  851.7 19.6 %collective-permute-start.9 = (bf16[1024,256]{1,0:T(8,128)(2,1)}, bf16[1024,256]{1,0:T(8,128)(2,1)}, u32[]{:S(2)}, u32[]{:S(2)}) collective-permute-start(bf16[1024,256]{1,0:T(8,128)(2,1)} %get-tuple-element.117), channel_id=1, source_target_pairs={{0,16},{16,0},{1,17},{17,1},{2,18},{18,2},{3,19},{19,3},{4,20},{20... | collective-permute-start | bytes 1572872 | tf_op jit(solution)/shard_map/ppermute | solution.py:1155
  860.5 9.5 copy-start.45
  866.3 7.2 collective-permute-start.6
  867.9 4.5 collective-permute-start.8
  869.1 3.5 collective-permute-start.13
  885.0 15.5 %copy-start.42 = (f32[16,2,1168]{2,0,1:T(8,128)S(1)}, f32[16,2,1168]{2,0,1:T(8,128)}, u32[]{:S(2)}) copy-start(f32[16,2,1168]{2,0,1:T(8,128)} %concatenate.36) | copy-start | bytes 448516
  886.0 14.5 %collective-permute-start.7 = (f32[16,1168]{1,0:T(8,128)S(1)}, f32[16,1168]{1,0:T(8,128)S(1)}, u32[]{:S(2)}, u32[]{:S(2)}) collective-permute-start(f32[16,1168]{1,0:T(8,128)S(1)} %dynamic-slice_bitcast_fusion.4), channel_id=1, source_target_pairs={{0,16},{16,0},{1,17},{17,1},{2,18},{18,2},{3,19},{19,3},{4,20},{20... | collective-permute-start | bytes 224264 | tf_op jit(solution)/shard_map/ppermute | solution.py:1271
  900.6 72.8 %copy-start.1 = (bf16[128,2048]{1,0:T(8,128)(2,1)S(1)}, bf16[128,2048]{1,0:T(8,128)(2,1)}, u32[]{:S(2)}) copy-start(bf16[128,2048]{1,0:T(8,128)(2,1)} %param.24) | copy-start | bytes 1572868
  960.6 11.9 %copy-start.15 = (f32[64,2816]{1,0:T(8,128)S(1)}, f32[64,2816]{1,0:T(8,128)}, u32[]{:S(2)}) copy-start(f32[64,2816]{1,0:T(8,128)} %copy-done.14) | copy-start | bytes 2162692
  (44 other events, 131.3 us)
Sparse Core Ops, SparseCore 0:
  10.8 177.2 all-gather.2
  401.3 92.7 all-gather.4
  707.2 125.8 reduce-scatter.1

commit v9 on v8

--- a/solution.py
+++ b/solution.py
@@ -535,9 +535,10 @@
 
 
 def front_kernel(
-    x_ref, cos_ref, sin_ref, gain_ref, lat_gain_ref, wq_ref, wl_ref, we_ref,
-    normed_ref, query_ref, keys_ref, values_ref, latent_ref,
+    x_ref, w_ref, cos_ref, sin_ref, gain_ref, lat_gain_ref, wq_ref, wl_ref, we_ref,
+    normed_ref, query_ref, keys_ref, values_ref, latent_ref, out_w_ref,
 ):
+    out_w_ref[...] = w_ref[...].reshape(out_w_ref.shape)
     blocks, tokens = x_ref.shape[:2]
     rows = blocks * tokens
     x = x_ref[...].reshape(rows, gain_ref.shape[1]).astype(F32)
@@ -578,12 +579,13 @@
     def out(cols):
         return jax.ShapeDtypeStruct((length, cols), BF16)
 
-    cols = (model, wq.shape[0], NOPE + 2 * ROPE, VH, LATENT)
+    cols = (model, wq.shape[0], NOPE + 2 * ROPE, VH, LATENT, model // 2)
     return pl.pallas_call(
         front_kernel,
         grid=(n // blocks,),
         in_specs=[
             pl.BlockSpec((blocks, tokens, model), lambda i: (i, 0, 0)),
+            pl.BlockSpec((blocks, tokens, model // 2), lambda i: (i, 0, 2)),
             rows_of(2 * ROPE),
             rows_of(2 * ROPE),
         ]
@@ -592,7 +594,7 @@
         out_shape=[out(c) for c in cols],
         compiler_params=pltpu.CompilerParams(vmem_limit_bytes=48 << 20),
         name="front",
-    )(x, cos, sin, gain, lat_gain, wq, wl, we)
+    )(x, x, cos, sin, gain, lat_gain, wq, wl, we)
 
 
 def back_kernel(
@@ -1013,50 +1015,41 @@
     rows_out = D // (groups * n)
     expand_rows = LATENT // (groups * n)
 
-    pad = jnp.zeros((rows_dev - latent_rows,), BF16)
-    first_block = jnp.concatenate(
-        [
-            layer_input,
-            latent_weight,
-            router_weight,
-            attention_gain[:, None],
-            feedforward_gain[:, None],
-            jnp.concatenate([latent_gain, pad])[:, None],
-            expert_routes.astype(BF16),
-        ],
-        axis=1,
-    )
-    width = first_block.shape[1]
     out_w_half = lax.dynamic_slice_in_dim(output_weight, half * (D // 2), D // 2, 1)
     first_block = jnp.concatenate(
-        [first_block, jnp.zeros((tokens, -width % 128), BF16), out_w_half], axis=1
-    )
+        [layer_input, out_w_half, latent_weight, router_weight, expert_routes.astype(BF16)], axis=1
+    )
+    width = first_block.shape[1]
+    first_block = jnp.pad(first_block, ((0, 0), (0, -width % 128)))
+    gains = jnp.zeros((16, rows_dev), BF16)
+    gains = gains.at[0].set(attention_gain).at[1].set(feedforward_gain)
+    gains = gains.at[2, :latent_rows].set(latent_gain)
     shared_half = jnp.where(even, shared_gate, shared_up)
     expand_half = lax.dynamic_index_in_dim(
         expand_weight.reshape(latent_rows, n, 2, -1), half, 2, keepdims=False
     ).transpose(1, 0, 2)
-    first_all, q_blocks, x_blocks, shared_blocks = gather(
+    first_all, q_blocks, x_blocks, shared_blocks, gain_blocks = gather(
         first_block,
         0,
         swaps=(
             column_halves(query_weight, n, half),
             expand_half,
             shared_half.T.reshape(n, shared_half.shape[1] // n, rows_dev),
+            jnp.broadcast_to(gains, (n,) + gains.shape),
         ),
     )
-    c0 = D
+    c0 = D + D // 2
     c1 = c0 + LATENT + ROPE
     c2 = c1 + n
     latent_w = first_all[:, :, c0:c1].reshape(D, LATENT + ROPE)
     router_w = first_all[:, :, c1:c2].reshape(D, n)
-    attn_gain = first_all[:, :, c2].reshape(D).astype(F32)
-    ffn_gain = first_all[:, :, c2 + 1].reshape(D).astype(F32)
-    lat_gain = first_all[:, :latent_rows, c2 + 2].reshape(LATENT).astype(F32)
-    routes = first_all[:, :, c2 + 3 : c2 + 3 + TOPK].astype(jnp.int32)
-
-    out_w_mine = first_all[:, :, -(D // 2) :].reshape(D, D // 2)
-    out_w_other = from_partner(out_w_mine)
-    all_out_grad = lax.all_gather(output_grad, "ep", axis=0, tiled=True)
+    routes = first_all[:, :, c2 : c2 + TOPK].astype(jnp.int32)
+    attn_gain = gain_blocks[:, 0].reshape(D).astype(F32)
+    ffn_gain = gain_blocks[:, 1].reshape(D).astype(F32)
+    lat_gain = gain_blocks[:, 2, :latent_rows].reshape(LATENT).astype(F32)
+
+    later_grad, q_blocks = lax.optimization_barrier((output_grad, q_blocks))
+    all_out_grad = lax.all_gather(later_grad, "ep", axis=0, tiled=True)
 
     q_mine, x_mine = columns_in(q_blocks), x_blocks.reshape(LATENT, -1)
     query_t = both_halves(q_mine, from_partner(q_mine), even)
@@ -1077,9 +1070,10 @@
         [latent_w, latent_w[:, LATENT + ROPE // 2 :], latent_w[:, LATENT : LATENT + ROPE // 2]],
         axis=1,
     )
-    normed, query, keys, values, latent = front(
+    normed, query, keys, values, latent, out_w_mine = front(
         first_all, cos_table, sin_table, attn_gain[None], lat_gain[None], turned, latent_turned, expand_w
     )
+    out_w_other = from_partner(out_w_mine)
     attended_head, attended_exact, lse = attend(prefix_length, query, keys, values)
     (attended_blocks,) = exchange(2, swaps=(attended_head.reshape(n, tokens, VH),))
     attended = attended_blocks.transpose(1, 0, 2).reshape(tokens, HEADS * VH)
@@ -1148,17 +1142,6 @@
     def by_group(values):
         return over_groups(values.reshape(groups, values.shape[0] // groups, -1))
 
-    def blocks_over_groups(blocks):
-        total = blocks[0].astype(F32)
-        for k in range(1, groups):
-            shift = [(g, (g + k) % groups) for g in range(groups)]
-            total = total + lax.ppermute(blocks[k], "grp", shift).astype(F32)
-        return total
-
-    expert_down_grad, expert_gate_grad, expert_up_grad = (
-        blocks_over_groups(products[k * groups : (k + 1) * groups])[None] for k in range(3)
-    )
-
     router_own = lax.dynamic_index_in_dim(router_all, e, 0, keepdims=False)[:, :n]
     grad_probs = dot_sum[:, :n]
     grad_logits = (
@@ -1178,10 +1161,20 @@
     (grad_att_blocks,) = exchange(
         5, swaps=(grad_attended.reshape(tokens, HEADS, VH).transpose(1, 0, 2),)
     )
+    *products, grad_att_blocks = lax.optimization_barrier((*products, grad_att_blocks))
     grad_att = grad_att_blocks.reshape(length, VH)
-    output_weight_grad = lax.psum_scatter(
-        output_w_partial.reshape(n, rows_out, D), "ep", scatter_dimension=0
-    ).astype(F32)
+
+    def blocks_over_groups(blocks):
+        total = blocks[0].astype(F32)
+        for k in range(1, groups):
+            shift = [(g, (g + k) % groups) for g in range(groups)]
+            total = total + lax.ppermute(blocks[k], "grp", shift).astype(F32)
+        return total
+
+    expert_down_grad, expert_gate_grad, expert_up_grad = (
+        blocks_over_groups(products[k * groups : (k + 1) * groups])[None] for k in range(3)
+    )
+
     grad_router = product("te,td->ed", grad_logits, own_ffn_in)
 
     delta = jnp.sum(grad_att.astype(F32) * attended_exact, axis=-1)[None]
@@ -1194,6 +1187,7 @@
     (
         latent_sum,
         rope_sum,
+        output_weight_grad,
         query_blocks,
         side_down,
         *products,
@@ -1202,6 +1196,7 @@
         sums=(
             latent_partial.reshape(n, tokens, LATENT),
             rope_partial.reshape(n, tokens, 2 * ROPE),
+            output_w_partial.reshape(n, rows_out, D),
         ),
         swaps=(grad_query.reshape(n, tokens, -1),),
         jobs=(

time: 996 us -> 939 us (0.943)
  Pallas kernels: 758 us -> 728 us
  local copies, waits for them, and re-layouts: 94.4 us -> 79.9 us
    pallas_call x2, Pallas kernels: 296 us -> 245 us  [gather(): pl.pallas_call(functools.partial(gather_kernel, n, w), out_shape=[jax.Sha...]
    pallas_call x5, Pallas kernels: 329 us -> 341 us  [exchange(): pl.pallas_call(functools.partial(exchange_kernel, n, m, w, laid, groups,...]
    ppermute x7, starting transfers between devices: 2.1 us -> 13.7 us  [blocks_over_groups(): total = total + lax.ppermute(blocks[k], 'grp', shift).astype(F32)]
    ppermute x1, starting transfers between devices: 10 us -> 0.01 us  [per_device(): small = mine + lax.ppermute(theirs, 'grp', [(0, 1), (1, 0)])]
    unnamed x121 -> x138, local copies, waits for them, and re-layouts: 33.9 us -> 28.2 us
  transfers between devices with their start and end apart: 20 -> 19, of which waited for: 0 -> 1; matrix products, arithmetic and copies ran while one was open for 16% -> 14% of each run, Pallas kernels for 77% -> 62%
where the time goes in v9:
time: 939 us; the launch traced here: 931 us
  Pallas kernels  728 us (78%)
  local copies, waits for them, and re-layouts  79.9 us (9%)
  other arithmetic  46.5 us (5%)
  matrix products  44.3 us (5%)
  starting transfers between devices  16.4 us (2%)
  between operations  16 us (2%)
    pallas_call x5, Pallas kernels, exchange(): pl.pallas_call(functools.partial(exchange_kernel, n, m, w, laid, groups,...  341 us
    pallas_call x2, Pallas kernels, gather(): pl.pallas_call(functools.partial(gather_kernel, n, w), out_shape=[jax.Sha...  245 us
    pallas_call x1, Pallas kernels, ffn(): pl.pallas_call(functools.partial(ffn_kernel, n), grid=(n // group,), in_s...  93.7 us
    dot_general x14, matrix products, product(): return jnp.einsum(form, left, right, preferred_element_type=F32)  44.3 us
    unnamed x138, local copies, waits for them, and re-layouts  28.2 us
  transfers between devices with their start and end apart: 19, of which 1 were waited for; matrix products, arithmetic and copies ran while one was open for 14% of the time, Pallas kernels for 62%

profile of v9, /device:TPU:0, one launch (start us, length us, event | category | flops | bytes accessed | tf_op | source)
XLA Modules:
  0.0 931.2 jit_solution(2890083905624196642)
XLA Ops:
  20.7 146.5 %gather.2 = (bf16[16,128,3712]{2,1,0:T(8,128)(2,1)}, bf16[16,96,128]{2,1,0:T(8,128)(2,1)}, bf16[16,32,128]{2,1,0:T(8,128)(2,1)}, bf16[16,176,128]{2,1,0:T(8,128)(2,1)}, bf16[16,16,128]{2,1,0:T(8,128)(2,1)}) custom-call(bf16[128,3712]{1,0:T(8,128)(2,1)} %pad.30.x_ref, bf16[16,96,128]{2,1,0:T(8,128)(2,1)} %dynamic-slice_bitcast_fusion.2.refs_0_, ...), custom_call_target="tpu_custom_call" | custom-call | tf_op jit(solution)/shard_map/gather/pallas_call | solution.py:207
  168.9 2.1 slice.145
  172.1 2.1 pad_maximum_fusion.wl_ref
  176.0 18.2 %front.1 = (bf16[2048,2048]{1,0:T(8,128)(2,1)}, bf16[2048,256]{1,0:T(8,128)(2,1)S(1)}, bf16[2048,256]{1,0:T(8,128)(2,1)S(1)}, bf16[2048,128]{1,0:T(8,128)(2,1)S(...) custom-call(bf16[16,128,3712]{2,1,0:T(8,128)(2,1)} %get-tuple-element.124.x_ref.w_ref, ...), custom_call_target="tpu_custom_call" | custom-call | tf_op jit(solution)/shard_map/front/pallas_call | solution.py:583
  204.0 12.7 %attend.1 = (bf16[2048,128]{1,0:T(8,128)(2,1)S(1)}, f32[2048,128]{1,0:T(8,128)S(1)}, f32[1,2048]{1,0:T(1,128)S(1)}) custom-call(s32[1]{0:T(128)S(6)} %copy.82.prefix_ref, bf16[2048,256]{1,0:T(8,128)(2,1)S(1)} %get-tuple-element.129.q_ref, bf16[4,512,256]{2,1,0:T(8,128)(2,1)S(1)} %bitcast.151, bf16[4,128,512]{2,1,0:T(8,128)(2,1)S(1)} %copy-done.10), custom_call_target="tpu_custom_call" | custom-call | tf_op jit(solution)/shard_map/attend/pallas_call | solution.py:688
  218.4 15.0 %exchange.5 = bf16[16,128,128]{2,1,0:T(8,128)(2,1)} custom-call(bf16[16,128,128]{2,1,0:T(8,128)(2,1)} %bitcast.163), custom_call_target="tpu_custom_call" | custom-call | tf_op jit(solution)/shard_map/exchange/pallas_call | solution.py:470
  235.5 3.2 fusion.56
  238.7 3.0 broadcast_select_fusion.5
  244.8 98.7 %gather.3.x_ref = bf16[16,128,2048]{2,1,0:T(8,128)(2,1)} custom-call(bf16[128,2048]{1,0:T(8,128)(2,1)} %multiply_convert_fusion.x_ref), custom_call_target="tpu_custom_call" | custom-call | tf_op jit(solution)/shard_map/gather/pallas_call | solution.py:207
  352.0 2.2 pad.34.sd_ref
  360.2 93.7 %ffn.1 = (bf16[16,128,2048]{2,1,0:T(8,128)(2,1)}, bf16[16,128,2048]{2,1,0:T(8,128)(2,1)}, bf16[16,128,128]{2,1,0:T(8,128)(2,1)}, f32[16,128,128]{2,1,0:T(8,128)}...) custom-call(bf16[16,128,2048]{2,1,0:T(8,128)(2,1)} %gather.3.x_ref, ...), custom_call_target="tpu_custom_call" | custom-call | tf_op jit(solution)/shard_map/ffn/pallas_call | solution.py:889
  454.0 171.9 %exchange.6 = (f32[128,2048]{1,0:T(8,128)}, f32[128,128]{1,0:T(8,128)}, f32[128,2048]{1,0:T(8,128)}, bf16[704,2048]{1,0:T(8,128)(2,1)}, bf16[704,2048]{1,0:T(8,1...) custom-call(bf16[4,2,2,128,2048]{4,3,2,1,0:T(8,128)(2,1)} %bitcast.1, ...), custom_call_target="tpu_custom_call" | custom-call | tf_op jit(solution)/shard_map/exchange/pallas_call | solution.py:470
  628.8 2.7 multiply_reduce_fusion
  632.8 3.3 convolution_convert_fusion
  637.3 2.9 multiply_reduce_fusion.6
  647.7 3.9 fusion.27
  651.7 4.6 fusion
  656.2 5.4 add_convert_fusion
  665.8 13.1 %exchange.7 = bf16[16,128,128]{2,1,0:T(8,128)(2,1)} custom-call(bf16[16,128,128]{2,1,0:T(8,128)(2,1)} %bitcast.190), custom_call_target="tpu_custom_call" | custom-call | tf_op jit(solution)/shard_map/exchange/pallas_call | solution.py:470
  683.9 15.1 %attend_back.1 = (f32[2048,256]{1,0:T(8,128)S(1)}, f32[4,512,256]{2,1,0:T(8,128)S(1)}, f32[4,512,128]{2,1,0:T(8,128)S(1)}) custom-call(s32[1]{0:T(128)S(6)} %copy.82.prefix_ref, bf16[2048,256]{1,0:T(8,128)(2,1)S(1)} %get-tuple-element.129.q_ref, bf16[2048,128]{1,0:T(8,128)(2,1)S(1)} %bitcast.149, f32[1,2048]{1,0:T(1,128)S(1)} %get-tuple-element.156.lse_ref, ...), custom_call_target="tpu_custom_call" | custom-call | tf_op jit(solution)/shard_map/attend_back/pallas_call | solution.py:746
  704.5 88.6 %exchange.8 = (f32[128,512]{1,0:T(8,128)}, f32[128,128]{1,0:T(8,128)}, f32[64,2048]{1,0:T(8,128)}, bf16[16,128,256]{2,1,0:T(8,128)(2,1)}, bf16[256,2048]{1,0:T(8...) custom-call(bf16[4,2,2,128,512]{4,3,2,1,0:T(8,128)(2,1)} %bitcast.15, ...), custom_call_target="tpu_custom_call" | custom-call | tf_op jit(solution)/shard_map/exchange/pallas_call | solution.py:470
  795.6 2.1 dynamic-slice_bitcast_fusion
  803.9 5.2 fusion.57
  814.8 2.8 collective-permute-start.15
  817.7 9.7 %collective-permute-start.14 = (bf16[1024,1408]{1,0:T(8,128)(2,1)}, bf16[1024,1408]{1,0:T(8,128)(2,1)}, u32[]{:S(2)}, u32[]{:S(2)}) collective-permute-start(bf16[1024,1408]{1,0:T(8,128)(2,1)} %get-tuple-element.191), channel_id=1, source_target_pairs={{0,16},{16,0},{1,17},{17,1},{2,18},{18,2},{3,19},{19,3},{4,20},{20... | collective-permute-start | bytes 8650760 | tf_op jit(solution)/shard_map/ppermute | solution.py:1171
  828.9 5.2 convolution_add_fusion.3
  834.1 2.6 fusion.13
  841.4 3.8 fusion.12
  845.3 52.9 %exchange.9 = (f32[64,640]{1,0:T(8,128)S(1)}, f32[16,1,1168]{2,1,0:T(1,128)S(1)}, f32[64,3072]{1,0:T(8,128)S(1)}, f32[64,2816]{1,0:T(8,128)S(1)}, f32[64,2816]{1,0:T(8,128)S(1)}, /*index=5*/f32[16,4096]{1,0:T(8,128)S(1)}) custom-call(bf16[4,2,2,64,640]{4,3,2,1,0:T(8,128)(2,1)S(1)} %bitcast.148, f32[16,1,1168]{2,1,0:T(1,128)S(1)} %broadcast_in_dim.24.refs_1_, ...), custom_call_target="tpu_custom_call" | custom-call | tf_op jit(solution)/shard_map/exchange/pallas_call | solution.py:470
  902.7 6.6 add_bitcast_fusion
  909.3 5.1 add_bitcast_fusion.1
  914.4 5.1 add_bitcast_fusion.2
  (276 shorter events, 105.7 us)
Async XLA Ops:
  7.2 10.5 %copy-start = (bf16[128,2048]{1,0:T(8,128)(2,1)S(1)}, bf16[128,2048]{1,0:T(8,128)(2,1)}, u32[]{:S(2)}) copy-start(bf16[128,2048]{1,0:T(8,128)(2,1)} %param.30) | copy-start | bytes 1572868
  7.2 9.3 copy-start.40
  7.2 9.3 copy-start.41
  7.2 10.5 %copy-start.25 = (bf16[128,2048]{1,0:T(8,128)(2,1)S(1)}, bf16[128,2048]{1,0:T(8,128)(2,1)}, u32[]{:S(2)}) copy-start(bf16[128,2048]{1,0:T(8,128)(2,1)} %param.24) | copy-start | bytes 1572868
  7.2 353.0 %all-gather.3.cloned.1.call-start = ((), (), s32[]{:S(2)}) async-start(), calls=%async_computation | async-start | bytes 8912896 | tf_op jit(solution)/shard_map/all_gather | solution.py:1052
  167.2 468.9 %all-gather.5.cloned.1.call-start = ((), (), s32[]{:S(2)}) async-start(), calls=%async_computation.1 | async-start | bytes 6684672 | tf_op jit(solution)/shard_map/all_gather | solution.py:1096
  167.3 7.1 collective-permute-start.1
  168.4 6.1 collective-permute-start
  174.3 67.4 %copy-start.49 = (f32[16,1,128]{2,1,0:T(1,128)}, f32[16,1,128]{2,1,0:T(1,128)S(1)}, u32[]{:S(2)}) copy-start(f32[16,1,128]{2,1,0:T(1,128)S(1)} %get-tuple-element.225) | copy-start | bytes 24580
  195.9 42.8 %collective-permute-start.2 = (bf16[2048,1024]{1,0:T(8,128)(2,1)}, bf16[2048,1024]{1,0:T(8,128)(2,1)}, u32[]{:S(2)}, u32[]{:S(2)}) collective-permute-start(bf16[2048,1024]{1,0:T(8,128)(2,1)} %get-tuple-element.133), channel_id=1, source_target_pairs={{0,16},{16,0},{1,17},{17,1},{2,18},{18,2},{3,19},{19,3},{4,20},{20... | collective-permute-start | bytes 12582920 | tf_op jit(solution)/shard_map/ppermute | solution.py:520
  197.9 43.9 %copy-start.56 = (f32[128]{0:T(128)}, f32[128]{0:T(128)S(1)}, u32[]{:S(2)}) copy-start(f32[128]{0:T(128)S(1)} %add_rsqrt_fusion.1) | copy-start | bytes 1540
  242.9 388.6 %copy-start.55 = (f32[128]{0:T(128)}, f32[128]{0:T(128)S(1)}, u32[]{:S(2)}) copy-start(f32[128]{0:T(128)S(1)} %add_rsqrt_fusion.2) | copy-start | bytes 1540
  345.6 10.8 %collective-permute-start.3 = (bf16[176,2048]{1,0:T(8,128)(2,1)}, bf16[176,2048]{1,0:T(8,128)(2,1)}, u32[]{:S(2)}, u32[]{:S(2)}) collective-permute-start(bf16[176,2048]{1,0:T(8,128)(2,1)} %copy_bitcast_fusion), channel_id=1, source_target_pairs={{0,16},{16,0},{1,17},{17,1},{2,18},{18,2},{3,19},{19,3},{4,20},{20... | collective-permute-start | bytes 2162696 | tf_op jit(solution)/shard_map/ppermute | solution.py:520
  454.0 174.8 %copy-start.35 = (bf16[16,128,16]{2,1,0:T(8,128)(2,1)S(1)}, bf16[16,128,16]{2,1,0:T(8,128)(2,1)}, u32[]{:S(2)}) copy-start(bf16[16,128,16]{2,1,0:T(8,128)(2,1)} %slice.150) | copy-start | bytes 196612
  636.0 20.2 %collective-permute-start.4 = (bf16[1024,2048]{1,0:T(8,128)(2,1)}, bf16[1024,2048]{1,0:T(8,128)(2,1)}, u32[]{:S(2)}, u32[]{:S(2)}) collective-permute-start(bf16[1024,2048]{1,0:T(8,128)(2,1)} %convolution_convert_fusion), channel_id=1, source_target_pairs={{0,16},{16,0},{1,17},{17,1},{2,18},{18,2},{3,19},{19,3},{4,20},{20... | collective-permute-start | bytes 12582920 | tf_op jit(solution)/shard_map/ppermute | solution.py:514
  636.1 192.7 %collective-permute-start.5 = (bf16[2048,1536]{1,0:T(8,128)(2,1)}, bf16[2048,1536]{1,0:T(8,128)(2,1)}, u32[]{:S(2)}, u32[]{:S(2)}) collective-permute-start(bf16[2048,1536]{1,0:T(8,128)(2,1)} %all-gather.5.cloned.1.call-done), channel_id=1, source_target_pairs={{0,16},{16,0},{1,17},{17,1},{2,18},{18,2},{3,19},{19,3},{4,20},{20... | collective-permute-start | bytes 18874376 | tf_op jit(solution)/shard_map/ppermute | solution.py:520
  678.8 223.9 %collective-permute-start.16 = (bf16[704,2048]{1,0:T(8,128)(2,1)}, bf16[704,2048]{1,0:T(8,128)(2,1)}, u32[]{:S(2)}, u32[]{:S(2)}) collective-permute-start(bf16[704,2048]{1,0:T(8,128)(2,1)} %get-tuple-element.195), channel_id=1, source_target_pairs={{0,16},{16,0},{1,17},{17,1},{2,18},{18,2},{3,19},{19,3},{4,20},{20... | collective-permute-start | bytes 8650760 | tf_op jit(solution)/shard_map/ppermute | solution.py:1171
  793.1 9.4 %copy-start.48 = (f32[128,128]{1,0:T(8,128)S(1)}, f32[128,128]{1,0:T(8,128)}, u32[]{:S(2)}) copy-start(f32[128,128]{1,0:T(8,128)} %get-tuple-element.173) | copy-start | bytes 196612
  795.1 15.3 %collective-permute-start.12 = (bf16[88,2048]{1,0:T(8,128)(2,1)}, bf16[88,2048]{1,0:T(8,128)(2,1)}, u32[]{:S(2)}, u32[]{:S(2)}) collective-permute-start(bf16[88,2048]{1,0:T(8,128)(2,1)} %dynamic-slice_bitcast_fusion.3), channel_id=1, source_target_pairs={{0,16},{16,0},{1,17},{17,1},{2,18},{18,2},{3,19},{19,3},{4,20},{20... | collective-permute-start | bytes 1081352 | tf_op jit(solution)/shard_map/ppermute | solution.py:494
  795.1 14.7 %collective-permute-start.11 = (bf16[256,256]{1,0:T(8,128)(2,1)}, bf16[256,256]{1,0:T(8,128)(2,1)S(1)}, u32[]{:S(2)}, u32[]{:S(2)}) collective-permute-start(bf16[256,256]{1,0:T(8,128)(2,1)} %get-tuple-element.181), channel_id=1, source_target_pairs={{0,16},{16,0},{1,17},{17,1},{2,18},{18,2},{3,19},{19,3},{4,20},{20... | collective-permute-start | bytes 393224 | tf_op jit(solution)/shard_map/ppermute | solution.py:1171
  795.6 16.0 %collective-permute-start.10 = (bf16[1024,256]{1,0:T(8,128)(2,1)}, bf16[1024,256]{1,0:T(8,128)(2,1)}, u32[]{:S(2)}, u32[]{:S(2)}) collective-permute-start(bf16[1024,256]{1,0:T(8,128)(2,1)} %get-tuple-element.179), channel_id=1, source_target_pairs={{0,16},{16,0},{1,17},{17,1},{2,18},{18,2},{3,19},{19,3},{4,20},{20... | collective-permute-start | bytes 1572872 | tf_op jit(solution)/shard_map/ppermute | solution.py:1171
  803.9 8.2 copy-start.45
  809.2 8.4 copy-start.43
  809.7 18.5 %collective-permute-start.6 = (bf16[1024,640]{1,0:T(8,128)(2,1)S(1)}, bf16[1024,640]{1,0:T(8,128)(2,1)S(1)}, u32[]{:S(2)}, u32[]{:S(2)}) collective-permute-start(bf16[1024,640]{1,0:T(8,128)(2,1)S(1)} %convolution_convert_fusion.1), channel_id=1, source_target_pairs={{0,16},{16,0},{1,17},{17,1},{2,18},{18,2},{3,19},{19,3},{4,20},{20... | collective-permute-start | bytes 3932168 | tf_op jit(solution)/shard_map/ppermute | solution.py:514
  810.4 3.4 collective-permute-start.9
  811.6 3.2 collective-permute-start.8
  812.1 16.7 %copy-start.39 = (bf16[128,8,192]{0,2,1:T(8,128)(2,1)S(1)}, bf16[128,8,192]{0,2,1:T(8,128)(2,1)}, u32[]{:S(2)}) copy-start(bf16[128,8,192]{0,2,1:T(8,128)(2,1)} %copy.57) | copy-start | bytes 1179652
  813.7 3.9 collective-permute-start.13
  814.8 94.5 %collective-permute-start.15 = (bf16[1024,1408]{1,0:T(8,128)(2,1)}, bf16[1024,1408]{1,0:T(8,128)(2,1)}, u32[]{:S(2)}, u32[]{:S(2)}) collective-permute-start(bf16[1024,1408]{1,0:T(8,128)(2,1)} %get-tuple-element.193), channel_id=1, source_target_pairs={{0,16},{16,0},{1,17},{17,1},{2,18},{18,2},{3,19},{19,3},{4,20},{20... | collective-permute-start | bytes 8650760 | tf_op jit(solution)/shard_map/ppermute | solution.py:1171
  817.7 96.7 %collective-permute-start.14 = (bf16[1024,1408]{1,0:T(8,128)(2,1)}, bf16[1024,1408]{1,0:T(8,128)(2,1)}, u32[]{:S(2)}, u32[]{:S(2)}) collective-permute-start(bf16[1024,1408]{1,0:T(8,128)(2,1)} %get-tuple-element.191), channel_id=1, source_target_pairs={{0,16},{16,0},{1,17},{17,1},{2,18},{18,2},{3,19},{19,3},{4,20},{20... | collective-permute-start | bytes 8650760 | tf_op jit(solution)/shard_map/ppermute | solution.py:1171
  840.7 4.5 collective-permute-start.7
  914.4 9.8 %copy-start.1 = (bf16[128,2048]{1,0:T(8,128)(2,1)S(1)}, bf16[128,2048]{1,0:T(8,128)(2,1)}, u32[]{:S(2)}) copy-start(bf16[128,2048]{1,0:T(8,128)(2,1)} %param.30) | copy-start | bytes 1572868
  (51 other events, 189.4 us)
Sparse Core Ops, SparseCore 0:
  167.3 124.5 all-gather.2
  343.7 99.2 all-gather.4

commit v10 on v9

--- a/solution.py
+++ b/solution.py
@@ -388,7 +388,7 @@
                 loads[2 * j + 1].wait()
             lax.fori_loop(low, high, lambda i, c, j=j: (tile(j, i), c)[1], 0)
 
-    steps = [(j, k) for j in range(m) for k in order]
+    steps = [(j, k) for k in order for j in range(m)]
     ahead = 3 if jobs else 2
     for i in range(min(ahead, len(steps))):
         stage_one(*steps[i])
@@ -1157,11 +1157,9 @@
         + product("td,ad->ta", jnp.where(even, mid_right, mid_left), out_w_other)
     ).astype(BF16)
     output_w_partial = product_over_groups(attended, grad_mid_b).astype(BF16)
-    output_w_partial, grad_attended = lax.optimization_barrier((output_w_partial, grad_attended))
     (grad_att_blocks,) = exchange(
         5, swaps=(grad_attended.reshape(tokens, HEADS, VH).transpose(1, 0, 2),)
     )
-    *products, grad_att_blocks = lax.optimization_barrier((*products, grad_att_blocks))
     grad_att = grad_att_blocks.reshape(length, VH)
 
     def blocks_over_groups(blocks):

time: 939 us -> 925 us (0.985)
  Pallas kernels: 728 us -> 706 us
    pallas_call x5, Pallas kernels: 341 us -> 319 us  [exchange(): pl.pallas_call(functools.partial(exchange_kernel, n, m, w, laid, groups,...]
    ppermute x7, starting transfers between devices: 13.7 us -> 2.12 us  [blocks_over_groups(): total = total + lax.ppermute(blocks[k], 'grp', shift).astype(F32)]
    ppermute x1, starting transfers between devices: 0.01 us -> 10.1 us  [per_device(): small = mine + lax.ppermute(theirs, 'grp', [(0, 1), (1, 0)])]
    unnamed x138 -> x140, local copies, waits for them, and re-layouts: 28.2 us -> 36.2 us
  transfers between devices with their start and end apart: 19 -> 19, of which waited for: 1 -> 0; matrix products, arithmetic and copies ran while one was open for 14% -> 13% of each run, Pallas kernels for 62% -> 55%
where the time goes in v10:
time: 925 us; the launch traced here: 917 us
  Pallas kernels  706 us (76%)
  local copies, waits for them, and re-layouts  87.9 us (10%)
  other arithmetic  49.4 us (5%)
  matrix products  44.3 us (5%)
  between operations  16 us (2%)
  starting transfers between devices  13.9 us (2%)
    pallas_call x5, Pallas kernels, exchange(): pl.pallas_call(functools.partial(exchange_kernel, n, m, w, laid, groups,...  319 us
    pallas_call x2, Pallas kernels, gather(): pl.pallas_call(functools.partial(gather_kernel, n, w), out_shape=[jax.Sha...  245 us
    pallas_call x1, Pallas kernels, ffn(): pl.pallas_call(functools.partial(ffn_kernel, n), grid=(n // group,), in_s...  93.8 us
    dot_general x14, matrix products, product(): return jnp.einsum(form, left, right, preferred_element_type=F32)  44.3 us
    unnamed x140, local copies, waits for them, and re-layouts  36.2 us
  transfers between devices with their start and end apart: 19, of which 0 were waited for; matrix products, arithmetic and copies ran while one was open for 13% of the time, Pallas kernels for 55%

profile of v10, /device:TPU:0, one launch (start us, length us, event | category | flops | bytes accessed | tf_op | source)
XLA Modules:
  0.0 917.2 jit_solution(17217560441902290749)
XLA Ops:
  20.7 146.5 %gather.2 = (bf16[16,128,3712]{2,1,0:T(8,128)(2,1)}, bf16[16,96,128]{2,1,0:T(8,128)(2,1)}, bf16[16,32,128]{2,1,0:T(8,128)(2,1)}, bf16[16,176,128]{2,1,0:T(8,128)(2,1)}, bf16[16,16,128]{2,1,0:T(8,128)(2,1)}) custom-call(bf16[128,3712]{1,0:T(8,128)(2,1)} %pad.30.x_ref, bf16[16,96,128]{2,1,0:T(8,128)(2,1)} %dynamic-slice_bitcast_fusion.2.refs_0_, ...), custom_call_target="tpu_custom_call" | custom-call | tf_op jit(solution)/shard_map/gather/pallas_call | solution.py:207
  168.9 2.1 slice.145
  172.1 2.1 pad_maximum_fusion.wl_ref
  176.0 18.2 %front.1 = (bf16[2048,2048]{1,0:T(8,128)(2,1)}, bf16[2048,256]{1,0:T(8,128)(2,1)S(1)}, bf16[2048,256]{1,0:T(8,128)(2,1)S(1)}, bf16[2048,128]{1,0:T(8,128)(2,1)S(...) custom-call(bf16[16,128,3712]{2,1,0:T(8,128)(2,1)} %get-tuple-element.115.x_ref.w_ref, ...), custom_call_target="tpu_custom_call" | custom-call | tf_op jit(solution)/shard_map/front/pallas_call | solution.py:583
  204.0 12.7 %attend.1 = (bf16[2048,128]{1,0:T(8,128)(2,1)S(1)}, f32[2048,128]{1,0:T(8,128)S(1)}, f32[1,2048]{1,0:T(1,128)S(1)}) custom-call(s32[1]{0:T(128)S(6)} %copy.82.prefix_ref, bf16[2048,256]{1,0:T(8,128)(2,1)S(1)} %get-tuple-element.120.q_ref, bf16[4,512,256]{2,1,0:T(8,128)(2,1)S(1)} %bitcast.151, bf16[4,128,512]{2,1,0:T(8,128)(2,1)S(1)} %copy-done.10), custom_call_target="tpu_custom_call" | custom-call | tf_op jit(solution)/shard_map/attend/pallas_call | solution.py:688
  218.5 15.1 %exchange.5 = bf16[16,128,128]{2,1,0:T(8,128)(2,1)} custom-call(bf16[16,128,128]{2,1,0:T(8,128)(2,1)} %bitcast.163), custom_call_target="tpu_custom_call" | custom-call | tf_op jit(solution)/shard_map/exchange/pallas_call | solution.py:470
  235.6 3.2 fusion.56
  238.8 3.0 broadcast_select_fusion.5
  244.9 98.7 %gather.3.x_ref = bf16[16,128,2048]{2,1,0:T(8,128)(2,1)} custom-call(bf16[128,2048]{1,0:T(8,128)(2,1)} %multiply_convert_fusion.x_ref), custom_call_target="tpu_custom_call" | custom-call | tf_op jit(solution)/shard_map/gather/pallas_call | solution.py:207
  352.1 2.2 pad.34.sd_ref
  360.4 93.8 %ffn.1 = (bf16[16,128,2048]{2,1,0:T(8,128)(2,1)}, bf16[16,128,2048]{2,1,0:T(8,128)(2,1)}, bf16[16,128,128]{2,1,0:T(8,128)(2,1)}, f32[16,128,128]{2,1,0:T(8,128)}...) custom-call(bf16[16,128,2048]{2,1,0:T(8,128)(2,1)} %gather.3.x_ref, ...), custom_call_target="tpu_custom_call" | custom-call | tf_op jit(solution)/shard_map/ffn/pallas_call | solution.py:889
  454.1 157.3 %exchange.6 = (f32[128,2048]{1,0:T(8,128)}, f32[128,128]{1,0:T(8,128)}, f32[128,2048]{1,0:T(8,128)}, bf16[704,2048]{1,0:T(8,128)(2,1)}, bf16[704,2048]{1,0:T(8,1...) custom-call(bf16[4,2,2,128,2048]{4,3,2,1,0:T(8,128)(2,1)} %bitcast.1, ...), custom_call_target="tpu_custom_call" | custom-call | tf_op jit(solution)/shard_map/exchange/pallas_call | solution.py:470
  614.8 2.7 multiply_reduce_fusion
  618.9 3.3 convolution_convert_fusion
  623.0 3.0 multiply_reduce_fusion.6
  626.9 3.9 fusion.32
  630.8 4.5 fusion
  639.4 13.0 %exchange.7 = bf16[16,128,128]{2,1,0:T(8,128)(2,1)} custom-call(bf16[16,128,128]{2,1,0:T(8,128)(2,1)} %bitcast.190), custom_call_target="tpu_custom_call" | custom-call | tf_op jit(solution)/shard_map/exchange/pallas_call | solution.py:470
  664.4 15.1 %attend_back.1 = (f32[2048,256]{1,0:T(8,128)S(1)}, f32[4,512,256]{2,1,0:T(8,128)S(1)}, f32[4,512,128]{2,1,0:T(8,128)S(1)}) custom-call(s32[1]{0:T(128)S(6)} %copy.82.prefix_ref, bf16[2048,256]{1,0:T(8,128)(2,1)S(1)} %get-tuple-element.120.q_ref, bf16[2048,128]{1,0:T(8,128)(2,1)S(1)} %bitcast.149, f32[1,2048]{1,0:T(1,128)S(1)} %get-tuple-element.139.lse_ref, ...), custom_call_target="tpu_custom_call" | custom-call | tf_op jit(solution)/shard_map/attend_back/pallas_call | solution.py:746
  685.5 6.6 add_bitcast_fusion
  692.1 5.1 add_bitcast_fusion.1
  697.2 5.0 add_bitcast_fusion.2
  702.2 5.4 add_convert_fusion
  707.6 80.7 %exchange.8 = (f32[128,512]{1,0:T(8,128)}, f32[128,128]{1,0:T(8,128)}, f32[64,2048]{1,0:T(8,128)}, bf16[16,128,256]{2,1,0:T(8,128)(2,1)}, bf16[256,2048]{1,0:T(8...) custom-call(bf16[4,2,2,128,512]{4,3,2,1,0:T(8,128)(2,1)} %bitcast.15, ...), custom_call_target="tpu_custom_call" | custom-call | tf_op jit(solution)/shard_map/exchange/pallas_call | solution.py:470
  791.4 2.1 dynamic-slice_bitcast_fusion
  799.7 5.2 fusion.57
  813.1 5.2 convolution_add_fusion.3
  818.4 2.7 fusion.13
  825.1 10.1 %collective-permute-start.7 = (f32[16,1168]{1,0:T(8,128)S(1)}, f32[16,1168]{1,0:T(8,128)S(1)}, u32[]{:S(2)}, u32[]{:S(2)}) collective-permute-start(f32[16,1168]{1,0:T(8,128)S(1)} %dynamic-slice_bitcast_fusion.4), channel_id=1, source_target_pairs={{0,16},{16,0},{1,17},{17,1},{2,18},{18,2},{3,19},{19,3},{4,20},{20... | collective-permute-start | bytes 224264 | tf_op jit(solution)/shard_map/ppermute | solution.py:1264
  835.9 3.8 fusion.12
  839.8 52.8 %exchange.9 = (f32[64,640]{1,0:T(8,128)S(1)}, f32[16,1,1168]{2,1,0:T(1,128)S(1)}, f32[64,3072]{1,0:T(8,128)S(1)}, f32[64,2816]{1,0:T(8,128)S(1)}, f32[64,2816]{1,0:T(8,128)S(1)}, /*index=5*/f32[16,4096]{1,0:T(8,128)S(1)}) custom-call(bf16[4,2,2,64,640]{4,3,2,1,0:T(8,128)(2,1)S(1)} %bitcast.148, f32[16,1,1168]{2,1,0:T(1,128)S(1)} %broadcast_in_dim.24.refs_1_, ...), custom_call_target="tpu_custom_call" | custom-call | tf_op jit(solution)/shard_map/exchange/pallas_call | solution.py:470
  900.1 2.1 copy.83
  (278 shorter events, 114.3 us)
Async XLA Ops:
  7.2 10.5 %copy-start = (bf16[128,2048]{1,0:T(8,128)(2,1)S(1)}, bf16[128,2048]{1,0:T(8,128)(2,1)}, u32[]{:S(2)}) copy-start(bf16[128,2048]{1,0:T(8,128)(2,1)} %param.30) | copy-start | bytes 1572868
  7.2 9.3 %copy-start.42 = (bf16[128,2816]{1,0:T(8,128)(2,1)S(1)}, bf16[128,2816]{1,0:T(8,128)(2,1)}, u32[]{:S(2)}) copy-start(bf16[128,2816]{1,0:T(8,128)(2,1)} %param.33) | copy-start | bytes 2162692
  7.2 9.3 %copy-start.43 = (bf16[128,2816]{1,0:T(8,128)(2,1)S(1)}, bf16[128,2816]{1,0:T(8,128)(2,1)}, u32[]{:S(2)}) copy-start(bf16[128,2816]{1,0:T(8,128)(2,1)} %param.34) | copy-start | bytes 2162692
  7.2 10.5 %copy-start.26 = (bf16[128,2048]{1,0:T(8,128)(2,1)S(1)}, bf16[128,2048]{1,0:T(8,128)(2,1)}, u32[]{:S(2)}) copy-start(bf16[128,2048]{1,0:T(8,128)(2,1)} %param.24) | copy-start | bytes 1572868
  7.2 353.1 %all-gather.3.cloned.1.call-start = ((), (), s32[]{:S(2)}) async-start(), calls=%async_computation | async-start | bytes 8912896 | tf_op jit(solution)/shard_map/all_gather | solution.py:1052
  167.2 518.3 %all-gather.5.cloned.1.call-start = ((), (), s32[]{:S(2)}) async-start(), calls=%async_computation.1 | async-start | bytes 6684672 | tf_op jit(solution)/shard_map/all_gather | solution.py:1096
  167.3 7.1 collective-permute-start.1
  168.4 6.1 collective-permute-start
  174.3 67.6 %copy-start.50 = (f32[16,1,128]{2,1,0:T(1,128)}, f32[16,1,128]{2,1,0:T(1,128)S(1)}, u32[]{:S(2)}) copy-start(f32[16,1,128]{2,1,0:T(1,128)S(1)} %get-tuple-element.207) | copy-start | bytes 24580
  196.0 42.8 %collective-permute-start.2 = (bf16[2048,1024]{1,0:T(8,128)(2,1)}, bf16[2048,1024]{1,0:T(8,128)(2,1)}, u32[]{:S(2)}, u32[]{:S(2)}) collective-permute-start(bf16[2048,1024]{1,0:T(8,128)(2,1)} %get-tuple-element.124), channel_id=1, source_target_pairs={{0,16},{16,0},{1,17},{17,1},{2,18},{18,2},{3,19},{19,3},{4,20},{20... | collective-permute-start | bytes 12582920 | tf_op jit(solution)/shard_map/ppermute | solution.py:520
  197.9 44.0 %copy-start.58 = (f32[128]{0:T(128)}, f32[128]{0:T(128)S(1)}, u32[]{:S(2)}) copy-start(f32[128]{0:T(128)S(1)} %add_rsqrt_fusion.1) | copy-start | bytes 1540
  243.0 374.5 %copy-start.57 = (f32[128]{0:T(128)}, f32[128]{0:T(128)S(1)}, u32[]{:S(2)}) copy-start(f32[128]{0:T(128)S(1)} %add_rsqrt_fusion.2) | copy-start | bytes 1540
  345.7 10.8 %collective-permute-start.3 = (bf16[176,2048]{1,0:T(8,128)(2,1)}, bf16[176,2048]{1,0:T(8,128)(2,1)}, u32[]{:S(2)}, u32[]{:S(2)}) collective-permute-start(bf16[176,2048]{1,0:T(8,128)(2,1)} %copy_bitcast_fusion), channel_id=1, source_target_pairs={{0,16},{16,0},{1,17},{17,1},{2,18},{18,2},{3,19},{19,3},{4,20},{20... | collective-permute-start | bytes 2162696 | tf_op jit(solution)/shard_map/ppermute | solution.py:520
  454.1 160.7 %copy-start.37 = (bf16[16,128,16]{2,1,0:T(8,128)(2,1)S(1)}, bf16[16,128,16]{2,1,0:T(8,128)(2,1)}, u32[]{:S(2)}) copy-start(bf16[16,128,16]{2,1,0:T(8,128)(2,1)} %slice.150) | copy-start | bytes 196612
  611.5 74.0 %collective-permute-start.16 = (bf16[704,2048]{1,0:T(8,128)(2,1)}, bf16[704,2048]{1,0:T(8,128)(2,1)}, u32[]{:S(2)}, u32[]{:S(2)}) collective-permute-start(bf16[704,2048]{1,0:T(8,128)(2,1)} %get-tuple-element.177), channel_id=1, source_target_pairs={{0,16},{16,0},{1,17},{17,1},{2,18},{18,2},{3,19},{19,3},{4,20},{20... | collective-permute-start | bytes 8650760 | tf_op jit(solution)/shard_map/ppermute | solution.py:1169
  611.6 80.5 %collective-permute-start.15 = (bf16[1024,1408]{1,0:T(8,128)(2,1)}, bf16[1024,1408]{1,0:T(8,128)(2,1)}, u32[]{:S(2)}, u32[]{:S(2)}) collective-permute-start(bf16[1024,1408]{1,0:T(8,128)(2,1)} %get-tuple-element.175), channel_id=1, source_target_pairs={{0,16},{16,0},{1,17},{17,1},{2,18},{18,2},{3,19},{19,3},{4,20},{20... | collective-permute-start | bytes 8650760 | tf_op jit(solution)/shard_map/ppermute | solution.py:1169
  622.2 80.0 %collective-permute-start.4 = (bf16[1024,2048]{1,0:T(8,128)(2,1)}, bf16[1024,2048]{1,0:T(8,128)(2,1)}, u32[]{:S(2)}, u32[]{:S(2)}) collective-permute-start(bf16[1024,2048]{1,0:T(8,128)(2,1)} %convolution_convert_fusion), channel_id=1, source_target_pairs={{0,16},{16,0},{1,17},{17,1},{2,18},{18,2},{3,19},{19,3},{4,20},{20... | collective-permute-start | bytes 12582920 | tf_op jit(solution)/shard_map/ppermute | solution.py:514
  626.0 71.2 %collective-permute-start.14 = (bf16[1024,1408]{1,0:T(8,128)(2,1)}, bf16[1024,1408]{1,0:T(8,128)(2,1)}, u32[]{:S(2)}, u32[]{:S(2)}) collective-permute-start(bf16[1024,1408]{1,0:T(8,128)(2,1)} %get-tuple-element.173), channel_id=1, source_target_pairs={{0,16},{16,0},{1,17},{17,1},{2,18},{18,2},{3,19},{19,3},{4,20},{20... | collective-permute-start | bytes 8650760 | tf_op jit(solution)/shard_map/ppermute | solution.py:1169
  685.5 127.6 %collective-permute-start.5 = (bf16[2048,1536]{1,0:T(8,128)(2,1)}, bf16[2048,1536]{1,0:T(8,128)(2,1)}, u32[]{:S(2)}, u32[]{:S(2)}) collective-permute-start(bf16[2048,1536]{1,0:T(8,128)(2,1)} %all-gather.5.cloned.1.call-done), channel_id=1, source_target_pairs={{0,16},{16,0},{1,17},{17,1},{2,18},{18,2},{3,19},{19,3},{4,20},{20... | collective-permute-start | bytes 18874376 | tf_op jit(solution)/shard_map/ppermute | solution.py:520
  788.4 9.9 %copy-start.49 = (f32[128,128]{1,0:T(8,128)S(1)}, f32[128,128]{1,0:T(8,128)}, u32[]{:S(2)}) copy-start(f32[128,128]{1,0:T(8,128)} %get-tuple-element.155) | copy-start | bytes 196612
  790.3 16.8 %collective-permute-start.12 = (bf16[88,2048]{1,0:T(8,128)(2,1)}, bf16[88,2048]{1,0:T(8,128)(2,1)}, u32[]{:S(2)}, u32[]{:S(2)}) collective-permute-start(bf16[88,2048]{1,0:T(8,128)(2,1)} %dynamic-slice_bitcast_fusion.3), channel_id=1, source_target_pairs={{0,16},{16,0},{1,17},{17,1},{2,18},{18,2},{3,19},{19,3},{4,20},{20... | collective-permute-start | bytes 1081352 | tf_op jit(solution)/shard_map/ppermute | solution.py:494
  790.3 15.1 %collective-permute-start.11 = (bf16[256,256]{1,0:T(8,128)(2,1)}, bf16[256,256]{1,0:T(8,128)(2,1)S(1)}, u32[]{:S(2)}, u32[]{:S(2)}) collective-permute-start(bf16[256,256]{1,0:T(8,128)(2,1)} %get-tuple-element.163), channel_id=1, source_target_pairs={{0,16},{16,0},{1,17},{17,1},{2,18},{18,2},{3,19},{19,3},{4,20},{20... | collective-permute-start | bytes 393224 | tf_op jit(solution)/shard_map/ppermute | solution.py:1169
  790.8 17.4 %collective-permute-start.10 = (bf16[1024,256]{1,0:T(8,128)(2,1)}, bf16[1024,256]{1,0:T(8,128)(2,1)}, u32[]{:S(2)}, u32[]{:S(2)}) collective-permute-start(bf16[1024,256]{1,0:T(8,128)(2,1)} %get-tuple-element.161), channel_id=1, source_target_pairs={{0,16},{16,0},{1,17},{17,1},{2,18},{18,2},{3,19},{19,3},{4,20},{20... | collective-permute-start | bytes 1572872 | tf_op jit(solution)/shard_map/ppermute | solution.py:1169
  790.9 19.4 %collective-permute-start.9 = (bf16[1024,256]{1,0:T(8,128)(2,1)}, bf16[1024,256]{1,0:T(8,128)(2,1)}, u32[]{:S(2)}, u32[]{:S(2)}) collective-permute-start(bf16[1024,256]{1,0:T(8,128)(2,1)} %get-tuple-element.159), channel_id=1, source_target_pairs={{0,16},{16,0},{1,17},{17,1},{2,18},{18,2},{3,19},{19,3},{4,20},{20... | collective-permute-start | bytes 1572872 | tf_op jit(solution)/shard_map/ppermute | solution.py:1169
  799.7 9.3 %copy-start.47 = (bf16[1024,256]{1,0:T(8,128)(2,1)S(1)}, bf16[1024,256]{1,0:T(8,128)(2,1)}, u32[]{:S(2)}) copy-start(bf16[1024,256]{1,0:T(8,128)(2,1)} %get-tuple-element.160) | copy-start | bytes 1572868
  805.5 7.0 collective-permute-start.6
  807.1 4.3 collective-permute-start.8
  808.3 3.3 collective-permute-start.13
  824.1 15.6 %copy-start.44 = (f32[16,2,1168]{2,0,1:T(8,128)S(1)}, f32[16,2,1168]{2,0,1:T(8,128)}, u32[]{:S(2)}) copy-start(f32[16,2,1168]{2,0,1:T(8,128)} %concatenate.38) | copy-start | bytes 448516
  825.1 14.6 %collective-permute-start.7 = (f32[16,1168]{1,0:T(8,128)S(1)}, f32[16,1168]{1,0:T(8,128)S(1)}, u32[]{:S(2)}, u32[]{:S(2)}) collective-permute-start(f32[16,1168]{1,0:T(8,128)S(1)} %dynamic-slice_bitcast_fusion.4), channel_id=1, source_target_pairs={{0,16},{16,0},{1,17},{17,1},{2,18},{18,2},{3,19},{19,3},{4,20},{20... | collective-permute-start | bytes 224264 | tf_op jit(solution)/shard_map/ppermute | solution.py:1264
  839.8 70.4 %copy-start.1 = (bf16[128,2048]{1,0:T(8,128)(2,1)S(1)}, bf16[128,2048]{1,0:T(8,128)(2,1)}, u32[]{:S(2)}) copy-start(bf16[128,2048]{1,0:T(8,128)(2,1)} %param.30) | copy-start | bytes 1572868
  897.3 12.0 %copy-start.15 = (f32[64,2816]{1,0:T(8,128)S(1)}, f32[64,2816]{1,0:T(8,128)}, u32[]{:S(2)}) copy-start(f32[64,2816]{1,0:T(8,128)} %copy-done.14) | copy-start | bytes 2162692
  (52 other events, 177.5 us)
Sparse Core Ops, SparseCore 0:
  167.3 124.6 all-gather.2
  343.7 98.8 all-gather.4

commit v11 on v10

--- a/solution.py
+++ b/solution.py
@@ -1256,14 +1256,6 @@
         ],
         axis=2,
     )
-    small = small.transpose(1, 0, 2)
-    if groups == 2:
-        g = lax.axis_index("grp")
-        mine = lax.dynamic_index_in_dim(small, g, 0, keepdims=False)
-        theirs = lax.dynamic_index_in_dim(small, 1 - g, 0, keepdims=False)
-        small = mine + lax.ppermute(theirs, "grp", [(0, 1), (1, 0)])
-    else:
-        small = lax.psum_scatter(small, "grp", scatter_dimension=0)
     (
         latent_weight_sum,
         small_all,
@@ -1275,7 +1267,7 @@
         7,
         sums=(latent_w_partial.reshape(n, rows_out, -1),),
         swaps=(
-            small[:, None],
+            small,
             side_query.reshape(n, rows_out, -1),
             side_gate.reshape(n, rows_out, -1),
             side_up.reshape(n, rows_out, -1),
@@ -1287,7 +1279,14 @@
         grad_mid + norm_back(grad_normed * attn_gain, input_unit, input_scale)
     ).astype(BF16)
     latent_weight_grad = latent_weight_sum[:, : LATENT + ROPE]
-    small_sum = jnp.sum(small_all[:, 0], axis=0)
+    small_sum = jnp.sum(small_all, axis=0)
+    if groups == 2:
+        g = lax.axis_index("grp")
+        mine = lax.dynamic_index_in_dim(small_sum, g, 0, keepdims=False)
+        theirs = lax.dynamic_index_in_dim(small_sum, 1 - g, 0, keepdims=False)
+        small_sum = mine + lax.ppermute(theirs, "grp", [(0, 1), (1, 0)])
+    else:
+        small_sum = lax.psum_scatter(small_sum, "grp", scatter_dimension=0)
     attention_gain_grad = small_sum[:rows_out]
     feedforward_gain_grad = small_sum[rows_out : 2 * rows_out]
     router_weight_grad = small_sum[2 * rows_out : (2 + n) * rows_out].reshape(n, rows_out).T

time: 925 us -> 919 us (level)
  Pallas kernels: 706 us -> 718 us
  local copies, waits for them, and re-layouts: 87.9 us -> 77.4 us
  starting transfers between devices: 13.9 us -> 4.29 us
    pallas_call x5, Pallas kernels: 319 us -> 332 us  [exchange(): pl.pallas_call(functools.partial(exchange_kernel, n, m, w, laid, groups,...]
    ppermute x1, starting transfers between devices: 10.1 us -> 0.07 us  [per_device(): small_sum = mine + lax.ppermute(theirs, 'grp', [(0, 1), (1, 0)])]
    unnamed x140 -> x142, local copies, waits for them, and re-layouts: 36.2 us -> 30.7 us
  transfers between devices with their start and end apart: 19 -> 19, of which waited for: 0 -> 0; matrix products, arithmetic and copies ran while one was open for 13% -> 13% of each run, Pallas kernels for 55% -> 56%
where the time goes in v11:
time: 919 us; the launch traced here: 910 us
  Pallas kernels  718 us (78%)
  local copies, waits for them, and re-layouts  77.4 us (8%)
  other arithmetic  49.7 us (5%)
  matrix products  44.2 us (5%)
  between operations  16.1 us (2%)
    pallas_call x5, Pallas kernels, exchange(): pl.pallas_call(functools.partial(exchange_kernel, n, m, w, laid, groups,...  332 us
    pallas_call x2, Pallas kernels, gather(): pl.pallas_call(functools.partial(gather_kernel, n, w), out_shape=[jax.Sha...  245 us
    pallas_call x1, Pallas kernels, ffn(): pl.pallas_call(functools.partial(ffn_kernel, n), grid=(n // group,), in_s...  93.8 us
    dot_general x14, matrix products, product(): return jnp.einsum(form, left, right, preferred_element_type=F32)  44.2 us
    unnamed x142, local copies, waits for them, and re-layouts  30.7 us
  transfers between devices with their start and end apart: 19, of which 0 were waited for; matrix products, arithmetic and copies ran while one was open for 13% of the time, Pallas kernels for 56%

profile of v11, /device:TPU:0, one launch (start us, length us, event | category | flops | bytes accessed | tf_op | source)
XLA Modules:
  0.0 909.8 jit_solution(4482260101068705674)
XLA Ops:
  20.7 146.5 %gather.2 = (bf16[16,128,3712]{2,1,0:T(8,128)(2,1)}, bf16[16,96,128]{2,1,0:T(8,128)(2,1)}, bf16[16,32,128]{2,1,0:T(8,128)(2,1)}, bf16[16,176,128]{2,1,0:T(8,128)(2,1)}, bf16[16,16,128]{2,1,0:T(8,128)(2,1)}) custom-call(bf16[128,3712]{1,0:T(8,128)(2,1)} %pad.30.x_ref, bf16[16,96,128]{2,1,0:T(8,128)(2,1)} %dynamic-slice_bitcast_fusion.2.refs_0_, ...), custom_call_target="tpu_custom_call" | custom-call | tf_op jit(solution)/shard_map/gather/pallas_call | solution.py:207
  168.9 2.1 slice.145
  172.1 2.1 pad_maximum_fusion.wl_ref
  176.0 18.2 %front.1 = (bf16[2048,2048]{1,0:T(8,128)(2,1)}, bf16[2048,256]{1,0:T(8,128)(2,1)S(1)}, bf16[2048,256]{1,0:T(8,128)(2,1)S(1)}, bf16[2048,128]{1,0:T(8,128)(2,1)S(...) custom-call(bf16[16,128,3712]{2,1,0:T(8,128)(2,1)} %get-tuple-element.115.x_ref.w_ref, ...), custom_call_target="tpu_custom_call" | custom-call | tf_op jit(solution)/shard_map/front/pallas_call | solution.py:583
  204.0 12.7 %attend.1 = (bf16[2048,128]{1,0:T(8,128)(2,1)S(1)}, f32[2048,128]{1,0:T(8,128)S(1)}, f32[1,2048]{1,0:T(1,128)S(1)}) custom-call(s32[1]{0:T(128)S(6)} %copy.91.prefix_ref, bf16[2048,256]{1,0:T(8,128)(2,1)S(1)} %get-tuple-element.120.q_ref, bf16[4,512,256]{2,1,0:T(8,128)(2,1)S(1)} %bitcast.151, bf16[4,128,512]{2,1,0:T(8,128)(2,1)S(1)} %copy-done.10), custom_call_target="tpu_custom_call" | custom-call | tf_op jit(solution)/shard_map/attend/pallas_call | solution.py:688
  218.4 15.1 %exchange.5 = bf16[16,128,128]{2,1,0:T(8,128)(2,1)} custom-call(bf16[16,128,128]{2,1,0:T(8,128)(2,1)} %bitcast.163), custom_call_target="tpu_custom_call" | custom-call | tf_op jit(solution)/shard_map/exchange/pallas_call | solution.py:470
  233.5 2.0 copy.52
  235.6 3.1 fusion.56
  238.8 3.0 broadcast_select_fusion.5
  244.9 98.1 %gather.3.x_ref = bf16[16,128,2048]{2,1,0:T(8,128)(2,1)} custom-call(bf16[128,2048]{1,0:T(8,128)(2,1)} %multiply_convert_fusion.x_ref), custom_call_target="tpu_custom_call" | custom-call | tf_op jit(solution)/shard_map/gather/pallas_call | solution.py:207
  343.0 2.0 copy_bitcast_fusion
  351.4 2.2 pad.34.sd_ref
  359.7 93.8 %ffn.1 = (bf16[16,128,2048]{2,1,0:T(8,128)(2,1)}, bf16[16,128,2048]{2,1,0:T(8,128)(2,1)}, bf16[16,128,128]{2,1,0:T(8,128)(2,1)}, f32[16,128,128]{2,1,0:T(8,128)}...) custom-call(bf16[16,128,2048]{2,1,0:T(8,128)(2,1)} %gather.3.x_ref, ...), custom_call_target="tpu_custom_call" | custom-call | tf_op jit(solution)/shard_map/ffn/pallas_call | solution.py:889
  453.5 157.9 %exchange.6 = (f32[128,2048]{1,0:T(8,128)}, f32[128,128]{1,0:T(8,128)}, f32[128,2048]{1,0:T(8,128)}, bf16[704,2048]{1,0:T(8,128)(2,1)}, bf16[704,2048]{1,0:T(8,1...) custom-call(bf16[4,2,2,128,2048]{4,3,2,1,0:T(8,128)(2,1)} %bitcast.1, ...), custom_call_target="tpu_custom_call" | custom-call | tf_op jit(solution)/shard_map/exchange/pallas_call | solution.py:470
  614.8 2.7 multiply_reduce_fusion
  618.8 3.3 convolution_convert_fusion
  622.9 3.0 multiply_reduce_fusion.6
  626.9 3.9 fusion.32
  630.7 4.5 fusion
  639.3 13.0 %exchange.7 = bf16[16,128,128]{2,1,0:T(8,128)(2,1)} custom-call(bf16[16,128,128]{2,1,0:T(8,128)(2,1)} %bitcast.190), custom_call_target="tpu_custom_call" | custom-call | tf_op jit(solution)/shard_map/exchange/pallas_call | solution.py:470
  663.7 15.1 %attend_back.1 = (f32[2048,256]{1,0:T(8,128)S(1)}, f32[4,512,256]{2,1,0:T(8,128)S(1)}, f32[4,512,128]{2,1,0:T(8,128)S(1)}) custom-call(s32[1]{0:T(128)S(6)} %copy.91.prefix_ref, bf16[2048,256]{1,0:T(8,128)(2,1)S(1)} %get-tuple-element.120.q_ref, bf16[2048,128]{1,0:T(8,128)(2,1)S(1)} %bitcast.149, f32[1,2048]{1,0:T(1,128)S(1)} %get-tuple-element.139.lse_ref, ...), custom_call_target="tpu_custom_call" | custom-call | tf_op jit(solution)/shard_map/attend_back/pallas_call | solution.py:746
  684.8 6.6 add_bitcast_fusion
  691.4 5.1 add_bitcast_fusion.1
  696.5 5.0 add_bitcast_fusion.2
  701.5 5.4 add_convert_fusion
  706.9 80.7 %exchange.8 = (f32[128,512]{1,0:T(8,128)}, f32[128,128]{1,0:T(8,128)}, f32[64,2048]{1,0:T(8,128)}, bf16[16,128,256]{2,1,0:T(8,128)(2,1)}, bf16[256,2048]{1,0:T(8...) custom-call(bf16[4,2,2,128,512]{4,3,2,1,0:T(8,128)(2,1)} %bitcast.15, ...), custom_call_target="tpu_custom_call" | custom-call | tf_op jit(solution)/shard_map/exchange/pallas_call | solution.py:470
  790.6 2.1 dynamic-slice_bitcast_fusion
  798.4 5.2 fusion.57
  811.8 5.2 convolution_add_fusion.3
  817.0 2.6 fusion.13
  819.9 65.3 %exchange.9 = (f32[64,640]{1,0:T(8,128)S(1)}, f32[16,2,1168]{2,1,0:T(2,128)S(1)}, f32[64,3072]{1,0:T(8,128)S(1)}, f32[64,2816]{1,0:T(8,128)S(1)}, f32[64,2816]{1,0:T(8,128)S(1)}, /*index=5*/f32[16,4096]{1,0:T(8,128)S(1)}) custom-call(bf16[4,2,2,64,640]{4,3,2,1,0:T(8,128)(2,1)S(1)} %bitcast.148, f32[16,2,1168]{2,1,0:T(2,128)S(1)} %concatenate.38.refs_1_, ...), custom_call_target="tpu_custom_call" | custom-call | tf_op jit(solution)/shard_map/exchange/pallas_call | solution.py:470
  891.0 4.1 fusion.12
  (281 shorter events, 102.4 us)
Async XLA Ops:
  7.2 10.5 %copy-start = (bf16[128,2048]{1,0:T(8,128)(2,1)S(1)}, bf16[128,2048]{1,0:T(8,128)(2,1)}, u32[]{:S(2)}) copy-start(bf16[128,2048]{1,0:T(8,128)(2,1)} %param.30) | copy-start | bytes 1572868
  7.2 9.3 %copy-start.44 = (bf16[128,2816]{1,0:T(8,128)(2,1)S(1)}, bf16[128,2816]{1,0:T(8,128)(2,1)}, u32[]{:S(2)}) copy-start(bf16[128,2816]{1,0:T(8,128)(2,1)} %param.33) | copy-start | bytes 2162692
  7.2 9.3 %copy-start.45 = (bf16[128,2816]{1,0:T(8,128)(2,1)S(1)}, bf16[128,2816]{1,0:T(8,128)(2,1)}, u32[]{:S(2)}) copy-start(bf16[128,2816]{1,0:T(8,128)(2,1)} %param.34) | copy-start | bytes 2162692
  7.2 10.5 %copy-start.28 = (bf16[128,2048]{1,0:T(8,128)(2,1)S(1)}, bf16[128,2048]{1,0:T(8,128)(2,1)}, u32[]{:S(2)}) copy-start(bf16[128,2048]{1,0:T(8,128)(2,1)} %param.24) | copy-start | bytes 1572868
  7.2 352.5 %all-gather.3.cloned.1.call-start = ((), (), s32[]{:S(2)}) async-start(), calls=%async_computation | async-start | bytes 8912896 | tf_op jit(solution)/shard_map/all_gather | solution.py:1052
  167.2 517.6 %all-gather.5.cloned.1.call-start = ((), (), s32[]{:S(2)}) async-start(), calls=%async_computation.1 | async-start | bytes 6684672 | tf_op jit(solution)/shard_map/all_gather | solution.py:1096
  167.3 7.1 collective-permute-start.1
  168.4 6.1 collective-permute-start
  174.3 67.5 %copy-start.51 = (f32[16,1,128]{2,1,0:T(1,128)}, f32[16,1,128]{2,1,0:T(1,128)S(1)}, u32[]{:S(2)}) copy-start(f32[16,1,128]{2,1,0:T(1,128)S(1)} %get-tuple-element.209) | copy-start | bytes 24580
  195.9 42.8 %collective-permute-start.2 = (bf16[2048,1024]{1,0:T(8,128)(2,1)}, bf16[2048,1024]{1,0:T(8,128)(2,1)}, u32[]{:S(2)}, u32[]{:S(2)}) collective-permute-start(bf16[2048,1024]{1,0:T(8,128)(2,1)} %get-tuple-element.124), channel_id=1, source_target_pairs={{0,16},{16,0},{1,17},{17,1},{2,18},{18,2},{3,19},{19,3},{4,20},{20... | collective-permute-start | bytes 12582920 | tf_op jit(solution)/shard_map/ppermute | solution.py:520
  197.9 43.9 %copy-start.59 = (f32[128]{0:T(128)}, f32[128]{0:T(128)S(1)}, u32[]{:S(2)}) copy-start(f32[128]{0:T(128)S(1)} %add_rsqrt_fusion.1) | copy-start | bytes 1540
  242.9 374.5 %copy-start.58 = (f32[128]{0:T(128)}, f32[128]{0:T(128)S(1)}, u32[]{:S(2)}) copy-start(f32[128]{0:T(128)S(1)} %add_rsqrt_fusion.2) | copy-start | bytes 1540
  345.0 10.8 %collective-permute-start.3 = (bf16[176,2048]{1,0:T(8,128)(2,1)}, bf16[176,2048]{1,0:T(8,128)(2,1)}, u32[]{:S(2)}, u32[]{:S(2)}) collective-permute-start(bf16[176,2048]{1,0:T(8,128)(2,1)} %copy_bitcast_fusion), channel_id=1, source_target_pairs={{0,16},{16,0},{1,17},{17,1},{2,18},{18,2},{3,19},{19,3},{4,20},{20... | collective-permute-start | bytes 2162696 | tf_op jit(solution)/shard_map/ppermute | solution.py:520
  453.5 161.3 %copy-start.39 = (bf16[16,128,16]{2,1,0:T(8,128)(2,1)S(1)}, bf16[16,128,16]{2,1,0:T(8,128)(2,1)}, u32[]{:S(2)}) copy-start(bf16[16,128,16]{2,1,0:T(8,128)(2,1)} %slice.150) | copy-start | bytes 196612
  611.4 73.4 %collective-permute-start.16 = (bf16[704,2048]{1,0:T(8,128)(2,1)}, bf16[704,2048]{1,0:T(8,128)(2,1)}, u32[]{:S(2)}, u32[]{:S(2)}) collective-permute-start(bf16[704,2048]{1,0:T(8,128)(2,1)} %get-tuple-element.177), channel_id=1, source_target_pairs={{0,16},{16,0},{1,17},{17,1},{2,18},{18,2},{3,19},{19,3},{4,20},{20... | collective-permute-start | bytes 8650760 | tf_op jit(solution)/shard_map/ppermute | solution.py:1169
  611.5 79.9 %collective-permute-start.15 = (bf16[1024,1408]{1,0:T(8,128)(2,1)}, bf16[1024,1408]{1,0:T(8,128)(2,1)}, u32[]{:S(2)}, u32[]{:S(2)}) collective-permute-start(bf16[1024,1408]{1,0:T(8,128)(2,1)} %get-tuple-element.175), channel_id=1, source_target_pairs={{0,16},{16,0},{1,17},{17,1},{2,18},{18,2},{3,19},{19,3},{4,20},{20... | collective-permute-start | bytes 8650760 | tf_op jit(solution)/shard_map/ppermute | solution.py:1169
  622.1 79.3 %collective-permute-start.4 = (bf16[1024,2048]{1,0:T(8,128)(2,1)}, bf16[1024,2048]{1,0:T(8,128)(2,1)}, u32[]{:S(2)}, u32[]{:S(2)}) collective-permute-start(bf16[1024,2048]{1,0:T(8,128)(2,1)} %convolution_convert_fusion), channel_id=1, source_target_pairs={{0,16},{16,0},{1,17},{17,1},{2,18},{18,2},{3,19},{19,3},{4,20},{20... | collective-permute-start | bytes 12582920 | tf_op jit(solution)/shard_map/ppermute | solution.py:514
  625.9 70.6 %collective-permute-start.14 = (bf16[1024,1408]{1,0:T(8,128)(2,1)}, bf16[1024,1408]{1,0:T(8,128)(2,1)}, u32[]{:S(2)}, u32[]{:S(2)}) collective-permute-start(bf16[1024,1408]{1,0:T(8,128)(2,1)} %get-tuple-element.173), channel_id=1, source_target_pairs={{0,16},{16,0},{1,17},{17,1},{2,18},{18,2},{3,19},{19,3},{4,20},{20... | collective-permute-start | bytes 8650760 | tf_op jit(solution)/shard_map/ppermute | solution.py:1169
  684.8 126.9 %collective-permute-start.5 = (bf16[2048,1536]{1,0:T(8,128)(2,1)}, bf16[2048,1536]{1,0:T(8,128)(2,1)}, u32[]{:S(2)}, u32[]{:S(2)}) collective-permute-start(bf16[2048,1536]{1,0:T(8,128)(2,1)} %all-gather.5.cloned.1.call-done), channel_id=1, source_target_pairs={{0,16},{16,0},{1,17},{17,1},{2,18},{18,2},{3,19},{19,3},{4,20},{20... | collective-permute-start | bytes 18874376 | tf_op jit(solution)/shard_map/ppermute | solution.py:520
  787.7 9.4 %copy-start.50 = (f32[128,128]{1,0:T(8,128)S(1)}, f32[128,128]{1,0:T(8,128)}, u32[]{:S(2)}) copy-start(f32[128,128]{1,0:T(8,128)} %get-tuple-element.155) | copy-start | bytes 196612
  789.6 15.6 %collective-permute-start.12 = (bf16[88,2048]{1,0:T(8,128)(2,1)}, bf16[88,2048]{1,0:T(8,128)(2,1)}, u32[]{:S(2)}, u32[]{:S(2)}) collective-permute-start(bf16[88,2048]{1,0:T(8,128)(2,1)} %dynamic-slice_bitcast_fusion.3), channel_id=1, source_target_pairs={{0,16},{16,0},{1,17},{17,1},{2,18},{18,2},{3,19},{19,3},{4,20},{20... | collective-permute-start | bytes 1081352 | tf_op jit(solution)/shard_map/ppermute | solution.py:494
  789.6 14.6 %collective-permute-start.10 = (bf16[256,256]{1,0:T(8,128)(2,1)}, bf16[256,256]{1,0:T(8,128)(2,1)}, u32[]{:S(2)}, u32[]{:S(2)}) collective-permute-start(bf16[256,256]{1,0:T(8,128)(2,1)} %get-tuple-element.163), channel_id=1, source_target_pairs={{0,16},{16,0},{1,17},{17,1},{2,18},{18,2},{3,19},{19,3},{4,20},{20... | collective-permute-start | bytes 393224 | tf_op jit(solution)/shard_map/ppermute | solution.py:1169
  790.1 16.8 %collective-permute-start.9 = (bf16[1024,256]{1,0:T(8,128)(2,1)}, bf16[1024,256]{1,0:T(8,128)(2,1)}, u32[]{:S(2)}, u32[]{:S(2)}) collective-permute-start(bf16[1024,256]{1,0:T(8,128)(2,1)} %get-tuple-element.161), channel_id=1, source_target_pairs={{0,16},{16,0},{1,17},{17,1},{2,18},{18,2},{3,19},{19,3},{4,20},{20... | collective-permute-start | bytes 1572872 | tf_op jit(solution)/shard_map/ppermute | solution.py:1169
  790.1 18.7 %collective-permute-start.8 = (bf16[1024,256]{1,0:T(8,128)(2,1)}, bf16[1024,256]{1,0:T(8,128)(2,1)}, u32[]{:S(2)}, u32[]{:S(2)}) collective-permute-start(bf16[1024,256]{1,0:T(8,128)(2,1)} %get-tuple-element.159), channel_id=1, source_target_pairs={{0,16},{16,0},{1,17},{17,1},{2,18},{18,2},{3,19},{19,3},{4,20},{20... | collective-permute-start | bytes 1572872 | tf_op jit(solution)/shard_map/ppermute | solution.py:1169
  798.4 9.2 %copy-start.48 = (bf16[1024,256]{1,0:T(8,128)(2,1)S(1)}, bf16[1024,256]{1,0:T(8,128)(2,1)}, u32[]{:S(2)}) copy-start(bf16[1024,256]{1,0:T(8,128)(2,1)} %get-tuple-element.160) | copy-start | bytes 1572868
  804.2 7.0 collective-permute-start.6
  805.3 4.8 collective-permute-start.7
  806.9 3.3 collective-permute-start.13
  890.2 4.9 collective-permute-start.11
  891.0 10.0 %copy-start.18 = (f32[64,2816]{1,0:T(8,128)S(1)}, f32[64,2816]{1,0:T(8,128)}, u32[]{:S(2)}) copy-start(f32[64,2816]{1,0:T(8,128)} %copy-done.17) | copy-start | bytes 2162692
  891.0 10.9 %copy-start.16 = (f32[64,2816]{1,0:T(8,128)S(1)}, f32[64,2816]{1,0:T(8,128)}, u32[]{:S(2)}) copy-start(f32[64,2816]{1,0:T(8,128)} %copy-done.15) | copy-start | bytes 2162692
  891.0 11.7 %copy-start.1 = (bf16[128,2048]{1,0:T(8,128)(2,1)S(1)}, bf16[128,2048]{1,0:T(8,128)(2,1)}, u32[]{:S(2)}) copy-start(bf16[128,2048]{1,0:T(8,128)(2,1)} %param.30) | copy-start | bytes 1572868
  (53 other events, 193.7 us)
Sparse Core Ops, SparseCore 0:
  167.3 124.5 all-gather.2
  343.1 99.4 all-gather.4
